TPU v7x, 32 devices: a whole 2x2x4 slice. The times are simulated.
32 devices in a mesh: groups: 2 (over x), weight: 16 (over z, y, core).
Axes of the slice: x: 2, y: 2, z: 4, core: 2. Of those that a mesh axis runs over, the one named last changes fastest.
Arguments:
- hidden: bfloat16 [128, 8192], P(('groups', 'weight')), parts along dimension 0, may hold values from -6 to 6
- norm_gain: float32 [8192], replicated, may hold values from 0.1 to 1.9
- in_weight: bfloat16 [8192, 2, 8192], P(None, None, 'weight'), may hold values from -0.0625 to 0.0625
- conv_weight: float32 [4, 8192], P(None, 'weight'), may hold values from -0.6 to 0.6
- conv_offset: float32 [8192], P('weight'), may hold values from -0.5 to 0.5
- coef_weight: bfloat16 [8192, 544], P('weight'), may hold values from -0.0625 to 0.0625
- step_weight: bfloat16 [512, 8192], P(None, 'weight'), may hold values from -0.25 to 0.25
- step_bias: float32 [8192], P('weight'), may hold values from -3 to 0.5
- log_rates: float32 [16, 8192], P(None, 'weight'), may hold values from 0 to 2.77
- skip_gain: float32 [8192], P('weight'), may hold values from 0.5 to 1.5
- out_weight: bfloat16 [8192, 8192], P('weight'), may hold values from -0.0625 to 0.0625
- ssm_state: bfloat16 [128, 16, 8192], P('groups', None, 'weight'), parts along dimension 0, may hold values from -6 to 6
- conv_state: bfloat16 [128, 3, 8192], P('groups', None, 'weight'), parts along dimension 0, may hold values from -6 to 6
- live_counts: int32 [32], P('groups'), parts along dimension 0, may hold values from 1 to 3, as said below
Outputs:
- mixed: bfloat16 [128, 8192], P(('groups', 'weight')), parts along dimension 0
- new_state: bfloat16 [128, 16, 8192], P('groups', None, 'weight'), parts along dimension 0
- new_conv: bfloat16 [128, 3, 8192], P('groups', None, 'weight'), parts along dimension 0
There are 2 independent parts, one for each index of `groups`. A program takes and returns all parts, laid end to end along the dimension named above; an argument that names none is the same for every part. Nothing has to cross between parts.
Inputs may be any that keep to these rules, and one draw needn't show every extreme that they name: The live rows of a microbatch are its first live_counts rows; the most, 3, is reached by some microbatch.
All inputs are finite; a program needn't handle non-finite values.
Results may differ from a plain program's by a relative error of at most 0.0039.
Values may be sent and summed in bfloat16 or wider, within the bound.
No kernel may reach another device: no remote copies, remote signals or barrier semaphores. Data moves between devices by JAX's collectives and lax.ppermute only.
A program may use at most 64 MiB of HBM per device.

v0:
```python
import jax
import jax.numpy as jnp
from jax import lax
from jax.sharding import PartitionSpec as P

NSTATE = 16
DTR = 512
LIVE_MAX = 3


def rms_normed(hidden, norm_gain):
    wide = hidden.astype(jnp.float32)
    factor = lax.rsqrt(jnp.mean(wide * wide, axis=-1, keepdims=True) + 1e-05)
    return (wide * factor * norm_gain).astype(jnp.bfloat16)


def body(
    hidden,
    norm_gain,
    in_weight,
    conv_weight,
    conv_offset,
    coef_weight,
    step_weight,
    step_bias,
    log_rates,
    skip_gain,
    out_weight,
    ssm_state,
    conv_state,
    live_counts,
):
    devices = lax.axis_size("weight")
    rows_dev = hidden.shape[0]
    channels = in_weight.shape[2]
    states_n = ssm_state.shape[1]
    kept = LIVE_MAX
    normed = rms_normed(hidden[:kept], norm_gain)
    joined = in_weight.reshape(in_weight.shape[0], 2 * channels)
    both = jnp.dot(
        lax.all_gather(normed, "weight", axis=0, tiled=True),
        joined,
        preferred_element_type=jnp.float32,
    )
    total_rows = both.shape[0]
    conv_input = both[:, :channels].astype(jnp.bfloat16)
    gate_branch = both[:, channels:]
    state_grid = ssm_state.reshape(devices, rows_dev, states_n, channels)
    conv_grid = conv_state.reshape(devices, rows_dev, 3, channels)
    state_kept = state_grid[:, :kept].reshape(total_rows, states_n, channels)
    conv_kept = conv_grid[:, :kept].reshape(total_rows, 3, channels)
    row_ids = jnp.arange(total_rows, dtype=jnp.int32)
    per_row = jnp.repeat(live_counts, kept, total_repeat_length=total_rows)
    alive = row_ids % kept < per_row
    window = jnp.concatenate([conv_kept, conv_input[:, None, :]], axis=1)
    convolved = jnp.sum(window.astype(jnp.float32) * conv_weight[None], axis=1) + conv_offset
    mixed_x = jax.nn.silu(convolved).astype(jnp.bfloat16)
    partial_low = jnp.dot(mixed_x, coef_weight, preferred_element_type=jnp.float32)
    low_rank = lax.psum(partial_low, "weight")
    step_low = low_rank[:, :DTR].astype(jnp.bfloat16)
    in_coef = low_rank[:, DTR : DTR + NSTATE]
    out_coef = low_rank[:, DTR + NSTATE :]
    step_size = jax.nn.softplus(
        jnp.dot(step_low, step_weight, preferred_element_type=jnp.float32) + step_bias
    )
    x_wide = mixed_x.astype(jnp.float32)
    decays = jnp.exp(-step_size[:, None, :] * jnp.exp(log_rates)[None])
    old_state = state_kept.astype(jnp.float32)
    updated = decays * old_state + step_size[:, None, :] * in_coef[:, :, None] * x_wide[:, None, :]
    readout = jnp.sum(out_coef[:, :, None] * updated, axis=1) + skip_gain * x_wide
    gated_out = jnp.where(alive[:, None], readout * jax.nn.silu(gate_branch), 0.0).astype(
        jnp.bfloat16
    )
    block = lax.slice_in_dim(gated_out, 0, lax.axis_size("weight") * kept, axis=0)
    mixer_term = lax.psum_scatter(
        jnp.dot(block, out_weight, preferred_element_type=jnp.float32),
        "weight",
        scatter_dimension=0,
        tiled=True,
    )
    own_mixed = (hidden[:kept].astype(jnp.float32) + mixer_term).astype(jnp.bfloat16)
    mixed = jnp.concatenate([own_mixed, hidden[kept:]], axis=0)
    state_new_kept = jnp.where(alive[:, None, None], updated, old_state).astype(jnp.bfloat16)
    conv_new_kept = jnp.where(alive[:, None, None], window[:, 1:], conv_kept)
    new_state = jnp.concatenate(
        [state_new_kept.reshape(devices, kept, states_n, channels), state_grid[:, kept:]], axis=1
    ).reshape(ssm_state.shape)
    new_conv = jnp.concatenate(
        [conv_new_kept.reshape(devices, kept, 3, channels), conv_grid[:, kept:]], axis=1
    ).reshape(conv_state.shape)
    return (mixed, new_state, new_conv)


def solution(mesh):
    in_specs = (
        P(("groups", "weight"), None),
        P(),
        P(None, None, "weight"),
        P(None, "weight"),
        P("weight"),
        P("weight", None),
        P(None, "weight"),
        P("weight"),
        P(None, "weight"),
        P("weight"),
        P("weight", None),
        P("groups", None, "weight"),
        P("groups", None, "weight"),
        P("groups"),
    )
    out_specs = (
        P(("groups", "weight"), None),
        P("groups", None, "weight"),
        P("groups", None, "weight"),
    )
    return jax.shard_map(body, mesh=mesh, in_specs=in_specs, out_specs=out_specs, check_vma=False)
```

profile of v0, /device:TPU:0, one launch (start us, length us, event | category | flops | bytes accessed | tf_op | source)
XLA Modules:
  0.0 253.5 jit_solution(7793074444627123706)
XLA Ops:
  7.2 0.0 copy-start
  7.2 0.0 all-reduce.4.cloned.1.call-start
  7.2 1.1 fusion.4
  8.3 1.0 fusion.8
  9.3 26.2 %all-gather = bf16[16,3,8192]{2,1,0:T(4,128)(2,1)S(1)} all-gather(bf16[1,3,8192]{2,1,0:T(4,128)(2,1)S(1)} %fusion.8), channel_id=1, replica_groups=mesh['groups'=2,'weight'=16] {'weight'}, dimensions={0}, use_global_device_ids=true | all-gather | bytes 835584 | tf_op jit(solution)/shard_map/all_gather | solution.py:41
  35.5 0.7 reshape.164
  36.2 11.4 %copy.19 = bf16[1024,8,2,512]{3,1,2,0:T(8,128)(2,1)S(1)} copy(bf16[1024,8,2,512]{3,2,1,0:T(2,128)(2,1)} %bitcast.24) | data formatting | bytes 33554432
  47.6 0.0 copy-start.7
  47.6 0.0 copy-start.10
  47.6 0.0 copy-start.8
  47.7 3.1 %fusion.26 = f32[48,1024]{1,0:T(8,128)S(1)} fusion(bf16[48,8192]{1,0:T(8,128)(2,1)S(1)} %reshape.164, bf16[8192,1024]{1,0:T(8,128)(2,1)S(1)} %bitcast.23), kind=kOutput, calls=%fused_computation.53 | convolution fusion | flops 805306368 | bytes 17760256 | tf_op jit(solution)/shard_map/dot_general | solution.py:40
  50.8 0.0 copy-start.1
  50.8 0.0 copy-start.5
  50.8 0.0 copy-start.9
  50.8 0.1 reshape.148
  50.9 0.0 copy-start.4
  50.9 0.0 copy-start.12
  50.9 0.1 reshape.149
  51.1 0.9 fusion.23
  52.0 0.0 all-reduce.4.cloned.1.call-update
  52.1 0.0 all-reduce.6.cloned.1.call-start
  52.2 0.1 fusion.14
  52.3 0.8 gather_fusion
  53.0 0.1 gather.7
  53.1 0.6 fusion.16
  53.8 0.6 fusion.20
  54.3 0.1 copy.18
  54.4 0.6 exp.27
  55.0 80.8 %all-reduce.4.cloned.1.call-done = f32[48,544]{1,0:T(8,128)} async-done(((f32[48,544]{1,0:T(8,128)}), f32[48,544]{1,0:T(8,128)}) %all-reduce.4.cloned.1.call-update) | async-done | bytes 104464 | tf_op jit(solution)/shard_map/psum | solution.py:59
  135.8 0.9 fusion.24
  136.7 0.6 mul.130
  137.4 1.1 fusion.25
  138.6 0.6 mul.121
  139.2 1.7 fusion.1
  141.0 0.1 reduce_sum.35
  141.0 6.2 %fusion.9 = f32[48,8192]{1,0:T(8,128)} fusion(bf16[512,8192]{1,0:T(8,128)(2,1)} %param.26, f32[48,1024]{1,0:T(8,128)S(1)} %fusion.26, f32[48,512]{1,0:T(8,128)S(1)} %reduce_sum.35, f32[512]{0:T(512)} %param.25, pred[48]{0:T(512)(128)(4,1)} %fusion.20, f32[48,512]{1,0:T(8,128)S(1)} %multiply_reduce_fusion.1, f32[512]{0:T(512)} %param.20), kind=kOutput, calls=%fused_computation.31 | convolution fusion | flops 403046400 | bytes 10260528 | tf_op jit(solution)/shard_map/dot_general | solution.py:76
  147.2 0.0 all-reduce.6.cloned.1.call-update
  147.2 0.8 copy-done.3
  148.1 0.1 slice.76
  148.3 0.1 fusion.3
  148.3 0.1 reshape.153
  148.4 0.2 pad_maximum_fusion.2
  148.7 0.7 reshape.154
  149.4 0.6 dynamic-slice.6
  150.6 1.1 pad_maximum_fusion
  151.7 93.2 %all-reduce.6.cloned.1.call-done = f32[48,8192]{1,0:T(8,128)} async-done(((f32[48,8192]{1,0:T(8,128)}), f32[48,8192]{1,0:T(8,128)}) %all-reduce.6.cloned.1.call-update) | async-done | bytes 1572880
  244.9 1.1 fusion.7
  246.0 0.7 pad_maximum_fusion.3
  (29 shorter events, 0.3 us)
Async XLA Ops:
  7.2 43.9 %copy-start = (bf16[512,544]{0,1:T(8,128)(2,1)S(1)}, bf16[512,544]{0,1:T(8,128)(2,1)}, u32[]{:S(2)}) copy-start(bf16[512,544]{0,1:T(8,128)(2,1)} %param.21) | copy-start | bytes 1671172
  7.2 128.7 %all-reduce.4.cloned.1.call-start = ((), (), s32[]{:S(2)}) async-start(), calls=%async_computation | async-start | bytes 245760 | tf_op jit(solution)/shard_map/psum | solution.py:59
  47.6 3.2 %copy-start.7 = (bf16[64,3,512]{2,0,1:T(8,128)(2,1)S(1)}, bf16[64,3,512]{2,0,1:T(8,128)(2,1)}, u32[]{:S(2)}) copy-start(bf16[64,3,512]{2,0,1:T(8,128)(2,1)} %param.28) | copy-start | bytes 589828
  47.6 3.4 %copy-start.10 = (f32[4,512]{1,0:T(4,128)S(1)}, f32[4,512]{1,0:T(4,128)}, u32[]{:S(2)}) copy-start(f32[4,512]{1,0:T(4,128)} %param.19) | copy-start | bytes 24580
  47.6 3.5 %copy-start.8 = (f32[512]{0:T(512)S(1)}, f32[512]{0:T(512)}, u32[]{:S(2)}) copy-start(f32[512]{0:T(512)} %param.20) | copy-start | bytes 6148
  50.7 1.5 copy-start.13
  50.8 1.5 copy-start.1
  50.8 3.6 %copy-start.5 = (bf16[48,1,512]{2,0,1:T(8,128)(2,1)}, bf16[48,1,512]{2,0,1:T(8,128)(2,1)S(1)}, u32[]{:S(2)}) copy-start(bf16[48,1,512]{2,0,1:T(8,128)(2,1)S(1)} %fusion.10) | copy-start | bytes 147460
  50.8 3.6 %copy-start.9 = (f32[16,512]{1,0:T(8,128)S(1)}, f32[16,512]{1,0:T(8,128)}, u32[]{:S(2)}) copy-start(f32[16,512]{1,0:T(8,128)} %param.24) | copy-start | bytes 98308
  50.9 86.5 %copy-start.4 = (bf16[512,512]{1,0:T(8,128)(2,1)S(1)}, bf16[512,512]{1,0:T(8,128)(2,1)}, u32[]{:S(2)}) copy-start(bf16[512,512]{1,0:T(8,128)(2,1)} %param.22) | copy-start | bytes 1572868
  50.9 86.5 %copy-start.12 = (f32[512]{0:T(512)S(1)}, f32[512]{0:T(512)}, u32[]{:S(2)}) copy-start(f32[512]{0:T(512)} %param.23) | copy-start | bytes 6148
  52.0 87.2 %copy-start.2 = (bf16[64,16,512]{2,1,0:T(8,128)(2,1)S(1)}, bf16[64,16,512]{2,1,0:T(8,128)(2,1)}, u32[]{:S(2)}) copy-start(bf16[64,16,512]{2,1,0:T(8,128)(2,1)} %param.27) | copy-start | bytes 3145732
  52.1 192.8 %all-reduce.6.cloned.1.call-start = ((), (), s32[]{:S(2)}) async-start(), calls=%async_computation.1 | async-start | bytes 3145728
  147.2 0.8 copy-start.3
  147.2 1.0 copy-start.6
  147.2 1.0 copy-start.11
  148.0 1.3 copy-start.14
Sparse Core Ops, SparseCore 0:
  52.2 83.5 all-reduce.3
  147.4 97.5 all-reduce.5
where the time goes:
time: 254 us
  waiting for transfers between devices  174 us (69%)
  blocking collectives  26.2 us (10%)
  local copies, waits for them, and re-layouts  18.6 us (7%)
  between operations  15 us (6%)
  matrix products  11.4 us (4%)
  other arithmetic  8.21 us (3%)
    unnamed x3, waiting for transfers between devices  93.3 us
    psum x1, waiting for transfers between devices, body(): low_rank = lax.psum(partial_low, 'weight')  80.8 us
    all_gather x1, blocking collectives, body(): lax.all_gather(normed, 'weight', axis=0, tiled=True)  26.2 us
    unnamed x33, local copies, waits for them, and re-layouts  13.6 us
    dot_general x1, matrix products, body(): jnp.dot(block, out_weight, preferred_element_type=jnp.float32)  6.19 us
  transfers between devices with their start and end apart: 2, of which 2 were waited for; matrix products, arithmetic and copies ran while one was open for 2% of the time, Pallas kernels for 0%

commit v1 on v0

v1 whole, which is shorter than its diff:
```python
import jax
import jax.numpy as jnp
from jax import lax
from jax.experimental import pallas as pl
from jax.experimental.pallas import tpu as pltpu
from jax.sharding import PartitionSpec as P

NSTATE = 16
DTR = 512
LIVE_MAX = 3
TAPS = 4
BF16 = jnp.bfloat16
F32 = jnp.float32


def gather_phases(devices):
    phases, high = [], devices
    while high > 2:
        if high >= 8:
            step = high // 4
            phases.append((step, 2 * step, 3 * step))
            high //= 4
        else:
            phases.append((high // 2,))
            high //= 2
    phases.append((1,))
    return phases


def sum_phases(devices):
    phases, step = [], 2
    while step < devices:
        if 4 * step <= devices:
            phases.append((step, 2 * step, 3 * step))
            step *= 4
        else:
            phases.append((step,))
            step *= 2
    return phases


def swap(value, shift, devices):
    return lax.ppermute(value, "weight", [(i, i ^ shift) for i in range(devices)])


def rms_normed(hidden, norm_gain):
    wide = hidden.astype(F32)
    factor = lax.rsqrt(jnp.mean(wide * wide, axis=-1, keepdims=True) + 1e-05)
    return (wide * factor * norm_gain).astype(BF16)


def silu(v):
    return v / (1.0 + jnp.exp(-v))


def softplus(v):
    return jnp.maximum(v, 0.0) + jnp.log1p(jnp.exp(-jnp.abs(v)))


def conv_kernel(
    core_ref,
    both_ref,
    place_ref,
    alive_ref,
    conv_ref,
    taps_ref,
    offset_ref,
    coef_ref,
    keep_ref,
    send_ref,
    mixed_ref,
    gate_ref,
    new_conv_ref,
    low_ref,
):
    place = place_ref[...]
    fresh = jnp.dot(place, both_ref[0].astype(BF16), preferred_element_type=F32)
    alive = alive_ref[...] > 0.0
    states = [conv_ref[k].astype(F32) for k in range(TAPS - 1)] + [fresh]
    total = states[0] * taps_ref[0:1, :]
    for k in range(1, TAPS):
        total = total + states[k] * taps_ref[k : k + 1, :]
    mixed = silu(total + offset_ref[...]).astype(BF16)
    mixed_ref[...] = mixed
    low_ref[...] = lax.dot_general(
        mixed, coef_ref[...], (((1,), (1,)), ((), ())), preferred_element_type=F32
    )
    half = keep_ref.shape[0]
    core = core_ref[0]
    keep_ref[...] = low_ref[pl.ds(pl.multiple_of(core * half, half), half), :]
    send_ref[...] = low_ref[pl.ds(pl.multiple_of((1 - core) * half, half), half), :]
    for k in range(TAPS - 1):
        new_conv_ref[k] = jnp.where(alive, states[k + 1], states[k]).astype(BF16)
    gate_ref[...] = jnp.dot(
        place.astype(F32),
        silu(both_ref[1]),
        precision=lax.Precision.HIGHEST,
        preferred_element_type=F32,
    )


def state_kernel(
    core_ref,
    mine_ref,
    other_ref,
    mixed_ref,
    gate_ref,
    alive_ref,
    step_weight_ref,
    bias_ref,
    rates_ref,
    skip_ref,
    state_ref,
    pick_ref,
    out_weight_ref,
    new_state_ref,
    keep_ref,
    send_ref,
    low_ref,
    read_ref,
    weight_ref,
    sems,
):
    chunks, depth, width = weight_ref.shape
    copies = [
        pltpu.make_async_copy(
            out_weight_ref.at[:, pl.ds(c * width, width)], weight_ref.at[c], sems.at[c]
        )
        for c in range(chunks)
    ]
    for copy in copies:
        copy.start()
    half = mine_ref.shape[0]
    rows = 2 * half
    core = core_ref[0]
    low_ref[pl.ds(pl.multiple_of(core * half, half), half), :] = mine_ref[...]
    low_ref[pl.ds(pl.multiple_of((1 - core) * half, half), half), :] = other_ref[...]
    step_size = softplus(
        jnp.dot(
            low_ref[:, :DTR].astype(BF16), step_weight_ref[...], preferred_element_type=F32
        )
        + bias_ref[...]
    )
    coefs = low_ref[:, DTR:].T
    x_wide = mixed_ref[...].astype(F32)
    driven = step_size * x_wide
    rates = -jnp.exp(rates_ref[...])
    alive = alive_ref[...]
    for r in range(rows):
        old = state_ref[r]
        wide = old.astype(F32)
        updated = (
            jnp.exp(step_size[r : r + 1, :] * rates) * wide
            + coefs[:NSTATE, r : r + 1] * driven[r : r + 1, :]
        )
        read_ref[r : r + 1, :] = jnp.sum(
            coefs[NSTATE:, r : r + 1] * updated, axis=0, keepdims=True
        )
        new_state_ref[r] = jnp.where(alive[r : r + 1, :] > 0.0, updated, wide).astype(BF16)
    readout = read_ref[...] + skip_ref[...] * x_wide
    gated = jnp.where(alive > 0.0, readout * gate_ref[...], 0.0).astype(BF16)
    picked = jnp.dot(pick_ref[...], gated, preferred_element_type=F32).astype(BF16)
    kept = keep_ref.shape[0]
    for c in range(chunks):
        copies[c].wait()
        part = jnp.dot(picked, weight_ref[c], preferred_element_type=F32)
        keep_ref[:, c * width : (c + 1) * width] = part[:kept]
        send_ref[:, c * width : (c + 1) * width] = part[kept:].astype(send_ref.dtype)


def vmem(count):
    return [pl.BlockSpec(memory_space=pltpu.VMEM)] * count


def body(
    hidden,
    norm_gain,
    in_weight,
    conv_weight,
    conv_offset,
    coef_weight,
    step_weight,
    step_bias,
    log_rates,
    skip_gain,
    out_weight,
    ssm_state,
    conv_state,
    live_counts,
):
    devices = lax.axis_size("weight")
    rows_dev, width = hidden.shape
    rows = devices * rows_dev
    kept = devices * LIVE_MAX
    channels = in_weight.shape[2]
    low_width = coef_weight.shape[1]
    index = lax.axis_index("weight")
    core = (index % 2).reshape(1)
    phases = gather_phases(devices)
    order = [0]
    for phase in phases:
        order = order + [o ^ s for s in phase for o in order]

    blocks = jnp.bitwise_xor(index, jnp.array(order, jnp.int32))
    row_of = (blocks[:, None] * rows_dev + jnp.arange(rows_dev)[None]).reshape(-1)
    place = (jnp.arange(rows)[:, None] == row_of[None]).astype(BF16)
    kept_of = (blocks[:, None] * rows_dev + jnp.arange(LIVE_MAX)[None]).reshape(-1)
    pick = (kept_of[:, None] == jnp.arange(rows)[None]).astype(BF16)
    alive = (
        (jnp.arange(rows_dev)[None] < live_counts[:, None]).astype(F32).reshape(rows, 1)
    )

    gathered = rms_normed(hidden, norm_gain)
    for phase in phases:
        gathered = jnp.concatenate(
            [gathered] + [swap(gathered, s, devices) for s in phase], axis=0
        )
    both = jnp.einsum("rd,dbc->brc", gathered, in_weight, preferred_element_type=F32)

    keep, send, mixed_x, gate, new_conv = pl.pallas_call(
        conv_kernel,
        out_shape=(
            jax.ShapeDtypeStruct((rows // 2, low_width), F32),
            jax.ShapeDtypeStruct((rows // 2, low_width), F32),
            jax.ShapeDtypeStruct((rows, channels), BF16),
            jax.ShapeDtypeStruct((rows, channels), F32),
            jax.ShapeDtypeStruct((TAPS - 1, rows, channels), BF16),
        ),
        in_specs=[pl.BlockSpec(memory_space=pltpu.SMEM)] + vmem(7),
        out_specs=tuple(vmem(5)),
        scratch_shapes=[pltpu.VMEM((rows, low_width), F32)],
        compiler_params=pltpu.CompilerParams(vmem_limit_bytes=16 * 1024 * 1024),
    )(
        core,
        both,
        place,
        alive,
        conv_state.transpose(1, 0, 2),
        conv_weight,
        conv_offset.reshape(1, channels),
        coef_weight.T,
    )

    low = keep + swap(send, 1, devices)
    for phase in sum_phases(devices):
        low = low + sum(swap(low, s, devices) for s in phase)
    other = swap(low, 1, devices)

    chunks = 4
    new_state, keep, send = pl.pallas_call(
        state_kernel,
        out_shape=(
            jax.ShapeDtypeStruct(ssm_state.shape, BF16),
            jax.ShapeDtypeStruct((kept // 2, width), F32),
            jax.ShapeDtypeStruct((kept // 2, width), F32),
        ),
        in_specs=[pl.BlockSpec(memory_space=pltpu.SMEM)]
        + vmem(11)
        + [pl.BlockSpec(memory_space=pl.ANY)],
        out_specs=tuple(vmem(3)),
        scratch_shapes=[
            pltpu.VMEM((rows, low_width), F32),
            pltpu.VMEM((rows, channels), F32),
            pltpu.VMEM((chunks, channels, width // chunks), BF16),
            pltpu.SemaphoreType.DMA((chunks,)),
        ],
        compiler_params=pltpu.CompilerParams(vmem_limit_bytes=32 * 1024 * 1024),
    )(
        core,
        low,
        other,
        mixed_x,
        gate,
        alive,
        step_weight,
        step_bias.reshape(1, channels),
        log_rates,
        skip_gain.reshape(1, channels),
        ssm_state,
        pick,
        out_weight,
    )

    total = keep + swap(send, 1, devices)
    for phase in reversed(phases[:-1]):
        parts = jnp.split(total, len(phase) + 1, axis=0)
        total = parts[0]
        for part, s in zip(parts[1:], phase):
            total = total + swap(part.astype(BF16), s, devices).astype(F32)
    own = (hidden[:LIVE_MAX].astype(F32) + total).astype(BF16)
    mixed = jnp.concatenate([own, hidden[LIVE_MAX:]], axis=0)
    return (mixed, new_state, new_conv.transpose(1, 0, 2))


def solution(mesh):
    in_specs = (
        P(("groups", "weight"), None),
        P(),
        P(None, None, "weight"),
        P(None, "weight"),
        P("weight"),
        P("weight", None),
        P(None, "weight"),
        P("weight"),
        P(None, "weight"),
        P("weight"),
        P("weight", None),
        P("groups", None, "weight"),
        P("groups", None, "weight"),
        P("groups"),
    )
    out_specs = (
        P(("groups", "weight"), None),
        P("groups", None, "weight"),
        P("groups", None, "weight"),
    )
    return jax.shard_map(body, mesh=mesh, in_specs=in_specs, out_specs=out_specs, check_vma=False)
```

time: 254 us -> 80.7 us (0.32)
  waiting for transfers between devices: 174 us -> 36 us
  blocking collectives: 26.2 us -> 0 us
  starting transfers between devices: 0.08 us -> 19.1 us
  between operations: 15 us -> 0.89 us
  local copies, waits for them, and re-layouts: 18.6 us -> 4.55 us
  Pallas kernels: 0 us -> 6.25 us
  other arithmetic: 8.21 us -> 4.75 us
    unnamed x3 -> x0, waiting for transfers between devices: 93.3 us -> none
    psum x1 -> x0, waiting for transfers between devices: 80.8 us -> none  [body(): low_rank = lax.psum(partial_low, 'weight')]
    ppermute x0 -> x16, waiting for transfers between devices: none -> 36 us  [swap(): lax.ppermute(value, 'weight', [(i, i ^ shift) for i in range(devices)])]
    all_gather x1 -> x0, blocking collectives: 26.2 us -> none  [body(): lax.all_gather(normed, 'weight', axis=0, tiled=True)]
    ppermute x0 -> x16, starting transfers between devices: none -> 19.1 us  [swap(): lax.ppermute(value, 'weight', [(i, i ^ shift) for i in range(devices)])]
    unnamed x33 -> x22, local copies, waits for them, and re-layouts: 13.6 us -> 3.44 us
    pallas_call x0 -> x2, Pallas kernels: none -> 6.25 us  [the longest x1 5.15 us: body(): pl.pallas_call(state_kernel, out_shape=(jax.ShapeDtypeStruct(ssm_state.sh...]
    dot_general x4 -> x1, matrix products: 11.4 us -> 8.91 us  [body(): jnp.einsum('rd,dbc->brc', gathered, in_weight, preferred_element_type=F32)]
  transfers between devices with their start and end apart: 2 -> 16, of which waited for: 2 -> 15; matrix products, arithmetic and copies ran while one was open for 2% -> 2% of each run, Pallas kernels for 0% -> 0%
where the time goes in v1:
time: 80.7 us; the launch traced here: 80.4 us
  waiting for transfers between devices  36 us (45%)
  starting transfers between devices  19.1 us (24%)
  matrix products  8.91 us (11%)
  Pallas kernels  6.25 us (8%)
  other arithmetic  4.75 us (6%)
  local copies, waits for them, and re-layouts  4.55 us (6%)
  between operations  0.89 us (1%)
    ppermute x16, waiting for transfers between devices, swap(): lax.ppermute(value, 'weight', [(i, i ^ shift) for i in range(devices)])  36 us
    ppermute x16, starting transfers between devices, swap(): lax.ppermute(value, 'weight', [(i, i ^ shift) for i in range(devices)])  19.1 us
    dot_general x1, matrix products, body(): jnp.einsum('rd,dbc->brc', gathered, in_weight, preferred_element_type=F32)  8.91 us
    pallas_call x1, Pallas kernels, body(): pl.pallas_call(state_kernel, out_shape=(jax.ShapeDtypeStruct(ssm_state.sh...  5.15 us
    unnamed x22, local copies, waits for them, and re-layouts  3.44 us
  transfers between devices with their start and end apart: 16, of which 15 were waited for; matrix products, arithmetic and copies ran while one was open for 2% of the time, Pallas kernels for 0%

profile of v1, /device:TPU:0, one launch (start us, length us, event | category | flops | bytes accessed | tf_op | source)
XLA Modules:
  0.0 80.4 jit_solution(17521263630580674550)
XLA Ops:
  0.6 1.0 %fusion.6 = f32[4]{0:T(128)S(1)} fusion(bf16[4,8192]{1,0:T(4,128)(2,1)} %param.15), kind=kLoop, calls=%fused_computation.9 | loop fusion | flops 98300 | bytes 65552 | tf_op jit(solution)/shard_map/reduce_sum | solution.py:48
  1.7 0.9 %fusion.8 = bf16[4,8192]{1,0:T(4,128)(2,1)S(1)} fusion(bf16[4,8192]{1,0:T(4,128)(2,1)} %param.15, f32[8192]{0:T(1024)} %param.16, f32[4]{0:T(128)S(1)} %add_rsqrt_fusion), kind=kLoop, calls=%fused_computation.11 | loop fusion | flops 131072 | bytes 163856 | tf_op jit(solution)/shard_map/convert_element_type | solution.py:49
  2.6 3.1 %collective-permute-start = (bf16[4,8192]{1,0:T(4,128)(2,1)S(1)}, bf16[4,8192]{1,0:T(4,128)(2,1)S(1)}, u32[]{:S(2)}, u32[]{:S(2)}) collective-permute-start(bf16[4,8192]{1,0:T(4,128)(2,1)S(1)} %fusion.8), channel_id=1, source_target_pairs={{0,4},{1,5},{2,6},{3,7},{4,0},{5,1},{6,2},{7,3},{8,12},{9,13},{10,... | collective-permute-start | bytes 196616 | tf_op jit(solution)/shard_map/ppermute | solution.py:43
  5.7 2.6 %collective-permute-start.1 = (bf16[4,8192]{1,0:T(4,128)(2,1)S(1)}, bf16[4,8192]{1,0:T(4,128)(2,1)S(1)}, u32[]{:S(2)}, u32[]{:S(2)}) collective-permute-start(bf16[4,8192]{1,0:T(4,128)(2,1)S(1)} %fusion.8), channel_id=1, source_target_pairs={{0,8},{1,9},{2,10},{3,11},{4,12},{5,13},{6,14},{7,15},{8,0},{9,1},... | collective-permute-start | bytes 196616 | tf_op jit(solution)/shard_map/ppermute | solution.py:43
  8.3 4.7 %collective-permute-done.1 = bf16[4,8192]{1,0:T(4,128)(2,1)S(1)} collective-permute-done((bf16[4,8192]{1,0:T(4,128)(2,1)S(1)}, bf16[4,8192]{1,0:T(4,128)(2,1)S(1)}, u32[]{:S(2)}, u32[]{:S(2)}) %collective-permute-start.1) | collective-permute-done | bytes 65568 | tf_op jit(solution)/shard_map/ppermute | solution.py:43
  13.0 1.4 %collective-permute-done.2 = bf16[4,8192]{1,0:T(4,128)(2,1)S(1)} collective-permute-done((bf16[4,8192]{1,0:T(4,128)(2,1)S(1)}, bf16[4,8192]{1,0:T(4,128)(2,1)S(1)}, u32[]{:S(2)}, u32[]{:S(2)}) %collective-permute-start.2) | collective-permute-done | bytes 65568 | tf_op jit(solution)/shard_map/ppermute | solution.py:43
  14.4 0.2 pad_maximum_fusion
  14.5 1.6 %collective-permute-start.3 = (bf16[16,8192]{1,0:T(8,128)(2,1)S(1)}, bf16[16,8192]{1,0:T(8,128)(2,1)S(1)}, u32[]{:S(2)}, u32[]{:S(2)}) collective-permute-start(bf16[16,8192]{1,0:T(8,128)(2,1)S(1)} %pad_maximum_fusion), channel_id=1, source_target_pairs={{0,2},{1,3},{2,0},{3,1},{4,6},{5,7},{6,4},{7,5},{8,10},{9,11},{10,... | collective-permute-start | bytes 786440 | tf_op jit(solution)/shard_map/ppermute | solution.py:43
  16.1 0.7 xor_multiply_fusion
  16.8 4.2 %collective-permute-done.3 = bf16[16,8192]{1,0:T(8,128)(2,1)S(1)} collective-permute-done((bf16[16,8192]{1,0:T(8,128)(2,1)S(1)}, bf16[16,8192]{1,0:T(8,128)(2,1)S(1)}, u32[]{:S(2)}, u32[]{:S(2)}) %collective-permute-start.3) | collective-permute-done | bytes 262176 | tf_op jit(solution)/shard_map/ppermute | solution.py:43
  21.0 0.3 concatenate.15
  21.4 0.1 iota_add_fusion.1
  21.4 0.1 add.92
  21.5 0.7 fusion.15
  22.3 0.1 reshape.92.alive_ref
  22.3 0.9 %collective-permute-done.4 = bf16[32,8192]{1,0:T(8,128)(2,1)S(1)} collective-permute-done((bf16[32,8192]{1,0:T(8,128)(2,1)S(1)}, bf16[32,8192]{1,0:T(8,128)(2,1)S(1)}, u32[]{:S(2)}, u32[]{:S(2)}) %collective-permute-start.4) | collective-permute-done | bytes 524320 | tf_op jit(solution)/shard_map/ppermute | solution.py:43
  23.3 0.4 concatenate.16
  23.8 8.9 %fusion.2.both_ref = f32[2,64,512]{2,1,0:T(8,128)S(1)} fusion(bf16[8192,2,512]{2,1,0:T(2,128)(2,1)} %param.17, bf16[64,8192]{1,0:T(8,128)(2,1)S(1)} %concatenate.16), kind=kOutput, calls=%fused_computation.2 | convolution fusion | flops 1073741824 | bytes 18087936 | tf_op jit(solution)/shard_map/rd,dbc->brc/dot_general | solution.py:218
  32.8 1.1 %shard_map.166 = (f32[32,544]{1,0:T(8,128)S(1)}, f32[32,544]{1,0:T(8,128)S(1)}, bf16[64,512]{1,0:T(8,128)(2,1)S(1)}, f32[64,512]{1,0:T(8,128)S(1)}, bf16[3,64,512]{2,1,0:T(8,128)(2,1)}) custom-call(s32[1]{0:T(128)} %bitcast.core_ref, f32[2,64,512]{2,1,0:T(8,128)S(1)} %fusion.2.both_ref, bf16[64,64]{1,0:T(8,128)(2,1)S(1)} %fusion.13.place_ref, ...), custom_call_target="tpu_custom_call" | custom-call | tf_op jit(solution)/shard_map/pallas_call | solution.py:220
  33.9 0.1 collective-permute-start.5
  34.0 1.1 %collective-permute-done.5 = f32[32,544]{1,0:T(8,128)S(1)} collective-permute-done((f32[32,544]{1,0:T(8,128)S(1)}, f32[32,544]{1,0:T(8,128)S(1)}, u32[]{:S(2)}, u32[]{:S(2)}) %collective-permute-start.5) | collective-permute-done | bytes 69664 | tf_op jit(solution)/shard_map/ppermute | solution.py:43
  35.2 1.6 %collective-permute-start.6 = (f32[32,544]{1,0:T(8,128)S(1)}, f32[32,544]{1,0:T(8,128)S(1)}, u32[]{:S(2)}, u32[]{:S(2)}) collective-permute-start(f32[32,544]{1,0:T(8,128)S(1)} %add.94), channel_id=1, source_target_pairs={{0,2},{1,3},{2,0},{3,1},{4,6},{5,7},{6,4},{7,5},{8,10},{9,11},{10,... | collective-permute-start | bytes 208904 | tf_op jit(solution)/shard_map/ppermute | solution.py:43
  36.8 0.7 collective-permute-start.7
  37.4 1.3 %collective-permute-start.8 = (f32[32,544]{1,0:T(8,128)S(1)}, f32[32,544]{1,0:T(8,128)S(1)}, u32[]{:S(2)}, u32[]{:S(2)}) collective-permute-start(f32[32,544]{1,0:T(8,128)S(1)} %add.94), channel_id=1, source_target_pairs={{0,6},{1,7},{2,4},{3,5},{4,2},{5,3},{6,0},{7,1},{8,14},{9,15},{10,... | collective-permute-start | bytes 208904 | tf_op jit(solution)/shard_map/ppermute | solution.py:43
  38.7 1.0 %collective-permute-done.6 = f32[32,544]{1,0:T(8,128)S(1)} collective-permute-done((f32[32,544]{1,0:T(8,128)S(1)}, f32[32,544]{1,0:T(8,128)S(1)}, u32[]{:S(2)}, u32[]{:S(2)}) %collective-permute-start.6) | collective-permute-done | bytes 69664 | tf_op jit(solution)/shard_map/ppermute | solution.py:43
  39.7 2.1 %collective-permute-done.7 = f32[32,544]{1,0:T(8,128)S(1)} collective-permute-done((f32[32,544]{1,0:T(8,128)S(1)}, f32[32,544]{1,0:T(8,128)S(1)}, u32[]{:S(2)}, u32[]{:S(2)}) %collective-permute-start.7) | collective-permute-done | bytes 69664 | tf_op jit(solution)/shard_map/ppermute | solution.py:43
  41.9 1.0 %collective-permute-done.8 = f32[32,544]{1,0:T(8,128)S(1)} collective-permute-done((f32[32,544]{1,0:T(8,128)S(1)}, f32[32,544]{1,0:T(8,128)S(1)}, u32[]{:S(2)}, u32[]{:S(2)}) %collective-permute-start.8) | collective-permute-done | bytes 69664 | tf_op jit(solution)/shard_map/ppermute | solution.py:43
  42.9 1.9 %collective-permute-start.9 = (f32[32,544]{1,0:T(8,128)S(1)}, f32[32,544]{1,0:T(8,128)S(1)}, u32[]{:S(2)}, u32[]{:S(2)}) collective-permute-start(f32[32,544]{1,0:T(8,128)S(1)} %add_add_fusion), channel_id=1, source_target_pairs={{0,8},{1,9},{2,10},{3,11},{4,12},{5,13},{6,14},{7,15},{8,0},{9,1},... | collective-permute-start | bytes 208904 | tf_op jit(solution)/shard_map/ppermute | solution.py:43
  44.9 0.1 add.102
  45.0 4.2 %collective-permute-done.9 = f32[32,544]{1,0:T(8,128)S(1)} collective-permute-done((f32[32,544]{1,0:T(8,128)S(1)}, f32[32,544]{1,0:T(8,128)S(1)}, u32[]{:S(2)}, u32[]{:S(2)}) %collective-permute-start.9) | collective-permute-done | bytes 69664 | tf_op jit(solution)/shard_map/ppermute | solution.py:43
  49.3 0.1 fusion.14.pick_ref
  49.4 1.2 %collective-permute-done.10.other_ref = f32[32,544]{1,0:T(8,128)S(1)} collective-permute-done((f32[32,544]{1,0:T(8,128)S(1)}, f32[32,544]{1,0:T(8,128)S(1)}, u32[]{:S(2)}, u32[]{:S(2)}) %collective-permute-start.10) | collective-permute-done | bytes 69664 | tf_op jit(solution)/shard_map/ppermute | solution.py:43
  50.6 3.4 %copy-done = bf16[512,8192]{1,0:T(8,128)(2,1)S(1)} copy-done((bf16[512,8192]{1,0:T(8,128)(2,1)S(1)}, bf16[512,8192]{1,0:T(8,128)(2,1)}, u32[]{:S(2)}) %copy-start) | copy-done | bytes 8388632
  54.0 5.2 %shard_map.167 = (bf16[64,16,512]{2,1,0:T(8,128)(2,1)}, f32[24,8192]{1,0:T(8,128)S(1)}, f32[24,8192]{1,0:T(8,128)S(1)}) custom-call(s32[1]{0:T(128)} %bitcast.core_ref, f32[32,544]{1,0:T(8,128)S(1)} %add.98.mine_ref, f32[32,544]{1,0:T(8,128)S(1)} %collective-permute-done.10.other_ref, bf16[64,512]{1,0:T(8,128)(2,1)S(1)} %get-tuple-element.13.mixed_ref, ...), custom_call_target="tpu_custom_call" | custom-call | tf_op jit(solution)/shard_map/pallas_call | solution.py:250
  59.1 0.2 collective-permute-start.11
  59.3 2.1 %collective-permute-done.11 = f32[24,8192]{1,0:T(8,128)S(1)} collective-permute-done((f32[24,8192]{1,0:T(8,128)S(1)}, f32[24,8192]{1,0:T(8,128)S(1)}, u32[]{:S(2)}, u32[]{:S(2)}) %collective-permute-start.11) | collective-permute-done | bytes 786464 | tf_op jit(solution)/shard_map/ppermute | solution.py:43
  61.5 0.1 add.103
  61.6 1.4 %collective-permute-start.12 = (bf16[12,8192]{1,0:T(8,128)(2,1)S(1)}, bf16[12,8192]{1,0:T(8,128)(2,1)S(1)}, u32[]{:S(2)}, u32[]{:S(2)}) collective-permute-start(bf16[12,8192]{1,0:T(8,128)(2,1)S(1)} %split.45), channel_id=1, source_target_pairs={{0,2},{1,3},{2,0},{3,1},{4,6},{5,7},{6,4},{7,5},{8,10},{9,11},{10,... | collective-permute-start | bytes 589832 | tf_op jit(solution)/shard_map/ppermute | solution.py:43
  63.0 7.1 %collective-permute-done.12 = bf16[12,8192]{1,0:T(8,128)(2,1)S(1)} collective-permute-done((bf16[12,8192]{1,0:T(8,128)(2,1)S(1)}, bf16[12,8192]{1,0:T(8,128)(2,1)S(1)}, u32[]{:S(2)}, u32[]{:S(2)}) %collective-permute-start.12) | collective-permute-done | bytes 196640 | tf_op jit(solution)/shard_map/ppermute | solution.py:43
  70.1 0.1 fusion.17
  70.2 0.5 collective-permute-start.13
  70.8 2.8 %collective-permute-start.14 = (bf16[3,8192]{1,0:T(4,128)(2,1)S(1)}, bf16[3,8192]{1,0:T(4,128)(2,1)S(1)}, u32[]{:S(2)}, u32[]{:S(2)}) collective-permute-start(bf16[3,8192]{1,0:T(4,128)(2,1)S(1)} %get-tuple-element.23), channel_id=1, source_target_pairs={{0,8},{1,9},{2,10},{3,11},{4,12},{5,13},{6,14},{7,15},{8,0},{9,1},... | collective-permute-start | bytes 147464 | tf_op jit(solution)/shard_map/ppermute | solution.py:43
  73.6 1.1 %collective-permute-start.15 = (bf16[3,8192]{1,0:T(4,128)(2,1)S(1)}, bf16[3,8192]{1,0:T(4,128)(2,1)S(1)}, u32[]{:S(2)}, u32[]{:S(2)}) collective-permute-start(bf16[3,8192]{1,0:T(4,128)(2,1)S(1)} %get-tuple-element.22), channel_id=1, source_target_pairs={{0,12},{1,13},{2,14},{3,15},{4,8},{5,9},{6,10},{7,11},{8,4},{9,5},... | collective-permute-start | bytes 147464 | tf_op jit(solution)/shard_map/ppermute | solution.py:43
  74.7 0.1 collective-permute-done.13
  74.9 3.1 %collective-permute-done.14 = bf16[3,8192]{1,0:T(4,128)(2,1)S(1)} collective-permute-done((bf16[3,8192]{1,0:T(4,128)(2,1)S(1)}, bf16[3,8192]{1,0:T(4,128)(2,1)S(1)}, u32[]{:S(2)}, u32[]{:S(2)}) %collective-permute-start.14) | collective-permute-done | bytes 49184 | tf_op jit(solution)/shard_map/ppermute | solution.py:43
  77.9 1.7 %collective-permute-done.15 = bf16[3,8192]{1,0:T(4,128)(2,1)S(1)} collective-permute-done((bf16[3,8192]{1,0:T(4,128)(2,1)S(1)}, bf16[3,8192]{1,0:T(4,128)(2,1)S(1)}, u32[]{:S(2)}, u32[]{:S(2)}) %collective-permute-start.15) | collective-permute-done | bytes 49184 | tf_op jit(solution)/shard_map/ppermute | solution.py:43
  79.6 0.1 fusion.12
  79.7 0.7 pad_maximum_fusion.1
  (34 shorter events, 0.5 us)
Async XLA Ops:
  2.6 5.7 %collective-permute-start = (bf16[4,8192]{1,0:T(4,128)(2,1)S(1)}, bf16[4,8192]{1,0:T(4,128)(2,1)S(1)}, u32[]{:S(2)}, u32[]{:S(2)}) collective-permute-start(bf16[4,8192]{1,0:T(4,128)(2,1)S(1)} %fusion.8), channel_id=1, source_target_pairs={{0,4},{1,5},{2,6},{3,7},{4,0},{5,1},{6,2},{7,3},{8,12},{9,13},{10,... | collective-permute-start | bytes 196616 | tf_op jit(solution)/shard_map/ppermute | solution.py:43
  5.7 7.3 %collective-permute-start.1 = (bf16[4,8192]{1,0:T(4,128)(2,1)S(1)}, bf16[4,8192]{1,0:T(4,128)(2,1)S(1)}, u32[]{:S(2)}, u32[]{:S(2)}) collective-permute-start(bf16[4,8192]{1,0:T(4,128)(2,1)S(1)} %fusion.8), channel_id=1, source_target_pairs={{0,8},{1,9},{2,10},{3,11},{4,12},{5,13},{6,14},{7,15},{8,0},{9,1},... | collective-permute-start | bytes 196616 | tf_op jit(solution)/shard_map/ppermute | solution.py:43
  8.3 6.1 %collective-permute-start.2 = (bf16[4,8192]{1,0:T(4,128)(2,1)S(1)}, bf16[4,8192]{1,0:T(4,128)(2,1)S(1)}, u32[]{:S(2)}, u32[]{:S(2)}) collective-permute-start(bf16[4,8192]{1,0:T(4,128)(2,1)S(1)} %fusion.8), channel_id=1, source_target_pairs={{0,12},{1,13},{2,14},{3,15},{4,8},{5,9},{6,10},{7,11},{8,4},{9,5},... | collective-permute-start | bytes 196616 | tf_op jit(solution)/shard_map/ppermute | solution.py:43
  14.5 6.5 %collective-permute-start.3 = (bf16[16,8192]{1,0:T(8,128)(2,1)S(1)}, bf16[16,8192]{1,0:T(8,128)(2,1)S(1)}, u32[]{:S(2)}, u32[]{:S(2)}) collective-permute-start(bf16[16,8192]{1,0:T(8,128)(2,1)S(1)} %pad_maximum_fusion), channel_id=1, source_target_pairs={{0,2},{1,3},{2,0},{3,1},{4,6},{5,7},{6,4},{7,5},{8,10},{9,11},{10,... | collective-permute-start | bytes 786440 | tf_op jit(solution)/shard_map/ppermute | solution.py:43
  21.3 2.0 %collective-permute-start.4 = (bf16[32,8192]{1,0:T(8,128)(2,1)S(1)}, bf16[32,8192]{1,0:T(8,128)(2,1)S(1)}, u32[]{:S(2)}, u32[]{:S(2)}) collective-permute-start(bf16[32,8192]{1,0:T(8,128)(2,1)S(1)} %concatenate.15), channel_id=1, source_target_pairs={{0,1},{1,0},{2,3},{3,2},{4,5},{5,4},{6,7},{7,6},{8,9},{9,8},{10,11... | collective-permute-start | bytes 1572872 | tf_op jit(solution)/shard_map/ppermute | solution.py:43
  23.7 9.0 %copy-start.2 = (bf16[512,544]{0,1:T(8,128)(2,1)S(1)}, bf16[512,544]{0,1:T(8,128)(2,1)}, u32[]{:S(2)}) copy-start(bf16[512,544]{0,1:T(8,128)(2,1)} %param.20) | copy-start | bytes 1671172
  23.7 9.0 %copy-start.4 = (bf16[64,3,512]{2,0,1:T(8,128)(2,1)S(1)}, bf16[64,3,512]{2,0,1:T(8,128)(2,1)}, u32[]{:S(2)}) copy-start(bf16[64,3,512]{2,0,1:T(8,128)(2,1)} %param.27) | copy-start | bytes 589828
  23.7 9.0 %copy-start.6 = (f32[4,512]{1,0:T(4,128)S(1)}, f32[4,512]{1,0:T(4,128)}, u32[]{:S(2)}) copy-start(f32[4,512]{1,0:T(4,128)} %taps_ref.1) | copy-start | bytes 24580
  23.7 9.0 %copy-start.7 = (f32[512]{0:T(512)S(1)}, f32[512]{0:T(512)}, u32[]{:S(2)}) copy-start(f32[512]{0:T(512)} %param.19) | copy-start | bytes 6148
  23.7 26.8 %copy-start.1 = (bf16[64,16,512]{2,1,0:T(8,128)(2,1)S(1)}, bf16[64,16,512]{2,1,0:T(8,128)(2,1)}, u32[]{:S(2)}) copy-start(bf16[64,16,512]{2,1,0:T(8,128)(2,1)} %state_ref.1) | copy-start | bytes 3145732
  23.7 26.8 %copy-start.3 = (bf16[512,512]{1,0:T(8,128)(2,1)S(1)}, bf16[512,512]{1,0:T(8,128)(2,1)}, u32[]{:S(2)}) copy-start(bf16[512,512]{1,0:T(8,128)(2,1)} %step_weight_ref.1) | copy-start | bytes 1572868
  23.8 26.8 %copy-start.5 = (f32[16,512]{1,0:T(8,128)S(1)}, f32[16,512]{1,0:T(8,128)}, u32[]{:S(2)}) copy-start(f32[16,512]{1,0:T(8,128)} %rates_ref.1) | copy-start | bytes 98308
  23.8 26.8 %copy-start.8 = (f32[512]{0:T(512)S(1)}, f32[512]{0:T(512)}, u32[]{:S(2)}) copy-start(f32[512]{0:T(512)} %param.22) | copy-start | bytes 6148
  23.8 26.8 %copy-start.9 = (f32[512]{0:T(512)S(1)}, f32[512]{0:T(512)}, u32[]{:S(2)}) copy-start(f32[512]{0:T(512)} %param.24) | copy-start | bytes 6148
  32.7 42.0 %copy-start.10 = (bf16[4,8192]{1,0:T(4,128)(2,1)S(1)}, bf16[4,8192]{1,0:T(4,128)(2,1)}, u32[]{:S(2)}) copy-start(bf16[4,8192]{1,0:T(4,128)(2,1)} %param.15) | copy-start | bytes 196612
  33.9 1.3 %collective-permute-start.5 = (f32[32,544]{1,0:T(8,128)S(1)}, f32[32,544]{1,0:T(8,128)S(1)}, u32[]{:S(2)}, u32[]{:S(2)}) collective-permute-start(f32[32,544]{1,0:T(8,128)S(1)} %get-tuple-element.12), channel_id=1, source_target_pairs={{0,1},{1,0},{2,3},{3,2},{4,5},{5,4},{6,7},{7,6},{8,9},{9,8},{10,11... | collective-permute-start | bytes 208904 | tf_op jit(solution)/shard_map/ppermute | solution.py:43
  35.2 4.6 %collective-permute-start.6 = (f32[32,544]{1,0:T(8,128)S(1)}, f32[32,544]{1,0:T(8,128)S(1)}, u32[]{:S(2)}, u32[]{:S(2)}) collective-permute-start(f32[32,544]{1,0:T(8,128)S(1)} %add.94), channel_id=1, source_target_pairs={{0,2},{1,3},{2,0},{3,1},{4,6},{5,7},{6,4},{7,5},{8,10},{9,11},{10,... | collective-permute-start | bytes 208904 | tf_op jit(solution)/shard_map/ppermute | solution.py:43
  36.8 5.1 %collective-permute-start.7 = (f32[32,544]{1,0:T(8,128)S(1)}, f32[32,544]{1,0:T(8,128)S(1)}, u32[]{:S(2)}, u32[]{:S(2)}) collective-permute-start(f32[32,544]{1,0:T(8,128)S(1)} %add.94), channel_id=1, source_target_pairs={{0,4},{1,5},{2,6},{3,7},{4,0},{5,1},{6,2},{7,3},{8,12},{9,13},{10,... | collective-permute-start | bytes 208904 | tf_op jit(solution)/shard_map/ppermute | solution.py:43
  37.4 5.5 %collective-permute-start.8 = (f32[32,544]{1,0:T(8,128)S(1)}, f32[32,544]{1,0:T(8,128)S(1)}, u32[]{:S(2)}, u32[]{:S(2)}) collective-permute-start(f32[32,544]{1,0:T(8,128)S(1)} %add.94), channel_id=1, source_target_pairs={{0,6},{1,7},{2,4},{3,5},{4,2},{5,3},{6,0},{7,1},{8,14},{9,15},{10,... | collective-permute-start | bytes 208904 | tf_op jit(solution)/shard_map/ppermute | solution.py:43
  42.9 6.3 %collective-permute-start.9 = (f32[32,544]{1,0:T(8,128)S(1)}, f32[32,544]{1,0:T(8,128)S(1)}, u32[]{:S(2)}, u32[]{:S(2)}) collective-permute-start(f32[32,544]{1,0:T(8,128)S(1)} %add_add_fusion), channel_id=1, source_target_pairs={{0,8},{1,9},{2,10},{3,11},{4,12},{5,13},{6,14},{7,15},{8,0},{9,1},... | collective-permute-start | bytes 208904 | tf_op jit(solution)/shard_map/ppermute | solution.py:43
  49.2 1.3 %collective-permute-start.10 = (f32[32,544]{1,0:T(8,128)S(1)}, f32[32,544]{1,0:T(8,128)S(1)}, u32[]{:S(2)}, u32[]{:S(2)}) collective-permute-start(f32[32,544]{1,0:T(8,128)S(1)} %add.98.mine_ref), channel_id=1, source_target_pairs={{0,1},{1,0},{2,3},{3,2},{4,5},{5,4},{6,7},{7,6},{8,9},{9,8},{10,11... | collective-permute-start | bytes 208904 | tf_op jit(solution)/shard_map/ppermute | solution.py:43
  50.6 3.4 %copy-start = (bf16[512,8192]{1,0:T(8,128)(2,1)S(1)}, bf16[512,8192]{1,0:T(8,128)(2,1)}, u32[]{:S(2)}) copy-start(bf16[512,8192]{1,0:T(8,128)(2,1)} %out_weight_ref.1) | copy-start | bytes 25165828
  59.1 2.4 %collective-permute-start.11 = (f32[24,8192]{1,0:T(8,128)S(1)}, f32[24,8192]{1,0:T(8,128)S(1)}, u32[]{:S(2)}, u32[]{:S(2)}) collective-permute-start(f32[24,8192]{1,0:T(8,128)S(1)} %get-tuple-element.16), channel_id=1, source_target_pairs={{0,1},{1,0},{2,3},{3,2},{4,5},{5,4},{6,7},{7,6},{8,9},{9,8},{10,11... | collective-permute-start | bytes 2359304 | tf_op jit(solution)/shard_map/ppermute | solution.py:43
  61.6 8.4 %collective-permute-start.12 = (bf16[12,8192]{1,0:T(8,128)(2,1)S(1)}, bf16[12,8192]{1,0:T(8,128)(2,1)S(1)}, u32[]{:S(2)}, u32[]{:S(2)}) collective-permute-start(bf16[12,8192]{1,0:T(8,128)(2,1)S(1)} %split.45), channel_id=1, source_target_pairs={{0,2},{1,3},{2,0},{3,1},{4,6},{5,7},{6,4},{7,5},{8,10},{9,11},{10,... | collective-permute-start | bytes 589832 | tf_op jit(solution)/shard_map/ppermute | solution.py:43
  70.2 4.6 %collective-permute-start.13 = (bf16[3,8192]{1,0:T(4,128)(2,1)S(1)}, bf16[3,8192]{1,0:T(4,128)(2,1)S(1)}, u32[]{:S(2)}, u32[]{:S(2)}) collective-permute-start(bf16[3,8192]{1,0:T(4,128)(2,1)S(1)} %get-tuple-element.21), channel_id=1, source_target_pairs={{0,4},{1,5},{2,6},{3,7},{4,0},{5,1},{6,2},{7,3},{8,12},{9,13},{10,... | collective-permute-start | bytes 147464 | tf_op jit(solution)/shard_map/ppermute | solution.py:43
  70.8 7.1 %collective-permute-start.14 = (bf16[3,8192]{1,0:T(4,128)(2,1)S(1)}, bf16[3,8192]{1,0:T(4,128)(2,1)S(1)}, u32[]{:S(2)}, u32[]{:S(2)}) collective-permute-start(bf16[3,8192]{1,0:T(4,128)(2,1)S(1)} %get-tuple-element.23), channel_id=1, source_target_pairs={{0,8},{1,9},{2,10},{3,11},{4,12},{5,13},{6,14},{7,15},{8,0},{9,1},... | collective-permute-start | bytes 147464 | tf_op jit(solution)/shard_map/ppermute | solution.py:43
  73.6 6.1 %collective-permute-start.15 = (bf16[3,8192]{1,0:T(4,128)(2,1)S(1)}, bf16[3,8192]{1,0:T(4,128)(2,1)S(1)}, u32[]{:S(2)}, u32[]{:S(2)}) collective-permute-start(bf16[3,8192]{1,0:T(4,128)(2,1)S(1)} %get-tuple-element.22), channel_id=1, source_target_pairs={{0,12},{1,13},{2,14},{3,15},{4,8},{5,9},{6,10},{7,11},{8,4},{9,5},... | collective-permute-start | bytes 147464 | tf_op jit(solution)/shard_map/ppermute | solution.py:43

commit v2 on v1

v2 whole, which is shorter than its diff:
```python
import functools

import jax
import jax.numpy as jnp
from jax import lax
from jax.experimental import pallas as pl
from jax.experimental.pallas import tpu as pltpu
from jax.sharding import PartitionSpec as P

NSTATE = 16
DTR = 512
LIVE_MAX = 3
TAPS = 4
LANES = 128
MIB = 1024 * 1024
BF16 = jnp.bfloat16
F32 = jnp.float32


def gather_phases(devices):
    phases, high = [], devices
    while high > 2:
        if high >= 8:
            step = high // 4
            phases.append((step, 2 * step, 3 * step))
            high //= 4
        else:
            phases.append((high // 2,))
            high //= 2
    phases.append((1,))
    return phases


def sum_phases(devices):
    phases, step = [], 2
    while step < devices:
        if 4 * step <= devices:
            phases.append((step, 2 * step, 3 * step))
            step *= 4
        else:
            phases.append((step,))
            step *= 2
    return phases


def swap(value, shift, devices):
    return lax.ppermute(value, "weight", [(i, i ^ shift) for i in range(devices)])


def silu(v):
    return v / (1.0 + jnp.exp(-v))


def softplus(v):
    return jnp.maximum(v, 0.0) + jnp.log1p(jnp.exp(-jnp.abs(v)))


def vmem(count):
    return [pl.BlockSpec(memory_space=pltpu.VMEM)] * count


def shape(dims, kind=F32):
    return jax.ShapeDtypeStruct(dims, kind)


def call(kernel, outs, operands, scalars=0, far=0, scratch=(), limit=8):
    many = isinstance(outs, tuple)
    return pl.pallas_call(
        kernel,
        out_shape=outs,
        in_specs=[pl.BlockSpec(memory_space=pltpu.SMEM)] * scalars
        + vmem(len(operands) - scalars - far)
        + [pl.BlockSpec(memory_space=pl.ANY)] * far,
        out_specs=tuple(vmem(len(outs))) if many else vmem(1)[0],
        scratch_shapes=list(scratch),
        compiler_params=pltpu.CompilerParams(vmem_limit_bytes=limit * MIB),
    )(*operands)


def fold(wide, folded_ref):
    rows, pieces = wide.shape[0], wide.shape[1] // LANES
    for c in range(pieces):
        folded_ref[pl.ds(c, rows, stride=pieces), :] = wide[:, c * LANES : (c + 1) * LANES]


def norm_kernel(far_hidden_ref, far_gain_ref, out_ref, fold_ref, hidden_ref, gain_ref, sems):
    copies = [
        pltpu.make_async_copy(far_hidden_ref, hidden_ref, sems.at[0]),
        pltpu.make_async_copy(far_gain_ref, gain_ref, sems.at[1]),
    ]
    for copy in copies:
        copy.start()
    for copy in copies:
        copy.wait()
    wide = hidden_ref[...].astype(F32)[:LIVE_MAX]
    factor = lax.rsqrt(jnp.mean(wide * wide, axis=-1, keepdims=True) + 1e-05)
    fold(wide * factor * gain_ref[...], fold_ref)
    out_ref[...] = fold_ref[...].astype(BF16)


def join_kernel(count, *refs):
    start = 0
    for ref in refs[:count]:
        refs[-1][start : start + ref.shape[0]] = ref[...]
        start += ref.shape[0]


def join(parts, after=()):
    rows = sum(part.shape[0] for part in parts)
    return call(
        functools.partial(join_kernel, len(parts)),
        shape((rows, parts[0].shape[1]), parts[0].dtype),
        (*parts, *after),
        far=len(after),
    )


def unfold_kernel(mine_ref, other_ref, out_ref, fold_ref):
    half = mine_ref.shape[0]
    fold_ref[:half] = mine_ref[...].astype(F32)
    fold_ref[half:] = other_ref[...].astype(F32)
    rows, pieces = out_ref.shape[0], out_ref.shape[1] // LANES
    for c in range(pieces):
        out_ref[:, c * LANES : (c + 1) * LANES] = fold_ref[
            pl.ds(c, rows, stride=pieces), :
        ].astype(BF16)


def load_kernel(far_ref, out_ref, sem):
    copy = pltpu.make_async_copy(far_ref, out_ref, sem)
    copy.start()
    copy.wait()


def load(array, limit):
    return pl.pallas_call(
        load_kernel,
        out_shape=pltpu.VMEM(array.shape, array.dtype),
        in_specs=[pl.BlockSpec(memory_space=pl.ANY)],
        out_specs=vmem(1)[0],
        scratch_shapes=[pltpu.SemaphoreType.DMA],
        compiler_params=pltpu.CompilerParams(vmem_limit_bytes=limit * MIB),
    )(array)


def add_kernel(count, *refs):
    total = refs[0][...]
    for ref in refs[1:count]:
        total = total + ref[...]
    refs[-1][...] = total


def conv_kernel(
    live_ref,
    both_ref,
    spot_ref,
    conv_ref,
    taps_ref,
    offset_ref,
    coef_ref,
    keep_ref,
    send_ref,
    mixed_ref,
    gate_ref,
    new_conv_ref,
    low_ref,
    alive_ref,
):
    index = lax.axis_index("weight")
    blocks = live_ref.shape[0]
    rows = conv_ref.shape[1]
    rows_dev = rows // blocks
    kept = mixed_ref.shape[0]
    block = jnp.bitwise_xor(spot_ref[0:1, :], index)
    turn = spot_ref[1:2, :]

    def places(height, span):
        line = lax.broadcasted_iota(jnp.int32, (height, kept), 0)
        return jnp.where(line == block * span + turn, 1.0, 0.0)

    fresh = jnp.dot(
        places(rows, rows_dev).astype(BF16),
        both_ref[0].astype(BF16),
        preferred_element_type=F32,
    )
    row_iota = lax.broadcasted_iota(jnp.int32, (rows_dev, 128), 0)
    for b in range(blocks):
        alive_ref[b * rows_dev : (b + 1) * rows_dev, :] = jnp.where(
            row_iota < live_ref[b], 1.0, 0.0
        )
    alive = alive_ref[:, 0:1] > 0.0
    states = [conv_ref[k].astype(F32) for k in range(TAPS - 1)] + [fresh]
    total = states[0] * taps_ref[0:1, :]
    for k in range(1, TAPS):
        total = total + states[k] * taps_ref[k : k + 1, :]
    mixed = silu(total + offset_ref[...]).astype(BF16)
    line = lax.broadcasted_iota(jnp.int32, (kept, rows), 0)
    column = lax.broadcasted_iota(jnp.int32, (kept, rows), 1)
    chosen = (line // LIVE_MAX) * rows_dev + line % LIVE_MAX == column
    mixed = jnp.dot(
        jnp.where(chosen, 1.0, 0.0).astype(BF16), mixed, preferred_element_type=F32
    ).astype(BF16)
    mixed_ref[...] = mixed
    low_ref[...] = lax.dot_general(
        mixed, coef_ref[...], (((1,), (1,)), ((), ())), preferred_element_type=F32
    )
    half = keep_ref.shape[0]
    core = index % 2
    keep_ref[...] = low_ref[pl.ds(pl.multiple_of(core * half, 8), half), :]
    send_ref[...] = low_ref[pl.ds(pl.multiple_of((1 - core) * half, 8), half), :]
    for k in range(TAPS - 1):
        new_conv_ref[k] = jnp.where(alive, states[k + 1], states[k]).astype(BF16)
    gate_ref[...] = jnp.dot(
        places(kept, LIVE_MAX),
        silu(both_ref[1]),
        precision=lax.Precision.HIGHEST,
        preferred_element_type=F32,
    )


def state_kernel(
    live_ref,
    mine_ref,
    other_ref,
    spot_ref,
    mixed_ref,
    gate_ref,
    step_weight_ref,
    bias_ref,
    rates_ref,
    skip_ref,
    state_ref,
    out_weight_ref,
    new_state_ref,
    keep_ref,
    send_ref,
    low_ref,
    read_ref,
    alive_ref,
):
    index = lax.axis_index("weight")
    blocks = live_ref.shape[0]
    rows_dev = state_ref.shape[0] // blocks
    kept = mixed_ref.shape[0]
    half = mine_ref.shape[0]
    core = index % 2
    low_ref[pl.ds(pl.multiple_of(core * half, 8), half), :] = mine_ref[...]
    low_ref[pl.ds(pl.multiple_of((1 - core) * half, 8), half), :] = other_ref[...]
    step_size = softplus(
        jnp.dot(
            low_ref[:, :DTR].astype(BF16), step_weight_ref[...], preferred_element_type=F32
        )
        + bias_ref[...]
    )
    coefs = low_ref[:, DTR:].T
    x_wide = mixed_ref[...].astype(F32)
    driven = step_size * x_wide
    rates = -jnp.exp(rates_ref[...])
    for b in range(blocks):
        for t in range(LIVE_MAX):
            r = b * LIVE_MAX + t
            wide = state_ref[b * rows_dev + t].astype(F32)
            updated = (
                jnp.exp(step_size[r : r + 1, :] * rates) * wide
                + coefs[:NSTATE, r : r + 1] * driven[r : r + 1, :]
            )
            read_ref[r : r + 1, :] = jnp.sum(
                coefs[NSTATE:, r : r + 1] * updated, axis=0, keepdims=True
            )
            live = t < live_ref[b]
            alive_ref[r : r + 1, :] = jnp.full((1, 128), jnp.where(live, 1.0, 0.0))
            new_state_ref[b * rows_dev + t] = jnp.where(live, updated, wide).astype(BF16)
        for t in range(LIVE_MAX, rows_dev):
            new_state_ref[b * rows_dev + t] = state_ref[b * rows_dev + t]
    readout = read_ref[...] + skip_ref[...] * x_wide
    gated = jnp.where(alive_ref[:, 0:1] > 0.0, readout * gate_ref[...], 0.0).astype(BF16)
    block = jnp.bitwise_xor(spot_ref[:, 0:1], index)
    column = lax.broadcasted_iota(jnp.int32, (kept, kept), 1)
    pick = jnp.where(column == block * LIVE_MAX + spot_ref[:, 1:2], 1.0, 0.0).astype(BF16)
    picked = jnp.dot(pick, gated, preferred_element_type=F32).astype(BF16)
    width = out_weight_ref.shape[1] // 4
    for c in range(4):
        cols = slice(c * width, (c + 1) * width)
        part = jnp.dot(picked, out_weight_ref[:, cols], preferred_element_type=F32)
        keep_ref[:, cols] = part[: kept // 2]
        send_ref[:, cols] = part[kept // 2 :].astype(send_ref.dtype)


def first_sum_kernel(keep_ref, got_ref, *refs):
    outs, fold_ref = refs[:-1], refs[-1]
    fold(keep_ref[...] + got_ref[...].astype(F32), fold_ref)
    size = outs[0].shape[0]
    for k, out in enumerate(outs):
        out[...] = fold_ref[k * size : (k + 1) * size].astype(out.dtype)


def next_sum_kernel(count, *refs):
    parts, outs = refs[:count], refs[count:]
    size = outs[0].shape[0]
    for k, out in enumerate(outs):
        rows = slice(k * size, (k + 1) * size)
        total = parts[0][rows]
        for part in parts[1:]:
            total = total + part[rows].astype(F32)
        out[...] = total.astype(out.dtype)


def last_sum_kernel(*refs):
    hidden_ref, parts, out_ref, fold_ref = refs[0], refs[1:-2], refs[-2], refs[-1]
    total = parts[0][...]
    for part in parts[1:]:
        total = total + part[...].astype(F32)
    fold_ref[...] = total
    pieces = out_ref.shape[1] // LANES
    for c in range(pieces):
        span = slice(c * LANES, (c + 1) * LANES)
        wide = hidden_ref[:, span].astype(F32)
        own = wide[:LIVE_MAX] + fold_ref[pl.ds(c, LIVE_MAX, stride=pieces), :]
        out_ref[:, span] = jnp.concatenate([own, wide[LIVE_MAX:]], axis=0).astype(BF16)


def body(
    hidden,
    norm_gain,
    in_weight,
    conv_weight,
    conv_offset,
    coef_weight,
    step_weight,
    step_bias,
    log_rates,
    skip_gain,
    out_weight,
    ssm_state,
    conv_state,
    live_counts,
):
    devices = lax.axis_size("weight")
    rows_dev, width = hidden.shape
    rows = devices * rows_dev
    kept = devices * LIVE_MAX
    channels = in_weight.shape[2]
    low_width = coef_weight.shape[1]
    phases = gather_phases(devices)
    order = [0]
    for phase in phases:
        order = order + [o ^ s for s in phase for o in order]
    spots = jnp.array(
        [[o for o in order for _ in range(LIVE_MAX)], list(range(LIVE_MAX)) * devices],
        jnp.int32,
    )
    pieces = width // LANES
    slab = LIVE_MAX * pieces

    gathered = call(
        norm_kernel,
        pltpu.VMEM((slab, LANES), BF16),
        (hidden, norm_gain.reshape(1, width)),
        far=2,
        scratch=[
            pltpu.VMEM((slab, LANES), F32),
            pltpu.VMEM(hidden.shape, BF16),
            pltpu.VMEM((1, width), F32),
            pltpu.SemaphoreType.DMA((2,)),
        ],
        limit=60,
    )
    for k, phase in enumerate(phases[:-1]):
        after = ()
        if k == len(phases) - 2:
            near_weight = load(in_weight, 34)
            after = (near_weight,)
        gathered = join([gathered] + [swap(gathered, s, devices) for s in phase], after)
    normed = call(
        unfold_kernel,
        shape((kept, width), BF16),
        (gathered, swap(gathered, 1, devices)),
        scratch=[pltpu.VMEM((kept * pieces, LANES), F32)],
        limit=12,
    )
    both = jnp.einsum("rd,dbc->brc", normed, near_weight, preferred_element_type=F32)

    keep, send, mixed_x, gate, new_conv = call(
        conv_kernel,
        (
            shape((kept // 2, low_width)),
            shape((kept // 2, low_width)),
            shape((kept, channels), BF16),
            shape((kept, channels)),
            shape((TAPS - 1, rows, channels), BF16),
        ),
        (
            live_counts,
            both,
            spots,
            conv_state.transpose(1, 0, 2),
            conv_weight,
            conv_offset.reshape(1, channels),
            coef_weight.T,
        ),
        scalars=1,
        scratch=[pltpu.VMEM((kept, low_width), F32), pltpu.VMEM((rows, 128), F32)],
        limit=16,
    )

    def add(*parts, after=()):
        return call(
            functools.partial(add_kernel, len(parts)),
            shape(parts[0].shape),
            (*parts, *after),
            far=len(after),
        )

    low = add(keep, swap(send, 1, devices))
    exchanges = sum_phases(devices)
    for k, phase in enumerate(exchanges):
        after = ()
        if k == len(exchanges) - 1:
            near_out = load(out_weight, 50)
            after = (near_out,)
        low = add(low, *[swap(low, s, devices) for s in phase], after=after)
    other = swap(low, 1, devices)

    new_state, keep, send = call(
        state_kernel,
        (
            shape(ssm_state.shape, BF16),
            shape((kept // 2, width)),
            shape((kept // 2, width)),
        ),
        (
            live_counts,
            low,
            other,
            spots.T,
            mixed_x,
            gate,
            step_weight,
            step_bias.reshape(1, channels),
            log_rates,
            skip_gain.reshape(1, channels),
            ssm_state,
            near_out,
        ),
        scalars=1,
        scratch=[
            pltpu.VMEM((kept, low_width), F32),
            pltpu.VMEM((kept, channels), F32),
            pltpu.VMEM((kept, 128), F32),
        ],
        limit=32,
    )

    scatter = list(reversed(phases[:-1]))
    total, kernel = (keep, swap(send, 1, devices)), first_sum_kernel
    size = kept // 2 * pieces
    scratch = [pltpu.VMEM((size, LANES), F32)]
    for phase in scatter:
        size //= len(phase) + 1
        parts = call(
            kernel,
            (shape((size, LANES)),) + (shape((size, LANES), BF16),) * len(phase),
            total,
            scratch=scratch,
        )
        total = (parts[0],) + tuple(swap(p, s, devices) for p, s in zip(parts[1:], phase))
        kernel, scratch = functools.partial(next_sum_kernel, len(total)), ()
    mixed = call(
        last_sum_kernel,
        shape(hidden.shape, BF16),
        (hidden,) + total,
        scratch=[pltpu.VMEM((slab, LANES), F32)],
    )
    return (mixed, new_state, new_conv.transpose(1, 0, 2))


def solution(mesh):
    in_specs = (
        P(("groups", "weight"), None),
        P(),
        P(None, None, "weight"),
        P(None, "weight"),
        P("weight"),
        P("weight", None),
        P(None, "weight"),
        P("weight"),
        P(None, "weight"),
        P("weight"),
        P("weight", None),
        P("groups", None, "weight"),
        P("groups", None, "weight"),
        P("groups"),
    )
    out_specs = (
        P(("groups", "weight"), None),
        P("groups", None, "weight"),
        P("groups", None, "weight"),
    )
    return jax.shard_map(body, mesh=mesh, in_specs=in_specs, out_specs=out_specs, check_vma=False)
```

time: 80.7 us -> 66.3 us (0.82)
  Pallas kernels: 6.25 us -> 18.5 us
  waiting for transfers between devices: 36 us -> 27.1 us
  matrix products: 8.91 us -> 3.15 us
  other arithmetic: 4.75 us -> 0 us
  local copies, waits for them, and re-layouts: 4.55 us -> 0.09 us
  starting transfers between devices: 19.1 us -> 16.3 us
    pallas_call x2 -> x14, Pallas kernels: 6.25 us -> 18.5 us  [the longest x12 9.3 us: call(): pl.pallas_call(kernel, out_shape=outs, in_specs=[pl.BlockSpec(memory_spac...]
    ppermute x16, waiting for transfers between devices: 36 us -> 27.1 us  [swap(): lax.ppermute(value, 'weight', [(i, i ^ shift) for i in range(devices)])]
    dot_general x1, matrix products: 8.91 us -> 3.15 us  [body(): jnp.einsum('rd,dbc->brc', normed, near_weight, preferred_element_type=F32)]
    unnamed x22 -> x26, local copies, waits for them, and re-layouts: 3.44 us -> 0.09 us
    ppermute x16, starting transfers between devices: 19.1 us -> 16.3 us  [swap(): lax.ppermute(value, 'weight', [(i, i ^ shift) for i in range(devices)])]
    convert_element_type x5 -> x0, other arithmetic: 1.84 us -> none  [the longest x1 0.95 us: rms_normed(): return (wide * factor * norm_gain).astype(BF16)]
    reduce_sum x1 -> x0, other arithmetic: 1.02 us -> none  [rms_normed(): factor = lax.rsqrt(jnp.mean(wide * wide, axis=-1, keepdims=True) + 1e-05)]
    concatenate x2 -> x0, other arithmetic: 0.86 us -> none  [the longest x1 0.7 us: body(): mixed = jnp.concatenate([own, hidden[LIVE_MAX:]], axis=0)]
  transfers between devices with their start and end apart: 16 -> 16, of which waited for: 15 -> 13; matrix products, arithmetic and copies ran while one was open for 2% -> 0% of each run, Pallas kernels for 0% -> 14%
where the time goes in v2:
time: 66.3 us; the launch traced here: 66.1 us
  waiting for transfers between devices  27.1 us (41%)
  Pallas kernels  18.5 us (28%)
  starting transfers between devices  16.3 us (25%)
  matrix products  3.15 us (5%)
  between operations  0.91 us (1%)
    ppermute x16, waiting for transfers between devices, swap(): lax.ppermute(value, 'weight', [(i, i ^ shift) for i in range(devices)])  27.1 us
    ppermute x16, starting transfers between devices, swap(): lax.ppermute(value, 'weight', [(i, i ^ shift) for i in range(devices)])  16.3 us
    pallas_call x12, Pallas kernels, call(): pl.pallas_call(kernel, out_shape=outs, in_specs=[pl.BlockSpec(memory_spac...  9.3 us
    pallas_call x2, Pallas kernels, load(): pl.pallas_call(load_kernel, out_shape=pltpu.VMEM(array.shape, array.dtype...  9.17 us
    dot_general x1, matrix products, body(): jnp.einsum('rd,dbc->brc', normed, near_weight, preferred_element_type=F32)  3.15 us
  transfers between devices with their start and end apart: 16, of which 13 were waited for; matrix products, arithmetic and copies ran while one was open for 0% of the time, Pallas kernels for 14%

profile of v2, /device:TPU:0, one launch (start us, length us, event | category | flops | bytes accessed | tf_op | source)
XLA Modules:
  0.0 66.1 jit_solution(8237982807876926450)
XLA Ops:
  0.6 1.1 %shard_map.166.refs_0_ = bf16[192,128]{1,0:T(8,128)(2,1)S(1)} custom-call(bf16[4,8192]{1,0:T(4,128)(2,1)} %refs_0_.1, f32[1,8192]{1,0:T(1,128)} %bitcast.17), custom_call_target="tpu_custom_call" | custom-call | tf_op jit(solution)/shard_map/pallas_call | solution.py:68
  1.7 3.1 %collective-permute-start = (bf16[192,128]{1,0:T(8,128)(2,1)S(1)}, bf16[192,128]{1,0:T(8,128)(2,1)S(1)}, u32[]{:S(2)}, u32[]{:S(2)}) collective-permute-start(bf16[192,128]{1,0:T(8,128)(2,1)S(1)} %shard_map.166.refs_0_), channel_id=1, source_target_pairs={{0,4},{1,5},{2,6},{3,7},{4,0},{5,1},{6,2},{7,3},{8,12},{9,13},{10,... | collective-permute-start | bytes 147464 | tf_op jit(solution)/shard_map/ppermute | solution.py:47
  4.8 2.6 %collective-permute-start.1 = (bf16[192,128]{1,0:T(8,128)(2,1)S(1)}, bf16[192,128]{1,0:T(8,128)(2,1)S(1)}, u32[]{:S(2)}, u32[]{:S(2)}) collective-permute-start(bf16[192,128]{1,0:T(8,128)(2,1)S(1)} %shard_map.166.refs_0_), channel_id=1, source_target_pairs={{0,8},{1,9},{2,10},{3,11},{4,12},{5,13},{6,14},{7,15},{8,0},{9,1},... | collective-permute-start | bytes 147464 | tf_op jit(solution)/shard_map/ppermute | solution.py:47
  7.4 3.3 %collective-permute-done.1.refs_2_ = bf16[192,128]{1,0:T(8,128)(2,1)S(1)} collective-permute-done((bf16[192,128]{1,0:T(8,128)(2,1)S(1)}, bf16[192,128]{1,0:T(8,128)(2,1)S(1)}, u32[]{:S(2)}, u32[]{:S(2)}) %collective-permute-start.1) | collective-permute-done | bytes 49184 | tf_op jit(solution)/shard_map/ppermute | solution.py:47
  10.7 2.6 %collective-permute-done.2.refs_3_ = bf16[192,128]{1,0:T(8,128)(2,1)S(1)} collective-permute-done((bf16[192,128]{1,0:T(8,128)(2,1)S(1)}, bf16[192,128]{1,0:T(8,128)(2,1)S(1)}, u32[]{:S(2)}, u32[]{:S(2)}) %collective-permute-start.2) | collective-permute-done | bytes 49184 | tf_op jit(solution)/shard_map/ppermute | solution.py:47
  13.3 1.6 %collective-permute-start.3 = (bf16[768,128]{1,0:T(8,128)(2,1)S(1)}, bf16[768,128]{1,0:T(8,128)(2,1)S(1)}, u32[]{:S(2)}, u32[]{:S(2)}) collective-permute-start(bf16[768,128]{1,0:T(8,128)(2,1)S(1)} %shard_map.167.refs_0_), channel_id=1, source_target_pairs={{0,2},{1,3},{2,0},{3,1},{4,6},{5,7},{6,4},{7,5},{8,10},{9,11},{10,... | collective-permute-start | bytes 589832 | tf_op jit(solution)/shard_map/ppermute | solution.py:47
  14.9 5.8 %shard_map.168.refs_2_ = bf16[8192,2,512]{2,1,0:T(2,128)(2,1)S(1)} custom-call(bf16[8192,2,512]{2,1,0:T(2,128)(2,1)} %far_ref.2), custom_call_target="tpu_custom_call" | custom-call | tf_op jit(solution)/shard_map/pallas_call | solution.py:136
  20.7 0.1 collective-permute-start.4
  20.8 1.7 %collective-permute-done.4.other_ref = bf16[1536,128]{1,0:T(8,128)(2,1)S(1)} collective-permute-done((bf16[1536,128]{1,0:T(8,128)(2,1)S(1)}, bf16[1536,128]{1,0:T(8,128)(2,1)S(1)}, u32[]{:S(2)}, u32[]{:S(2)}) %collective-permute-start.4) | collective-permute-done | bytes 393248 | tf_op jit(solution)/shard_map/ppermute | solution.py:47
  22.5 1.0 %shard_map.170 = bf16[48,8192]{1,0:T(8,128)(2,1)S(1)} custom-call(bf16[1536,128]{1,0:T(8,128)(2,1)S(1)} %shard_map.169.mine_ref, bf16[1536,128]{1,0:T(8,128)(2,1)S(1)} %collective-permute-done.4.other_ref), custom_call_target="tpu_custom_call" | custom-call | tf_op jit(solution)/shard_map/pallas_call | solution.py:68
  23.5 0.0 copy-start.1
  23.5 0.0 copy-start.4
  23.5 0.0 copy-start.7
  23.6 0.0 copy-start.8
  23.6 0.0 copy-start.11
  23.6 0.0 copy-start.12
  23.6 3.1 %fusion.2.both_ref = f32[2,48,512]{2,1,0:T(8,128)S(1)} fusion(bf16[8192,2,512]{2,1,0:T(2,128)(2,1)S(1)} %shard_map.168.refs_2_, bf16[48,8192]{1,0:T(8,128)(2,1)S(1)} %shard_map.170), kind=kOutput, calls=%fused_computation.2 | convolution fusion | flops 805306368 | bytes 17760256 | tf_op jit(solution)/shard_map/rd,dbc->brc/dot_general | solution.py:381
  26.7 0.0 copy-start
  26.8 0.0 copy-start.2
  26.8 0.0 copy-start.5
  26.8 0.0 copy-start.6
  26.8 0.0 copy-start.9
  26.8 0.0 copy-start.10
  26.9 1.6 %shard_map.171 = (f32[24,544]{1,0:T(8,128)S(1)}, f32[24,544]{1,0:T(8,128)S(1)}, bf16[48,512]{1,0:T(8,128)(2,1)S(1)}, f32[48,512]{1,0:T(8,128)S(1)}, bf16[3,64,512]{2,1,0:T(8,128)(2,1)}) custom-call(s32[16]{0:T(128)S(1)} %copy-done.11, f32[2,48,512]{2,1,0:T(8,128)S(1)} %fusion.2.both_ref, s32[2,48]{1,0:T(2,128)S(1)} %copy-done.12, ...), custom_call_target="tpu_custom_call" | custom-call | tf_op jit(solution)/shard_map/pallas_call | solution.py:68
  28.5 0.1 collective-permute-start.5
  28.6 1.1 %collective-permute-done.5.refs_1_ = f32[24,544]{1,0:T(8,128)S(1)} collective-permute-done((f32[24,544]{1,0:T(8,128)S(1)}, f32[24,544]{1,0:T(8,128)S(1)}, u32[]{:S(2)}, u32[]{:S(2)}) %collective-permute-start.5) | collective-permute-done | bytes 52256 | tf_op jit(solution)/shard_map/ppermute | solution.py:47
  29.8 0.6 collective-permute-start.6
  30.3 3.0 %collective-permute-start.8 = (f32[24,544]{1,0:T(8,128)S(1)}, f32[24,544]{1,0:T(8,128)S(1)}, u32[]{:S(2)}, u32[]{:S(2)}) collective-permute-start(f32[24,544]{1,0:T(8,128)S(1)} %shard_map.172.refs_0_), channel_id=1, source_target_pairs={{0,6},{1,7},{2,4},{3,5},{4,2},{5,3},{6,0},{7,1},{8,14},{9,15},{10,... | collective-permute-start | bytes 156680 | tf_op jit(solution)/shard_map/ppermute | solution.py:47
  33.3 0.7 %collective-permute-done.6.refs_1_ = f32[24,544]{1,0:T(8,128)S(1)} collective-permute-done((f32[24,544]{1,0:T(8,128)S(1)}, f32[24,544]{1,0:T(8,128)S(1)}, u32[]{:S(2)}, u32[]{:S(2)}) %collective-permute-start.6) | collective-permute-done | bytes 52256 | tf_op jit(solution)/shard_map/ppermute | solution.py:47
  34.1 1.0 %collective-permute-done.7.refs_2_ = f32[24,544]{1,0:T(8,128)S(1)} collective-permute-done((f32[24,544]{1,0:T(8,128)S(1)}, f32[24,544]{1,0:T(8,128)S(1)}, u32[]{:S(2)}, u32[]{:S(2)}) %collective-permute-start.7) | collective-permute-done | bytes 52256 | tf_op jit(solution)/shard_map/ppermute | solution.py:47
  35.1 1.3 %collective-permute-done.8.refs_3_ = f32[24,544]{1,0:T(8,128)S(1)} collective-permute-done((f32[24,544]{1,0:T(8,128)S(1)}, f32[24,544]{1,0:T(8,128)S(1)}, u32[]{:S(2)}, u32[]{:S(2)}) %collective-permute-start.8) | collective-permute-done | bytes 52256 | tf_op jit(solution)/shard_map/ppermute | solution.py:47
  36.4 0.4 collective-permute-start.9
  36.9 3.4 %shard_map.174.refs_2_.out_weight_ref = bf16[512,8192]{1,0:T(8,128)(2,1)S(1)} custom-call(bf16[512,8192]{1,0:T(8,128)(2,1)} %far_ref.3), custom_call_target="tpu_custom_call" | custom-call | tf_op jit(solution)/shard_map/pallas_call | solution.py:136
  40.3 2.0 %collective-permute-done.9.refs_1_ = f32[24,544]{1,0:T(8,128)S(1)} collective-permute-done((f32[24,544]{1,0:T(8,128)S(1)}, f32[24,544]{1,0:T(8,128)S(1)}, u32[]{:S(2)}, u32[]{:S(2)}) %collective-permute-start.9) | collective-permute-done | bytes 52256 | tf_op jit(solution)/shard_map/ppermute | solution.py:47
  42.3 0.1 collective-permute-start.10
  42.4 1.2 %collective-permute-done.10.other_ref = f32[24,544]{1,0:T(8,128)S(1)} collective-permute-done((f32[24,544]{1,0:T(8,128)S(1)}, f32[24,544]{1,0:T(8,128)S(1)}, u32[]{:S(2)}, u32[]{:S(2)}) %collective-permute-start.10) | collective-permute-done | bytes 52256 | tf_op jit(solution)/shard_map/ppermute | solution.py:47
  43.7 4.2 %shard_map.176 = (bf16[64,16,512]{2,1,0:T(8,128)(2,1)}, f32[24,8192]{1,0:T(8,128)S(1)}, f32[24,8192]{1,0:T(8,128)S(1)}) custom-call(s32[16]{0:T(128)S(1)} %copy-done.11, f32[24,544]{1,0:T(8,128)S(1)} %shard_map.175.mine_ref, f32[24,544]{1,0:T(8,128)S(1)} %collective-permute-done.10.other_ref, s32[48,2]{1,0:T(8,128)S(1)} %copy-done.6, ...), custom_call_target="tpu_custom_call" | custom-call | tf_op jit(solution)/shard_map/pallas_call | solution.py:68
  47.9 0.2 collective-permute-start.11
  48.0 2.1 %collective-permute-done.11.got_ref = f32[24,8192]{1,0:T(8,128)S(1)} collective-permute-done((f32[24,8192]{1,0:T(8,128)S(1)}, f32[24,8192]{1,0:T(8,128)S(1)}, u32[]{:S(2)}, u32[]{:S(2)}) %collective-permute-start.11) | collective-permute-done | bytes 786464 | tf_op jit(solution)/shard_map/ppermute | solution.py:47
  50.2 0.5 shard_map.177
  50.7 0.2 collective-permute-start.12
  50.9 6.8 %collective-permute-done.12.refs_1_ = bf16[768,128]{1,0:T(8,128)(2,1)S(1)} collective-permute-done((bf16[768,128]{1,0:T(8,128)(2,1)S(1)}, bf16[768,128]{1,0:T(8,128)(2,1)S(1)}, u32[]{:S(2)}, u32[]{:S(2)}) %collective-permute-start.12) | collective-permute-done | bytes 196640 | tf_op jit(solution)/shard_map/ppermute | solution.py:47
  57.7 0.6 collective-permute-start.13
  58.3 1.1 %collective-permute-start.14 = (bf16[192,128]{1,0:T(8,128)(2,1)S(1)}, bf16[192,128]{1,0:T(8,128)(2,1)S(1)}, u32[]{:S(2)}, u32[]{:S(2)}) collective-permute-start(bf16[192,128]{1,0:T(8,128)(2,1)S(1)} %get-tuple-element.27), channel_id=1, source_target_pairs={{0,8},{1,9},{2,10},{3,11},{4,12},{5,13},{6,14},{7,15},{8,0},{9,1},... | collective-permute-start | bytes 147464 | tf_op jit(solution)/shard_map/ppermute | solution.py:47
  59.4 2.7 %collective-permute-start.15 = (bf16[192,128]{1,0:T(8,128)(2,1)S(1)}, bf16[192,128]{1,0:T(8,128)(2,1)S(1)}, u32[]{:S(2)}, u32[]{:S(2)}) collective-permute-start(bf16[192,128]{1,0:T(8,128)(2,1)S(1)} %get-tuple-element.28), channel_id=1, source_target_pairs={{0,12},{1,13},{2,14},{3,15},{4,8},{5,9},{6,10},{7,11},{8,4},{9,5},... | collective-permute-start | bytes 147464 | tf_op jit(solution)/shard_map/ppermute | solution.py:47
  62.2 1.5 %collective-permute-done.14.refs_3_ = bf16[192,128]{1,0:T(8,128)(2,1)S(1)} collective-permute-done((bf16[192,128]{1,0:T(8,128)(2,1)S(1)}, bf16[192,128]{1,0:T(8,128)(2,1)S(1)}, u32[]{:S(2)}, u32[]{:S(2)}) %collective-permute-start.14) | collective-permute-done | bytes 49184 | tf_op jit(solution)/shard_map/ppermute | solution.py:47
  63.7 1.7 %collective-permute-done.15.refs_4_ = bf16[192,128]{1,0:T(8,128)(2,1)S(1)} collective-permute-done((bf16[192,128]{1,0:T(8,128)(2,1)S(1)}, bf16[192,128]{1,0:T(8,128)(2,1)S(1)}, u32[]{:S(2)}, u32[]{:S(2)}) %collective-permute-start.15) | collective-permute-done | bytes 49184 | tf_op jit(solution)/shard_map/ppermute | solution.py:47
  65.3 0.7 %shard_map.179 = bf16[4,8192]{1,0:T(4,128)(2,1)} custom-call(bf16[4,8192]{1,0:T(4,128)(2,1)S(1)} %copy-done.3, f32[192,128]{1,0:T(8,128)S(1)} %get-tuple-element.25.refs_1_, bf16[192,128]{1,0:T(8,128)(2,1)S(1)} %collective-permute-done.13.refs_2_, bf16[192,128]{1,0:T(8,128)(2,1)S(1)} %collective-permute-done.14.refs_3_, ...), custom_call_target="tpu_custom_call" | custom-call | tf_op jit(solution)/shard_map/pallas_call | solution.py:68
  (25 shorter events, 0.2 us)
Async XLA Ops:
  1.7 5.7 %collective-permute-start = (bf16[192,128]{1,0:T(8,128)(2,1)S(1)}, bf16[192,128]{1,0:T(8,128)(2,1)S(1)}, u32[]{:S(2)}, u32[]{:S(2)}) collective-permute-start(bf16[192,128]{1,0:T(8,128)(2,1)S(1)} %shard_map.166.refs_0_), channel_id=1, source_target_pairs={{0,4},{1,5},{2,6},{3,7},{4,0},{5,1},{6,2},{7,3},{8,12},{9,13},{10,... | collective-permute-start | bytes 147464 | tf_op jit(solution)/shard_map/ppermute | solution.py:47
  4.8 5.9 %collective-permute-start.1 = (bf16[192,128]{1,0:T(8,128)(2,1)S(1)}, bf16[192,128]{1,0:T(8,128)(2,1)S(1)}, u32[]{:S(2)}, u32[]{:S(2)}) collective-permute-start(bf16[192,128]{1,0:T(8,128)(2,1)S(1)} %shard_map.166.refs_0_), channel_id=1, source_target_pairs={{0,8},{1,9},{2,10},{3,11},{4,12},{5,13},{6,14},{7,15},{8,0},{9,1},... | collective-permute-start | bytes 147464 | tf_op jit(solution)/shard_map/ppermute | solution.py:47
  7.4 5.9 %collective-permute-start.2 = (bf16[192,128]{1,0:T(8,128)(2,1)S(1)}, bf16[192,128]{1,0:T(8,128)(2,1)S(1)}, u32[]{:S(2)}, u32[]{:S(2)}) collective-permute-start(bf16[192,128]{1,0:T(8,128)(2,1)S(1)} %shard_map.166.refs_0_), channel_id=1, source_target_pairs={{0,12},{1,13},{2,14},{3,15},{4,8},{5,9},{6,10},{7,11},{8,4},{9,5},... | collective-permute-start | bytes 147464 | tf_op jit(solution)/shard_map/ppermute | solution.py:47
  13.3 7.4 %collective-permute-start.3 = (bf16[768,128]{1,0:T(8,128)(2,1)S(1)}, bf16[768,128]{1,0:T(8,128)(2,1)S(1)}, u32[]{:S(2)}, u32[]{:S(2)}) collective-permute-start(bf16[768,128]{1,0:T(8,128)(2,1)S(1)} %shard_map.167.refs_0_), channel_id=1, source_target_pairs={{0,2},{1,3},{2,0},{3,1},{4,6},{5,7},{6,4},{7,5},{8,10},{9,11},{10,... | collective-permute-start | bytes 589832 | tf_op jit(solution)/shard_map/ppermute | solution.py:47
  20.7 1.8 %collective-permute-start.4 = (bf16[1536,128]{1,0:T(8,128)(2,1)S(1)}, bf16[1536,128]{1,0:T(8,128)(2,1)S(1)}, u32[]{:S(2)}, u32[]{:S(2)}) collective-permute-start(bf16[1536,128]{1,0:T(8,128)(2,1)S(1)} %shard_map.169.mine_ref), channel_id=1, source_target_pairs={{0,1},{1,0},{2,3},{3,2},{4,5},{5,4},{6,7},{7,6},{8,9},{9,8},{10,11... | collective-permute-start | bytes 1179656 | tf_op jit(solution)/shard_map/ppermute | solution.py:47
  23.5 3.3 %copy-start.1 = (bf16[512,544]{0,1:T(8,128)(2,1)S(1)}, bf16[512,544]{0,1:T(8,128)(2,1)}, u32[]{:S(2)}) copy-start(bf16[512,544]{0,1:T(8,128)(2,1)} %param.20) | copy-start | bytes 1671172
  23.5 3.3 %copy-start.4 = (bf16[64,3,512]{2,0,1:T(8,128)(2,1)S(1)}, bf16[64,3,512]{2,0,1:T(8,128)(2,1)}, u32[]{:S(2)}) copy-start(bf16[64,3,512]{2,0,1:T(8,128)(2,1)} %param.27) | copy-start | bytes 589828
  23.5 3.3 %copy-start.7 = (f32[4,512]{1,0:T(4,128)S(1)}, f32[4,512]{1,0:T(4,128)}, u32[]{:S(2)}) copy-start(f32[4,512]{1,0:T(4,128)} %taps_ref.1) | copy-start | bytes 24580
  23.6 3.3 %copy-start.8 = (f32[512]{0:T(512)S(1)}, f32[512]{0:T(512)}, u32[]{:S(2)}) copy-start(f32[512]{0:T(512)} %param.19) | copy-start | bytes 6148
  23.6 3.3 %copy-start.11 = (s32[16]{0:T(128)S(1)}, s32[16]{0:T(128)}, u32[]{:S(2)}) copy-start(s32[16]{0:T(128)} %live_ref.3) | copy-start | bytes 196
  23.6 3.3 %copy-start.12 = (s32[2,48]{1,0:T(2,128)S(1)}, s32[2,48]{1,0:T(2,128)}, u32[]{:S(2)}) copy-start(s32[2,48]{1,0:T(2,128)} %constant.2.clone.spot_ref) | copy-start | bytes 1156
  26.7 16.9 %copy-start = (bf16[64,16,512]{2,1,0:T(8,128)(2,1)S(1)}, bf16[64,16,512]{2,1,0:T(8,128)(2,1)}, u32[]{:S(2)}) copy-start(bf16[64,16,512]{2,1,0:T(8,128)(2,1)} %state_ref.1) | copy-start | bytes 3145732
  26.8 16.9 %copy-start.2 = (bf16[512,512]{1,0:T(8,128)(2,1)S(1)}, bf16[512,512]{1,0:T(8,128)(2,1)}, u32[]{:S(2)}) copy-start(bf16[512,512]{1,0:T(8,128)(2,1)} %step_weight_ref.1) | copy-start | bytes 1572868
  26.8 16.8 %copy-start.5 = (f32[16,512]{1,0:T(8,128)S(1)}, f32[16,512]{1,0:T(8,128)}, u32[]{:S(2)}) copy-start(f32[16,512]{1,0:T(8,128)} %rates_ref.1) | copy-start | bytes 98308
  26.8 16.8 %copy-start.6 = (s32[48,2]{1,0:T(8,128)S(1)}, s32[48,2]{1,0:T(8,128)}, u32[]{:S(2)}) copy-start(s32[48,2]{1,0:T(8,128)} %constant.4.spot_ref) | copy-start | bytes 1156
  26.8 16.8 %copy-start.9 = (f32[512]{0:T(512)S(1)}, f32[512]{0:T(512)}, u32[]{:S(2)}) copy-start(f32[512]{0:T(512)} %param.22) | copy-start | bytes 6148
  26.8 16.8 %copy-start.10 = (f32[512]{0:T(512)S(1)}, f32[512]{0:T(512)}, u32[]{:S(2)}) copy-start(f32[512]{0:T(512)} %param.24) | copy-start | bytes 6148
  28.5 1.2 %collective-permute-start.5 = (f32[24,544]{1,0:T(8,128)S(1)}, f32[24,544]{1,0:T(8,128)S(1)}, u32[]{:S(2)}, u32[]{:S(2)}) collective-permute-start(f32[24,544]{1,0:T(8,128)S(1)} %get-tuple-element.18), channel_id=1, source_target_pairs={{0,1},{1,0},{2,3},{3,2},{4,5},{5,4},{6,7},{7,6},{8,9},{9,8},{10,11... | collective-permute-start | bytes 156680 | tf_op jit(solution)/shard_map/ppermute | solution.py:47
  29.8 4.3 %collective-permute-start.6 = (f32[24,544]{1,0:T(8,128)S(1)}, f32[24,544]{1,0:T(8,128)S(1)}, u32[]{:S(2)}, u32[]{:S(2)}) collective-permute-start(f32[24,544]{1,0:T(8,128)S(1)} %shard_map.172.refs_0_), channel_id=1, source_target_pairs={{0,2},{1,3},{2,0},{3,1},{4,6},{5,7},{6,4},{7,5},{8,10},{9,11},{10,... | collective-permute-start | bytes 156680 | tf_op jit(solution)/shard_map/ppermute | solution.py:47
  30.3 4.7 %collective-permute-start.7 = (f32[24,544]{1,0:T(8,128)S(1)}, f32[24,544]{1,0:T(8,128)S(1)}, u32[]{:S(2)}, u32[]{:S(2)}) collective-permute-start(f32[24,544]{1,0:T(8,128)S(1)} %shard_map.172.refs_0_), channel_id=1, source_target_pairs={{0,4},{1,5},{2,6},{3,7},{4,0},{5,1},{6,2},{7,3},{8,12},{9,13},{10,... | collective-permute-start | bytes 156680 | tf_op jit(solution)/shard_map/ppermute | solution.py:47
  30.3 6.1 %collective-permute-start.8 = (f32[24,544]{1,0:T(8,128)S(1)}, f32[24,544]{1,0:T(8,128)S(1)}, u32[]{:S(2)}, u32[]{:S(2)}) collective-permute-start(f32[24,544]{1,0:T(8,128)S(1)} %shard_map.172.refs_0_), channel_id=1, source_target_pairs={{0,6},{1,7},{2,4},{3,5},{4,2},{5,3},{6,0},{7,1},{8,14},{9,15},{10,... | collective-permute-start | bytes 156680 | tf_op jit(solution)/shard_map/ppermute | solution.py:47
  36.4 28.9 %copy-start.3 = (bf16[4,8192]{1,0:T(4,128)(2,1)S(1)}, bf16[4,8192]{1,0:T(4,128)(2,1)}, u32[]{:S(2)}) copy-start(bf16[4,8192]{1,0:T(4,128)(2,1)} %refs_0_.1) | copy-start | bytes 196612
  36.4 5.8 %collective-permute-start.9 = (f32[24,544]{1,0:T(8,128)S(1)}, f32[24,544]{1,0:T(8,128)S(1)}, u32[]{:S(2)}, u32[]{:S(2)}) collective-permute-start(f32[24,544]{1,0:T(8,128)S(1)} %shard_map.173.refs_0_), channel_id=1, source_target_pairs={{0,8},{1,9},{2,10},{3,11},{4,12},{5,13},{6,14},{7,15},{8,0},{9,1},... | collective-permute-start | bytes 156680 | tf_op jit(solution)/shard_map/ppermute | solution.py:47
  42.3 1.3 %collective-permute-start.10 = (f32[24,544]{1,0:T(8,128)S(1)}, f32[24,544]{1,0:T(8,128)S(1)}, u32[]{:S(2)}, u32[]{:S(2)}) collective-permute-start(f32[24,544]{1,0:T(8,128)S(1)} %shard_map.175.mine_ref), channel_id=1, source_target_pairs={{0,1},{1,0},{2,3},{3,2},{4,5},{5,4},{6,7},{7,6},{8,9},{9,8},{10,11... | collective-permute-start | bytes 156680 | tf_op jit(solution)/shard_map/ppermute | solution.py:47
  47.9 2.3 %collective-permute-start.11 = (f32[24,8192]{1,0:T(8,128)S(1)}, f32[24,8192]{1,0:T(8,128)S(1)}, u32[]{:S(2)}, u32[]{:S(2)}) collective-permute-start(f32[24,8192]{1,0:T(8,128)S(1)} %get-tuple-element.22), channel_id=1, source_target_pairs={{0,1},{1,0},{2,3},{3,2},{4,5},{5,4},{6,7},{7,6},{8,9},{9,8},{10,11... | collective-permute-start | bytes 2359304 | tf_op jit(solution)/shard_map/ppermute | solution.py:47
  50.7 7.0 %collective-permute-start.12 = (bf16[768,128]{1,0:T(8,128)(2,1)S(1)}, bf16[768,128]{1,0:T(8,128)(2,1)S(1)}, u32[]{:S(2)}, u32[]{:S(2)}) collective-permute-start(bf16[768,128]{1,0:T(8,128)(2,1)S(1)} %get-tuple-element.24), channel_id=1, source_target_pairs={{0,2},{1,3},{2,0},{3,1},{4,6},{5,7},{6,4},{7,5},{8,10},{9,11},{10,... | collective-permute-start | bytes 589832 | tf_op jit(solution)/shard_map/ppermute | solution.py:47
  57.7 4.5 %collective-permute-start.13 = (bf16[192,128]{1,0:T(8,128)(2,1)S(1)}, bf16[192,128]{1,0:T(8,128)(2,1)S(1)}, u32[]{:S(2)}, u32[]{:S(2)}) collective-permute-start(bf16[192,128]{1,0:T(8,128)(2,1)S(1)} %get-tuple-element.26), channel_id=1, source_target_pairs={{0,4},{1,5},{2,6},{3,7},{4,0},{5,1},{6,2},{7,3},{8,12},{9,13},{10,... | collective-permute-start | bytes 147464 | tf_op jit(solution)/shard_map/ppermute | solution.py:47
  58.3 5.3 %collective-permute-start.14 = (bf16[192,128]{1,0:T(8,128)(2,1)S(1)}, bf16[192,128]{1,0:T(8,128)(2,1)S(1)}, u32[]{:S(2)}, u32[]{:S(2)}) collective-permute-start(bf16[192,128]{1,0:T(8,128)(2,1)S(1)} %get-tuple-element.27), channel_id=1, source_target_pairs={{0,8},{1,9},{2,10},{3,11},{4,12},{5,13},{6,14},{7,15},{8,0},{9,1},... | collective-permute-start | bytes 147464 | tf_op jit(solution)/shard_map/ppermute | solution.py:47
  59.4 5.9 %collective-permute-start.15 = (bf16[192,128]{1,0:T(8,128)(2,1)S(1)}, bf16[192,128]{1,0:T(8,128)(2,1)S(1)}, u32[]{:S(2)}, u32[]{:S(2)}) collective-permute-start(bf16[192,128]{1,0:T(8,128)(2,1)S(1)} %get-tuple-element.28), channel_id=1, source_target_pairs={{0,12},{1,13},{2,14},{3,15},{4,8},{5,9},{6,10},{7,11},{8,4},{9,5},... | collective-permute-start | bytes 147464 | tf_op jit(solution)/shard_map/ppermute | solution.py:47

commit v3 on v2

--- a/solution.py
+++ b/solution.py
@@ -115,32 +115,44 @@
     )
 
 
-def unfold_kernel(mine_ref, other_ref, out_ref, fold_ref):
-    half = mine_ref.shape[0]
-    fold_ref[:half] = mine_ref[...].astype(F32)
-    fold_ref[half:] = other_ref[...].astype(F32)
+def half_kernel(mine_ref, out_ref, fold_ref):
+    fold_ref[...] = mine_ref[...].astype(F32)
     rows, pieces = out_ref.shape[0], out_ref.shape[1] // LANES
     for c in range(pieces):
-        out_ref[:, c * LANES : (c + 1) * LANES] = fold_ref[
-            pl.ds(c, rows, stride=pieces), :
-        ].astype(BF16)
-
-
-def load_kernel(far_ref, out_ref, sem):
-    copy = pltpu.make_async_copy(far_ref, out_ref, sem)
+        out_ref[:, c * LANES : (c + 1) * LANES] = fold_ref[pl.ds(c, rows, stride=pieces), :]
+
+
+def unfold_kernel(half_ref, other_ref, out_ref, fold_ref):
+    fold_ref[...] = other_ref[...].astype(F32)
+    rows, pieces = half_ref.shape[0], out_ref.shape[1] // LANES
+    for c in range(pieces):
+        span = slice(c * LANES, (c + 1) * LANES)
+        other = fold_ref[pl.ds(c, rows, stride=pieces), :]
+        out_ref[:, span] = jnp.concatenate([half_ref[:, span], other], axis=0).astype(BF16)
+
+
+def load_kernel(start, size, far_ref, *refs):
+    out_ref, sem = refs[-2:]
+    rows = pl.ds(start, size)
+    copy = pltpu.make_async_copy(far_ref.at[rows], out_ref.at[rows], sem)
     copy.start()
     copy.wait()
 
 
-def load(array, limit):
+def load(array, limit, step=0, steps=1, so_far=None):
+    total = array.shape[0]
+    start = total * step // steps
+    size = total * (step + 1) // steps - start
+    operands = (array,) if so_far is None else (array, so_far)
     return pl.pallas_call(
-        load_kernel,
+        functools.partial(load_kernel, start, size),
         out_shape=pltpu.VMEM(array.shape, array.dtype),
-        in_specs=[pl.BlockSpec(memory_space=pl.ANY)],
+        in_specs=[pl.BlockSpec(memory_space=pl.ANY)] * len(operands),
         out_specs=vmem(1)[0],
+        input_output_aliases={} if so_far is None else {1: 0},
         scratch_shapes=[pltpu.SemaphoreType.DMA],
         compiler_params=pltpu.CompilerParams(vmem_limit_bytes=limit * MIB),
-    )(array)
+    )(*operands)
 
 
 def add_kernel(count, *refs):
@@ -150,8 +162,21 @@
     refs[-1][...] = total
 
 
+def places(block, turn, height, span):
+    line = lax.broadcasted_iota(jnp.int32, (height, block.shape[1]), 0)
+    return jnp.where(line == block * span + turn, 1.0, 0.0)
+
+
+def fresh_input(both_ref, block, turn, rows, rows_dev):
+    return jnp.dot(
+        places(block, turn, rows, rows_dev).astype(BF16),
+        both_ref[0].astype(BF16),
+        preferred_element_type=F32,
+    )
+
+
 def conv_kernel(
-    live_ref,
+    rows_dev,
     both_ref,
     spot_ref,
     conv_ref,
@@ -161,34 +186,13 @@
     keep_ref,
     send_ref,
     mixed_ref,
-    gate_ref,
-    new_conv_ref,
     low_ref,
-    alive_ref,
 ):
     index = lax.axis_index("weight")
-    blocks = live_ref.shape[0]
     rows = conv_ref.shape[1]
-    rows_dev = rows // blocks
     kept = mixed_ref.shape[0]
     block = jnp.bitwise_xor(spot_ref[0:1, :], index)
-    turn = spot_ref[1:2, :]
-
-    def places(height, span):
-        line = lax.broadcasted_iota(jnp.int32, (height, kept), 0)
-        return jnp.where(line == block * span + turn, 1.0, 0.0)
-
-    fresh = jnp.dot(
-        places(rows, rows_dev).astype(BF16),
-        both_ref[0].astype(BF16),
-        preferred_element_type=F32,
-    )
-    row_iota = lax.broadcasted_iota(jnp.int32, (rows_dev, 128), 0)
-    for b in range(blocks):
-        alive_ref[b * rows_dev : (b + 1) * rows_dev, :] = jnp.where(
-            row_iota < live_ref[b], 1.0, 0.0
-        )
-    alive = alive_ref[:, 0:1] > 0.0
+    fresh = fresh_input(both_ref, block, spot_ref[1:2, :], rows, rows_dev)
     states = [conv_ref[k].astype(F32) for k in range(TAPS - 1)] + [fresh]
     total = states[0] * taps_ref[0:1, :]
     for k in range(1, TAPS):
@@ -208,17 +212,42 @@
     core = index % 2
     keep_ref[...] = low_ref[pl.ds(pl.multiple_of(core * half, 8), half), :]
     send_ref[...] = low_ref[pl.ds(pl.multiple_of((1 - core) * half, 8), half), :]
+
+
+def gate_kernel(
+    live_ref, both_ref, spot_ref, conv_ref, mixed_ref, gate_ref, new_conv_ref, alive_ref
+):
+    blocks = live_ref.shape[0]
+    rows = conv_ref.shape[1]
+    rows_dev = rows // blocks
+    block = jnp.bitwise_xor(spot_ref[0:1, :], lax.axis_index("weight"))
+    turn = spot_ref[1:2, :]
+    row_iota = lax.broadcasted_iota(jnp.int32, (rows_dev, 128), 0)
+    for b in range(blocks):
+        alive_ref[b * rows_dev : (b + 1) * rows_dev, :] = jnp.where(
+            row_iota < live_ref[b], 1.0, 0.0
+        )
+    alive = alive_ref[:, 0:1] > 0.0
+    fresh = fresh_input(both_ref, block, turn, rows, rows_dev)
+    states = [conv_ref[k].astype(F32) for k in range(TAPS - 1)] + [fresh]
     for k in range(TAPS - 1):
         new_conv_ref[k] = jnp.where(alive, states[k + 1], states[k]).astype(BF16)
     gate_ref[...] = jnp.dot(
-        places(kept, LIVE_MAX),
+        places(block, turn, mixed_ref.shape[0], LIVE_MAX),
         silu(both_ref[1]),
         precision=lax.Precision.HIGHEST,
         preferred_element_type=F32,
     )
 
 
-def state_kernel(
+def join_low(mine_ref, other_ref, low_ref):
+    half = mine_ref.shape[0]
+    core = lax.axis_index("weight") % 2
+    low_ref[pl.ds(pl.multiple_of(core * half, 8), half), :] = mine_ref[...]
+    low_ref[pl.ds(pl.multiple_of((1 - core) * half, 8), half), :] = other_ref[...]
+
+
+def readout_kernel(
     live_ref,
     mine_ref,
     other_ref,
@@ -231,30 +260,80 @@
     skip_ref,
     state_ref,
     out_weight_ref,
-    new_state_ref,
     keep_ref,
     send_ref,
+    step_ref,
     low_ref,
     read_ref,
     alive_ref,
+    fold_ref,
 ):
-    index = lax.axis_index("weight")
     blocks = live_ref.shape[0]
     rows_dev = state_ref.shape[0] // blocks
     kept = mixed_ref.shape[0]
-    half = mine_ref.shape[0]
-    core = index % 2
-    low_ref[pl.ds(pl.multiple_of(core * half, 8), half), :] = mine_ref[...]
-    low_ref[pl.ds(pl.multiple_of((1 - core) * half, 8), half), :] = other_ref[...]
+    join_low(mine_ref, other_ref, low_ref)
     step_size = softplus(
         jnp.dot(
             low_ref[:, :DTR].astype(BF16), step_weight_ref[...], preferred_element_type=F32
         )
         + bias_ref[...]
     )
-    coefs = low_ref[:, DTR:].T
+    step_ref[...] = step_size
+    coefs = low_ref[:, DTR:]
+    both_coefs = jnp.sum(coefs[:, :NSTATE] * coefs[:, NSTATE:], axis=1, keepdims=True)
+    out_coefs = coefs[:, NSTATE:].T
     x_wide = mixed_ref[...].astype(F32)
-    driven = step_size * x_wide
+    rates = -jnp.exp(rates_ref[...])
+    for b in range(blocks):
+        for t in range(LIVE_MAX):
+            r = b * LIVE_MAX + t
+            wide = state_ref[b * rows_dev + t].astype(F32)
+            decayed = jnp.exp(step_size[r : r + 1, :] * rates) * wide
+            read_ref[r : r + 1, :] = jnp.sum(
+                out_coefs[:, r : r + 1] * decayed, axis=0, keepdims=True
+            )
+            alive_ref[r : r + 1, :] = jnp.full(
+                (1, 128), jnp.where(t < live_ref[b], 1.0, 0.0)
+            )
+    readout = read_ref[...] + (both_coefs * step_size + skip_ref[...]) * x_wide
+    gated = jnp.where(alive_ref[:, 0:1] > 0.0, readout * gate_ref[...], 0.0).astype(BF16)
+    block = jnp.bitwise_xor(spot_ref[:, 0:1], lax.axis_index("weight"))
+    column = lax.broadcasted_iota(jnp.int32, (kept, kept), 1)
+    pick = jnp.where(column == block * LIVE_MAX + spot_ref[:, 1:2], 1.0, 0.0).astype(BF16)
+    picked = jnp.dot(pick, gated, preferred_element_type=F32).astype(BF16)
+    width = out_weight_ref.shape[1]
+    pieces = width // LANES
+    group = 4
+    for c in range(0, pieces, group):
+        part = jnp.dot(
+            picked,
+            out_weight_ref[:, c * LANES : (c + group) * LANES],
+            preferred_element_type=F32,
+        )
+        for g in range(group):
+            piece = part[:, g * LANES : (g + 1) * LANES]
+            keep_ref[pl.ds(c + g, kept // 2, stride=pieces), :] = piece[: kept // 2]
+            fold_ref[pl.ds(c + g, kept // 2, stride=pieces), :] = piece[kept // 2 :]
+    send_ref[...] = fold_ref[...].astype(BF16)
+
+
+def state_kernel(
+    live_ref,
+    mine_ref,
+    other_ref,
+    mixed_ref,
+    step_ref,
+    rates_ref,
+    state_ref,
+    new_state_ref,
+    low_ref,
+):
+    blocks = live_ref.shape[0]
+    rows_dev = state_ref.shape[0] // blocks
+    join_low(mine_ref, other_ref, low_ref)
+    in_coefs = low_ref[:, DTR : DTR + NSTATE].T
+    step_size = step_ref[...]
+    driven = step_size * mixed_ref[...].astype(F32)
     rates = -jnp.exp(rates_ref[...])
     for b in range(blocks):
         for t in range(LIVE_MAX):
@@ -262,39 +341,16 @@
             wide = state_ref[b * rows_dev + t].astype(F32)
             updated = (
                 jnp.exp(step_size[r : r + 1, :] * rates) * wide
-                + coefs[:NSTATE, r : r + 1] * driven[r : r + 1, :]
+                + in_coefs[:, r : r + 1] * driven[r : r + 1, :]
             )
-            read_ref[r : r + 1, :] = jnp.sum(
-                coefs[NSTATE:, r : r + 1] * updated, axis=0, keepdims=True
-            )
-            live = t < live_ref[b]
-            alive_ref[r : r + 1, :] = jnp.full((1, 128), jnp.where(live, 1.0, 0.0))
-            new_state_ref[b * rows_dev + t] = jnp.where(live, updated, wide).astype(BF16)
+            new_state_ref[b * rows_dev + t] = jnp.where(
+                t < live_ref[b], updated, wide
+            ).astype(BF16)
         for t in range(LIVE_MAX, rows_dev):
             new_state_ref[b * rows_dev + t] = state_ref[b * rows_dev + t]
-    readout = read_ref[...] + skip_ref[...] * x_wide
-    gated = jnp.where(alive_ref[:, 0:1] > 0.0, readout * gate_ref[...], 0.0).astype(BF16)
-    block = jnp.bitwise_xor(spot_ref[:, 0:1], index)
-    column = lax.broadcasted_iota(jnp.int32, (kept, kept), 1)
-    pick = jnp.where(column == block * LIVE_MAX + spot_ref[:, 1:2], 1.0, 0.0).astype(BF16)
-    picked = jnp.dot(pick, gated, preferred_element_type=F32).astype(BF16)
-    width = out_weight_ref.shape[1] // 4
-    for c in range(4):
-        cols = slice(c * width, (c + 1) * width)
-        part = jnp.dot(picked, out_weight_ref[:, cols], preferred_element_type=F32)
-        keep_ref[:, cols] = part[: kept // 2]
-        send_ref[:, cols] = part[kept // 2 :].astype(send_ref.dtype)
-
-
-def first_sum_kernel(keep_ref, got_ref, *refs):
-    outs, fold_ref = refs[:-1], refs[-1]
-    fold(keep_ref[...] + got_ref[...].astype(F32), fold_ref)
-    size = outs[0].shape[0]
-    for k, out in enumerate(outs):
-        out[...] = fold_ref[k * size : (k + 1) * size].astype(out.dtype)
-
-
-def next_sum_kernel(count, *refs):
+
+
+def sum_kernel(count, *refs):
     parts, outs = refs[:count], refs[count:]
     size = outs[0].shape[0]
     for k, out in enumerate(outs):
@@ -365,41 +421,48 @@
         ],
         limit=60,
     )
+    near_weight = None
     for k, phase in enumerate(phases[:-1]):
-        after = ()
-        if k == len(phases) - 2:
-            near_weight = load(in_weight, 34)
-            after = (near_weight,)
-        gathered = join([gathered] + [swap(gathered, s, devices) for s in phase], after)
+        near_weight = load(in_weight, 43, k, len(phases) - 1, near_weight)
+        gathered = join(
+            [gathered] + [swap(gathered, s, devices) for s in phase], (near_weight,)
+        )
+    folded = [pltpu.VMEM((kept // 2 * pieces, LANES), F32)]
+    half = call(half_kernel, shape((kept // 2, width)), (gathered,), scratch=folded, limit=12)
     normed = call(
         unfold_kernel,
         shape((kept, width), BF16),
-        (gathered, swap(gathered, 1, devices)),
-        scratch=[pltpu.VMEM((kept * pieces, LANES), F32)],
+        (half, swap(gathered, 1, devices)),
+        scratch=folded,
         limit=12,
     )
     both = jnp.einsum("rd,dbc->brc", normed, near_weight, preferred_element_type=F32)
 
-    keep, send, mixed_x, gate, new_conv = call(
-        conv_kernel,
+    conv_turned = conv_state.transpose(1, 0, 2)
+    keep, send, mixed_x = call(
+        functools.partial(conv_kernel, rows_dev),
         (
             shape((kept // 2, low_width)),
             shape((kept // 2, low_width)),
             shape((kept, channels), BF16),
-            shape((kept, channels)),
-            shape((TAPS - 1, rows, channels), BF16),
         ),
         (
-            live_counts,
             both,
             spots,
-            conv_state.transpose(1, 0, 2),
+            conv_turned,
             conv_weight,
             conv_offset.reshape(1, channels),
             coef_weight.T,
         ),
+        scratch=[pltpu.VMEM((kept, low_width), F32)],
+        limit=16,
+    )
+    gate, new_conv = call(
+        gate_kernel,
+        (shape((kept, channels)), shape((TAPS - 1, rows, channels), BF16)),
+        (live_counts, both, spots, conv_turned, mixed_x),
         scalars=1,
-        scratch=[pltpu.VMEM((kept, low_width), F32), pltpu.VMEM((rows, 128), F32)],
+        scratch=[pltpu.VMEM((rows, 128), F32)],
         limit=16,
     )
 
@@ -414,20 +477,17 @@
     low = add(keep, swap(send, 1, devices))
     exchanges = sum_phases(devices)
     for k, phase in enumerate(exchanges):
-        after = ()
+        after = (gate,)
         if k == len(exchanges) - 1:
             near_out = load(out_weight, 50)
             after = (near_out,)
         low = add(low, *[swap(low, s, devices) for s in phase], after=after)
     other = swap(low, 1, devices)
 
-    new_state, keep, send = call(
-        state_kernel,
-        (
-            shape(ssm_state.shape, BF16),
-            shape((kept // 2, width)),
-            shape((kept // 2, width)),
-        ),
+    size = kept // 2 * pieces
+    keep, send, step_size = call(
+        readout_kernel,
+        (shape((size, LANES)), shape((size, LANES), BF16), shape((kept, channels))),
         (
             live_counts,
             low,
@@ -447,24 +507,28 @@
             pltpu.VMEM((kept, low_width), F32),
             pltpu.VMEM((kept, channels), F32),
             pltpu.VMEM((kept, 128), F32),
+            pltpu.VMEM((size, LANES), F32),
         ],
         limit=32,
     )
-
-    scatter = list(reversed(phases[:-1]))
-    total, kernel = (keep, swap(send, 1, devices)), first_sum_kernel
-    size = kept // 2 * pieces
-    scratch = [pltpu.VMEM((size, LANES), F32)]
-    for phase in scatter:
+    new_state = call(
+        state_kernel,
+        shape(ssm_state.shape, BF16),
+        (live_counts, low, other, mixed_x, step_size, log_rates, ssm_state),
+        scalars=1,
+        scratch=[pltpu.VMEM((kept, low_width), F32)],
+        limit=16,
+    )
+
+    total = (keep, swap(send, 1, devices))
+    for phase in reversed(phases[:-1]):
         size //= len(phase) + 1
         parts = call(
-            kernel,
+            functools.partial(sum_kernel, len(total)),
             (shape((size, LANES)),) + (shape((size, LANES), BF16),) * len(phase),
             total,
-            scratch=scratch,
         )
         total = (parts[0],) + tuple(swap(p, s, devices) for p, s in zip(parts[1:], phase))
-        kernel, scratch = functools.partial(next_sum_kernel, len(total)), ()
     mixed = call(
         last_sum_kernel,
         shape(hidden.shape, BF16),

time: 66.3 us -> 62.6 us (0.944)
  waiting for transfers between devices: 27.1 us -> 17.7 us
  starting transfers between devices: 16.3 us -> 19.6 us
  Pallas kernels: 18.5 us -> 20.9 us
    ppermute x16, waiting for transfers between devices: 27.1 us -> 17.7 us  [swap(): lax.ppermute(value, 'weight', [(i, i ^ shift) for i in range(devices)])]
    ppermute x16, starting transfers between devices: 16.3 us -> 19.6 us  [swap(): lax.ppermute(value, 'weight', [(i, i ^ shift) for i in range(devices)])]
    pallas_call x12 -> x15, Pallas kernels: 9.3 us -> 10.7 us  [call(): pl.pallas_call(kernel, out_shape=outs, in_specs=[pl.BlockSpec(memory_spac...]
    pallas_call x2 -> x3, Pallas kernels: 9.17 us -> 10.2 us  [load(): pl.pallas_call(functools.partial(load_kernel, start, size), out_shape=plt...]
  transfers between devices with their start and end apart: 16 -> 16, of which waited for: 13 -> 11; matrix products, arithmetic and copies ran while one was open for 0% -> 0% of each run, Pallas kernels for 14% -> 23%
where the time goes in v3:
time: 62.6 us; the launch traced here: 62.4 us
  Pallas kernels  20.9 us (33%)
  starting transfers between devices  19.6 us (31%)
  waiting for transfers between devices  17.7 us (28%)
  matrix products  3.15 us (5%)
  between operations  0.93 us (1%)
    ppermute x16, starting transfers between devices, swap(): lax.ppermute(value, 'weight', [(i, i ^ shift) for i in range(devices)])  19.6 us
    ppermute x16, waiting for transfers between devices, swap(): lax.ppermute(value, 'weight', [(i, i ^ shift) for i in range(devices)])  17.7 us
    pallas_call x15, Pallas kernels, call(): pl.pallas_call(kernel, out_shape=outs, in_specs=[pl.BlockSpec(memory_spac...  10.7 us
    pallas_call x3, Pallas kernels, load(): pl.pallas_call(functools.partial(load_kernel, start, size), out_shape=plt...  10.2 us
    dot_general x1, matrix products, body(): jnp.einsum('rd,dbc->brc', normed, near_weight, preferred_element_type=F32)  3.15 us
  transfers between devices with their start and end apart: 16, of which 11 were waited for; matrix products, arithmetic and copies ran while one was open for 0% of the time, Pallas kernels for 23%

profile of v3, /device:TPU:0, one launch (start us, length us, event | category | flops | bytes accessed | tf_op | source)
XLA Modules:
  0.0 62.4 jit_solution(11635918754354029111)
XLA Ops:
  0.6 1.1 %shard_map.168.refs_0_ = bf16[192,128]{1,0:T(8,128)(2,1)S(1)} custom-call(bf16[4,8192]{1,0:T(4,128)(2,1)} %refs_0_.1, f32[1,8192]{1,0:T(1,128)} %bitcast.18), custom_call_target="tpu_custom_call" | custom-call | tf_op jit(solution)/shard_map/pallas_call | solution.py:68
  1.7 3.1 %collective-permute-start = (bf16[192,128]{1,0:T(8,128)(2,1)S(1)}, bf16[192,128]{1,0:T(8,128)(2,1)S(1)}, u32[]{:S(2)}, u32[]{:S(2)}) collective-permute-start(bf16[192,128]{1,0:T(8,128)(2,1)S(1)} %shard_map.168.refs_0_), channel_id=1, source_target_pairs={{0,4},{1,5},{2,6},{3,7},{4,0},{5,1},{6,2},{7,3},{8,12},{9,13},{10,... | collective-permute-start | bytes 147464 | tf_op jit(solution)/shard_map/ppermute | solution.py:47
  4.8 2.6 %collective-permute-start.1 = (bf16[192,128]{1,0:T(8,128)(2,1)S(1)}, bf16[192,128]{1,0:T(8,128)(2,1)S(1)}, u32[]{:S(2)}, u32[]{:S(2)}) collective-permute-start(bf16[192,128]{1,0:T(8,128)(2,1)S(1)} %shard_map.168.refs_0_), channel_id=1, source_target_pairs={{0,8},{1,9},{2,10},{3,11},{4,12},{5,13},{6,14},{7,15},{8,0},{9,1},... | collective-permute-start | bytes 147464 | tf_op jit(solution)/shard_map/ppermute | solution.py:47
  7.4 3.4 %shard_map.166.refs_0_.refs_4_ = bf16[8192,2,512]{2,1,0:T(2,128)(2,1)S(1)} custom-call(bf16[8192,2,512]{2,1,0:T(2,128)(2,1)} %far_ref.4), custom_call_target="tpu_custom_call" | custom-call | tf_op jit(solution)/shard_map/pallas_call | solution.py:147
  10.8 2.5 %collective-permute-done.2.refs_3_ = bf16[192,128]{1,0:T(8,128)(2,1)S(1)} collective-permute-done((bf16[192,128]{1,0:T(8,128)(2,1)S(1)}, bf16[192,128]{1,0:T(8,128)(2,1)S(1)}, u32[]{:S(2)}, u32[]{:S(2)}) %collective-permute-start.2) | collective-permute-done | bytes 49184 | tf_op jit(solution)/shard_map/ppermute | solution.py:47
  13.3 1.6 %collective-permute-start.3 = (bf16[768,128]{1,0:T(8,128)(2,1)S(1)}, bf16[768,128]{1,0:T(8,128)(2,1)S(1)}, u32[]{:S(2)}, u32[]{:S(2)}) collective-permute-start(bf16[768,128]{1,0:T(8,128)(2,1)S(1)} %shard_map.169.refs_0_), channel_id=1, source_target_pairs={{0,2},{1,3},{2,0},{3,1},{4,6},{5,7},{6,4},{7,5},{8,10},{9,11},{10,... | collective-permute-start | bytes 589832 | tf_op jit(solution)/shard_map/ppermute | solution.py:47
  14.9 3.4 %shard_map.167.refs_2_ = bf16[8192,2,512]{2,1,0:T(2,128)(2,1)S(1)} custom-call(bf16[8192,2,512]{2,1,0:T(2,128)(2,1)} %far_ref.4, bf16[8192,2,512]{2,1,0:T(2,128)(2,1)S(1)} %shard_map.166.refs_0_.refs_4_), custom_call_target="tpu_custom_call", output_to_operand_aliasing={{}: (1, {})} | custom-call | tf_op jit(solution)/shard_map/pallas_call | solution.py:147
  18.3 0.8 %collective-permute-done.3.refs_1_ = bf16[768,128]{1,0:T(8,128)(2,1)S(1)} collective-permute-done((bf16[768,128]{1,0:T(8,128)(2,1)S(1)}, bf16[768,128]{1,0:T(8,128)(2,1)S(1)}, u32[]{:S(2)}, u32[]{:S(2)}) %collective-permute-start.3) | collective-permute-done | bytes 196640 | tf_op jit(solution)/shard_map/ppermute | solution.py:47
  19.1 0.1 collective-permute-start.4
  19.1 0.5 shard_map.171.half_ref
  19.7 1.2 %collective-permute-done.4.other_ref = bf16[1536,128]{1,0:T(8,128)(2,1)S(1)} collective-permute-done((bf16[1536,128]{1,0:T(8,128)(2,1)S(1)}, bf16[1536,128]{1,0:T(8,128)(2,1)S(1)}, u32[]{:S(2)}, u32[]{:S(2)}) %collective-permute-start.4) | collective-permute-done | bytes 393248 | tf_op jit(solution)/shard_map/ppermute | solution.py:47
  20.9 0.6 shard_map.172
  21.4 0.0 copy-start.1
  21.4 0.0 copy-start.2
  21.5 0.0 copy-start.7
  21.5 0.0 copy-start.9
  21.5 0.0 copy-start.10
  21.5 0.0 copy-start.8
  21.5 3.1 %fusion.2.both_ref = f32[2,48,512]{2,1,0:T(8,128)S(1)} fusion(bf16[8192,2,512]{2,1,0:T(2,128)(2,1)S(1)} %shard_map.167.refs_2_, bf16[48,8192]{1,0:T(8,128)(2,1)S(1)} %shard_map.172), kind=kOutput, calls=%fused_computation.2 | convolution fusion | flops 805306368 | bytes 17760256 | tf_op jit(solution)/shard_map/rd,dbc->brc/dot_general | solution.py:439
  24.7 0.0 copy-start
  24.7 0.0 copy-start.3
  24.7 0.0 copy-start.6
  24.7 0.0 copy-start.11
  24.8 0.5 shard_map.173
  25.3 0.2 collective-permute-start.5
  25.5 1.1 %collective-permute-done.5.refs_1_ = f32[24,544]{1,0:T(8,128)S(1)} collective-permute-done((f32[24,544]{1,0:T(8,128)S(1)}, f32[24,544]{1,0:T(8,128)S(1)}, u32[]{:S(2)}, u32[]{:S(2)}) %collective-permute-start.5) | collective-permute-done | bytes 52256 | tf_op jit(solution)/shard_map/ppermute | solution.py:47
  26.6 1.6 %collective-permute-start.6 = (f32[24,544]{1,0:T(8,128)S(1)}, f32[24,544]{1,0:T(8,128)S(1)}, u32[]{:S(2)}, u32[]{:S(2)}) collective-permute-start(f32[24,544]{1,0:T(8,128)S(1)} %shard_map.174.refs_0_), channel_id=1, source_target_pairs={{0,2},{1,3},{2,0},{3,1},{4,6},{5,7},{6,4},{7,5},{8,10},{9,11},{10,... | collective-permute-start | bytes 156680 | tf_op jit(solution)/shard_map/ppermute | solution.py:47
  28.2 2.0 %collective-permute-start.8 = (f32[24,544]{1,0:T(8,128)S(1)}, f32[24,544]{1,0:T(8,128)S(1)}, u32[]{:S(2)}, u32[]{:S(2)}) collective-permute-start(f32[24,544]{1,0:T(8,128)S(1)} %shard_map.174.refs_0_), channel_id=1, source_target_pairs={{0,6},{1,7},{2,4},{3,5},{4,2},{5,3},{6,0},{7,1},{8,14},{9,15},{10,... | collective-permute-start | bytes 156680 | tf_op jit(solution)/shard_map/ppermute | solution.py:47
  30.2 1.4 %shard_map.175 = (f32[48,512]{1,0:T(8,128)S(1)}, bf16[3,64,512]{2,1,0:T(8,128)(2,1)}) custom-call(s32[16]{0:T(128)S(1)} %copy-done.8, f32[2,48,512]{2,1,0:T(8,128)S(1)} %fusion.2.both_ref, s32[2,48]{1,0:T(2,128)S(1)} %copy-done.9, bf16[3,64,512]{2,1,0:T(8,128)(2,1)S(1)} %bitcast.13, bf16[48,512]{1,0:T(8,128)(2,1)S(1)} %get-tuple-element.19.mixed_ref), custom_call_target="tpu_custom_call" | custom-call | tf_op jit(solution)/shard_map/pallas_call | solution.py:68
  31.6 1.0 %collective-permute-done.7.refs_2_ = f32[24,544]{1,0:T(8,128)S(1)} collective-permute-done((f32[24,544]{1,0:T(8,128)S(1)}, f32[24,544]{1,0:T(8,128)S(1)}, u32[]{:S(2)}, u32[]{:S(2)}) %collective-permute-start.7) | collective-permute-done | bytes 52256 | tf_op jit(solution)/shard_map/ppermute | solution.py:47
  32.7 0.9 %collective-permute-done.8.refs_3_ = f32[24,544]{1,0:T(8,128)S(1)} collective-permute-done((f32[24,544]{1,0:T(8,128)S(1)}, f32[24,544]{1,0:T(8,128)S(1)}, u32[]{:S(2)}, u32[]{:S(2)}) %collective-permute-start.8) | collective-permute-done | bytes 52256 | tf_op jit(solution)/shard_map/ppermute | solution.py:47
  33.6 1.9 %collective-permute-start.9 = (f32[24,544]{1,0:T(8,128)S(1)}, f32[24,544]{1,0:T(8,128)S(1)}, u32[]{:S(2)}, u32[]{:S(2)}) collective-permute-start(f32[24,544]{1,0:T(8,128)S(1)} %shard_map.176.refs_0_), channel_id=1, source_target_pairs={{0,8},{1,9},{2,10},{3,11},{4,12},{5,13},{6,14},{7,15},{8,0},{9,1},... | collective-permute-start | bytes 156680 | tf_op jit(solution)/shard_map/ppermute | solution.py:47
  35.5 3.4 %shard_map.177.refs_2_.out_weight_ref = bf16[512,8192]{1,0:T(8,128)(2,1)S(1)} custom-call(bf16[512,8192]{1,0:T(8,128)(2,1)} %far_ref.5), custom_call_target="tpu_custom_call" | custom-call | tf_op jit(solution)/shard_map/pallas_call | solution.py:147
  38.9 0.1 collective-permute-start.10
  39.0 1.2 %collective-permute-done.10.other_ref = f32[24,544]{1,0:T(8,128)S(1)} collective-permute-done((f32[24,544]{1,0:T(8,128)S(1)}, f32[24,544]{1,0:T(8,128)S(1)}, u32[]{:S(2)}, u32[]{:S(2)}) %collective-permute-start.10) | collective-permute-done | bytes 52256 | tf_op jit(solution)/shard_map/ppermute | solution.py:47
  40.3 3.5 %shard_map.179 = (f32[1536,128]{1,0:T(8,128)S(1)}, bf16[1536,128]{1,0:T(8,128)(2,1)S(1)}, f32[48,512]{1,0:T(8,128)S(1)}) custom-call(s32[16]{0:T(128)S(1)} %copy-done.8, f32[24,544]{1,0:T(8,128)S(1)} %shard_map.178.mine_ref, f32[24,544]{1,0:T(8,128)S(1)} %collective-permute-done.10.other_ref, s32[48,2]{1,0:T(8,128)S(1)} %copy-done.6, ...), custom_call_target="tpu_custom_call" | custom-call | tf_op jit(solution)/shard_map/pallas_call | solution.py:68
  43.8 0.2 collective-permute-start.11
  44.1 1.6 %collective-permute-done.11.refs_1_ = bf16[1536,128]{1,0:T(8,128)(2,1)S(1)} collective-permute-done((bf16[1536,128]{1,0:T(8,128)(2,1)S(1)}, bf16[1536,128]{1,0:T(8,128)(2,1)S(1)}, u32[]{:S(2)}, u32[]{:S(2)}) %collective-permute-start.11) | collective-permute-done | bytes 393248 | tf_op jit(solution)/shard_map/ppermute | solution.py:47
  45.6 0.1 shard_map.180
  45.7 1.8 %collective-permute-start.12 = (bf16[768,128]{1,0:T(8,128)(2,1)S(1)}, bf16[768,128]{1,0:T(8,128)(2,1)S(1)}, u32[]{:S(2)}, u32[]{:S(2)}) collective-permute-start(bf16[768,128]{1,0:T(8,128)(2,1)S(1)} %get-tuple-element.24), channel_id=1, source_target_pairs={{0,2},{1,3},{2,0},{3,1},{4,6},{5,7},{6,4},{7,5},{8,10},{9,11},{10,... | collective-permute-start | bytes 589832 | tf_op jit(solution)/shard_map/ppermute | solution.py:47
  47.5 5.2 %collective-permute-done.12.refs_1_ = bf16[768,128]{1,0:T(8,128)(2,1)S(1)} collective-permute-done((bf16[768,128]{1,0:T(8,128)(2,1)S(1)}, bf16[768,128]{1,0:T(8,128)(2,1)S(1)}, u32[]{:S(2)}, u32[]{:S(2)}) %collective-permute-start.12) | collective-permute-done | bytes 196640 | tf_op jit(solution)/shard_map/ppermute | solution.py:47
  52.8 1.7 %collective-permute-start.13 = (bf16[192,128]{1,0:T(8,128)(2,1)S(1)}, bf16[192,128]{1,0:T(8,128)(2,1)S(1)}, u32[]{:S(2)}, u32[]{:S(2)}) collective-permute-start(bf16[192,128]{1,0:T(8,128)(2,1)S(1)} %get-tuple-element.26), channel_id=1, source_target_pairs={{0,4},{1,5},{2,6},{3,7},{4,0},{5,1},{6,2},{7,3},{8,12},{9,13},{10,... | collective-permute-start | bytes 147464 | tf_op jit(solution)/shard_map/ppermute | solution.py:47
  54.5 1.2 %collective-permute-start.14 = (bf16[192,128]{1,0:T(8,128)(2,1)S(1)}, bf16[192,128]{1,0:T(8,128)(2,1)S(1)}, u32[]{:S(2)}, u32[]{:S(2)}) collective-permute-start(bf16[192,128]{1,0:T(8,128)(2,1)S(1)} %get-tuple-element.27), channel_id=1, source_target_pairs={{0,8},{1,9},{2,10},{3,11},{4,12},{5,13},{6,14},{7,15},{8,0},{9,1},... | collective-permute-start | bytes 147464 | tf_op jit(solution)/shard_map/ppermute | solution.py:47
  55.7 1.5 %collective-permute-start.15 = (bf16[192,128]{1,0:T(8,128)(2,1)S(1)}, bf16[192,128]{1,0:T(8,128)(2,1)S(1)}, u32[]{:S(2)}, u32[]{:S(2)}) collective-permute-start(bf16[192,128]{1,0:T(8,128)(2,1)S(1)} %get-tuple-element.28), channel_id=1, source_target_pairs={{0,12},{1,13},{2,14},{3,15},{4,8},{5,9},{6,10},{7,11},{8,4},{9,5},... | collective-permute-start | bytes 147464 | tf_op jit(solution)/shard_map/ppermute | solution.py:47
  57.2 2.1 %shard_map.183 = bf16[64,16,512]{2,1,0:T(8,128)(2,1)} custom-call(s32[16]{0:T(128)S(1)} %copy-done.8, f32[24,544]{1,0:T(8,128)S(1)} %shard_map.178.mine_ref, f32[24,544]{1,0:T(8,128)S(1)} %collective-permute-done.10.other_ref, bf16[48,512]{1,0:T(8,128)(2,1)S(1)} %get-tuple-element.19.mixed_ref, f32[48,512]{1,0:T(8,128)S(1)} %get-tuple-element.29.step_ref, ...), custom_call_target="tpu_custom_call" | custom-call | tf_op jit(solution)/shard_map/pallas_call | solution.py:68
  59.4 1.0 %collective-permute-done.14.refs_3_ = bf16[192,128]{1,0:T(8,128)(2,1)S(1)} collective-permute-done((bf16[192,128]{1,0:T(8,128)(2,1)S(1)}, bf16[192,128]{1,0:T(8,128)(2,1)S(1)}, u32[]{:S(2)}, u32[]{:S(2)}) %collective-permute-start.14) | collective-permute-done | bytes 49184 | tf_op jit(solution)/shard_map/ppermute | solution.py:47
  60.4 1.3 %collective-permute-done.15.refs_4_ = bf16[192,128]{1,0:T(8,128)(2,1)S(1)} collective-permute-done((bf16[192,128]{1,0:T(8,128)(2,1)S(1)}, bf16[192,128]{1,0:T(8,128)(2,1)S(1)}, u32[]{:S(2)}, u32[]{:S(2)}) %collective-permute-start.15) | collective-permute-done | bytes 49184 | tf_op jit(solution)/shard_map/ppermute | solution.py:47
  61.6 0.7 %shard_map.182 = bf16[4,8192]{1,0:T(4,128)(2,1)} custom-call(bf16[4,8192]{1,0:T(4,128)(2,1)S(1)} %copy-done.4, f32[192,128]{1,0:T(8,128)S(1)} %get-tuple-element.25.refs_1_, bf16[192,128]{1,0:T(8,128)(2,1)S(1)} %collective-permute-done.13.refs_2_, bf16[192,128]{1,0:T(8,128)(2,1)S(1)} %collective-permute-done.14.refs_3_, ...), custom_call_target="tpu_custom_call" | custom-call | tf_op jit(solution)/shard_map/pallas_call | solution.py:68
  (29 shorter events, 0.2 us)
Async XLA Ops:
  1.7 9.1 %collective-permute-start = (bf16[192,128]{1,0:T(8,128)(2,1)S(1)}, bf16[192,128]{1,0:T(8,128)(2,1)S(1)}, u32[]{:S(2)}, u32[]{:S(2)}) collective-permute-start(bf16[192,128]{1,0:T(8,128)(2,1)S(1)} %shard_map.168.refs_0_), channel_id=1, source_target_pairs={{0,4},{1,5},{2,6},{3,7},{4,0},{5,1},{6,2},{7,3},{8,12},{9,13},{10,... | collective-permute-start | bytes 147464 | tf_op jit(solution)/shard_map/ppermute | solution.py:47
  4.8 6.0 %collective-permute-start.1 = (bf16[192,128]{1,0:T(8,128)(2,1)S(1)}, bf16[192,128]{1,0:T(8,128)(2,1)S(1)}, u32[]{:S(2)}, u32[]{:S(2)}) collective-permute-start(bf16[192,128]{1,0:T(8,128)(2,1)S(1)} %shard_map.168.refs_0_), channel_id=1, source_target_pairs={{0,8},{1,9},{2,10},{3,11},{4,12},{5,13},{6,14},{7,15},{8,0},{9,1},... | collective-permute-start | bytes 147464 | tf_op jit(solution)/shard_map/ppermute | solution.py:47
  7.4 5.9 %collective-permute-start.2 = (bf16[192,128]{1,0:T(8,128)(2,1)S(1)}, bf16[192,128]{1,0:T(8,128)(2,1)S(1)}, u32[]{:S(2)}, u32[]{:S(2)}) collective-permute-start(bf16[192,128]{1,0:T(8,128)(2,1)S(1)} %shard_map.168.refs_0_), channel_id=1, source_target_pairs={{0,12},{1,13},{2,14},{3,15},{4,8},{5,9},{6,10},{7,11},{8,4},{9,5},... | collective-permute-start | bytes 147464 | tf_op jit(solution)/shard_map/ppermute | solution.py:47
  13.3 5.7 %collective-permute-start.3 = (bf16[768,128]{1,0:T(8,128)(2,1)S(1)}, bf16[768,128]{1,0:T(8,128)(2,1)S(1)}, u32[]{:S(2)}, u32[]{:S(2)}) collective-permute-start(bf16[768,128]{1,0:T(8,128)(2,1)S(1)} %shard_map.169.refs_0_), channel_id=1, source_target_pairs={{0,2},{1,3},{2,0},{3,1},{4,6},{5,7},{6,4},{7,5},{8,10},{9,11},{10,... | collective-permute-start | bytes 589832 | tf_op jit(solution)/shard_map/ppermute | solution.py:47
  19.1 1.8 %collective-permute-start.4 = (bf16[1536,128]{1,0:T(8,128)(2,1)S(1)}, bf16[1536,128]{1,0:T(8,128)(2,1)S(1)}, u32[]{:S(2)}, u32[]{:S(2)}) collective-permute-start(bf16[1536,128]{1,0:T(8,128)(2,1)S(1)} %shard_map.170.mine_ref), channel_id=1, source_target_pairs={{0,1},{1,0},{2,3},{3,2},{4,5},{5,4},{6,7},{7,6},{8,9},{9,8},{10,11... | collective-permute-start | bytes 1179656 | tf_op jit(solution)/shard_map/ppermute | solution.py:47
  21.4 3.3 %copy-start.1 = (bf16[64,3,512]{2,0,1:T(8,128)(2,1)S(1)}, bf16[64,3,512]{2,0,1:T(8,128)(2,1)}, u32[]{:S(2)}) copy-start(bf16[64,3,512]{2,0,1:T(8,128)(2,1)} %param.27) | copy-start | bytes 589828
  21.4 3.3 %copy-start.2 = (bf16[512,544]{0,1:T(8,128)(2,1)S(1)}, bf16[512,544]{0,1:T(8,128)(2,1)}, u32[]{:S(2)}) copy-start(bf16[512,544]{0,1:T(8,128)(2,1)} %param.20) | copy-start | bytes 1671172
  21.5 3.3 %copy-start.7 = (f32[4,512]{1,0:T(4,128)S(1)}, f32[4,512]{1,0:T(4,128)}, u32[]{:S(2)}) copy-start(f32[4,512]{1,0:T(4,128)} %taps_ref.1) | copy-start | bytes 24580
  21.5 3.3 %copy-start.9 = (s32[2,48]{1,0:T(2,128)S(1)}, s32[2,48]{1,0:T(2,128)}, u32[]{:S(2)}) copy-start(s32[2,48]{1,0:T(2,128)} %constant.2.clone.spot_ref) | copy-start | bytes 1156
  21.5 3.3 %copy-start.10 = (f32[512]{0:T(512)S(1)}, f32[512]{0:T(512)}, u32[]{:S(2)}) copy-start(f32[512]{0:T(512)} %param.19) | copy-start | bytes 6148
  21.5 8.7 %copy-start.8 = (s32[16]{0:T(128)S(1)}, s32[16]{0:T(128)}, u32[]{:S(2)}) copy-start(s32[16]{0:T(128)} %live_ref.5) | copy-start | bytes 196
  24.7 15.6 %copy-start = (bf16[64,16,512]{2,1,0:T(8,128)(2,1)S(1)}, bf16[64,16,512]{2,1,0:T(8,128)(2,1)}, u32[]{:S(2)}) copy-start(bf16[64,16,512]{2,1,0:T(8,128)(2,1)} %state_ref.3) | copy-start | bytes 3145732
  24.7 15.6 %copy-start.3 = (bf16[512,512]{1,0:T(8,128)(2,1)S(1)}, bf16[512,512]{1,0:T(8,128)(2,1)}, u32[]{:S(2)}) copy-start(bf16[512,512]{1,0:T(8,128)(2,1)} %step_weight_ref.1) | copy-start | bytes 1572868
  24.7 15.6 %copy-start.5 = (f32[16,512]{1,0:T(8,128)S(1)}, f32[16,512]{1,0:T(8,128)}, u32[]{:S(2)}) copy-start(f32[16,512]{1,0:T(8,128)} %rates_ref.3) | copy-start | bytes 98308
  24.7 15.6 %copy-start.6 = (s32[48,2]{1,0:T(8,128)S(1)}, s32[48,2]{1,0:T(8,128)}, u32[]{:S(2)}) copy-start(s32[48,2]{1,0:T(8,128)} %constant.4.spot_ref) | copy-start | bytes 1156
  24.7 15.6 %copy-start.11 = (f32[512]{0:T(512)S(1)}, f32[512]{0:T(512)}, u32[]{:S(2)}) copy-start(f32[512]{0:T(512)} %param.22) | copy-start | bytes 6148
  24.7 15.6 %copy-start.12 = (f32[512]{0:T(512)S(1)}, f32[512]{0:T(512)}, u32[]{:S(2)}) copy-start(f32[512]{0:T(512)} %param.24) | copy-start | bytes 6148
  25.3 1.3 %collective-permute-start.5 = (f32[24,544]{1,0:T(8,128)S(1)}, f32[24,544]{1,0:T(8,128)S(1)}, u32[]{:S(2)}, u32[]{:S(2)}) collective-permute-start(f32[24,544]{1,0:T(8,128)S(1)} %get-tuple-element.18), channel_id=1, source_target_pairs={{0,1},{1,0},{2,3},{3,2},{4,5},{5,4},{6,7},{7,6},{8,9},{9,8},{10,11... | collective-permute-start | bytes 156680 | tf_op jit(solution)/shard_map/ppermute | solution.py:47
  26.6 5.0 %collective-permute-start.6 = (f32[24,544]{1,0:T(8,128)S(1)}, f32[24,544]{1,0:T(8,128)S(1)}, u32[]{:S(2)}, u32[]{:S(2)}) collective-permute-start(f32[24,544]{1,0:T(8,128)S(1)} %shard_map.174.refs_0_), channel_id=1, source_target_pairs={{0,2},{1,3},{2,0},{3,1},{4,6},{5,7},{6,4},{7,5},{8,10},{9,11},{10,... | collective-permute-start | bytes 156680 | tf_op jit(solution)/shard_map/ppermute | solution.py:47
  28.2 4.4 %collective-permute-start.7 = (f32[24,544]{1,0:T(8,128)S(1)}, f32[24,544]{1,0:T(8,128)S(1)}, u32[]{:S(2)}, u32[]{:S(2)}) collective-permute-start(f32[24,544]{1,0:T(8,128)S(1)} %shard_map.174.refs_0_), channel_id=1, source_target_pairs={{0,4},{1,5},{2,6},{3,7},{4,0},{5,1},{6,2},{7,3},{8,12},{9,13},{10,... | collective-permute-start | bytes 156680 | tf_op jit(solution)/shard_map/ppermute | solution.py:47
  28.2 5.3 %collective-permute-start.8 = (f32[24,544]{1,0:T(8,128)S(1)}, f32[24,544]{1,0:T(8,128)S(1)}, u32[]{:S(2)}, u32[]{:S(2)}) collective-permute-start(f32[24,544]{1,0:T(8,128)S(1)} %shard_map.174.refs_0_), channel_id=1, source_target_pairs={{0,6},{1,7},{2,4},{3,5},{4,2},{5,3},{6,0},{7,1},{8,14},{9,15},{10,... | collective-permute-start | bytes 156680 | tf_op jit(solution)/shard_map/ppermute | solution.py:47
  33.6 28.0 %copy-start.4 = (bf16[4,8192]{1,0:T(4,128)(2,1)S(1)}, bf16[4,8192]{1,0:T(4,128)(2,1)}, u32[]{:S(2)}) copy-start(bf16[4,8192]{1,0:T(4,128)(2,1)} %refs_0_.1) | copy-start | bytes 196612
  33.6 5.3 %collective-permute-start.9 = (f32[24,544]{1,0:T(8,128)S(1)}, f32[24,544]{1,0:T(8,128)S(1)}, u32[]{:S(2)}, u32[]{:S(2)}) collective-permute-start(f32[24,544]{1,0:T(8,128)S(1)} %shard_map.176.refs_0_), channel_id=1, source_target_pairs={{0,8},{1,9},{2,10},{3,11},{4,12},{5,13},{6,14},{7,15},{8,0},{9,1},... | collective-permute-start | bytes 156680 | tf_op jit(solution)/shard_map/ppermute | solution.py:47
  38.9 1.3 %collective-permute-start.10 = (f32[24,544]{1,0:T(8,128)S(1)}, f32[24,544]{1,0:T(8,128)S(1)}, u32[]{:S(2)}, u32[]{:S(2)}) collective-permute-start(f32[24,544]{1,0:T(8,128)S(1)} %shard_map.178.mine_ref), channel_id=1, source_target_pairs={{0,1},{1,0},{2,3},{3,2},{4,5},{5,4},{6,7},{7,6},{8,9},{9,8},{10,11... | collective-permute-start | bytes 156680 | tf_op jit(solution)/shard_map/ppermute | solution.py:47
  43.8 1.8 %collective-permute-start.11 = (bf16[1536,128]{1,0:T(8,128)(2,1)S(1)}, bf16[1536,128]{1,0:T(8,128)(2,1)S(1)}, u32[]{:S(2)}, u32[]{:S(2)}) collective-permute-start(bf16[1536,128]{1,0:T(8,128)(2,1)S(1)} %get-tuple-element.22), channel_id=1, source_target_pairs={{0,1},{1,0},{2,3},{3,2},{4,5},{5,4},{6,7},{7,6},{8,9},{9,8},{10,11... | collective-permute-start | bytes 1179656 | tf_op jit(solution)/shard_map/ppermute | solution.py:47
  45.7 7.0 %collective-permute-start.12 = (bf16[768,128]{1,0:T(8,128)(2,1)S(1)}, bf16[768,128]{1,0:T(8,128)(2,1)S(1)}, u32[]{:S(2)}, u32[]{:S(2)}) collective-permute-start(bf16[768,128]{1,0:T(8,128)(2,1)S(1)} %get-tuple-element.24), channel_id=1, source_target_pairs={{0,2},{1,3},{2,0},{3,1},{4,6},{5,7},{6,4},{7,5},{8,10},{9,11},{10,... | collective-permute-start | bytes 589832 | tf_op jit(solution)/shard_map/ppermute | solution.py:47
  52.8 6.6 %collective-permute-start.13 = (bf16[192,128]{1,0:T(8,128)(2,1)S(1)}, bf16[192,128]{1,0:T(8,128)(2,1)S(1)}, u32[]{:S(2)}, u32[]{:S(2)}) collective-permute-start(bf16[192,128]{1,0:T(8,128)(2,1)S(1)} %get-tuple-element.26), channel_id=1, source_target_pairs={{0,4},{1,5},{2,6},{3,7},{4,0},{5,1},{6,2},{7,3},{8,12},{9,13},{10,... | collective-permute-start | bytes 147464 | tf_op jit(solution)/shard_map/ppermute | solution.py:47
  54.5 5.8 %collective-permute-start.14 = (bf16[192,128]{1,0:T(8,128)(2,1)S(1)}, bf16[192,128]{1,0:T(8,128)(2,1)S(1)}, u32[]{:S(2)}, u32[]{:S(2)}) collective-permute-start(bf16[192,128]{1,0:T(8,128)(2,1)S(1)} %get-tuple-element.27), channel_id=1, source_target_pairs={{0,8},{1,9},{2,10},{3,11},{4,12},{5,13},{6,14},{7,15},{8,0},{9,1},... | collective-permute-start | bytes 147464 | tf_op jit(solution)/shard_map/ppermute | solution.py:47
  55.7 5.9 %collective-permute-start.15 = (bf16[192,128]{1,0:T(8,128)(2,1)S(1)}, bf16[192,128]{1,0:T(8,128)(2,1)S(1)}, u32[]{:S(2)}, u32[]{:S(2)}) collective-permute-start(bf16[192,128]{1,0:T(8,128)(2,1)S(1)} %get-tuple-element.28), channel_id=1, source_target_pairs={{0,12},{1,13},{2,14},{3,15},{4,8},{5,9},{6,10},{7,11},{8,4},{9,5},... | collective-permute-start | bytes 147464 | tf_op jit(solution)/shard_map/ppermute | solution.py:47

commit v4 on v3

--- a/solution.py
+++ b/solution.py
@@ -17,30 +17,59 @@
 F32 = jnp.float32
 
 
-def gather_phases(devices):
-    phases, high = [], devices
+def chip_steps(devices):
+    steps, high = [], devices
     while high > 2:
         if high >= 8:
-            step = high // 4
-            phases.append((step, 2 * step, 3 * step))
+            steps.append((high // 4, high // 2))
             high //= 4
         else:
-            phases.append((high // 2,))
+            steps.append((high // 2,))
             high //= 2
-    phases.append((1,))
-    return phases
+    steps = [tuple(step) for step in steps]
+    if len(steps[-1]) == 1:
+        bits = [bit for step in steps for bit in step]
+        bits.sort()
+        top = bits.pop()
+        steps = [(top,)] + [tuple(bits[k : k + 2]) for k in range(len(bits) - 2, -1, -2)]
+    return steps
+
+
+def gather_phases(devices):
+    whole = [step if len(step) == 1 else (sum(step), step[1], step[0]) for step in chip_steps(devices)]
+    return whole + [(1,)]
+
+
+def scatter_phases(devices):
+    whole = [step if len(step) == 1 else (step[1], step[0], sum(step)) for step in chip_steps(devices)]
+    return whole[::-1]
 
 
 def sum_phases(devices):
-    phases, step = [], 2
-    while step < devices:
-        if 4 * step <= devices:
-            phases.append((step, 2 * step, 3 * step))
-            step *= 4
-        else:
-            phases.append((step,))
-            step *= 2
-    return phases
+    return [
+        (step[0] + 1,) if len(step) == 1 else (step[0] + 1, step[1] + 1, sum(step))
+        for step in chip_steps(devices)
+    ]
+
+
+def order_of(phases):
+    order = [0]
+    for phase in phases:
+        order = order + [o ^ s for s in phase for o in order]
+    return order
+
+
+def spots_of(order):
+    return jnp.array(
+        [[o for o in order for _ in range(LIVE_MAX)], list(range(LIVE_MAX)) * len(order)],
+        jnp.int32,
+    )
+
+
+def side(index):
+    for shift in (4, 2, 1):
+        index = jnp.bitwise_xor(index, lax.shift_right_logical(index, shift))
+    return jnp.bitwise_and(index, 1)
 
 
 def swap(value, shift, devices):
@@ -132,11 +161,16 @@
 
 
 def load_kernel(start, size, far_ref, *refs):
-    out_ref, sem = refs[-2:]
-    rows = pl.ds(start, size)
-    copy = pltpu.make_async_copy(far_ref.at[rows], out_ref.at[rows], sem)
-    copy.start()
-    copy.wait()
+    out_ref, sems = refs[-2:]
+    count = sems.shape[0]
+    copies = []
+    for k in range(count):
+        rows = pl.ds(start + size * k // count, size // count)
+        copies.append(pltpu.make_async_copy(far_ref.at[rows], out_ref.at[rows], sems.at[k]))
+    for copy in copies:
+        copy.start()
+    for copy in copies:
+        copy.wait()
 
 
 def load(array, limit, step=0, steps=1, so_far=None):
@@ -150,16 +184,31 @@
         in_specs=[pl.BlockSpec(memory_space=pl.ANY)] * len(operands),
         out_specs=vmem(1)[0],
         input_output_aliases={} if so_far is None else {1: 0},
-        scratch_shapes=[pltpu.SemaphoreType.DMA],
+        scratch_shapes=[pltpu.SemaphoreType.DMA((4,))],
         compiler_params=pltpu.CompilerParams(vmem_limit_bytes=limit * MIB),
     )(*operands)
+
+
+def pack(low):
+    coefs = low[:, DTR:]
+    high = coefs.astype(BF16)
+    rest = (coefs - high.astype(F32)).astype(BF16)
+    return jnp.concatenate([low[:, :DTR].astype(BF16), high, rest], axis=1)
+
+
+def unpack(packed):
+    wide = packed.astype(F32)
+    count = (wide.shape[1] - DTR) // 2
+    coefs = wide[:, DTR : DTR + count] + wide[:, DTR + count :]
+    return jnp.concatenate([wide[:, :DTR], coefs], axis=1)
 
 
 def add_kernel(count, *refs):
     total = refs[0][...]
     for ref in refs[1:count]:
-        total = total + ref[...]
-    refs[-1][...] = total
+        total = total + (ref[...] if ref.dtype == F32 else unpack(ref[...]))
+    refs[-2][...] = total
+    refs[-1][...] = pack(total)
 
 
 def places(block, turn, height, span):
@@ -209,7 +258,7 @@
         mixed, coef_ref[...], (((1,), (1,)), ((), ())), preferred_element_type=F32
     )
     half = keep_ref.shape[0]
-    core = index % 2
+    core = side(index)
     keep_ref[...] = low_ref[pl.ds(pl.multiple_of(core * half, 8), half), :]
     send_ref[...] = low_ref[pl.ds(pl.multiple_of((1 - core) * half, 8), half), :]
 
@@ -242,9 +291,9 @@
 
 def join_low(mine_ref, other_ref, low_ref):
     half = mine_ref.shape[0]
-    core = lax.axis_index("weight") % 2
+    core = side(lax.axis_index("weight"))
     low_ref[pl.ds(pl.multiple_of(core * half, 8), half), :] = mine_ref[...]
-    low_ref[pl.ds(pl.multiple_of((1 - core) * half, 8), half), :] = other_ref[...]
+    low_ref[pl.ds(pl.multiple_of((1 - core) * half, 8), half), :] = unpack(other_ref[...])
 
 
 def readout_kernel(
@@ -398,13 +447,9 @@
     channels = in_weight.shape[2]
     low_width = coef_weight.shape[1]
     phases = gather_phases(devices)
-    order = [0]
-    for phase in phases:
-        order = order + [o ^ s for s in phase for o in order]
-    spots = jnp.array(
-        [[o for o in order for _ in range(LIVE_MAX)], list(range(LIVE_MAX)) * devices],
-        jnp.int32,
-    )
+    spots = spots_of(order_of(phases))
+    scatter = scatter_phases(devices)
+    ends = spots_of(order_of(scatter[::-1] + [(1,)])).T
     pieces = width // LANES
     slab = LIVE_MAX * pieces
 
@@ -466,23 +511,25 @@
         limit=16,
     )
 
+    packed_width = low_width + 2 * NSTATE
+
     def add(*parts, after=()):
         return call(
             functools.partial(add_kernel, len(parts)),
-            shape(parts[0].shape),
+            (shape(parts[0].shape), shape((kept // 2, packed_width), BF16)),
             (*parts, *after),
             far=len(after),
         )
 
-    low = add(keep, swap(send, 1, devices))
+    low, packed = add(keep, swap(send, 1, devices))
     exchanges = sum_phases(devices)
     for k, phase in enumerate(exchanges):
         after = (gate,)
         if k == len(exchanges) - 1:
             near_out = load(out_weight, 50)
             after = (near_out,)
-        low = add(low, *[swap(low, s, devices) for s in phase], after=after)
-    other = swap(low, 1, devices)
+        low, packed = add(low, *[swap(packed, s, devices) for s in phase], after=after)
+    other = swap(packed, 1, devices)
 
     size = kept // 2 * pieces
     keep, send, step_size = call(
@@ -492,7 +539,7 @@
             live_counts,
             low,
             other,
-            spots.T,
+            ends,
             mixed_x,
             gate,
             step_weight,
@@ -521,7 +568,7 @@
     )
 
     total = (keep, swap(send, 1, devices))
-    for phase in reversed(phases[:-1]):
+    for phase in scatter:
         size //= len(phase) + 1
         parts = call(
             functools.partial(sum_kernel, len(total)),

time: 62.6 us -> 57.7 us (0.922)
  waiting for transfers between devices: 17.7 us -> 13.3 us
  starting transfers between devices: 19.6 us -> 18.3 us
  Pallas kernels: 20.9 us -> 21.6 us
    ppermute x16, waiting for transfers between devices: 17.7 us -> 13.3 us  [swap(): lax.ppermute(value, 'weight', [(i, i ^ shift) for i in range(devices)])]
    ppermute x16, starting transfers between devices: 19.6 us -> 18.3 us  [swap(): lax.ppermute(value, 'weight', [(i, i ^ shift) for i in range(devices)])]
  transfers between devices with their start and end apart: 16 -> 16, of which waited for: 11 -> 11; matrix products, arithmetic and copies ran while one was open for 0% -> 0% of each run, Pallas kernels for 23% -> 25%
where the time goes in v4:
time: 57.7 us; the launch traced here: 57.5 us
  Pallas kernels  21.6 us (37%)
  starting transfers between devices  18.3 us (32%)
  waiting for transfers between devices  13.3 us (23%)
  matrix products  3.15 us (5%)
  between operations  0.93 us (2%)
    ppermute x16, starting transfers between devices, swap(): lax.ppermute(value, 'weight', [(i, i ^ shift) for i in range(devices)])  18.3 us
    ppermute x16, waiting for transfers between devices, swap(): lax.ppermute(value, 'weight', [(i, i ^ shift) for i in range(devices)])  13.3 us
    pallas_call x15, Pallas kernels, call(): pl.pallas_call(kernel, out_shape=outs, in_specs=[pl.BlockSpec(memory_spac...  11.1 us
    pallas_call x3, Pallas kernels, load(): pl.pallas_call(functools.partial(load_kernel, start, size), out_shape=plt...  10.5 us
    dot_general x1, matrix products, body(): jnp.einsum('rd,dbc->brc', normed, near_weight, preferred_element_type=F32)  3.15 us
  transfers between devices with their start and end apart: 16, of which 11 were waited for; matrix products, arithmetic and copies ran while one was open for 0% of the time, Pallas kernels for 25%

profile of v4, /device:TPU:0, one launch (start us, length us, event | category | flops | bytes accessed | tf_op | source)
XLA Modules:
  0.0 57.5 jit_solution(5803499948797344948)
XLA Ops:
  0.6 1.1 %shard_map.177.refs_0_ = bf16[192,128]{1,0:T(8,128)(2,1)S(1)} custom-call(bf16[4,8192]{1,0:T(4,128)(2,1)} %refs_0_.1, f32[1,8192]{1,0:T(1,128)} %bitcast.18), custom_call_target="tpu_custom_call" | custom-call | tf_op jit(solution)/shard_map/pallas_call | solution.py:97
  1.7 4.1 %collective-permute-start = (bf16[192,128]{1,0:T(8,128)(2,1)S(1)}, bf16[192,128]{1,0:T(8,128)(2,1)S(1)}, u32[]{:S(2)}, u32[]{:S(2)}) collective-permute-start(bf16[192,128]{1,0:T(8,128)(2,1)S(1)} %shard_map.177.refs_0_), channel_id=1, source_target_pairs={{0,8},{1,9},{2,10},{3,11},{4,12},{5,13},{6,14},{7,15},{8,0},{9,1},... | collective-permute-start | bytes 147464 | tf_op jit(solution)/shard_map/ppermute | solution.py:76
  5.8 3.5 %shard_map.175.refs_0_.refs_2_ = bf16[8192,2,512]{2,1,0:T(2,128)(2,1)S(1)} custom-call(bf16[8192,2,512]{2,1,0:T(2,128)(2,1)} %far_ref.4), custom_call_target="tpu_custom_call" | custom-call | tf_op jit(solution)/shard_map/pallas_call | solution.py:181
  9.4 2.6 %collective-permute-start.1 = (bf16[384,128]{1,0:T(8,128)(2,1)S(1)}, bf16[384,128]{1,0:T(8,128)(2,1)S(1)}, u32[]{:S(2)}, u32[]{:S(2)}) collective-permute-start(bf16[384,128]{1,0:T(8,128)(2,1)S(1)} %shard_map.178.refs_0_), channel_id=1, source_target_pairs={{0,6},{1,7},{2,4},{3,5},{4,2},{5,3},{6,0},{7,1},{8,14},{9,15},{10,... | collective-permute-start | bytes 294920 | tf_op jit(solution)/shard_map/ppermute | solution.py:76
  12.0 0.4 collective-permute-start.2
  12.4 0.5 collective-permute-start.3
  12.9 3.5 %shard_map.176.refs_4_ = bf16[8192,2,512]{2,1,0:T(2,128)(2,1)S(1)} custom-call(bf16[8192,2,512]{2,1,0:T(2,128)(2,1)} %far_ref.4, bf16[8192,2,512]{2,1,0:T(2,128)(2,1)S(1)} %shard_map.175.refs_0_.refs_2_), custom_call_target="tpu_custom_call", output_to_operand_aliasing={{}: (1, {})} | custom-call | tf_op jit(solution)/shard_map/pallas_call | solution.py:181
  16.4 0.6 collective-permute-done.2.refs_2_
  17.0 0.1 collective-permute-done.3.refs_3_
  17.1 0.1 collective-permute-start.4
  17.2 0.5 shard_map.180.half_ref
  17.7 1.2 %collective-permute-done.4.other_ref = bf16[1536,128]{1,0:T(8,128)(2,1)S(1)} collective-permute-done((bf16[1536,128]{1,0:T(8,128)(2,1)S(1)}, bf16[1536,128]{1,0:T(8,128)(2,1)S(1)}, u32[]{:S(2)}, u32[]{:S(2)}) %collective-permute-start.4) | collective-permute-done | bytes 393248 | tf_op jit(solution)/shard_map/ppermute | solution.py:76
  18.9 0.6 %shard_map.181 = bf16[48,8192]{1,0:T(8,128)(2,1)S(1)} custom-call(f32[24,8192]{1,0:T(8,128)S(1)} %shard_map.180.half_ref, bf16[1536,128]{1,0:T(8,128)(2,1)S(1)} %collective-permute-done.4.other_ref), custom_call_target="tpu_custom_call" | custom-call | tf_op jit(solution)/shard_map/pallas_call | solution.py:97
  19.5 0.0 copy-start.1
  19.5 0.0 copy-start.7
  19.5 0.0 copy-start.9
  19.6 0.0 copy-start.8
  19.6 3.1 %fusion.2.both_ref = f32[2,48,512]{2,1,0:T(8,128)S(1)} fusion(bf16[8192,2,512]{2,1,0:T(2,128)(2,1)S(1)} %shard_map.176.refs_4_, bf16[48,8192]{1,0:T(8,128)(2,1)S(1)} %shard_map.181), kind=kOutput, calls=%fused_computation.2 | convolution fusion | flops 805306368 | bytes 17760256 | tf_op jit(solution)/shard_map/rd,dbc->brc/dot_general | solution.py:484
  22.7 0.0 copy-start
  22.8 0.0 copy-start.6
  22.8 0.5 shard_map.182
  23.4 0.2 collective-permute-start.5
  23.6 1.1 %collective-permute-done.5.refs_1_ = f32[24,544]{1,0:T(8,128)S(1)} collective-permute-done((f32[24,544]{1,0:T(8,128)S(1)}, f32[24,544]{1,0:T(8,128)S(1)}, u32[]{:S(2)}, u32[]{:S(2)}) %collective-permute-start.5) | collective-permute-done | bytes 52256 | tf_op jit(solution)/shard_map/ppermute | solution.py:76
  24.7 0.1 shard_map.183
  24.8 1.2 %collective-permute-start.6 = (bf16[24,576]{1,0:T(8,128)(2,1)S(1)}, bf16[24,576]{1,0:T(8,128)(2,1)S(1)}, u32[]{:S(2)}, u32[]{:S(2)}) collective-permute-start(bf16[24,576]{1,0:T(8,128)(2,1)S(1)} %get-tuple-element.26), channel_id=1, source_target_pairs={{0,9},{1,8},{2,11},{3,10},{4,13},{5,12},{6,15},{7,14},{8,1},{9,0},... | collective-permute-start | bytes 82952 | tf_op jit(solution)/shard_map/ppermute | solution.py:76
  26.0 1.4 %shard_map.184 = (f32[48,512]{1,0:T(8,128)S(1)}, bf16[3,64,512]{2,1,0:T(8,128)(2,1)}) custom-call(s32[16]{0:T(128)S(1)} %copy-done.8, f32[2,48,512]{2,1,0:T(8,128)S(1)} %fusion.2.both_ref, s32[2,48]{1,0:T(2,128)S(1)} %copy-done.9, bf16[3,64,512]{2,1,0:T(8,128)(2,1)S(1)} %bitcast.13, bf16[48,512]{1,0:T(8,128)(2,1)S(1)} %get-tuple-element.27.mixed_ref), custom_call_target="tpu_custom_call" | custom-call | tf_op jit(solution)/shard_map/pallas_call | solution.py:97
  27.4 1.6 %collective-permute-done.6.refs_1_ = bf16[24,576]{1,0:T(8,128)(2,1)S(1)} collective-permute-done((bf16[24,576]{1,0:T(8,128)(2,1)S(1)}, bf16[24,576]{1,0:T(8,128)(2,1)S(1)}, u32[]{:S(2)}, u32[]{:S(2)}) %collective-permute-start.6) | collective-permute-done | bytes 27680 | tf_op jit(solution)/shard_map/ppermute | solution.py:76
  29.0 0.1 shard_map.185
  29.1 0.9 %collective-permute-start.7 = (bf16[24,576]{1,0:T(8,128)(2,1)S(1)}, bf16[24,576]{1,0:T(8,128)(2,1)S(1)}, u32[]{:S(2)}, u32[]{:S(2)}) collective-permute-start(bf16[24,576]{1,0:T(8,128)(2,1)S(1)} %get-tuple-element.30), channel_id=1, source_target_pairs={{0,3},{1,2},{2,1},{3,0},{4,7},{5,6},{6,5},{7,4},{8,11},{9,10},{10,... | collective-permute-start | bytes 82952 | tf_op jit(solution)/shard_map/ppermute | solution.py:76
  30.0 1.5 %collective-permute-start.8 = (bf16[24,576]{1,0:T(8,128)(2,1)S(1)}, bf16[24,576]{1,0:T(8,128)(2,1)S(1)}, u32[]{:S(2)}, u32[]{:S(2)}) collective-permute-start(bf16[24,576]{1,0:T(8,128)(2,1)S(1)} %get-tuple-element.30), channel_id=1, source_target_pairs={{0,5},{1,4},{2,7},{3,6},{4,1},{5,0},{6,3},{7,2},{8,13},{9,12},{10,... | collective-permute-start | bytes 82952 | tf_op jit(solution)/shard_map/ppermute | solution.py:76
  31.5 0.8 %collective-permute-start.9 = (bf16[24,576]{1,0:T(8,128)(2,1)S(1)}, bf16[24,576]{1,0:T(8,128)(2,1)S(1)}, u32[]{:S(2)}, u32[]{:S(2)}) collective-permute-start(bf16[24,576]{1,0:T(8,128)(2,1)S(1)} %get-tuple-element.30), channel_id=1, source_target_pairs={{0,6},{1,7},{2,4},{3,5},{4,2},{5,3},{6,0},{7,1},{8,14},{9,15},{10,... | collective-permute-start | bytes 82952 | tf_op jit(solution)/shard_map/ppermute | solution.py:76
  32.4 3.5 %shard_map.186.refs_4_.out_weight_ref = bf16[512,8192]{1,0:T(8,128)(2,1)S(1)} custom-call(bf16[512,8192]{1,0:T(8,128)(2,1)} %far_ref.5), custom_call_target="tpu_custom_call" | custom-call | tf_op jit(solution)/shard_map/pallas_call | solution.py:181
  35.9 0.5 collective-permute-done.9.refs_3_
  36.3 0.2 shard_map.187
  36.5 1.2 %collective-permute-done.10.other_ref = bf16[24,576]{1,0:T(8,128)(2,1)S(1)} collective-permute-done((bf16[24,576]{1,0:T(8,128)(2,1)S(1)}, bf16[24,576]{1,0:T(8,128)(2,1)S(1)}, u32[]{:S(2)}, u32[]{:S(2)}) %collective-permute-start.10) | collective-permute-done | bytes 27680 | tf_op jit(solution)/shard_map/ppermute | solution.py:76
  37.7 3.6 %shard_map.188 = (f32[1536,128]{1,0:T(8,128)S(1)}, bf16[1536,128]{1,0:T(8,128)(2,1)S(1)}, f32[48,512]{1,0:T(8,128)S(1)}) custom-call(s32[16]{0:T(128)S(1)} %copy-done.8, f32[24,544]{1,0:T(8,128)S(1)} %get-tuple-element.31.mine_ref, bf16[24,576]{1,0:T(8,128)(2,1)S(1)} %collective-permute-done.10.other_ref, s32[48,2]{1,0:T(8,128)S(1)} %copy-done.6, ...), custom_call_target="tpu_custom_call" | custom-call | tf_op jit(solution)/shard_map/pallas_call | solution.py:97
  41.3 0.2 collective-permute-start.11
  41.5 1.6 %collective-permute-done.11.refs_1_ = bf16[1536,128]{1,0:T(8,128)(2,1)S(1)} collective-permute-done((bf16[1536,128]{1,0:T(8,128)(2,1)S(1)}, bf16[1536,128]{1,0:T(8,128)(2,1)S(1)}, u32[]{:S(2)}, u32[]{:S(2)}) %collective-permute-start.11) | collective-permute-done | bytes 393248 | tf_op jit(solution)/shard_map/ppermute | solution.py:76
  43.1 0.1 shard_map.189
  43.2 1.2 %collective-permute-start.12 = (bf16[384,128]{1,0:T(8,128)(2,1)S(1)}, bf16[384,128]{1,0:T(8,128)(2,1)S(1)}, u32[]{:S(2)}, u32[]{:S(2)}) collective-permute-start(bf16[384,128]{1,0:T(8,128)(2,1)S(1)} %get-tuple-element.36), channel_id=1, source_target_pairs={{0,4},{1,5},{2,6},{3,7},{4,0},{5,1},{6,2},{7,3},{8,12},{9,13},{10,... | collective-permute-start | bytes 294920 | tf_op jit(solution)/shard_map/ppermute | solution.py:76
  44.4 1.1 %collective-permute-start.13 = (bf16[384,128]{1,0:T(8,128)(2,1)S(1)}, bf16[384,128]{1,0:T(8,128)(2,1)S(1)}, u32[]{:S(2)}, u32[]{:S(2)}) collective-permute-start(bf16[384,128]{1,0:T(8,128)(2,1)S(1)} %get-tuple-element.37), channel_id=1, source_target_pairs={{0,2},{1,3},{2,0},{3,1},{4,6},{5,7},{6,4},{7,5},{8,10},{9,11},{10,... | collective-permute-start | bytes 294920 | tf_op jit(solution)/shard_map/ppermute | solution.py:76
  45.5 1.3 %collective-permute-start.14 = (bf16[384,128]{1,0:T(8,128)(2,1)S(1)}, bf16[384,128]{1,0:T(8,128)(2,1)S(1)}, u32[]{:S(2)}, u32[]{:S(2)}) collective-permute-start(bf16[384,128]{1,0:T(8,128)(2,1)S(1)} %get-tuple-element.38), channel_id=1, source_target_pairs={{0,6},{1,7},{2,4},{3,5},{4,2},{5,3},{6,0},{7,1},{8,14},{9,15},{10,... | collective-permute-start | bytes 294920 | tf_op jit(solution)/shard_map/ppermute | solution.py:76
  46.7 1.4 %collective-permute-done.12.refs_1_ = bf16[384,128]{1,0:T(8,128)(2,1)S(1)} collective-permute-done((bf16[384,128]{1,0:T(8,128)(2,1)S(1)}, bf16[384,128]{1,0:T(8,128)(2,1)S(1)}, u32[]{:S(2)}, u32[]{:S(2)}) %collective-permute-start.12) | collective-permute-done | bytes 98336 | tf_op jit(solution)/shard_map/ppermute | solution.py:76
  48.1 3.0 %collective-permute-done.13.refs_2_ = bf16[384,128]{1,0:T(8,128)(2,1)S(1)} collective-permute-done((bf16[384,128]{1,0:T(8,128)(2,1)S(1)}, bf16[384,128]{1,0:T(8,128)(2,1)S(1)}, u32[]{:S(2)}, u32[]{:S(2)}) %collective-permute-start.13) | collective-permute-done | bytes 98336 | tf_op jit(solution)/shard_map/ppermute | solution.py:76
  51.2 2.2 %collective-permute-start.15 = (bf16[192,128]{1,0:T(8,128)(2,1)S(1)}, bf16[192,128]{1,0:T(8,128)(2,1)S(1)}, u32[]{:S(2)}, u32[]{:S(2)}) collective-permute-start(bf16[192,128]{1,0:T(8,128)(2,1)S(1)} %get-tuple-element.40), channel_id=1, source_target_pairs={{0,8},{1,9},{2,10},{3,11},{4,12},{5,13},{6,14},{7,15},{8,0},{9,1},... | collective-permute-start | bytes 147464 | tf_op jit(solution)/shard_map/ppermute | solution.py:76
  53.4 2.2 %shard_map.192 = bf16[64,16,512]{2,1,0:T(8,128)(2,1)} custom-call(s32[16]{0:T(128)S(1)} %copy-done.8, f32[24,544]{1,0:T(8,128)S(1)} %get-tuple-element.31.mine_ref, bf16[24,576]{1,0:T(8,128)(2,1)S(1)} %collective-permute-done.10.other_ref, bf16[48,512]{1,0:T(8,128)(2,1)S(1)} %get-tuple-element.27.mixed_ref, f32[48,512]{1,0:T(8,128)S(1)} %get-tuple-element.41.step_ref, ...), custom_call_target="tpu_custom_call" | custom-call | tf_op jit(solution)/shard_map/pallas_call | solution.py:97
  55.6 1.1 %collective-permute-done.15.refs_2_ = bf16[192,128]{1,0:T(8,128)(2,1)S(1)} collective-permute-done((bf16[192,128]{1,0:T(8,128)(2,1)S(1)}, bf16[192,128]{1,0:T(8,128)(2,1)S(1)}, u32[]{:S(2)}, u32[]{:S(2)}) %collective-permute-start.15) | collective-permute-done | bytes 49184 | tf_op jit(solution)/shard_map/ppermute | solution.py:76
  56.8 0.7 %shard_map.191 = bf16[4,8192]{1,0:T(4,128)(2,1)} custom-call(bf16[4,8192]{1,0:T(4,128)(2,1)S(1)} %copy-done.4, f32[192,128]{1,0:T(8,128)S(1)} %get-tuple-element.39.refs_1_, bf16[192,128]{1,0:T(8,128)(2,1)S(1)} %collective-permute-done.15.refs_2_), custom_call_target="tpu_custom_call" | custom-call | tf_op jit(solution)/shard_map/pallas_call | solution.py:97
  (29 shorter events, 0.2 us)
Async XLA Ops:
  1.7 7.6 %collective-permute-start = (bf16[192,128]{1,0:T(8,128)(2,1)S(1)}, bf16[192,128]{1,0:T(8,128)(2,1)S(1)}, u32[]{:S(2)}, u32[]{:S(2)}) collective-permute-start(bf16[192,128]{1,0:T(8,128)(2,1)S(1)} %shard_map.177.refs_0_), channel_id=1, source_target_pairs={{0,8},{1,9},{2,10},{3,11},{4,12},{5,13},{6,14},{7,15},{8,0},{9,1},... | collective-permute-start | bytes 147464 | tf_op jit(solution)/shard_map/ppermute | solution.py:76
  9.4 7.1 %collective-permute-start.1 = (bf16[384,128]{1,0:T(8,128)(2,1)S(1)}, bf16[384,128]{1,0:T(8,128)(2,1)S(1)}, u32[]{:S(2)}, u32[]{:S(2)}) collective-permute-start(bf16[384,128]{1,0:T(8,128)(2,1)S(1)} %shard_map.178.refs_0_), channel_id=1, source_target_pairs={{0,6},{1,7},{2,4},{3,5},{4,2},{5,3},{6,0},{7,1},{8,14},{9,15},{10,... | collective-permute-start | bytes 294920 | tf_op jit(solution)/shard_map/ppermute | solution.py:76
  12.0 5.0 %collective-permute-start.2 = (bf16[384,128]{1,0:T(8,128)(2,1)S(1)}, bf16[384,128]{1,0:T(8,128)(2,1)S(1)}, u32[]{:S(2)}, u32[]{:S(2)}) collective-permute-start(bf16[384,128]{1,0:T(8,128)(2,1)S(1)} %shard_map.178.refs_0_), channel_id=1, source_target_pairs={{0,4},{1,5},{2,6},{3,7},{4,0},{5,1},{6,2},{7,3},{8,12},{9,13},{10,... | collective-permute-start | bytes 294920 | tf_op jit(solution)/shard_map/ppermute | solution.py:76
  12.4 4.7 %collective-permute-start.3 = (bf16[384,128]{1,0:T(8,128)(2,1)S(1)}, bf16[384,128]{1,0:T(8,128)(2,1)S(1)}, u32[]{:S(2)}, u32[]{:S(2)}) collective-permute-start(bf16[384,128]{1,0:T(8,128)(2,1)S(1)} %shard_map.178.refs_0_), channel_id=1, source_target_pairs={{0,2},{1,3},{2,0},{3,1},{4,6},{5,7},{6,4},{7,5},{8,10},{9,11},{10,... | collective-permute-start | bytes 294920 | tf_op jit(solution)/shard_map/ppermute | solution.py:76
  17.1 1.8 %collective-permute-start.4 = (bf16[1536,128]{1,0:T(8,128)(2,1)S(1)}, bf16[1536,128]{1,0:T(8,128)(2,1)S(1)}, u32[]{:S(2)}, u32[]{:S(2)}) collective-permute-start(bf16[1536,128]{1,0:T(8,128)(2,1)S(1)} %shard_map.179.mine_ref), channel_id=1, source_target_pairs={{0,1},{1,0},{2,3},{3,2},{4,5},{5,4},{6,7},{7,6},{8,9},{9,8},{10,11... | collective-permute-start | bytes 1179656 | tf_op jit(solution)/shard_map/ppermute | solution.py:76
  19.5 3.3 %copy-start.1 = (bf16[64,3,512]{2,0,1:T(8,128)(2,1)S(1)}, bf16[64,3,512]{2,0,1:T(8,128)(2,1)}, u32[]{:S(2)}) copy-start(bf16[64,3,512]{2,0,1:T(8,128)(2,1)} %param.28) | copy-start | bytes 589828
  19.5 3.3 %copy-start.2 = (bf16[512,544]{0,1:T(8,128)(2,1)S(1)}, bf16[512,544]{0,1:T(8,128)(2,1)}, u32[]{:S(2)}) copy-start(bf16[512,544]{0,1:T(8,128)(2,1)} %param.21) | copy-start | bytes 1671172
  19.5 3.3 %copy-start.7 = (f32[4,512]{1,0:T(4,128)S(1)}, f32[4,512]{1,0:T(4,128)}, u32[]{:S(2)}) copy-start(f32[4,512]{1,0:T(4,128)} %taps_ref.1) | copy-start | bytes 24580
  19.5 3.3 %copy-start.9 = (s32[2,48]{1,0:T(2,128)S(1)}, s32[2,48]{1,0:T(2,128)}, u32[]{:S(2)}) copy-start(s32[2,48]{1,0:T(2,128)} %constant.4.clone.spot_ref) | copy-start | bytes 1156
  19.5 3.3 %copy-start.10 = (f32[512]{0:T(512)S(1)}, f32[512]{0:T(512)}, u32[]{:S(2)}) copy-start(f32[512]{0:T(512)} %param.20) | copy-start | bytes 6148
  19.6 6.4 %copy-start.8 = (s32[16]{0:T(128)S(1)}, s32[16]{0:T(128)}, u32[]{:S(2)}) copy-start(s32[16]{0:T(128)} %live_ref.5) | copy-start | bytes 196
  22.7 15.0 %copy-start = (bf16[64,16,512]{2,1,0:T(8,128)(2,1)S(1)}, bf16[64,16,512]{2,1,0:T(8,128)(2,1)}, u32[]{:S(2)}) copy-start(bf16[64,16,512]{2,1,0:T(8,128)(2,1)} %state_ref.3) | copy-start | bytes 3145732
  22.7 15.0 %copy-start.3 = (bf16[512,512]{1,0:T(8,128)(2,1)S(1)}, bf16[512,512]{1,0:T(8,128)(2,1)}, u32[]{:S(2)}) copy-start(bf16[512,512]{1,0:T(8,128)(2,1)} %step_weight_ref.1) | copy-start | bytes 1572868
  22.7 15.0 %copy-start.5 = (f32[16,512]{1,0:T(8,128)S(1)}, f32[16,512]{1,0:T(8,128)}, u32[]{:S(2)}) copy-start(f32[16,512]{1,0:T(8,128)} %rates_ref.3) | copy-start | bytes 98308
  22.8 15.0 %copy-start.6 = (s32[48,2]{1,0:T(8,128)S(1)}, s32[48,2]{1,0:T(8,128)}, u32[]{:S(2)}) copy-start(s32[48,2]{1,0:T(8,128)} %constant.7.spot_ref) | copy-start | bytes 1156
  22.8 15.0 %copy-start.11 = (f32[512]{0:T(512)S(1)}, f32[512]{0:T(512)}, u32[]{:S(2)}) copy-start(f32[512]{0:T(512)} %param.23) | copy-start | bytes 6148
  22.8 15.0 %copy-start.12 = (f32[512]{0:T(512)S(1)}, f32[512]{0:T(512)}, u32[]{:S(2)}) copy-start(f32[512]{0:T(512)} %param.25) | copy-start | bytes 6148
  23.4 1.3 %collective-permute-start.5 = (f32[24,544]{1,0:T(8,128)S(1)}, f32[24,544]{1,0:T(8,128)S(1)}, u32[]{:S(2)}, u32[]{:S(2)}) collective-permute-start(f32[24,544]{1,0:T(8,128)S(1)} %get-tuple-element.24), channel_id=1, source_target_pairs={{0,1},{1,0},{2,3},{3,2},{4,5},{5,4},{6,7},{7,6},{8,9},{9,8},{10,11... | collective-permute-start | bytes 156680 | tf_op jit(solution)/shard_map/ppermute | solution.py:76
  24.8 4.2 %collective-permute-start.6 = (bf16[24,576]{1,0:T(8,128)(2,1)S(1)}, bf16[24,576]{1,0:T(8,128)(2,1)S(1)}, u32[]{:S(2)}, u32[]{:S(2)}) collective-permute-start(bf16[24,576]{1,0:T(8,128)(2,1)S(1)} %get-tuple-element.26), channel_id=1, source_target_pairs={{0,9},{1,8},{2,11},{3,10},{4,13},{5,12},{6,15},{7,14},{8,1},{9,0},... | collective-permute-start | bytes 82952 | tf_op jit(solution)/shard_map/ppermute | solution.py:76
  29.1 27.6 %copy-start.4 = (bf16[4,8192]{1,0:T(4,128)(2,1)S(1)}, bf16[4,8192]{1,0:T(4,128)(2,1)}, u32[]{:S(2)}) copy-start(bf16[4,8192]{1,0:T(4,128)(2,1)} %refs_0_.1) | copy-start | bytes 196612
  29.1 6.7 %collective-permute-start.7 = (bf16[24,576]{1,0:T(8,128)(2,1)S(1)}, bf16[24,576]{1,0:T(8,128)(2,1)S(1)}, u32[]{:S(2)}, u32[]{:S(2)}) collective-permute-start(bf16[24,576]{1,0:T(8,128)(2,1)S(1)} %get-tuple-element.30), channel_id=1, source_target_pairs={{0,3},{1,2},{2,1},{3,0},{4,7},{5,6},{6,5},{7,4},{8,11},{9,10},{10,... | collective-permute-start | bytes 82952 | tf_op jit(solution)/shard_map/ppermute | solution.py:76
  30.0 5.9 %collective-permute-start.8 = (bf16[24,576]{1,0:T(8,128)(2,1)S(1)}, bf16[24,576]{1,0:T(8,128)(2,1)S(1)}, u32[]{:S(2)}, u32[]{:S(2)}) collective-permute-start(bf16[24,576]{1,0:T(8,128)(2,1)S(1)} %get-tuple-element.30), channel_id=1, source_target_pairs={{0,5},{1,4},{2,7},{3,6},{4,1},{5,0},{6,3},{7,2},{8,13},{9,12},{10,... | collective-permute-start | bytes 82952 | tf_op jit(solution)/shard_map/ppermute | solution.py:76
  31.5 4.8 %collective-permute-start.9 = (bf16[24,576]{1,0:T(8,128)(2,1)S(1)}, bf16[24,576]{1,0:T(8,128)(2,1)S(1)}, u32[]{:S(2)}, u32[]{:S(2)}) collective-permute-start(bf16[24,576]{1,0:T(8,128)(2,1)S(1)} %get-tuple-element.30), channel_id=1, source_target_pairs={{0,6},{1,7},{2,4},{3,5},{4,2},{5,3},{6,0},{7,1},{8,14},{9,15},{10,... | collective-permute-start | bytes 82952 | tf_op jit(solution)/shard_map/ppermute | solution.py:76
  36.5 1.2 %collective-permute-start.10 = (bf16[24,576]{1,0:T(8,128)(2,1)S(1)}, bf16[24,576]{1,0:T(8,128)(2,1)S(1)}, u32[]{:S(2)}, u32[]{:S(2)}) collective-permute-start(bf16[24,576]{1,0:T(8,128)(2,1)S(1)} %get-tuple-element.32), channel_id=1, source_target_pairs={{0,1},{1,0},{2,3},{3,2},{4,5},{5,4},{6,7},{7,6},{8,9},{9,8},{10,11... | collective-permute-start | bytes 82952 | tf_op jit(solution)/shard_map/ppermute | solution.py:76
  41.3 1.8 %collective-permute-start.11 = (bf16[1536,128]{1,0:T(8,128)(2,1)S(1)}, bf16[1536,128]{1,0:T(8,128)(2,1)S(1)}, u32[]{:S(2)}, u32[]{:S(2)}) collective-permute-start(bf16[1536,128]{1,0:T(8,128)(2,1)S(1)} %get-tuple-element.34), channel_id=1, source_target_pairs={{0,1},{1,0},{2,3},{3,2},{4,5},{5,4},{6,7},{7,6},{8,9},{9,8},{10,11... | collective-permute-start | bytes 1179656 | tf_op jit(solution)/shard_map/ppermute | solution.py:76
  43.2 4.9 %collective-permute-start.12 = (bf16[384,128]{1,0:T(8,128)(2,1)S(1)}, bf16[384,128]{1,0:T(8,128)(2,1)S(1)}, u32[]{:S(2)}, u32[]{:S(2)}) collective-permute-start(bf16[384,128]{1,0:T(8,128)(2,1)S(1)} %get-tuple-element.36), channel_id=1, source_target_pairs={{0,4},{1,5},{2,6},{3,7},{4,0},{5,1},{6,2},{7,3},{8,12},{9,13},{10,... | collective-permute-start | bytes 294920 | tf_op jit(solution)/shard_map/ppermute | solution.py:76
  44.4 6.7 %collective-permute-start.13 = (bf16[384,128]{1,0:T(8,128)(2,1)S(1)}, bf16[384,128]{1,0:T(8,128)(2,1)S(1)}, u32[]{:S(2)}, u32[]{:S(2)}) collective-permute-start(bf16[384,128]{1,0:T(8,128)(2,1)S(1)} %get-tuple-element.37), channel_id=1, source_target_pairs={{0,2},{1,3},{2,0},{3,1},{4,6},{5,7},{6,4},{7,5},{8,10},{9,11},{10,... | collective-permute-start | bytes 294920 | tf_op jit(solution)/shard_map/ppermute | solution.py:76
  45.5 5.7 %collective-permute-start.14 = (bf16[384,128]{1,0:T(8,128)(2,1)S(1)}, bf16[384,128]{1,0:T(8,128)(2,1)S(1)}, u32[]{:S(2)}, u32[]{:S(2)}) collective-permute-start(bf16[384,128]{1,0:T(8,128)(2,1)S(1)} %get-tuple-element.38), channel_id=1, source_target_pairs={{0,6},{1,7},{2,4},{3,5},{4,2},{5,3},{6,0},{7,1},{8,14},{9,15},{10,... | collective-permute-start | bytes 294920 | tf_op jit(solution)/shard_map/ppermute | solution.py:76
  51.2 5.6 %collective-permute-start.15 = (bf16[192,128]{1,0:T(8,128)(2,1)S(1)}, bf16[192,128]{1,0:T(8,128)(2,1)S(1)}, u32[]{:S(2)}, u32[]{:S(2)}) collective-permute-start(bf16[192,128]{1,0:T(8,128)(2,1)S(1)} %get-tuple-element.40), channel_id=1, source_target_pairs={{0,8},{1,9},{2,10},{3,11},{4,12},{5,13},{6,14},{7,15},{8,0},{9,1},... | collective-permute-start | bytes 147464 | tf_op jit(solution)/shard_map/ppermute | solution.py:76

commit v5 on v4

--- a/solution.py
+++ b/solution.py
@@ -13,6 +13,8 @@
 TAPS = 4
 LANES = 128
 MIB = 1024 * 1024
+FIRST_SHARE = 0.4375
+FIRST_COLUMNS = 5
 BF16 = jnp.bfloat16
 F32 = jnp.float32
 
@@ -92,18 +94,41 @@
     return jax.ShapeDtypeStruct(dims, kind)
 
 
-def call(kernel, outs, operands, scalars=0, far=0, scratch=(), limit=8):
+def call(kernel, outs, operands, scalars=0, far=0, scratch=(), limit=8, after=(), aliases=None):
     many = isinstance(outs, tuple)
     return pl.pallas_call(
         kernel,
         out_shape=outs,
         in_specs=[pl.BlockSpec(memory_space=pltpu.SMEM)] * scalars
         + vmem(len(operands) - scalars - far)
-        + [pl.BlockSpec(memory_space=pl.ANY)] * far,
+        + [pl.BlockSpec(memory_space=pl.ANY)] * (far + len(after)),
         out_specs=tuple(vmem(len(outs))) if many else vmem(1)[0],
         scratch_shapes=list(scratch),
+        input_output_aliases=aliases or {},
         compiler_params=pltpu.CompilerParams(vmem_limit_bytes=limit * MIB),
-    )(*operands)
+    )(*operands, *after)
+
+
+def share_copies(far_ref, near_ref, sems, share):
+    rows = far_ref.shape[0]
+    start, end = (int(rows * part) // 8 * 8 for part in share)
+    count = sems.shape[0]
+    size = (end - start) // count
+    spans = [pl.ds(start + size * k, size) for k in range(count)]
+    return [
+        pltpu.make_async_copy(far_ref.at[span], near_ref.at[span], sems.at[k])
+        for k, span in enumerate(spans)
+    ]
+
+
+def start_all(copies):
+    for copy in copies:
+        copy.start()
+
+
+def wait_all(copies):
+    for copy in copies:
+        copy.wait()
 
 
 def fold(wide, folded_ref):
@@ -117,10 +142,8 @@
         pltpu.make_async_copy(far_hidden_ref, hidden_ref, sems.at[0]),
         pltpu.make_async_copy(far_gain_ref, gain_ref, sems.at[1]),
     ]
-    for copy in copies:
-        copy.start()
-    for copy in copies:
-        copy.wait()
+    start_all(copies)
+    wait_all(copies)
     wide = hidden_ref[...].astype(F32)[:LIVE_MAX]
     factor = lax.rsqrt(jnp.mean(wide * wide, axis=-1, keepdims=True) + 1e-05)
     fold(wide * factor * gain_ref[...], fold_ref)
@@ -139,8 +162,8 @@
     return call(
         functools.partial(join_kernel, len(parts)),
         shape((rows, parts[0].shape[1]), parts[0].dtype),
-        (*parts, *after),
-        far=len(after),
+        parts,
+        after=after,
     )
 
 
@@ -160,33 +183,18 @@
         out_ref[:, span] = jnp.concatenate([half_ref[:, span], other], axis=0).astype(BF16)
 
 
-def load_kernel(start, size, far_ref, *refs):
-    out_ref, sems = refs[-2:]
-    count = sems.shape[0]
-    copies = []
-    for k in range(count):
-        rows = pl.ds(start + size * k // count, size // count)
-        copies.append(pltpu.make_async_copy(far_ref.at[rows], out_ref.at[rows], sems.at[k]))
-    for copy in copies:
-        copy.start()
-    for copy in copies:
-        copy.wait()
-
-
-def load(array, limit, step=0, steps=1, so_far=None):
-    total = array.shape[0]
-    start = total * step // steps
-    size = total * (step + 1) // steps - start
-    operands = (array,) if so_far is None else (array, so_far)
-    return pl.pallas_call(
-        functools.partial(load_kernel, start, size),
-        out_shape=pltpu.VMEM(array.shape, array.dtype),
-        in_specs=[pl.BlockSpec(memory_space=pl.ANY)] * len(operands),
-        out_specs=vmem(1)[0],
-        input_output_aliases={} if so_far is None else {1: 0},
-        scratch_shapes=[pltpu.SemaphoreType.DMA((4,))],
-        compiler_params=pltpu.CompilerParams(vmem_limit_bytes=limit * MIB),
-    )(*operands)
+def columns_kernel(start, far_ref, near_ref, sems):
+    columns = pl.ds(start, near_ref.shape[1])
+    loads = share_copies(far_ref.at[:, columns], near_ref, sems, (0, 1))
+    start_all(loads)
+    wait_all(loads)
+
+
+def load_kernel(share, far_ref, *refs):
+    near_ref, sems = refs[-2:]
+    loads = share_copies(far_ref, near_ref, sems, share)
+    start_all(loads)
+    wait_all(loads)
 
 
 def pack(low):
@@ -263,30 +271,31 @@
     send_ref[...] = low_ref[pl.ds(pl.multiple_of((1 - core) * half, 8), half), :]
 
 
-def gate_kernel(
-    live_ref, both_ref, spot_ref, conv_ref, mixed_ref, gate_ref, new_conv_ref, alive_ref
-):
+def gate_kernel(both_ref, spot_ref, gate_ref):
+    block = jnp.bitwise_xor(spot_ref[0:1, :], lax.axis_index("weight"))
+    gate_ref[...] = jnp.dot(
+        places(block, spot_ref[1:2, :], gate_ref.shape[0], LIVE_MAX),
+        silu(both_ref[1]),
+        precision=lax.Precision.HIGHEST,
+        preferred_element_type=F32,
+    )
+
+
+def taps_kernel(live_ref, both_ref, spot_ref, conv_ref, new_conv_ref, alive_ref):
     blocks = live_ref.shape[0]
     rows = conv_ref.shape[1]
     rows_dev = rows // blocks
     block = jnp.bitwise_xor(spot_ref[0:1, :], lax.axis_index("weight"))
-    turn = spot_ref[1:2, :]
-    row_iota = lax.broadcasted_iota(jnp.int32, (rows_dev, 128), 0)
+    row_iota = lax.broadcasted_iota(jnp.int32, (rows_dev, LANES), 0)
     for b in range(blocks):
         alive_ref[b * rows_dev : (b + 1) * rows_dev, :] = jnp.where(
             row_iota < live_ref[b], 1.0, 0.0
         )
     alive = alive_ref[:, 0:1] > 0.0
-    fresh = fresh_input(both_ref, block, turn, rows, rows_dev)
+    fresh = fresh_input(both_ref, block, spot_ref[1:2, :], rows, rows_dev)
     states = [conv_ref[k].astype(F32) for k in range(TAPS - 1)] + [fresh]
     for k in range(TAPS - 1):
         new_conv_ref[k] = jnp.where(alive, states[k + 1], states[k]).astype(BF16)
-    gate_ref[...] = jnp.dot(
-        places(block, turn, mixed_ref.shape[0], LIVE_MAX),
-        silu(both_ref[1]),
-        precision=lax.Precision.HIGHEST,
-        preferred_element_type=F32,
-    )
 
 
 def join_low(mine_ref, other_ref, low_ref):
@@ -308,7 +317,8 @@
     rates_ref,
     skip_ref,
     state_ref,
-    out_weight_ref,
+    first_ref,
+    last_ref,
     keep_ref,
     send_ref,
     step_ref,
@@ -350,20 +360,26 @@
     column = lax.broadcasted_iota(jnp.int32, (kept, kept), 1)
     pick = jnp.where(column == block * LIVE_MAX + spot_ref[:, 1:2], 1.0, 0.0).astype(BF16)
     picked = jnp.dot(pick, gated, preferred_element_type=F32).astype(BF16)
-    width = out_weight_ref.shape[1]
-    pieces = width // LANES
+    half = kept // 2
+    near = first_ref.shape[1]
+    pieces = (near + last_ref.shape[1]) // LANES
     group = 4
     for c in range(0, pieces, group):
-        part = jnp.dot(
-            picked,
-            out_weight_ref[:, c * LANES : (c + group) * LANES],
-            preferred_element_type=F32,
-        )
+        start = c * LANES
+        if start < near:
+            weight = first_ref[:, start : start + group * LANES]
+        else:
+            weight = last_ref[:, start - near : start - near + group * LANES]
+        part = jnp.dot(picked, weight, preferred_element_type=F32)
         for g in range(group):
             piece = part[:, g * LANES : (g + 1) * LANES]
-            keep_ref[pl.ds(c + g, kept // 2, stride=pieces), :] = piece[: kept // 2]
-            fold_ref[pl.ds(c + g, kept // 2, stride=pieces), :] = piece[kept // 2 :]
-    send_ref[...] = fold_ref[...].astype(BF16)
+            fold_ref[pl.ds(c + g, kept, stride=pieces + 1), :] = piece
+    for r in range(half):
+        rows = slice(r * pieces, (r + 1) * pieces)
+        start = r * (pieces + 1)
+        keep_ref[rows] = fold_ref[start : start + pieces]
+        start = (half + r) * (pieces + 1)
+        send_ref[rows] = fold_ref[start : start + pieces].astype(BF16)
 
 
 def state_kernel(
@@ -375,8 +391,10 @@
     rates_ref,
     state_ref,
     new_state_ref,
+    token_ref,
     low_ref,
 ):
+    token_ref[...] = jnp.zeros_like(token_ref)
     blocks = live_ref.shape[0]
     rows_dev = state_ref.shape[0] // blocks
     join_low(mine_ref, other_ref, low_ref)
@@ -399,8 +417,8 @@
             new_state_ref[b * rows_dev + t] = state_ref[b * rows_dev + t]
 
 
-def sum_kernel(count, *refs):
-    parts, outs = refs[:count], refs[count:]
+def sum_kernel(count, skipped, *refs):
+    parts, outs = refs[:count], refs[count + skipped :]
     size = outs[0].shape[0]
     for k, out in enumerate(outs):
         rows = slice(k * size, (k + 1) * size)
@@ -453,6 +471,20 @@
     pieces = width // LANES
     slab = LIVE_MAX * pieces
 
+    weight_shape = pltpu.VMEM(in_weight.shape, BF16)
+
+    def load(share, so_far=None):
+        return call(
+            functools.partial(load_kernel, share),
+            weight_shape,
+            (in_weight,),
+            far=1,
+            scratch=[pltpu.SemaphoreType.DMA((4,))],
+            limit=43,
+            after=() if so_far is None else (so_far,),
+            aliases={} if so_far is None else {1: 0},
+        )
+
     gathered = call(
         norm_kernel,
         pltpu.VMEM((slab, LANES), BF16),
@@ -466,9 +498,11 @@
         ],
         limit=60,
     )
-    near_weight = None
+    done, near_weight = 0.0, None
     for k, phase in enumerate(phases[:-1]):
-        near_weight = load(in_weight, 43, k, len(phases) - 1, near_weight)
+        until = 1.0 if k == len(phases) - 2 else done + (1.0 - done) * FIRST_SHARE
+        near_weight = load((done, until), near_weight)
+        done = until
         gathered = join(
             [gathered] + [swap(gathered, s, devices) for s in phase], (near_weight,)
         )
@@ -502,13 +536,13 @@
         scratch=[pltpu.VMEM((kept, low_width), F32)],
         limit=16,
     )
-    gate, new_conv = call(
-        gate_kernel,
-        (shape((kept, channels)), shape((TAPS - 1, rows, channels), BF16)),
-        (live_counts, both, spots, conv_turned, mixed_x),
+    gate = call(gate_kernel, shape((kept, channels)), (both, spots))
+    new_conv = call(
+        taps_kernel,
+        shape((TAPS - 1, rows, channels), BF16),
+        (live_counts, both, spots, conv_turned),
         scalars=1,
-        scratch=[pltpu.VMEM((rows, 128), F32)],
-        limit=16,
+        scratch=[pltpu.VMEM((rows, LANES), F32)],
     )
 
     packed_width = low_width + 2 * NSTATE
@@ -517,17 +551,26 @@
         return call(
             functools.partial(add_kernel, len(parts)),
             (shape(parts[0].shape), shape((kept // 2, packed_width), BF16)),
-            (*parts, *after),
-            far=len(after),
+            parts,
+            after=after,
         )
 
-    low, packed = add(keep, swap(send, 1, devices))
+    low, packed = add(keep, swap(send, 1, devices), after=(gate,))
     exchanges = sum_phases(devices)
+    first_columns = width * FIRST_COLUMNS // 16 if len(exchanges) > 1 else width // 2
+    near_out = [
+        call(
+            functools.partial(columns_kernel, start),
+            pltpu.VMEM((channels, count), BF16),
+            (out_weight,),
+            far=1,
+            scratch=[pltpu.SemaphoreType.DMA((4,))],
+            limit=50,
+        )
+        for start, count in ((0, first_columns), (first_columns, width - first_columns))
+    ]
     for k, phase in enumerate(exchanges):
-        after = (gate,)
-        if k == len(exchanges) - 1:
-            near_out = load(out_weight, 50)
-            after = (near_out,)
+        after = (near_out[0],) if k == 0 else (near_out[1],)
         low, packed = add(low, *[swap(packed, s, devices) for s in phase], after=after)
     other = swap(packed, 1, devices)
 
@@ -547,20 +590,20 @@
             log_rates,
             skip_gain.reshape(1, channels),
             ssm_state,
-            near_out,
+            *near_out,
         ),
         scalars=1,
         scratch=[
             pltpu.VMEM((kept, low_width), F32),
             pltpu.VMEM((kept, channels), F32),
             pltpu.VMEM((kept, 128), F32),
-            pltpu.VMEM((size, LANES), F32),
+            pltpu.VMEM((kept * (pieces + 1), LANES), F32),
         ],
-        limit=32,
-    )
-    new_state = call(
+        limit=24,
+    )
+    new_state, token = call(
         state_kernel,
-        shape(ssm_state.shape, BF16),
+        (shape(ssm_state.shape, BF16), shape((8, LANES))),
         (live_counts, low, other, mixed_x, step_size, log_rates, ssm_state),
         scalars=1,
         scratch=[pltpu.VMEM((kept, low_width), F32)],
@@ -568,12 +611,13 @@
     )
 
     total = (keep, swap(send, 1, devices))
-    for phase in scatter:
+    for k, phase in enumerate(scatter):
         size //= len(phase) + 1
         parts = call(
-            functools.partial(sum_kernel, len(total)),
+            functools.partial(sum_kernel, len(total), 1 if k == 1 else 0),
             (shape((size, LANES)),) + (shape((size, LANES), BF16),) * len(phase),
             total,
+            after=(token,) if k == 1 else (),
         )
         total = (parts[0],) + tuple(swap(p, s, devices) for p, s in zip(parts[1:], phase))
     mixed = call(

time: 57.7 us -> 56 us (0.971)
  waiting for transfers between devices: 13.3 us -> 10.2 us
  Pallas kernels: 21.6 us -> 22.4 us
  starting transfers between devices: 18.3 us -> 19 us
    pallas_call x15 -> x20, Pallas kernels: 11.1 us -> 22.4 us  [call(): pl.pallas_call(kernel, out_shape=outs, in_specs=[pl.BlockSpec(memory_spac...]
    pallas_call x3 -> x0, Pallas kernels: 10.5 us -> none  [load(): pl.pallas_call(functools.partial(load_kernel, start, size), out_shape=plt...]
    ppermute x16, waiting for transfers between devices: 13.3 us -> 10.2 us  [swap(): lax.ppermute(value, 'weight', [(i, i ^ shift) for i in range(devices)])]
    ppermute x16, starting transfers between devices: 18.3 us -> 19 us  [swap(): lax.ppermute(value, 'weight', [(i, i ^ shift) for i in range(devices)])]
  transfers between devices with their start and end apart: 16 -> 16, of which waited for: 11 -> 10; matrix products, arithmetic and copies ran while one was open for 0% -> 0% of each run, Pallas kernels for 25% -> 28%
where the time goes in v5:
time: 56 us; the launch traced here: 55.8 us
  Pallas kernels  22.4 us (40%)
  starting transfers between devices  19 us (34%)
  waiting for transfers between devices  10.2 us (18%)
  matrix products  3.15 us (6%)
  between operations  0.93 us (2%)
    pallas_call x20, Pallas kernels, call(): pl.pallas_call(kernel, out_shape=outs, in_specs=[pl.BlockSpec(memory_spac...  22.4 us
    ppermute x16, starting transfers between devices, swap(): lax.ppermute(value, 'weight', [(i, i ^ shift) for i in range(devices)])  19 us
    ppermute x16, waiting for transfers between devices, swap(): lax.ppermute(value, 'weight', [(i, i ^ shift) for i in range(devices)])  10.2 us
    dot_general x1, matrix products, body(): jnp.einsum('rd,dbc->brc', normed, near_weight, preferred_element_type=F32)  3.15 us
  transfers between devices with their start and end apart: 16, of which 10 were waited for; matrix products, arithmetic and copies ran while one was open for 0% of the time, Pallas kernels for 28%

profile of v5, /device:TPU:0, one launch (start us, length us, event | category | flops | bytes accessed | tf_op | source)
XLA Modules:
  0.0 55.8 jit_solution(5650590647295565111)
XLA Ops:
  0.6 1.1 %shard_map.177.refs_0_ = bf16[192,128]{1,0:T(8,128)(2,1)S(1)} custom-call(bf16[4,8192]{1,0:T(4,128)(2,1)} %refs_0_.1, f32[1,8192]{1,0:T(1,128)} %bitcast.19), custom_call_target="tpu_custom_call" | custom-call | tf_op jit(solution)/shard_map/pallas_call | solution.py:99
  1.7 4.1 %collective-permute-start = (bf16[192,128]{1,0:T(8,128)(2,1)S(1)}, bf16[192,128]{1,0:T(8,128)(2,1)S(1)}, u32[]{:S(2)}, u32[]{:S(2)}) collective-permute-start(bf16[192,128]{1,0:T(8,128)(2,1)S(1)} %shard_map.177.refs_0_), channel_id=1, source_target_pairs={{0,8},{1,9},{2,10},{3,11},{4,12},{5,13},{6,14},{7,15},{8,0},{9,1},... | collective-permute-start | bytes 147464 | tf_op jit(solution)/shard_map/ppermute | solution.py:78
  5.8 3.2 %shard_map.175.refs_0_.refs_2_ = bf16[8192,2,512]{2,1,0:T(2,128)(2,1)S(1)} custom-call(bf16[8192,2,512]{2,1,0:T(2,128)(2,1)} %far_ref.5), custom_call_target="tpu_custom_call" | custom-call | tf_op jit(solution)/shard_map/pallas_call | solution.py:99
  9.0 2.6 %collective-permute-start.1 = (bf16[384,128]{1,0:T(8,128)(2,1)S(1)}, bf16[384,128]{1,0:T(8,128)(2,1)S(1)}, u32[]{:S(2)}, u32[]{:S(2)}) collective-permute-start(bf16[384,128]{1,0:T(8,128)(2,1)S(1)} %shard_map.178.refs_0_), channel_id=1, source_target_pairs={{0,6},{1,7},{2,4},{3,5},{4,2},{5,3},{6,0},{7,1},{8,14},{9,15},{10,... | collective-permute-start | bytes 294920 | tf_op jit(solution)/shard_map/ppermute | solution.py:78
  11.6 0.4 collective-permute-start.2
  12.1 0.5 collective-permute-start.3
  12.6 3.8 %shard_map.176.refs_4_ = bf16[8192,2,512]{2,1,0:T(2,128)(2,1)S(1)} custom-call(bf16[8192,2,512]{2,1,0:T(2,128)(2,1)} %far_ref.5, bf16[8192,2,512]{2,1,0:T(2,128)(2,1)S(1)} %shard_map.175.refs_0_.refs_2_), custom_call_target="tpu_custom_call", output_to_operand_aliasing={{}: (1, {})} | custom-call | tf_op jit(solution)/shard_map/pallas_call | solution.py:99
  16.4 0.3 collective-permute-done.2.refs_2_
  16.7 0.1 collective-permute-done.3.refs_3_
  16.8 0.1 collective-permute-start.4
  16.9 0.5 shard_map.180.half_ref
  17.4 1.2 %collective-permute-done.4.other_ref = bf16[1536,128]{1,0:T(8,128)(2,1)S(1)} collective-permute-done((bf16[1536,128]{1,0:T(8,128)(2,1)S(1)}, bf16[1536,128]{1,0:T(8,128)(2,1)S(1)}, u32[]{:S(2)}, u32[]{:S(2)}) %collective-permute-start.4) | collective-permute-done | bytes 393248 | tf_op jit(solution)/shard_map/ppermute | solution.py:78
  18.6 0.6 %shard_map.181 = bf16[48,8192]{1,0:T(8,128)(2,1)S(1)} custom-call(f32[24,8192]{1,0:T(8,128)S(1)} %shard_map.180.half_ref, bf16[1536,128]{1,0:T(8,128)(2,1)S(1)} %collective-permute-done.4.other_ref), custom_call_target="tpu_custom_call" | custom-call | tf_op jit(solution)/shard_map/pallas_call | solution.py:99
  19.2 0.0 copy-start.1
  19.2 0.0 copy-start.7
  19.2 0.0 copy-start.8
  19.2 3.1 %fusion.2.both_ref = f32[2,48,512]{2,1,0:T(8,128)S(1)} fusion(bf16[8192,2,512]{2,1,0:T(2,128)(2,1)S(1)} %shard_map.176.refs_4_, bf16[48,8192]{1,0:T(8,128)(2,1)S(1)} %shard_map.181), kind=kOutput, calls=%fused_computation.2 | convolution fusion | flops 805306368 | bytes 17760256 | tf_op jit(solution)/shard_map/rd,dbc->brc/dot_general | solution.py:518
  22.4 0.0 copy-done.1
  22.4 0.5 shard_map.182
  23.0 0.2 collective-permute-start.5
  23.2 0.2 shard_map.183.refs_2_.gate_ref
  23.4 0.9 %collective-permute-done.5.refs_1_ = f32[24,544]{1,0:T(8,128)S(1)} collective-permute-done((f32[24,544]{1,0:T(8,128)S(1)}, f32[24,544]{1,0:T(8,128)S(1)}, u32[]{:S(2)}, u32[]{:S(2)}) %collective-permute-start.5) | collective-permute-done | bytes 52256 | tf_op jit(solution)/shard_map/ppermute | solution.py:78
  24.3 0.1 shard_map.184
  24.4 0.0 copy-start.6
  24.4 1.6 %collective-permute-start.6 = (bf16[24,576]{1,0:T(8,128)(2,1)S(1)}, bf16[24,576]{1,0:T(8,128)(2,1)S(1)}, u32[]{:S(2)}, u32[]{:S(2)}) collective-permute-start(bf16[24,576]{1,0:T(8,128)(2,1)S(1)} %get-tuple-element.26), channel_id=1, source_target_pairs={{0,9},{1,8},{2,11},{3,10},{4,13},{5,12},{6,15},{7,14},{8,1},{9,0},... | collective-permute-start | bytes 82952 | tf_op jit(solution)/shard_map/ppermute | solution.py:78
  26.0 1.7 %shard_map.185.refs_2_.first_ref = bf16[512,2560]{1,0:T(8,128)(2,1)S(1)} custom-call(bf16[512,8192]{1,0:T(8,128)(2,1)} %far_ref.7), custom_call_target="tpu_custom_call" | custom-call | tf_op jit(solution)/shard_map/pallas_call | solution.py:99
  27.7 1.0 %collective-permute-done.6.refs_1_ = bf16[24,576]{1,0:T(8,128)(2,1)S(1)} collective-permute-done((bf16[24,576]{1,0:T(8,128)(2,1)S(1)}, bf16[24,576]{1,0:T(8,128)(2,1)S(1)}, u32[]{:S(2)}, u32[]{:S(2)}) %collective-permute-start.6) | collective-permute-done | bytes 27680 | tf_op jit(solution)/shard_map/ppermute | solution.py:78
  28.7 0.2 shard_map.186
  28.9 0.9 %collective-permute-start.7 = (bf16[24,576]{1,0:T(8,128)(2,1)S(1)}, bf16[24,576]{1,0:T(8,128)(2,1)S(1)}, u32[]{:S(2)}, u32[]{:S(2)}) collective-permute-start(bf16[24,576]{1,0:T(8,128)(2,1)S(1)} %get-tuple-element.28), channel_id=1, source_target_pairs={{0,3},{1,2},{2,1},{3,0},{4,7},{5,6},{6,5},{7,4},{8,11},{9,10},{10,... | collective-permute-start | bytes 82952 | tf_op jit(solution)/shard_map/ppermute | solution.py:78
  29.8 1.5 %collective-permute-start.8 = (bf16[24,576]{1,0:T(8,128)(2,1)S(1)}, bf16[24,576]{1,0:T(8,128)(2,1)S(1)}, u32[]{:S(2)}, u32[]{:S(2)}) collective-permute-start(bf16[24,576]{1,0:T(8,128)(2,1)S(1)} %get-tuple-element.28), channel_id=1, source_target_pairs={{0,5},{1,4},{2,7},{3,6},{4,1},{5,0},{6,3},{7,2},{8,13},{9,12},{10,... | collective-permute-start | bytes 82952 | tf_op jit(solution)/shard_map/ppermute | solution.py:78
  31.3 0.7 %collective-permute-start.9 = (bf16[24,576]{1,0:T(8,128)(2,1)S(1)}, bf16[24,576]{1,0:T(8,128)(2,1)S(1)}, u32[]{:S(2)}, u32[]{:S(2)}) collective-permute-start(bf16[24,576]{1,0:T(8,128)(2,1)S(1)} %get-tuple-element.28), channel_id=1, source_target_pairs={{0,6},{1,7},{2,4},{3,5},{4,2},{5,3},{6,0},{7,1},{8,14},{9,15},{10,... | collective-permute-start | bytes 82952 | tf_op jit(solution)/shard_map/ppermute | solution.py:78
  32.1 2.7 %shard_map.187.refs_4_.last_ref = bf16[512,5632]{1,0:T(8,128)(2,1)S(1)} custom-call(bf16[512,8192]{1,0:T(8,128)(2,1)} %far_ref.7), custom_call_target="tpu_custom_call" | custom-call | tf_op jit(solution)/shard_map/pallas_call | solution.py:99
  34.8 1.3 %collective-permute-done.9.refs_3_ = bf16[24,576]{1,0:T(8,128)(2,1)S(1)} collective-permute-done((bf16[24,576]{1,0:T(8,128)(2,1)S(1)}, bf16[24,576]{1,0:T(8,128)(2,1)S(1)}, u32[]{:S(2)}, u32[]{:S(2)}) %collective-permute-start.9) | collective-permute-done | bytes 27680 | tf_op jit(solution)/shard_map/ppermute | solution.py:78
  36.1 0.2 shard_map.188
  36.3 1.2 %collective-permute-done.10.other_ref = bf16[24,576]{1,0:T(8,128)(2,1)S(1)} collective-permute-done((bf16[24,576]{1,0:T(8,128)(2,1)S(1)}, bf16[24,576]{1,0:T(8,128)(2,1)S(1)}, u32[]{:S(2)}, u32[]{:S(2)}) %collective-permute-start.10) | collective-permute-done | bytes 27680 | tf_op jit(solution)/shard_map/ppermute | solution.py:78
  37.6 3.2 %shard_map.189 = (f32[1536,128]{1,0:T(8,128)S(1)}, bf16[1536,128]{1,0:T(8,128)(2,1)S(1)}, f32[48,512]{1,0:T(8,128)S(1)}) custom-call(s32[16]{0:T(128)S(1)} %copy-done.9, f32[24,544]{1,0:T(8,128)S(1)} %get-tuple-element.29.mine_ref, bf16[24,576]{1,0:T(8,128)(2,1)S(1)} %collective-permute-done.10.other_ref, s32[48,2]{1,0:T(8,128)S(1)} %copy-done.6, ...), custom_call_target="tpu_custom_call" | custom-call | tf_op jit(solution)/shard_map/pallas_call | solution.py:99
  40.8 0.2 collective-permute-start.11
  41.0 1.6 %collective-permute-done.11.refs_1_ = bf16[1536,128]{1,0:T(8,128)(2,1)S(1)} collective-permute-done((bf16[1536,128]{1,0:T(8,128)(2,1)S(1)}, bf16[1536,128]{1,0:T(8,128)(2,1)S(1)}, u32[]{:S(2)}, u32[]{:S(2)}) %collective-permute-start.11) | collective-permute-done | bytes 393248 | tf_op jit(solution)/shard_map/ppermute | solution.py:78
  42.6 0.1 shard_map.190
  42.6 0.5 collective-permute-start.12
  43.2 1.0 %collective-permute-start.13 = (bf16[384,128]{1,0:T(8,128)(2,1)S(1)}, bf16[384,128]{1,0:T(8,128)(2,1)S(1)}, u32[]{:S(2)}, u32[]{:S(2)}) collective-permute-start(bf16[384,128]{1,0:T(8,128)(2,1)S(1)} %get-tuple-element.36), channel_id=1, source_target_pairs={{0,2},{1,3},{2,0},{3,1},{4,6},{5,7},{6,4},{7,5},{8,10},{9,11},{10,... | collective-permute-start | bytes 294920 | tf_op jit(solution)/shard_map/ppermute | solution.py:78
  44.1 2.1 %collective-permute-start.14 = (bf16[384,128]{1,0:T(8,128)(2,1)S(1)}, bf16[384,128]{1,0:T(8,128)(2,1)S(1)}, u32[]{:S(2)}, u32[]{:S(2)}) collective-permute-start(bf16[384,128]{1,0:T(8,128)(2,1)S(1)} %get-tuple-element.37), channel_id=1, source_target_pairs={{0,6},{1,7},{2,4},{3,5},{4,2},{5,3},{6,0},{7,1},{8,14},{9,15},{10,... | collective-permute-start | bytes 294920 | tf_op jit(solution)/shard_map/ppermute | solution.py:78
  46.2 2.2 %shard_map.191 = (bf16[64,16,512]{2,1,0:T(8,128)(2,1)}, f32[8,128]{1,0:T(8,128)S(1)}) custom-call(s32[16]{0:T(128)S(1)} %copy-done.9, f32[24,544]{1,0:T(8,128)S(1)} %get-tuple-element.29.mine_ref, bf16[24,576]{1,0:T(8,128)(2,1)S(1)} %collective-permute-done.10.other_ref, bf16[48,512]{1,0:T(8,128)(2,1)S(1)} %get-tuple-element.31.mixed_ref, ...), custom_call_target="tpu_custom_call" | custom-call | tf_op jit(solution)/shard_map/pallas_call | solution.py:99
  48.4 1.6 %collective-permute-done.14.refs_3_ = bf16[384,128]{1,0:T(8,128)(2,1)S(1)} collective-permute-done((bf16[384,128]{1,0:T(8,128)(2,1)S(1)}, bf16[384,128]{1,0:T(8,128)(2,1)S(1)}, u32[]{:S(2)}, u32[]{:S(2)}) %collective-permute-start.14) | collective-permute-done | bytes 98336 | tf_op jit(solution)/shard_map/ppermute | solution.py:78
  50.0 2.5 %collective-permute-start.15 = (bf16[192,128]{1,0:T(8,128)(2,1)S(1)}, bf16[192,128]{1,0:T(8,128)(2,1)S(1)}, u32[]{:S(2)}, u32[]{:S(2)}) collective-permute-start(bf16[192,128]{1,0:T(8,128)(2,1)S(1)} %get-tuple-element.41), channel_id=1, source_target_pairs={{0,8},{1,9},{2,10},{3,11},{4,12},{5,13},{6,14},{7,15},{8,0},{9,1},... | collective-permute-start | bytes 147464 | tf_op jit(solution)/shard_map/ppermute | solution.py:78
  52.6 1.4 %shard_map.194 = bf16[3,64,512]{2,1,0:T(8,128)(2,1)} custom-call(s32[16]{0:T(128)S(1)} %copy-done.9, f32[2,48,512]{2,1,0:T(8,128)S(1)} %fusion.2.both_ref, s32[2,48]{1,0:T(2,128)S(1)} %copy-done.7, bf16[3,64,512]{2,1,0:T(8,128)(2,1)S(1)} %bitcast.13), custom_call_target="tpu_custom_call" | custom-call | tf_op jit(solution)/shard_map/pallas_call | solution.py:99
  53.9 1.1 %collective-permute-done.15.refs_2_ = bf16[192,128]{1,0:T(8,128)(2,1)S(1)} collective-permute-done((bf16[192,128]{1,0:T(8,128)(2,1)S(1)}, bf16[192,128]{1,0:T(8,128)(2,1)S(1)}, u32[]{:S(2)}, u32[]{:S(2)}) %collective-permute-start.15) | collective-permute-done | bytes 49184 | tf_op jit(solution)/shard_map/ppermute | solution.py:78
  55.1 0.7 %shard_map.193 = bf16[4,8192]{1,0:T(4,128)(2,1)} custom-call(bf16[4,8192]{1,0:T(4,128)(2,1)S(1)} %copy-done.4, f32[192,128]{1,0:T(8,128)S(1)} %get-tuple-element.40.refs_1_, bf16[192,128]{1,0:T(8,128)(2,1)S(1)} %collective-permute-done.15.refs_2_), custom_call_target="tpu_custom_call" | custom-call | tf_op jit(solution)/shard_map/pallas_call | solution.py:99
  (31 shorter events, 0.2 us)
Async XLA Ops:
  1.7 7.3 %collective-permute-start = (bf16[192,128]{1,0:T(8,128)(2,1)S(1)}, bf16[192,128]{1,0:T(8,128)(2,1)S(1)}, u32[]{:S(2)}, u32[]{:S(2)}) collective-permute-start(bf16[192,128]{1,0:T(8,128)(2,1)S(1)} %shard_map.177.refs_0_), channel_id=1, source_target_pairs={{0,8},{1,9},{2,10},{3,11},{4,12},{5,13},{6,14},{7,15},{8,0},{9,1},... | collective-permute-start | bytes 147464 | tf_op jit(solution)/shard_map/ppermute | solution.py:78
  9.0 7.4 %collective-permute-start.1 = (bf16[384,128]{1,0:T(8,128)(2,1)S(1)}, bf16[384,128]{1,0:T(8,128)(2,1)S(1)}, u32[]{:S(2)}, u32[]{:S(2)}) collective-permute-start(bf16[384,128]{1,0:T(8,128)(2,1)S(1)} %shard_map.178.refs_0_), channel_id=1, source_target_pairs={{0,6},{1,7},{2,4},{3,5},{4,2},{5,3},{6,0},{7,1},{8,14},{9,15},{10,... | collective-permute-start | bytes 294920 | tf_op jit(solution)/shard_map/ppermute | solution.py:78
  11.6 5.0 %collective-permute-start.2 = (bf16[384,128]{1,0:T(8,128)(2,1)S(1)}, bf16[384,128]{1,0:T(8,128)(2,1)S(1)}, u32[]{:S(2)}, u32[]{:S(2)}) collective-permute-start(bf16[384,128]{1,0:T(8,128)(2,1)S(1)} %shard_map.178.refs_0_), channel_id=1, source_target_pairs={{0,4},{1,5},{2,6},{3,7},{4,0},{5,1},{6,2},{7,3},{8,12},{9,13},{10,... | collective-permute-start | bytes 294920 | tf_op jit(solution)/shard_map/ppermute | solution.py:78
  12.1 4.7 %collective-permute-start.3 = (bf16[384,128]{1,0:T(8,128)(2,1)S(1)}, bf16[384,128]{1,0:T(8,128)(2,1)S(1)}, u32[]{:S(2)}, u32[]{:S(2)}) collective-permute-start(bf16[384,128]{1,0:T(8,128)(2,1)S(1)} %shard_map.178.refs_0_), channel_id=1, source_target_pairs={{0,2},{1,3},{2,0},{3,1},{4,6},{5,7},{6,4},{7,5},{8,10},{9,11},{10,... | collective-permute-start | bytes 294920 | tf_op jit(solution)/shard_map/ppermute | solution.py:78
  16.8 1.8 %collective-permute-start.4 = (bf16[1536,128]{1,0:T(8,128)(2,1)S(1)}, bf16[1536,128]{1,0:T(8,128)(2,1)S(1)}, u32[]{:S(2)}, u32[]{:S(2)}) collective-permute-start(bf16[1536,128]{1,0:T(8,128)(2,1)S(1)} %shard_map.179.mine_ref), channel_id=1, source_target_pairs={{0,1},{1,0},{2,3},{3,2},{4,5},{5,4},{6,7},{7,6},{8,9},{9,8},{10,11... | collective-permute-start | bytes 1179656 | tf_op jit(solution)/shard_map/ppermute | solution.py:78
  19.2 3.2 %copy-start.1 = (bf16[64,3,512]{2,0,1:T(8,128)(2,1)S(1)}, bf16[64,3,512]{2,0,1:T(8,128)(2,1)}, u32[]{:S(2)}) copy-start(bf16[64,3,512]{2,0,1:T(8,128)(2,1)} %param.28) | copy-start | bytes 589828
  19.2 3.2 %copy-start.2 = (bf16[512,544]{0,1:T(8,128)(2,1)S(1)}, bf16[512,544]{0,1:T(8,128)(2,1)}, u32[]{:S(2)}) copy-start(bf16[512,544]{0,1:T(8,128)(2,1)} %param.21) | copy-start | bytes 1671172
  19.2 3.2 %copy-start.7 = (s32[2,48]{1,0:T(2,128)S(1)}, s32[2,48]{1,0:T(2,128)}, u32[]{:S(2)}) copy-start(s32[2,48]{1,0:T(2,128)} %constant.4.clone.spot_ref) | copy-start | bytes 1156
  19.2 3.2 %copy-start.8 = (f32[4,512]{1,0:T(4,128)S(1)}, f32[4,512]{1,0:T(4,128)}, u32[]{:S(2)}) copy-start(f32[4,512]{1,0:T(4,128)} %taps_ref.1) | copy-start | bytes 24580
  19.2 3.2 %copy-start.10 = (f32[512]{0:T(512)S(1)}, f32[512]{0:T(512)}, u32[]{:S(2)}) copy-start(f32[512]{0:T(512)} %param.20) | copy-start | bytes 6148
  23.0 1.3 %collective-permute-start.5 = (f32[24,544]{1,0:T(8,128)S(1)}, f32[24,544]{1,0:T(8,128)S(1)}, u32[]{:S(2)}, u32[]{:S(2)}) collective-permute-start(f32[24,544]{1,0:T(8,128)S(1)} %get-tuple-element.24), channel_id=1, source_target_pairs={{0,1},{1,0},{2,3},{3,2},{4,5},{5,4},{6,7},{7,6},{8,9},{9,8},{10,11... | collective-permute-start | bytes 156680 | tf_op jit(solution)/shard_map/ppermute | solution.py:78
  24.4 13.1 %copy-start = (bf16[64,16,512]{2,1,0:T(8,128)(2,1)S(1)}, bf16[64,16,512]{2,1,0:T(8,128)(2,1)}, u32[]{:S(2)}) copy-start(bf16[64,16,512]{2,1,0:T(8,128)(2,1)} %state_ref.3) | copy-start | bytes 3145732
  24.4 13.1 %copy-start.3 = (bf16[512,512]{1,0:T(8,128)(2,1)S(1)}, bf16[512,512]{1,0:T(8,128)(2,1)}, u32[]{:S(2)}) copy-start(bf16[512,512]{1,0:T(8,128)(2,1)} %step_weight_ref.1) | copy-start | bytes 1572868
  24.4 13.1 %copy-start.5 = (f32[16,512]{1,0:T(8,128)S(1)}, f32[16,512]{1,0:T(8,128)}, u32[]{:S(2)}) copy-start(f32[16,512]{1,0:T(8,128)} %rates_ref.3) | copy-start | bytes 98308
  24.4 13.1 %copy-start.6 = (s32[48,2]{1,0:T(8,128)S(1)}, s32[48,2]{1,0:T(8,128)}, u32[]{:S(2)}) copy-start(s32[48,2]{1,0:T(8,128)} %constant.7.spot_ref) | copy-start | bytes 1156
  24.4 13.1 %copy-start.9 = (s32[16]{0:T(128)S(1)}, s32[16]{0:T(128)}, u32[]{:S(2)}) copy-start(s32[16]{0:T(128)} %live_ref.5) | copy-start | bytes 196
  24.4 13.1 %copy-start.11 = (f32[512]{0:T(512)S(1)}, f32[512]{0:T(512)}, u32[]{:S(2)}) copy-start(f32[512]{0:T(512)} %param.23) | copy-start | bytes 6148
  24.4 13.1 %copy-start.12 = (f32[512]{0:T(512)S(1)}, f32[512]{0:T(512)}, u32[]{:S(2)}) copy-start(f32[512]{0:T(512)} %param.25) | copy-start | bytes 6148
  24.4 4.3 %collective-permute-start.6 = (bf16[24,576]{1,0:T(8,128)(2,1)S(1)}, bf16[24,576]{1,0:T(8,128)(2,1)S(1)}, u32[]{:S(2)}, u32[]{:S(2)}) collective-permute-start(bf16[24,576]{1,0:T(8,128)(2,1)S(1)} %get-tuple-element.26), channel_id=1, source_target_pairs={{0,9},{1,8},{2,11},{3,10},{4,13},{5,12},{6,15},{7,14},{8,1},{9,0},... | collective-permute-start | bytes 82952 | tf_op jit(solution)/shard_map/ppermute | solution.py:78
  28.9 26.2 %copy-start.4 = (bf16[4,8192]{1,0:T(4,128)(2,1)S(1)}, bf16[4,8192]{1,0:T(4,128)(2,1)}, u32[]{:S(2)}) copy-start(bf16[4,8192]{1,0:T(4,128)(2,1)} %refs_0_.1) | copy-start | bytes 196612
  28.9 5.9 %collective-permute-start.7 = (bf16[24,576]{1,0:T(8,128)(2,1)S(1)}, bf16[24,576]{1,0:T(8,128)(2,1)S(1)}, u32[]{:S(2)}, u32[]{:S(2)}) collective-permute-start(bf16[24,576]{1,0:T(8,128)(2,1)S(1)} %get-tuple-element.28), channel_id=1, source_target_pairs={{0,3},{1,2},{2,1},{3,0},{4,7},{5,6},{6,5},{7,4},{8,11},{9,10},{10,... | collective-permute-start | bytes 82952 | tf_op jit(solution)/shard_map/ppermute | solution.py:78
  29.8 5.0 %collective-permute-start.8 = (bf16[24,576]{1,0:T(8,128)(2,1)S(1)}, bf16[24,576]{1,0:T(8,128)(2,1)S(1)}, u32[]{:S(2)}, u32[]{:S(2)}) collective-permute-start(bf16[24,576]{1,0:T(8,128)(2,1)S(1)} %get-tuple-element.28), channel_id=1, source_target_pairs={{0,5},{1,4},{2,7},{3,6},{4,1},{5,0},{6,3},{7,2},{8,13},{9,12},{10,... | collective-permute-start | bytes 82952 | tf_op jit(solution)/shard_map/ppermute | solution.py:78
  31.3 4.8 %collective-permute-start.9 = (bf16[24,576]{1,0:T(8,128)(2,1)S(1)}, bf16[24,576]{1,0:T(8,128)(2,1)S(1)}, u32[]{:S(2)}, u32[]{:S(2)}) collective-permute-start(bf16[24,576]{1,0:T(8,128)(2,1)S(1)} %get-tuple-element.28), channel_id=1, source_target_pairs={{0,6},{1,7},{2,4},{3,5},{4,2},{5,3},{6,0},{7,1},{8,14},{9,15},{10,... | collective-permute-start | bytes 82952 | tf_op jit(solution)/shard_map/ppermute | solution.py:78
  36.3 1.2 %collective-permute-start.10 = (bf16[24,576]{1,0:T(8,128)(2,1)S(1)}, bf16[24,576]{1,0:T(8,128)(2,1)S(1)}, u32[]{:S(2)}, u32[]{:S(2)}) collective-permute-start(bf16[24,576]{1,0:T(8,128)(2,1)S(1)} %get-tuple-element.30), channel_id=1, source_target_pairs={{0,1},{1,0},{2,3},{3,2},{4,5},{5,4},{6,7},{7,6},{8,9},{9,8},{10,11... | collective-permute-start | bytes 82952 | tf_op jit(solution)/shard_map/ppermute | solution.py:78
  40.8 1.8 %collective-permute-start.11 = (bf16[1536,128]{1,0:T(8,128)(2,1)S(1)}, bf16[1536,128]{1,0:T(8,128)(2,1)S(1)}, u32[]{:S(2)}, u32[]{:S(2)}) collective-permute-start(bf16[1536,128]{1,0:T(8,128)(2,1)S(1)} %get-tuple-element.33), channel_id=1, source_target_pairs={{0,1},{1,0},{2,3},{3,2},{4,5},{5,4},{6,7},{7,6},{8,9},{9,8},{10,11... | collective-permute-start | bytes 1179656 | tf_op jit(solution)/shard_map/ppermute | solution.py:78
  42.6 5.8 %collective-permute-start.12 = (bf16[384,128]{1,0:T(8,128)(2,1)S(1)}, bf16[384,128]{1,0:T(8,128)(2,1)S(1)}, u32[]{:S(2)}, u32[]{:S(2)}) collective-permute-start(bf16[384,128]{1,0:T(8,128)(2,1)S(1)} %get-tuple-element.35), channel_id=1, source_target_pairs={{0,4},{1,5},{2,6},{3,7},{4,0},{5,1},{6,2},{7,3},{8,12},{9,13},{10,... | collective-permute-start | bytes 294920 | tf_op jit(solution)/shard_map/ppermute | solution.py:78
  43.2 5.3 %collective-permute-start.13 = (bf16[384,128]{1,0:T(8,128)(2,1)S(1)}, bf16[384,128]{1,0:T(8,128)(2,1)S(1)}, u32[]{:S(2)}, u32[]{:S(2)}) collective-permute-start(bf16[384,128]{1,0:T(8,128)(2,1)S(1)} %get-tuple-element.36), channel_id=1, source_target_pairs={{0,2},{1,3},{2,0},{3,1},{4,6},{5,7},{6,4},{7,5},{8,10},{9,11},{10,... | collective-permute-start | bytes 294920 | tf_op jit(solution)/shard_map/ppermute | solution.py:78
  44.1 5.8 %collective-permute-start.14 = (bf16[384,128]{1,0:T(8,128)(2,1)S(1)}, bf16[384,128]{1,0:T(8,128)(2,1)S(1)}, u32[]{:S(2)}, u32[]{:S(2)}) collective-permute-start(bf16[384,128]{1,0:T(8,128)(2,1)S(1)} %get-tuple-element.37), channel_id=1, source_target_pairs={{0,6},{1,7},{2,4},{3,5},{4,2},{5,3},{6,0},{7,1},{8,14},{9,15},{10,... | collective-permute-start | bytes 294920 | tf_op jit(solution)/shard_map/ppermute | solution.py:78
  50.0 5.1 %collective-permute-start.15 = (bf16[192,128]{1,0:T(8,128)(2,1)S(1)}, bf16[192,128]{1,0:T(8,128)(2,1)S(1)}, u32[]{:S(2)}, u32[]{:S(2)}) collective-permute-start(bf16[192,128]{1,0:T(8,128)(2,1)S(1)} %get-tuple-element.41), channel_id=1, source_target_pairs={{0,8},{1,9},{2,10},{3,11},{4,12},{5,13},{6,14},{7,15},{8,0},{9,1},... | collective-permute-start | bytes 147464 | tf_op jit(solution)/shard_map/ppermute | solution.py:78

commit v6 on v5

--- a/solution.py
+++ b/solution.py
@@ -13,7 +13,8 @@
 TAPS = 4
 LANES = 128
 MIB = 1024 * 1024
-FIRST_SHARE = 0.4375
+CORE_SHARE = 0.9375
+FIRST_SHARE = 0.4
 FIRST_COLUMNS = 5
 BF16 = jnp.bfloat16
 F32 = jnp.float32
@@ -131,10 +132,24 @@
         copy.wait()
 
 
-def fold(wide, folded_ref):
+def fold(wide, fold_ref, folded_ref):
     rows, pieces = wide.shape[0], wide.shape[1] // LANES
     for c in range(pieces):
-        folded_ref[pl.ds(c, rows, stride=pieces), :] = wide[:, c * LANES : (c + 1) * LANES]
+        fold_ref[pl.ds(c, rows, stride=pieces + 1), :] = wide[:, c * LANES : (c + 1) * LANES]
+    for r in range(rows):
+        start = r * (pieces + 1)
+        folded_ref[r * pieces : (r + 1) * pieces] = fold_ref[start : start + pieces].astype(
+            folded_ref.dtype
+        )
+
+
+def spread(folded, fold_ref):
+    rows = fold_ref.shape[0] - folded.shape[0]
+    pieces = folded.shape[0] // rows
+    for r in range(rows):
+        start = r * (pieces + 1)
+        fold_ref[start : start + pieces] = folded[r * pieces : (r + 1) * pieces].astype(F32)
+    return rows, pieces
 
 
 def norm_kernel(far_hidden_ref, far_gain_ref, out_ref, fold_ref, hidden_ref, gain_ref, sems):
@@ -146,8 +161,7 @@
     wait_all(copies)
     wide = hidden_ref[...].astype(F32)[:LIVE_MAX]
     factor = lax.rsqrt(jnp.mean(wide * wide, axis=-1, keepdims=True) + 1e-05)
-    fold(wide * factor * gain_ref[...], fold_ref)
-    out_ref[...] = fold_ref[...].astype(BF16)
+    fold(wide * factor * gain_ref[...], fold_ref, out_ref)
 
 
 def join_kernel(count, *refs):
@@ -168,18 +182,16 @@
 
 
 def half_kernel(mine_ref, out_ref, fold_ref):
-    fold_ref[...] = mine_ref[...].astype(F32)
-    rows, pieces = out_ref.shape[0], out_ref.shape[1] // LANES
+    rows, pieces = spread(mine_ref, fold_ref)
     for c in range(pieces):
-        out_ref[:, c * LANES : (c + 1) * LANES] = fold_ref[pl.ds(c, rows, stride=pieces), :]
-
-
-def unfold_kernel(half_ref, other_ref, out_ref, fold_ref):
-    fold_ref[...] = other_ref[...].astype(F32)
-    rows, pieces = half_ref.shape[0], out_ref.shape[1] // LANES
+        out_ref[:, c * LANES : (c + 1) * LANES] = fold_ref[pl.ds(c, rows, stride=pieces + 1), :]
+
+
+def unfold_kernel(half_ref, other_ref, _, out_ref, fold_ref):
+    rows, pieces = spread(other_ref, fold_ref)
     for c in range(pieces):
         span = slice(c * LANES, (c + 1) * LANES)
-        other = fold_ref[pl.ds(c, rows, stride=pieces), :]
+        other = fold_ref[pl.ds(c, rows, stride=pieces + 1), :]
         out_ref[:, span] = jnp.concatenate([half_ref[:, span], other], axis=0).astype(BF16)
 
 
@@ -271,7 +283,13 @@
     send_ref[...] = low_ref[pl.ds(pl.multiple_of((1 - core) * half, 8), half), :]
 
 
-def gate_kernel(both_ref, spot_ref, gate_ref):
+def gate_kernel(live_ref, both_ref, spot_ref, gate_ref, alive_ref):
+    for b in range(live_ref.shape[0]):
+        for t in range(LIVE_MAX):
+            r = b * LIVE_MAX + t
+            alive_ref[r : r + 1, :] = jnp.full(
+                (1, LANES), jnp.where(t < live_ref[b], 1.0, 0.0)
+            )
     block = jnp.bitwise_xor(spot_ref[0:1, :], lax.axis_index("weight"))
     gate_ref[...] = jnp.dot(
         places(block, spot_ref[1:2, :], gate_ref.shape[0], LIVE_MAX),
@@ -306,12 +324,12 @@
 
 
 def readout_kernel(
-    live_ref,
     mine_ref,
     other_ref,
     spot_ref,
     mixed_ref,
     gate_ref,
+    alive_ref,
     step_weight_ref,
     bias_ref,
     rates_ref,
@@ -324,12 +342,11 @@
     step_ref,
     low_ref,
     read_ref,
-    alive_ref,
     fold_ref,
 ):
-    blocks = live_ref.shape[0]
+    kept = mixed_ref.shape[0]
+    blocks = kept // LIVE_MAX
     rows_dev = state_ref.shape[0] // blocks
-    kept = mixed_ref.shape[0]
     join_low(mine_ref, other_ref, low_ref)
     step_size = softplus(
         jnp.dot(
@@ -350,9 +367,6 @@
             decayed = jnp.exp(step_size[r : r + 1, :] * rates) * wide
             read_ref[r : r + 1, :] = jnp.sum(
                 out_coefs[:, r : r + 1] * decayed, axis=0, keepdims=True
-            )
-            alive_ref[r : r + 1, :] = jnp.full(
-                (1, 128), jnp.where(t < live_ref[b], 1.0, 0.0)
             )
     readout = read_ref[...] + (both_coefs * step_size + skip_ref[...]) * x_wide
     gated = jnp.where(alive_ref[:, 0:1] > 0.0, readout * gate_ref[...], 0.0).astype(BF16)
@@ -433,13 +447,12 @@
     total = parts[0][...]
     for part in parts[1:]:
         total = total + part[...].astype(F32)
-    fold_ref[...] = total
-    pieces = out_ref.shape[1] // LANES
+    rows, pieces = spread(total, fold_ref)
     for c in range(pieces):
         span = slice(c * LANES, (c + 1) * LANES)
         wide = hidden_ref[:, span].astype(F32)
-        own = wide[:LIVE_MAX] + fold_ref[pl.ds(c, LIVE_MAX, stride=pieces), :]
-        out_ref[:, span] = jnp.concatenate([own, wide[LIVE_MAX:]], axis=0).astype(BF16)
+        own = wide[:rows] + fold_ref[pl.ds(c, rows, stride=pieces + 1), :]
+        out_ref[:, span] = jnp.concatenate([own, wide[rows:]], axis=0).astype(BF16)
 
 
 def body(
@@ -491,7 +504,7 @@
         (hidden, norm_gain.reshape(1, width)),
         far=2,
         scratch=[
-            pltpu.VMEM((slab, LANES), F32),
+            pltpu.VMEM((slab + LIVE_MAX, LANES), F32),
             pltpu.VMEM(hidden.shape, BF16),
             pltpu.VMEM((1, width), F32),
             pltpu.SemaphoreType.DMA((2,)),
@@ -500,13 +513,14 @@
     )
     done, near_weight = 0.0, None
     for k, phase in enumerate(phases[:-1]):
-        until = 1.0 if k == len(phases) - 2 else done + (1.0 - done) * FIRST_SHARE
+        until = CORE_SHARE if k == len(phases) - 2 else done + (CORE_SHARE - done) * FIRST_SHARE
         near_weight = load((done, until), near_weight)
         done = until
         gathered = join(
             [gathered] + [swap(gathered, s, devices) for s in phase], (near_weight,)
         )
-    folded = [pltpu.VMEM((kept // 2 * pieces, LANES), F32)]
+    near_weight = load((done, 1.0), near_weight)
+    folded = [pltpu.VMEM((kept // 2 * (pieces + 1), LANES), F32)]
     half = call(half_kernel, shape((kept // 2, width)), (gathered,), scratch=folded, limit=12)
     normed = call(
         unfold_kernel,
@@ -514,6 +528,7 @@
         (half, swap(gathered, 1, devices)),
         scratch=folded,
         limit=12,
+        after=(near_weight,),
     )
     both = jnp.einsum("rd,dbc->brc", normed, near_weight, preferred_element_type=F32)
 
@@ -536,7 +551,12 @@
         scratch=[pltpu.VMEM((kept, low_width), F32)],
         limit=16,
     )
-    gate = call(gate_kernel, shape((kept, channels)), (both, spots))
+    gate, alive = call(
+        gate_kernel,
+        (shape((kept, channels)), shape((kept, LANES))),
+        (live_counts, both, spots),
+        scalars=1,
+    )
     new_conv = call(
         taps_kernel,
         shape((TAPS - 1, rows, channels), BF16),
@@ -579,12 +599,12 @@
         readout_kernel,
         (shape((size, LANES)), shape((size, LANES), BF16), shape((kept, channels))),
         (
-            live_counts,
             low,
             other,
             ends,
             mixed_x,
             gate,
+            alive,
             step_weight,
             step_bias.reshape(1, channels),
             log_rates,
@@ -592,11 +612,9 @@
             ssm_state,
             *near_out,
         ),
-        scalars=1,
         scratch=[
             pltpu.VMEM((kept, low_width), F32),
             pltpu.VMEM((kept, channels), F32),
-            pltpu.VMEM((kept, 128), F32),
             pltpu.VMEM((kept * (pieces + 1), LANES), F32),
         ],
         limit=24,
@@ -624,7 +642,7 @@
         last_sum_kernel,
         shape(hidden.shape, BF16),
         (hidden,) + total,
-        scratch=[pltpu.VMEM((slab, LANES), F32)],
+        scratch=[pltpu.VMEM((slab + LIVE_MAX, LANES), F32)],
     )
     return (mixed, new_state, new_conv.transpose(1, 0, 2))
 

time: 56 us -> 54.7 us (0.977)
  waiting for transfers between devices: 10.2 us -> 8.18 us
  starting transfers between devices: 19 us -> 19.7 us
    ppermute x16, waiting for transfers between devices: 10.2 us -> 8.18 us  [swap(): lax.ppermute(value, 'weight', [(i, i ^ shift) for i in range(devices)])]
    ppermute x16, starting transfers between devices: 19 us -> 19.7 us  [swap(): lax.ppermute(value, 'weight', [(i, i ^ shift) for i in range(devices)])]
    pallas_call x20 -> x21, Pallas kernels: 22.4 us -> 22.4 us  [call(): pl.pallas_call(kernel, out_shape=outs, in_specs=[pl.BlockSpec(memory_spac...]
  transfers between devices with their start and end apart: 16 -> 16, of which waited for: 10 -> 10; matrix products, arithmetic and copies ran while one was open for 0% -> 0% of each run, Pallas kernels for 28% -> 31%
where the time goes in v6:
time: 54.7 us; the launch traced here: 54.5 us
  Pallas kernels  22.4 us (41%)
  starting transfers between devices  19.7 us (36%)
  waiting for transfers between devices  8.18 us (15%)
  matrix products  3.15 us (6%)
  between operations  0.93 us (2%)
    pallas_call x21, Pallas kernels, call(): pl.pallas_call(kernel, out_shape=outs, in_specs=[pl.BlockSpec(memory_spac...  22.4 us
    ppermute x16, starting transfers between devices, swap(): lax.ppermute(value, 'weight', [(i, i ^ shift) for i in range(devices)])  19.7 us
    ppermute x16, waiting for transfers between devices, swap(): lax.ppermute(value, 'weight', [(i, i ^ shift) for i in range(devices)])  8.18 us
    dot_general x1, matrix products, body(): jnp.einsum('rd,dbc->brc', normed, near_weight, preferred_element_type=F32)  3.15 us
  transfers between devices with their start and end apart: 16, of which 10 were waited for; matrix products, arithmetic and copies ran while one was open for 0% of the time, Pallas kernels for 31%

profile of v6, /device:TPU:0, one launch (start us, length us, event | category | flops | bytes accessed | tf_op | source)
XLA Modules:
  0.0 54.5 jit_solution(9857627639506030940)
XLA Ops:
  0.6 1.0 %shard_map.178.refs_0_ = bf16[192,128]{1,0:T(8,128)(2,1)S(1)} custom-call(bf16[4,8192]{1,0:T(4,128)(2,1)} %refs_0_.1, f32[1,8192]{1,0:T(1,128)} %bitcast.19), custom_call_target="tpu_custom_call" | custom-call | tf_op jit(solution)/shard_map/pallas_call | solution.py:100
  1.7 4.1 %collective-permute-start = (bf16[192,128]{1,0:T(8,128)(2,1)S(1)}, bf16[192,128]{1,0:T(8,128)(2,1)S(1)}, u32[]{:S(2)}, u32[]{:S(2)}) collective-permute-start(bf16[192,128]{1,0:T(8,128)(2,1)S(1)} %shard_map.178.refs_0_), channel_id=1, source_target_pairs={{0,8},{1,9},{2,10},{3,11},{4,12},{5,13},{6,14},{7,15},{8,0},{9,1},... | collective-permute-start | bytes 147464 | tf_op jit(solution)/shard_map/ppermute | solution.py:79
  5.8 2.9 %shard_map.175.refs_0_.refs_2_ = bf16[8192,2,512]{2,1,0:T(2,128)(2,1)S(1)} custom-call(bf16[8192,2,512]{2,1,0:T(2,128)(2,1)} %far_ref.7), custom_call_target="tpu_custom_call" | custom-call | tf_op jit(solution)/shard_map/pallas_call | solution.py:100
  8.7 2.6 %collective-permute-start.1 = (bf16[384,128]{1,0:T(8,128)(2,1)S(1)}, bf16[384,128]{1,0:T(8,128)(2,1)S(1)}, u32[]{:S(2)}, u32[]{:S(2)}) collective-permute-start(bf16[384,128]{1,0:T(8,128)(2,1)S(1)} %shard_map.179.refs_0_), channel_id=1, source_target_pairs={{0,6},{1,7},{2,4},{3,5},{4,2},{5,3},{6,0},{7,1},{8,14},{9,15},{10,... | collective-permute-start | bytes 294920 | tf_op jit(solution)/shard_map/ppermute | solution.py:79
  11.3 0.4 collective-permute-start.2
  11.7 0.5 collective-permute-start.3
  12.2 3.8 %shard_map.176.refs_0_.refs_4_ = bf16[8192,2,512]{2,1,0:T(2,128)(2,1)S(1)} custom-call(bf16[8192,2,512]{2,1,0:T(2,128)(2,1)} %far_ref.7, bf16[8192,2,512]{2,1,0:T(2,128)(2,1)S(1)} %shard_map.175.refs_0_.refs_2_), custom_call_target="tpu_custom_call", output_to_operand_aliasing={{}: (1, {})} | custom-call | tf_op jit(solution)/shard_map/pallas_call | solution.py:100
  16.1 0.3 collective-permute-done.2.refs_2_
  16.3 0.1 collective-permute-done.3.refs_3_
  16.5 0.1 collective-permute-start.4
  16.5 1.2 %shard_map.177._ = bf16[8192,2,512]{2,1,0:T(2,128)(2,1)S(1)} custom-call(bf16[8192,2,512]{2,1,0:T(2,128)(2,1)} %far_ref.7, bf16[8192,2,512]{2,1,0:T(2,128)(2,1)S(1)} %shard_map.176.refs_0_.refs_4_), custom_call_target="tpu_custom_call", output_to_operand_aliasing={{}: (1, {})} | custom-call | tf_op jit(solution)/shard_map/pallas_call | solution.py:100
  17.8 0.1 shard_map.181.half_ref
  17.9 0.4 collective-permute-done.4.other_ref
  18.2 0.2 shard_map.182
  18.4 0.0 copy-start.1
  18.4 0.0 copy-start.7
  18.5 3.1 %fusion.2.both_ref = f32[2,48,512]{2,1,0:T(8,128)S(1)} fusion(bf16[8192,2,512]{2,1,0:T(2,128)(2,1)S(1)} %shard_map.177._, bf16[48,8192]{1,0:T(8,128)(2,1)S(1)} %shard_map.182), kind=kOutput, calls=%fused_computation.2 | convolution fusion | flops 805306368 | bytes 17760256 | tf_op jit(solution)/shard_map/rd,dbc->brc/dot_general | solution.py:533
  21.6 0.0 copy-done.1
  21.7 0.5 shard_map.183
  22.2 0.2 collective-permute-start.5
  22.4 0.8 %shard_map.184 = (f32[48,512]{1,0:T(8,128)S(1)}, f32[48,128]{1,0:T(8,128)S(1)}) custom-call(s32[16]{0:T(128)S(1)} %copy-done.9, f32[2,48,512]{2,1,0:T(8,128)S(1)} %fusion.2.both_ref, s32[2,48]{1,0:T(2,128)S(1)} %copy-done.7), custom_call_target="tpu_custom_call" | custom-call | tf_op jit(solution)/shard_map/pallas_call | solution.py:100
  23.3 0.3 collective-permute-done.5.refs_1_
  23.5 0.1 shard_map.185
  23.6 0.0 copy-start.6
  23.7 1.9 %collective-permute-start.6 = (bf16[24,576]{1,0:T(8,128)(2,1)S(1)}, bf16[24,576]{1,0:T(8,128)(2,1)S(1)}, u32[]{:S(2)}, u32[]{:S(2)}) collective-permute-start(bf16[24,576]{1,0:T(8,128)(2,1)S(1)} %get-tuple-element.29), channel_id=1, source_target_pairs={{0,9},{1,8},{2,11},{3,10},{4,13},{5,12},{6,15},{7,14},{8,1},{9,0},... | collective-permute-start | bytes 82952 | tf_op jit(solution)/shard_map/ppermute | solution.py:79
  25.6 1.7 %shard_map.186.refs_2_.first_ref = bf16[512,2560]{1,0:T(8,128)(2,1)S(1)} custom-call(bf16[512,8192]{1,0:T(8,128)(2,1)} %far_ref.9), custom_call_target="tpu_custom_call" | custom-call | tf_op jit(solution)/shard_map/pallas_call | solution.py:100
  27.3 0.7 %collective-permute-done.6.refs_1_ = bf16[24,576]{1,0:T(8,128)(2,1)S(1)} collective-permute-done((bf16[24,576]{1,0:T(8,128)(2,1)S(1)}, bf16[24,576]{1,0:T(8,128)(2,1)S(1)}, u32[]{:S(2)}, u32[]{:S(2)}) %collective-permute-start.6) | collective-permute-done | bytes 27680 | tf_op jit(solution)/shard_map/ppermute | solution.py:79
  28.0 0.1 shard_map.187
  28.1 0.9 %collective-permute-start.7 = (bf16[24,576]{1,0:T(8,128)(2,1)S(1)}, bf16[24,576]{1,0:T(8,128)(2,1)S(1)}, u32[]{:S(2)}, u32[]{:S(2)}) collective-permute-start(bf16[24,576]{1,0:T(8,128)(2,1)S(1)} %get-tuple-element.31), channel_id=1, source_target_pairs={{0,3},{1,2},{2,1},{3,0},{4,7},{5,6},{6,5},{7,4},{8,11},{9,10},{10,... | collective-permute-start | bytes 82952 | tf_op jit(solution)/shard_map/ppermute | solution.py:79
  29.1 1.5 %collective-permute-start.8 = (bf16[24,576]{1,0:T(8,128)(2,1)S(1)}, bf16[24,576]{1,0:T(8,128)(2,1)S(1)}, u32[]{:S(2)}, u32[]{:S(2)}) collective-permute-start(bf16[24,576]{1,0:T(8,128)(2,1)S(1)} %get-tuple-element.31), channel_id=1, source_target_pairs={{0,5},{1,4},{2,7},{3,6},{4,1},{5,0},{6,3},{7,2},{8,13},{9,12},{10,... | collective-permute-start | bytes 82952 | tf_op jit(solution)/shard_map/ppermute | solution.py:79
  30.6 0.7 %collective-permute-start.9 = (bf16[24,576]{1,0:T(8,128)(2,1)S(1)}, bf16[24,576]{1,0:T(8,128)(2,1)S(1)}, u32[]{:S(2)}, u32[]{:S(2)}) collective-permute-start(bf16[24,576]{1,0:T(8,128)(2,1)S(1)} %get-tuple-element.31), channel_id=1, source_target_pairs={{0,6},{1,7},{2,4},{3,5},{4,2},{5,3},{6,0},{7,1},{8,14},{9,15},{10,... | collective-permute-start | bytes 82952 | tf_op jit(solution)/shard_map/ppermute | solution.py:79
  31.3 2.7 %shard_map.188.refs_4_.last_ref = bf16[512,5632]{1,0:T(8,128)(2,1)S(1)} custom-call(bf16[512,8192]{1,0:T(8,128)(2,1)} %far_ref.9), custom_call_target="tpu_custom_call" | custom-call | tf_op jit(solution)/shard_map/pallas_call | solution.py:100
  34.0 1.3 %collective-permute-done.9.refs_3_ = bf16[24,576]{1,0:T(8,128)(2,1)S(1)} collective-permute-done((bf16[24,576]{1,0:T(8,128)(2,1)S(1)}, bf16[24,576]{1,0:T(8,128)(2,1)S(1)}, u32[]{:S(2)}, u32[]{:S(2)}) %collective-permute-start.9) | collective-permute-done | bytes 27680 | tf_op jit(solution)/shard_map/ppermute | solution.py:79
  35.4 0.2 shard_map.189
  35.5 1.2 %collective-permute-done.10.other_ref = bf16[24,576]{1,0:T(8,128)(2,1)S(1)} collective-permute-done((bf16[24,576]{1,0:T(8,128)(2,1)S(1)}, bf16[24,576]{1,0:T(8,128)(2,1)S(1)}, u32[]{:S(2)}, u32[]{:S(2)}) %collective-permute-start.10) | collective-permute-done | bytes 27680 | tf_op jit(solution)/shard_map/ppermute | solution.py:79
  36.8 2.7 %shard_map.190 = (f32[1536,128]{1,0:T(8,128)S(1)}, bf16[1536,128]{1,0:T(8,128)(2,1)S(1)}, f32[48,512]{1,0:T(8,128)S(1)}) custom-call(f32[24,544]{1,0:T(8,128)S(1)} %get-tuple-element.32.mine_ref, bf16[24,576]{1,0:T(8,128)(2,1)S(1)} %collective-permute-done.10.other_ref, s32[48,2]{1,0:T(8,128)S(1)} %copy-done.6, ...), custom_call_target="tpu_custom_call" | custom-call | tf_op jit(solution)/shard_map/pallas_call | solution.py:100
  39.5 0.2 collective-permute-start.11
  39.7 1.6 %collective-permute-done.11.refs_1_ = bf16[1536,128]{1,0:T(8,128)(2,1)S(1)} collective-permute-done((bf16[1536,128]{1,0:T(8,128)(2,1)S(1)}, bf16[1536,128]{1,0:T(8,128)(2,1)S(1)}, u32[]{:S(2)}, u32[]{:S(2)}) %collective-permute-start.11) | collective-permute-done | bytes 393248 | tf_op jit(solution)/shard_map/ppermute | solution.py:79
  41.2 0.1 shard_map.191
  41.3 0.5 collective-permute-start.12
  41.9 1.0 %collective-permute-start.13 = (bf16[384,128]{1,0:T(8,128)(2,1)S(1)}, bf16[384,128]{1,0:T(8,128)(2,1)S(1)}, u32[]{:S(2)}, u32[]{:S(2)}) collective-permute-start(bf16[384,128]{1,0:T(8,128)(2,1)S(1)} %get-tuple-element.40), channel_id=1, source_target_pairs={{0,2},{1,3},{2,0},{3,1},{4,6},{5,7},{6,4},{7,5},{8,10},{9,11},{10,... | collective-permute-start | bytes 294920 | tf_op jit(solution)/shard_map/ppermute | solution.py:79
  42.8 2.1 %collective-permute-start.14 = (bf16[384,128]{1,0:T(8,128)(2,1)S(1)}, bf16[384,128]{1,0:T(8,128)(2,1)S(1)}, u32[]{:S(2)}, u32[]{:S(2)}) collective-permute-start(bf16[384,128]{1,0:T(8,128)(2,1)S(1)} %get-tuple-element.41), channel_id=1, source_target_pairs={{0,6},{1,7},{2,4},{3,5},{4,2},{5,3},{6,0},{7,1},{8,14},{9,15},{10,... | collective-permute-start | bytes 294920 | tf_op jit(solution)/shard_map/ppermute | solution.py:79
  44.9 2.2 %shard_map.192 = (bf16[64,16,512]{2,1,0:T(8,128)(2,1)}, f32[8,128]{1,0:T(8,128)S(1)}) custom-call(s32[16]{0:T(128)S(1)} %copy-done.9, f32[24,544]{1,0:T(8,128)S(1)} %get-tuple-element.32.mine_ref, bf16[24,576]{1,0:T(8,128)(2,1)S(1)} %collective-permute-done.10.other_ref, bf16[48,512]{1,0:T(8,128)(2,1)S(1)} %get-tuple-element.34.mixed_ref, ...), custom_call_target="tpu_custom_call" | custom-call | tf_op jit(solution)/shard_map/pallas_call | solution.py:100
  47.1 1.6 %collective-permute-done.14.refs_3_ = bf16[384,128]{1,0:T(8,128)(2,1)S(1)} collective-permute-done((bf16[384,128]{1,0:T(8,128)(2,1)S(1)}, bf16[384,128]{1,0:T(8,128)(2,1)S(1)}, u32[]{:S(2)}, u32[]{:S(2)}) %collective-permute-start.14) | collective-permute-done | bytes 98336 | tf_op jit(solution)/shard_map/ppermute | solution.py:79
  48.7 2.9 %collective-permute-start.15 = (bf16[192,128]{1,0:T(8,128)(2,1)S(1)}, bf16[192,128]{1,0:T(8,128)(2,1)S(1)}, u32[]{:S(2)}, u32[]{:S(2)}) collective-permute-start(bf16[192,128]{1,0:T(8,128)(2,1)S(1)} %get-tuple-element.45), channel_id=1, source_target_pairs={{0,8},{1,9},{2,10},{3,11},{4,12},{5,13},{6,14},{7,15},{8,0},{9,1},... | collective-permute-start | bytes 147464 | tf_op jit(solution)/shard_map/ppermute | solution.py:79
  51.6 1.4 %shard_map.195 = bf16[3,64,512]{2,1,0:T(8,128)(2,1)} custom-call(s32[16]{0:T(128)S(1)} %copy-done.9, f32[2,48,512]{2,1,0:T(8,128)S(1)} %fusion.2.both_ref, s32[2,48]{1,0:T(2,128)S(1)} %copy-done.7, bf16[3,64,512]{2,1,0:T(8,128)(2,1)S(1)} %bitcast.13), custom_call_target="tpu_custom_call" | custom-call | tf_op jit(solution)/shard_map/pallas_call | solution.py:100
  53.0 0.8 %collective-permute-done.15.refs_2_ = bf16[192,128]{1,0:T(8,128)(2,1)S(1)} collective-permute-done((bf16[192,128]{1,0:T(8,128)(2,1)S(1)}, bf16[192,128]{1,0:T(8,128)(2,1)S(1)}, u32[]{:S(2)}, u32[]{:S(2)}) %collective-permute-start.15) | collective-permute-done | bytes 49184 | tf_op jit(solution)/shard_map/ppermute | solution.py:79
  53.8 0.7 %shard_map.194 = bf16[4,8192]{1,0:T(4,128)(2,1)} custom-call(bf16[4,8192]{1,0:T(4,128)(2,1)S(1)} %copy-done.4, f32[192,128]{1,0:T(8,128)S(1)} %get-tuple-element.44.refs_1_, bf16[192,128]{1,0:T(8,128)(2,1)S(1)} %collective-permute-done.15.refs_2_), custom_call_target="tpu_custom_call" | custom-call | tf_op jit(solution)/shard_map/pallas_call | solution.py:100
  (32 shorter events, 0.2 us)
Async XLA Ops:
  1.7 7.0 %collective-permute-start = (bf16[192,128]{1,0:T(8,128)(2,1)S(1)}, bf16[192,128]{1,0:T(8,128)(2,1)S(1)}, u32[]{:S(2)}, u32[]{:S(2)}) collective-permute-start(bf16[192,128]{1,0:T(8,128)(2,1)S(1)} %shard_map.178.refs_0_), channel_id=1, source_target_pairs={{0,8},{1,9},{2,10},{3,11},{4,12},{5,13},{6,14},{7,15},{8,0},{9,1},... | collective-permute-start | bytes 147464 | tf_op jit(solution)/shard_map/ppermute | solution.py:79
  8.7 7.4 %collective-permute-start.1 = (bf16[384,128]{1,0:T(8,128)(2,1)S(1)}, bf16[384,128]{1,0:T(8,128)(2,1)S(1)}, u32[]{:S(2)}, u32[]{:S(2)}) collective-permute-start(bf16[384,128]{1,0:T(8,128)(2,1)S(1)} %shard_map.179.refs_0_), channel_id=1, source_target_pairs={{0,6},{1,7},{2,4},{3,5},{4,2},{5,3},{6,0},{7,1},{8,14},{9,15},{10,... | collective-permute-start | bytes 294920 | tf_op jit(solution)/shard_map/ppermute | solution.py:79
  11.3 5.0 %collective-permute-start.2 = (bf16[384,128]{1,0:T(8,128)(2,1)S(1)}, bf16[384,128]{1,0:T(8,128)(2,1)S(1)}, u32[]{:S(2)}, u32[]{:S(2)}) collective-permute-start(bf16[384,128]{1,0:T(8,128)(2,1)S(1)} %shard_map.179.refs_0_), channel_id=1, source_target_pairs={{0,4},{1,5},{2,6},{3,7},{4,0},{5,1},{6,2},{7,3},{8,12},{9,13},{10,... | collective-permute-start | bytes 294920 | tf_op jit(solution)/shard_map/ppermute | solution.py:79
  11.7 4.7 %collective-permute-start.3 = (bf16[384,128]{1,0:T(8,128)(2,1)S(1)}, bf16[384,128]{1,0:T(8,128)(2,1)S(1)}, u32[]{:S(2)}, u32[]{:S(2)}) collective-permute-start(bf16[384,128]{1,0:T(8,128)(2,1)S(1)} %shard_map.179.refs_0_), channel_id=1, source_target_pairs={{0,2},{1,3},{2,0},{3,1},{4,6},{5,7},{6,4},{7,5},{8,10},{9,11},{10,... | collective-permute-start | bytes 294920 | tf_op jit(solution)/shard_map/ppermute | solution.py:79
  16.5 1.8 %collective-permute-start.4 = (bf16[1536,128]{1,0:T(8,128)(2,1)S(1)}, bf16[1536,128]{1,0:T(8,128)(2,1)S(1)}, u32[]{:S(2)}, u32[]{:S(2)}) collective-permute-start(bf16[1536,128]{1,0:T(8,128)(2,1)S(1)} %shard_map.180.mine_ref), channel_id=1, source_target_pairs={{0,1},{1,0},{2,3},{3,2},{4,5},{5,4},{6,7},{7,6},{8,9},{9,8},{10,11... | collective-permute-start | bytes 1179656 | tf_op jit(solution)/shard_map/ppermute | solution.py:79
  18.4 3.2 %copy-start.1 = (bf16[64,3,512]{2,0,1:T(8,128)(2,1)S(1)}, bf16[64,3,512]{2,0,1:T(8,128)(2,1)}, u32[]{:S(2)}) copy-start(bf16[64,3,512]{2,0,1:T(8,128)(2,1)} %param.28) | copy-start | bytes 589828
  18.4 3.2 %copy-start.2 = (bf16[512,544]{0,1:T(8,128)(2,1)S(1)}, bf16[512,544]{0,1:T(8,128)(2,1)}, u32[]{:S(2)}) copy-start(bf16[512,544]{0,1:T(8,128)(2,1)} %param.21) | copy-start | bytes 1671172
  18.4 3.2 %copy-start.7 = (s32[2,48]{1,0:T(2,128)S(1)}, s32[2,48]{1,0:T(2,128)}, u32[]{:S(2)}) copy-start(s32[2,48]{1,0:T(2,128)} %constant.4.clone.spot_ref) | copy-start | bytes 1156
  18.5 3.2 %copy-start.8 = (f32[4,512]{1,0:T(4,128)S(1)}, f32[4,512]{1,0:T(4,128)}, u32[]{:S(2)}) copy-start(f32[4,512]{1,0:T(4,128)} %taps_ref.1) | copy-start | bytes 24580
  18.5 3.2 %copy-start.10 = (f32[512]{0:T(512)S(1)}, f32[512]{0:T(512)}, u32[]{:S(2)}) copy-start(f32[512]{0:T(512)} %param.20) | copy-start | bytes 6148
  18.5 4.0 %copy-start.9 = (s32[16]{0:T(128)S(1)}, s32[16]{0:T(128)}, u32[]{:S(2)}) copy-start(s32[16]{0:T(128)} %live_ref.5) | copy-start | bytes 196
  22.2 1.3 %collective-permute-start.5 = (f32[24,544]{1,0:T(8,128)S(1)}, f32[24,544]{1,0:T(8,128)S(1)}, u32[]{:S(2)}, u32[]{:S(2)}) collective-permute-start(f32[24,544]{1,0:T(8,128)S(1)} %get-tuple-element.26), channel_id=1, source_target_pairs={{0,1},{1,0},{2,3},{3,2},{4,5},{5,4},{6,7},{7,6},{8,9},{9,8},{10,11... | collective-permute-start | bytes 156680 | tf_op jit(solution)/shard_map/ppermute | solution.py:79
  23.6 13.1 %copy-start = (bf16[64,16,512]{2,1,0:T(8,128)(2,1)S(1)}, bf16[64,16,512]{2,1,0:T(8,128)(2,1)}, u32[]{:S(2)}) copy-start(bf16[64,16,512]{2,1,0:T(8,128)(2,1)} %state_ref.3) | copy-start | bytes 3145732
  23.6 13.1 %copy-start.3 = (bf16[512,512]{1,0:T(8,128)(2,1)S(1)}, bf16[512,512]{1,0:T(8,128)(2,1)}, u32[]{:S(2)}) copy-start(bf16[512,512]{1,0:T(8,128)(2,1)} %step_weight_ref.1) | copy-start | bytes 1572868
  23.6 13.1 %copy-start.5 = (f32[16,512]{1,0:T(8,128)S(1)}, f32[16,512]{1,0:T(8,128)}, u32[]{:S(2)}) copy-start(f32[16,512]{1,0:T(8,128)} %rates_ref.3) | copy-start | bytes 98308
  23.6 13.1 %copy-start.6 = (s32[48,2]{1,0:T(8,128)S(1)}, s32[48,2]{1,0:T(8,128)}, u32[]{:S(2)}) copy-start(s32[48,2]{1,0:T(8,128)} %constant.7.spot_ref) | copy-start | bytes 1156
  23.6 13.1 %copy-start.11 = (f32[512]{0:T(512)S(1)}, f32[512]{0:T(512)}, u32[]{:S(2)}) copy-start(f32[512]{0:T(512)} %param.23) | copy-start | bytes 6148
  23.7 13.1 %copy-start.12 = (f32[512]{0:T(512)S(1)}, f32[512]{0:T(512)}, u32[]{:S(2)}) copy-start(f32[512]{0:T(512)} %param.25) | copy-start | bytes 6148
  23.7 4.3 %collective-permute-start.6 = (bf16[24,576]{1,0:T(8,128)(2,1)S(1)}, bf16[24,576]{1,0:T(8,128)(2,1)S(1)}, u32[]{:S(2)}, u32[]{:S(2)}) collective-permute-start(bf16[24,576]{1,0:T(8,128)(2,1)S(1)} %get-tuple-element.29), channel_id=1, source_target_pairs={{0,9},{1,8},{2,11},{3,10},{4,13},{5,12},{6,15},{7,14},{8,1},{9,0},... | collective-permute-start | bytes 82952 | tf_op jit(solution)/shard_map/ppermute | solution.py:79
  28.1 25.7 %copy-start.4 = (bf16[4,8192]{1,0:T(4,128)(2,1)S(1)}, bf16[4,8192]{1,0:T(4,128)(2,1)}, u32[]{:S(2)}) copy-start(bf16[4,8192]{1,0:T(4,128)(2,1)} %refs_0_.1) | copy-start | bytes 196612
  28.1 5.9 %collective-permute-start.7 = (bf16[24,576]{1,0:T(8,128)(2,1)S(1)}, bf16[24,576]{1,0:T(8,128)(2,1)S(1)}, u32[]{:S(2)}, u32[]{:S(2)}) collective-permute-start(bf16[24,576]{1,0:T(8,128)(2,1)S(1)} %get-tuple-element.31), channel_id=1, source_target_pairs={{0,3},{1,2},{2,1},{3,0},{4,7},{5,6},{6,5},{7,4},{8,11},{9,10},{10,... | collective-permute-start | bytes 82952 | tf_op jit(solution)/shard_map/ppermute | solution.py:79
  29.1 5.0 %collective-permute-start.8 = (bf16[24,576]{1,0:T(8,128)(2,1)S(1)}, bf16[24,576]{1,0:T(8,128)(2,1)S(1)}, u32[]{:S(2)}, u32[]{:S(2)}) collective-permute-start(bf16[24,576]{1,0:T(8,128)(2,1)S(1)} %get-tuple-element.31), channel_id=1, source_target_pairs={{0,5},{1,4},{2,7},{3,6},{4,1},{5,0},{6,3},{7,2},{8,13},{9,12},{10,... | collective-permute-start | bytes 82952 | tf_op jit(solution)/shard_map/ppermute | solution.py:79
  30.6 4.8 %collective-permute-start.9 = (bf16[24,576]{1,0:T(8,128)(2,1)S(1)}, bf16[24,576]{1,0:T(8,128)(2,1)S(1)}, u32[]{:S(2)}, u32[]{:S(2)}) collective-permute-start(bf16[24,576]{1,0:T(8,128)(2,1)S(1)} %get-tuple-element.31), channel_id=1, source_target_pairs={{0,6},{1,7},{2,4},{3,5},{4,2},{5,3},{6,0},{7,1},{8,14},{9,15},{10,... | collective-permute-start | bytes 82952 | tf_op jit(solution)/shard_map/ppermute | solution.py:79
  35.5 1.2 %collective-permute-start.10 = (bf16[24,576]{1,0:T(8,128)(2,1)S(1)}, bf16[24,576]{1,0:T(8,128)(2,1)S(1)}, u32[]{:S(2)}, u32[]{:S(2)}) collective-permute-start(bf16[24,576]{1,0:T(8,128)(2,1)S(1)} %get-tuple-element.33), channel_id=1, source_target_pairs={{0,1},{1,0},{2,3},{3,2},{4,5},{5,4},{6,7},{7,6},{8,9},{9,8},{10,11... | collective-permute-start | bytes 82952 | tf_op jit(solution)/shard_map/ppermute | solution.py:79
  39.5 1.8 %collective-permute-start.11 = (bf16[1536,128]{1,0:T(8,128)(2,1)S(1)}, bf16[1536,128]{1,0:T(8,128)(2,1)S(1)}, u32[]{:S(2)}, u32[]{:S(2)}) collective-permute-start(bf16[1536,128]{1,0:T(8,128)(2,1)S(1)} %get-tuple-element.37), channel_id=1, source_target_pairs={{0,1},{1,0},{2,3},{3,2},{4,5},{5,4},{6,7},{7,6},{8,9},{9,8},{10,11... | collective-permute-start | bytes 1179656 | tf_op jit(solution)/shard_map/ppermute | solution.py:79
  41.3 5.8 %collective-permute-start.12 = (bf16[384,128]{1,0:T(8,128)(2,1)S(1)}, bf16[384,128]{1,0:T(8,128)(2,1)S(1)}, u32[]{:S(2)}, u32[]{:S(2)}) collective-permute-start(bf16[384,128]{1,0:T(8,128)(2,1)S(1)} %get-tuple-element.39), channel_id=1, source_target_pairs={{0,4},{1,5},{2,6},{3,7},{4,0},{5,1},{6,2},{7,3},{8,12},{9,13},{10,... | collective-permute-start | bytes 294920 | tf_op jit(solution)/shard_map/ppermute | solution.py:79
  41.9 5.3 %collective-permute-start.13 = (bf16[384,128]{1,0:T(8,128)(2,1)S(1)}, bf16[384,128]{1,0:T(8,128)(2,1)S(1)}, u32[]{:S(2)}, u32[]{:S(2)}) collective-permute-start(bf16[384,128]{1,0:T(8,128)(2,1)S(1)} %get-tuple-element.40), channel_id=1, source_target_pairs={{0,2},{1,3},{2,0},{3,1},{4,6},{5,7},{6,4},{7,5},{8,10},{9,11},{10,... | collective-permute-start | bytes 294920 | tf_op jit(solution)/shard_map/ppermute | solution.py:79
  42.8 5.8 %collective-permute-start.14 = (bf16[384,128]{1,0:T(8,128)(2,1)S(1)}, bf16[384,128]{1,0:T(8,128)(2,1)S(1)}, u32[]{:S(2)}, u32[]{:S(2)}) collective-permute-start(bf16[384,128]{1,0:T(8,128)(2,1)S(1)} %get-tuple-element.41), channel_id=1, source_target_pairs={{0,6},{1,7},{2,4},{3,5},{4,2},{5,3},{6,0},{7,1},{8,14},{9,15},{10,... | collective-permute-start | bytes 294920 | tf_op jit(solution)/shard_map/ppermute | solution.py:79
  48.7 5.1 %collective-permute-start.15 = (bf16[192,128]{1,0:T(8,128)(2,1)S(1)}, bf16[192,128]{1,0:T(8,128)(2,1)S(1)}, u32[]{:S(2)}, u32[]{:S(2)}) collective-permute-start(bf16[192,128]{1,0:T(8,128)(2,1)S(1)} %get-tuple-element.45), channel_id=1, source_target_pairs={{0,8},{1,9},{2,10},{3,11},{4,12},{5,13},{6,14},{7,15},{8,0},{9,1},... | collective-permute-start | bytes 147464 | tf_op jit(solution)/shard_map/ppermute | solution.py:79

commit v7 on v6

--- a/solution.py
+++ b/solution.py
@@ -283,7 +283,8 @@
     send_ref[...] = low_ref[pl.ds(pl.multiple_of((1 - core) * half, 8), half), :]
 
 
-def gate_kernel(live_ref, both_ref, spot_ref, gate_ref, alive_ref):
+def gate_kernel(live_ref, both_ref, spot_ref, mixed_ref, gate_ref, alive_ref, x_ref):
+    x_ref[...] = mixed_ref[...].astype(F32)
     for b in range(live_ref.shape[0]):
         for t in range(LIVE_MAX):
             r = b * LIVE_MAX + t
@@ -316,18 +317,47 @@
         new_conv_ref[k] = jnp.where(alive, states[k + 1], states[k]).astype(BF16)
 
 
-def join_low(mine_ref, other_ref, low_ref):
-    half = mine_ref.shape[0]
-    core = side(lax.axis_index("weight"))
-    low_ref[pl.ds(pl.multiple_of(core * half, 8), half), :] = mine_ref[...]
-    low_ref[pl.ds(pl.multiple_of((1 - core) * half, 8), half), :] = unpack(other_ref[...])
-
-
-def readout_kernel(
-    mine_ref,
-    other_ref,
-    spot_ref,
-    mixed_ref,
+def half_rows(which, size):
+    return pl.ds(pl.multiple_of(which * size, 8), size)
+
+
+def join_halves(mine, other, out_ref):
+    size = mine.shape[0]
+    mine_side = side(lax.axis_index("weight"))
+    out_ref[half_rows(mine_side, size), :] = mine
+    out_ref[half_rows(1 - mine_side, size), :] = other
+
+
+def gated_rows(which, low, weights, rows_refs, state_ref, read_ref):
+    step_weight_ref, bias_ref, rates_ref, skip_ref = weights
+    size = low.shape[0]
+    x_wide, gate, alive = (ref[half_rows(which, size), :] for ref in rows_refs)
+    blocks = size // LIVE_MAX
+    rows_dev = state_ref.shape[0] // (2 * blocks)
+    step_size = softplus(
+        jnp.dot(low[:, :DTR].astype(BF16), step_weight_ref[...], preferred_element_type=F32)
+        + bias_ref[...]
+    )
+    coefs = low[:, DTR:]
+    both_coefs = jnp.sum(coefs[:, :NSTATE] * coefs[:, NSTATE:], axis=1, keepdims=True)
+    out_coefs = coefs[:, NSTATE:].T
+    rates = -jnp.exp(rates_ref[...])
+    first = which * (blocks * rows_dev)
+    for b in range(blocks):
+        for t in range(LIVE_MAX):
+            r = b * LIVE_MAX + t
+            wide = state_ref[first + (b * rows_dev + t)].astype(F32)
+            decayed = jnp.exp(step_size[r : r + 1, :] * rates) * wide
+            read_ref[r : r + 1, :] = jnp.sum(
+                out_coefs[:, r : r + 1] * decayed, axis=0, keepdims=True
+            )
+    readout = read_ref[...] + (both_coefs * step_size + skip_ref[...]) * x_wide
+    return step_size, jnp.where(alive[:, 0:1] > 0.0, readout * gate, 0.0)
+
+
+def own_kernel(
+    low_ref,
+    x_ref,
     gate_ref,
     alive_ref,
     step_weight_ref,
@@ -335,45 +365,57 @@
     rates_ref,
     skip_ref,
     state_ref,
+    gated_ref,
+    step_ref,
+    read_ref,
+):
+    step_ref[...], gated_ref[...] = gated_rows(
+        side(lax.axis_index("weight")),
+        low_ref[...],
+        (step_weight_ref, bias_ref, rates_ref, skip_ref),
+        (x_ref, gate_ref, alive_ref),
+        state_ref,
+        read_ref,
+    )
+
+
+def readout_kernel(
+    other_ref,
+    x_ref,
+    gate_ref,
+    alive_ref,
+    step_weight_ref,
+    bias_ref,
+    rates_ref,
+    skip_ref,
+    state_ref,
+    own_ref,
+    spot_ref,
     first_ref,
     last_ref,
     keep_ref,
     send_ref,
     step_ref,
-    low_ref,
     read_ref,
+    gated_ref,
     fold_ref,
 ):
-    kept = mixed_ref.shape[0]
-    blocks = kept // LIVE_MAX
-    rows_dev = state_ref.shape[0] // blocks
-    join_low(mine_ref, other_ref, low_ref)
-    step_size = softplus(
-        jnp.dot(
-            low_ref[:, :DTR].astype(BF16), step_weight_ref[...], preferred_element_type=F32
-        )
-        + bias_ref[...]
-    )
-    step_ref[...] = step_size
-    coefs = low_ref[:, DTR:]
-    both_coefs = jnp.sum(coefs[:, :NSTATE] * coefs[:, NSTATE:], axis=1, keepdims=True)
-    out_coefs = coefs[:, NSTATE:].T
-    x_wide = mixed_ref[...].astype(F32)
-    rates = -jnp.exp(rates_ref[...])
-    for b in range(blocks):
-        for t in range(LIVE_MAX):
-            r = b * LIVE_MAX + t
-            wide = state_ref[b * rows_dev + t].astype(F32)
-            decayed = jnp.exp(step_size[r : r + 1, :] * rates) * wide
-            read_ref[r : r + 1, :] = jnp.sum(
-                out_coefs[:, r : r + 1] * decayed, axis=0, keepdims=True
-            )
-    readout = read_ref[...] + (both_coefs * step_size + skip_ref[...]) * x_wide
-    gated = jnp.where(alive_ref[:, 0:1] > 0.0, readout * gate_ref[...], 0.0).astype(BF16)
+    kept = x_ref.shape[0]
+    step_ref[...], gated = gated_rows(
+        1 - side(lax.axis_index("weight")),
+        unpack(other_ref[...]),
+        (step_weight_ref, bias_ref, rates_ref, skip_ref),
+        (x_ref, gate_ref, alive_ref),
+        state_ref,
+        read_ref,
+    )
+    join_halves(own_ref[...], gated, gated_ref)
     block = jnp.bitwise_xor(spot_ref[:, 0:1], lax.axis_index("weight"))
     column = lax.broadcasted_iota(jnp.int32, (kept, kept), 1)
     pick = jnp.where(column == block * LIVE_MAX + spot_ref[:, 1:2], 1.0, 0.0).astype(BF16)
-    picked = jnp.dot(pick, gated, preferred_element_type=F32).astype(BF16)
+    picked = jnp.dot(
+        pick, gated_ref[...].astype(BF16), preferred_element_type=F32
+    ).astype(BF16)
     half = kept // 2
     near = first_ref.shape[1]
     pieces = (near + last_ref.shape[1]) // LANES
@@ -400,21 +442,24 @@
     live_ref,
     mine_ref,
     other_ref,
-    mixed_ref,
-    step_ref,
+    x_ref,
+    own_step_ref,
+    other_step_ref,
     rates_ref,
     state_ref,
     new_state_ref,
     token_ref,
     low_ref,
+    step_ref,
 ):
     token_ref[...] = jnp.zeros_like(token_ref)
     blocks = live_ref.shape[0]
     rows_dev = state_ref.shape[0] // blocks
-    join_low(mine_ref, other_ref, low_ref)
+    join_halves(mine_ref[...], unpack(other_ref[...]), low_ref)
+    join_halves(own_step_ref[...], other_step_ref[...], step_ref)
     in_coefs = low_ref[:, DTR : DTR + NSTATE].T
     step_size = step_ref[...]
-    driven = step_size * mixed_ref[...].astype(F32)
+    driven = step_size * x_ref[...]
     rates = -jnp.exp(rates_ref[...])
     for b in range(blocks):
         for t in range(LIVE_MAX):
@@ -551,10 +596,10 @@
         scratch=[pltpu.VMEM((kept, low_width), F32)],
         limit=16,
     )
-    gate, alive = call(
+    gate, alive, x_wide = call(
         gate_kernel,
-        (shape((kept, channels)), shape((kept, LANES))),
-        (live_counts, both, spots),
+        (shape((kept, channels)), shape((kept, LANES)), shape((kept, channels))),
+        (live_counts, both, spots, mixed_x),
         scalars=1,
     )
     new_conv = call(
@@ -595,25 +640,28 @@
     other = swap(packed, 1, devices)
 
     size = kept // 2 * pieces
-    keep, send, step_size = call(
+    rows_of = (x_wide, gate, alive)
+    weights = (
+        step_weight,
+        step_bias.reshape(1, channels),
+        log_rates,
+        skip_gain.reshape(1, channels),
+        ssm_state,
+    )
+    half_shape = (kept // 2, channels)
+    own_gated, own_step = call(
+        own_kernel,
+        (shape(half_shape), shape(half_shape)),
+        (low, *rows_of, *weights),
+        scratch=[pltpu.VMEM(half_shape, F32)],
+        limit=16,
+    )
+    keep, send, other_step = call(
         readout_kernel,
-        (shape((size, LANES)), shape((size, LANES), BF16), shape((kept, channels))),
-        (
-            low,
-            other,
-            ends,
-            mixed_x,
-            gate,
-            alive,
-            step_weight,
-            step_bias.reshape(1, channels),
-            log_rates,
-            skip_gain.reshape(1, channels),
-            ssm_state,
-            *near_out,
-        ),
+        (shape((size, LANES)), shape((size, LANES), BF16), shape(half_shape)),
+        (other, *rows_of, *weights, own_gated, ends, *near_out),
         scratch=[
-            pltpu.VMEM((kept, low_width), F32),
+            pltpu.VMEM(half_shape, F32),
             pltpu.VMEM((kept, channels), F32),
             pltpu.VMEM((kept * (pieces + 1), LANES), F32),
         ],
@@ -622,9 +670,12 @@
     new_state, token = call(
         state_kernel,
         (shape(ssm_state.shape, BF16), shape((8, LANES))),
-        (live_counts, low, other, mixed_x, step_size, log_rates, ssm_state),
+        (live_counts, low, other, x_wide, own_step, other_step, log_rates, ssm_state),
         scalars=1,
-        scratch=[pltpu.VMEM((kept, low_width), F32)],
+        scratch=[
+            pltpu.VMEM((kept, low_width), F32),
+            pltpu.VMEM((kept, channels), F32),
+        ],
         limit=16,
     )
 

time: 54.7 us -> 54.3 us (level)
  waiting for transfers between devices: 8.18 us -> 7.61 us
    ppermute x16, waiting for transfers between devices: 8.18 us -> 7.61 us  [swap(): lax.ppermute(value, 'weight', [(i, i ^ shift) for i in range(devices)])]
    pallas_call x21 -> x22, Pallas kernels: 22.4 us -> 22.6 us  [call(): pl.pallas_call(kernel, out_shape=outs, in_specs=[pl.BlockSpec(memory_spac...]
  transfers between devices with their start and end apart: 16 -> 16, of which waited for: 10 -> 10; matrix products, arithmetic and copies ran while one was open for 0% -> 0% of each run, Pallas kernels for 31% -> 32%
where the time goes in v7:
time: 54.3 us; the launch traced here: 54.1 us
  Pallas kernels  22.6 us (42%)
  starting transfers between devices  19.7 us (36%)
  waiting for transfers between devices  7.61 us (14%)
  matrix products  3.15 us (6%)
  between operations  0.95 us (2%)
    pallas_call x22, Pallas kernels, call(): pl.pallas_call(kernel, out_shape=outs, in_specs=[pl.BlockSpec(memory_spac...  22.6 us
    ppermute x16, starting transfers between devices, swap(): lax.ppermute(value, 'weight', [(i, i ^ shift) for i in range(devices)])  19.7 us
    ppermute x16, waiting for transfers between devices, swap(): lax.ppermute(value, 'weight', [(i, i ^ shift) for i in range(devices)])  7.61 us
    dot_general x1, matrix products, body(): jnp.einsum('rd,dbc->brc', normed, near_weight, preferred_element_type=F32)  3.15 us
  transfers between devices with their start and end apart: 16, of which 10 were waited for; matrix products, arithmetic and copies ran while one was open for 0% of the time, Pallas kernels for 32%

profile of v7, /device:TPU:0, one launch (start us, length us, event | category | flops | bytes accessed | tf_op | source)
XLA Modules:
  0.0 54.1 jit_solution(9471025746572497775)
XLA Ops:
  0.6 1.0 %shard_map.178.refs_0_ = bf16[192,128]{1,0:T(8,128)(2,1)S(1)} custom-call(bf16[4,8192]{1,0:T(4,128)(2,1)} %refs_0_.1, f32[1,8192]{1,0:T(1,128)} %bitcast.21), custom_call_target="tpu_custom_call" | custom-call | tf_op jit(solution)/shard_map/pallas_call | solution.py:100
  1.7 4.1 %collective-permute-start = (bf16[192,128]{1,0:T(8,128)(2,1)S(1)}, bf16[192,128]{1,0:T(8,128)(2,1)S(1)}, u32[]{:S(2)}, u32[]{:S(2)}) collective-permute-start(bf16[192,128]{1,0:T(8,128)(2,1)S(1)} %shard_map.178.refs_0_), channel_id=1, source_target_pairs={{0,8},{1,9},{2,10},{3,11},{4,12},{5,13},{6,14},{7,15},{8,0},{9,1},... | collective-permute-start | bytes 147464 | tf_op jit(solution)/shard_map/ppermute | solution.py:79
  5.8 2.9 %shard_map.175.refs_0_.refs_2_ = bf16[8192,2,512]{2,1,0:T(2,128)(2,1)S(1)} custom-call(bf16[8192,2,512]{2,1,0:T(2,128)(2,1)} %far_ref.7), custom_call_target="tpu_custom_call" | custom-call | tf_op jit(solution)/shard_map/pallas_call | solution.py:100
  8.7 2.6 %collective-permute-start.1 = (bf16[384,128]{1,0:T(8,128)(2,1)S(1)}, bf16[384,128]{1,0:T(8,128)(2,1)S(1)}, u32[]{:S(2)}, u32[]{:S(2)}) collective-permute-start(bf16[384,128]{1,0:T(8,128)(2,1)S(1)} %shard_map.179.refs_0_), channel_id=1, source_target_pairs={{0,6},{1,7},{2,4},{3,5},{4,2},{5,3},{6,0},{7,1},{8,14},{9,15},{10,... | collective-permute-start | bytes 294920 | tf_op jit(solution)/shard_map/ppermute | solution.py:79
  11.3 0.4 collective-permute-start.2
  11.7 0.5 collective-permute-start.3
  12.2 3.8 %shard_map.176.refs_0_.refs_4_ = bf16[8192,2,512]{2,1,0:T(2,128)(2,1)S(1)} custom-call(bf16[8192,2,512]{2,1,0:T(2,128)(2,1)} %far_ref.7, bf16[8192,2,512]{2,1,0:T(2,128)(2,1)S(1)} %shard_map.175.refs_0_.refs_2_), custom_call_target="tpu_custom_call", output_to_operand_aliasing={{}: (1, {})} | custom-call | tf_op jit(solution)/shard_map/pallas_call | solution.py:100
  16.1 0.3 collective-permute-done.2.refs_2_
  16.3 0.1 collective-permute-done.3.refs_3_
  16.5 0.1 collective-permute-start.4
  16.5 1.2 %shard_map.177._ = bf16[8192,2,512]{2,1,0:T(2,128)(2,1)S(1)} custom-call(bf16[8192,2,512]{2,1,0:T(2,128)(2,1)} %far_ref.7, bf16[8192,2,512]{2,1,0:T(2,128)(2,1)S(1)} %shard_map.176.refs_0_.refs_4_), custom_call_target="tpu_custom_call", output_to_operand_aliasing={{}: (1, {})} | custom-call | tf_op jit(solution)/shard_map/pallas_call | solution.py:100
  17.8 0.1 shard_map.181.half_ref
  17.9 0.4 collective-permute-done.4.other_ref
  18.2 0.2 shard_map.182
  18.4 0.0 copy-start.7
  18.5 3.1 %fusion.2.both_ref = f32[2,48,512]{2,1,0:T(8,128)S(1)} fusion(bf16[8192,2,512]{2,1,0:T(2,128)(2,1)S(1)} %shard_map.177._, bf16[48,8192]{1,0:T(8,128)(2,1)S(1)} %shard_map.182), kind=kOutput, calls=%fused_computation.2 | convolution fusion | flops 805306368 | bytes 17760256 | tf_op jit(solution)/shard_map/rd,dbc->brc/dot_general | solution.py:578
  21.6 0.0 copy-done.2
  21.7 0.5 shard_map.183
  22.2 0.2 collective-permute-start.5
  22.4 0.8 %shard_map.184 = (f32[48,512]{1,0:T(8,128)S(1)}, f32[48,128]{1,0:T(8,128)S(1)}, f32[48,512]{1,0:T(8,128)S(1)}) custom-call(s32[16]{0:T(128)S(1)} %copy-done.11, f32[2,48,512]{2,1,0:T(8,128)S(1)} %fusion.2.both_ref, s32[2,48]{1,0:T(2,128)S(1)} %copy-done.7, bf16[48,512]{1,0:T(8,128)(2,1)S(1)} %get-tuple-element.30.mixed_ref), custom_call_target="tpu_custom_call" | custom-call | tf_op jit(solution)/shard_map/pallas_call | solution.py:100
  23.3 0.3 collective-permute-done.5.refs_1_
  23.5 0.1 shard_map.185
  23.7 0.0 copy-start.6
  23.7 1.9 %collective-permute-start.6 = (bf16[24,576]{1,0:T(8,128)(2,1)S(1)}, bf16[24,576]{1,0:T(8,128)(2,1)S(1)}, u32[]{:S(2)}, u32[]{:S(2)}) collective-permute-start(bf16[24,576]{1,0:T(8,128)(2,1)S(1)} %get-tuple-element.33), channel_id=1, source_target_pairs={{0,9},{1,8},{2,11},{3,10},{4,13},{5,12},{6,15},{7,14},{8,1},{9,0},... | collective-permute-start | bytes 82952 | tf_op jit(solution)/shard_map/ppermute | solution.py:79
  25.6 1.7 %shard_map.186.refs_2_.first_ref = bf16[512,2560]{1,0:T(8,128)(2,1)S(1)} custom-call(bf16[512,8192]{1,0:T(8,128)(2,1)} %far_ref.9), custom_call_target="tpu_custom_call" | custom-call | tf_op jit(solution)/shard_map/pallas_call | solution.py:100
  27.3 0.7 %collective-permute-done.6.refs_1_ = bf16[24,576]{1,0:T(8,128)(2,1)S(1)} collective-permute-done((bf16[24,576]{1,0:T(8,128)(2,1)S(1)}, bf16[24,576]{1,0:T(8,128)(2,1)S(1)}, u32[]{:S(2)}, u32[]{:S(2)}) %collective-permute-start.6) | collective-permute-done | bytes 27680 | tf_op jit(solution)/shard_map/ppermute | solution.py:79
  28.0 0.2 shard_map.187
  28.1 0.9 %collective-permute-start.7 = (bf16[24,576]{1,0:T(8,128)(2,1)S(1)}, bf16[24,576]{1,0:T(8,128)(2,1)S(1)}, u32[]{:S(2)}, u32[]{:S(2)}) collective-permute-start(bf16[24,576]{1,0:T(8,128)(2,1)S(1)} %get-tuple-element.35), channel_id=1, source_target_pairs={{0,3},{1,2},{2,1},{3,0},{4,7},{5,6},{6,5},{7,4},{8,11},{9,10},{10,... | collective-permute-start | bytes 82952 | tf_op jit(solution)/shard_map/ppermute | solution.py:79
  29.1 1.5 %collective-permute-start.8 = (bf16[24,576]{1,0:T(8,128)(2,1)S(1)}, bf16[24,576]{1,0:T(8,128)(2,1)S(1)}, u32[]{:S(2)}, u32[]{:S(2)}) collective-permute-start(bf16[24,576]{1,0:T(8,128)(2,1)S(1)} %get-tuple-element.35), channel_id=1, source_target_pairs={{0,5},{1,4},{2,7},{3,6},{4,1},{5,0},{6,3},{7,2},{8,13},{9,12},{10,... | collective-permute-start | bytes 82952 | tf_op jit(solution)/shard_map/ppermute | solution.py:79
  30.6 0.7 %collective-permute-start.9 = (bf16[24,576]{1,0:T(8,128)(2,1)S(1)}, bf16[24,576]{1,0:T(8,128)(2,1)S(1)}, u32[]{:S(2)}, u32[]{:S(2)}) collective-permute-start(bf16[24,576]{1,0:T(8,128)(2,1)S(1)} %get-tuple-element.35), channel_id=1, source_target_pairs={{0,6},{1,7},{2,4},{3,5},{4,2},{5,3},{6,0},{7,1},{8,14},{9,15},{10,... | collective-permute-start | bytes 82952 | tf_op jit(solution)/shard_map/ppermute | solution.py:79
  31.3 2.7 %shard_map.188.refs_4_.last_ref = bf16[512,5632]{1,0:T(8,128)(2,1)S(1)} custom-call(bf16[512,8192]{1,0:T(8,128)(2,1)} %far_ref.9), custom_call_target="tpu_custom_call" | custom-call | tf_op jit(solution)/shard_map/pallas_call | solution.py:100
  34.0 1.3 %collective-permute-done.9.refs_3_ = bf16[24,576]{1,0:T(8,128)(2,1)S(1)} collective-permute-done((bf16[24,576]{1,0:T(8,128)(2,1)S(1)}, bf16[24,576]{1,0:T(8,128)(2,1)S(1)}, u32[]{:S(2)}, u32[]{:S(2)}) %collective-permute-start.9) | collective-permute-done | bytes 27680 | tf_op jit(solution)/shard_map/ppermute | solution.py:79
  35.4 0.2 shard_map.189
  35.6 0.5 shard_map.190
  36.1 0.6 %collective-permute-done.10.other_ref = bf16[24,576]{1,0:T(8,128)(2,1)S(1)} collective-permute-done((bf16[24,576]{1,0:T(8,128)(2,1)S(1)}, bf16[24,576]{1,0:T(8,128)(2,1)S(1)}, u32[]{:S(2)}, u32[]{:S(2)}) %collective-permute-start.10) | collective-permute-done | bytes 27680 | tf_op jit(solution)/shard_map/ppermute | solution.py:79
  36.7 2.3 %shard_map.191 = (f32[1536,128]{1,0:T(8,128)S(1)}, bf16[1536,128]{1,0:T(8,128)(2,1)S(1)}, f32[24,512]{1,0:T(8,128)S(1)}) custom-call(bf16[24,576]{1,0:T(8,128)(2,1)S(1)} %collective-permute-done.10.other_ref, f32[48,512]{1,0:T(8,128)S(1)} %get-tuple-element.37.x_ref, f32[48,512]{1,0:T(8,128)S(1)} %get-tuple-element.31.refs_2_.gate_ref, ...), custom_call_target="tpu_custom_call" | custom-call | tf_op jit(solution)/shard_map/pallas_call | solution.py:100
  39.1 0.2 collective-permute-start.11
  39.3 1.6 %collective-permute-done.11.refs_1_ = bf16[1536,128]{1,0:T(8,128)(2,1)S(1)} collective-permute-done((bf16[1536,128]{1,0:T(8,128)(2,1)S(1)}, bf16[1536,128]{1,0:T(8,128)(2,1)S(1)}, u32[]{:S(2)}, u32[]{:S(2)}) %collective-permute-start.11) | collective-permute-done | bytes 393248 | tf_op jit(solution)/shard_map/ppermute | solution.py:79
  40.9 0.1 shard_map.192
  41.0 0.5 collective-permute-start.12
  41.5 1.0 %collective-permute-start.13 = (bf16[384,128]{1,0:T(8,128)(2,1)S(1)}, bf16[384,128]{1,0:T(8,128)(2,1)S(1)}, u32[]{:S(2)}, u32[]{:S(2)}) collective-permute-start(bf16[384,128]{1,0:T(8,128)(2,1)S(1)} %get-tuple-element.45), channel_id=1, source_target_pairs={{0,2},{1,3},{2,0},{3,1},{4,6},{5,7},{6,4},{7,5},{8,10},{9,11},{10,... | collective-permute-start | bytes 294920 | tf_op jit(solution)/shard_map/ppermute | solution.py:79
  42.5 2.1 %collective-permute-start.14 = (bf16[384,128]{1,0:T(8,128)(2,1)S(1)}, bf16[384,128]{1,0:T(8,128)(2,1)S(1)}, u32[]{:S(2)}, u32[]{:S(2)}) collective-permute-start(bf16[384,128]{1,0:T(8,128)(2,1)S(1)} %get-tuple-element.46), channel_id=1, source_target_pairs={{0,6},{1,7},{2,4},{3,5},{4,2},{5,3},{6,0},{7,1},{8,14},{9,15},{10,... | collective-permute-start | bytes 294920 | tf_op jit(solution)/shard_map/ppermute | solution.py:79
  44.5 2.2 %shard_map.193 = (bf16[64,16,512]{2,1,0:T(8,128)(2,1)}, f32[8,128]{1,0:T(8,128)S(1)}) custom-call(s32[16]{0:T(128)S(1)} %copy-done.11, f32[24,544]{1,0:T(8,128)S(1)} %get-tuple-element.39.low_ref.mine_ref, bf16[24,576]{1,0:T(8,128)(2,1)S(1)} %collective-permute-done.10.other_ref, f32[48,512]{1,0:T(8,128)S(1)} %get-tuple-element.37.x_ref, ...), custom_call_target="tpu_custom_call" | custom-call | tf_op jit(solution)/shard_map/pallas_call | solution.py:100
  46.7 1.6 %collective-permute-done.14.refs_3_ = bf16[384,128]{1,0:T(8,128)(2,1)S(1)} collective-permute-done((bf16[384,128]{1,0:T(8,128)(2,1)S(1)}, bf16[384,128]{1,0:T(8,128)(2,1)S(1)}, u32[]{:S(2)}, u32[]{:S(2)}) %collective-permute-start.14) | collective-permute-done | bytes 98336 | tf_op jit(solution)/shard_map/ppermute | solution.py:79
  48.4 2.9 %collective-permute-start.15 = (bf16[192,128]{1,0:T(8,128)(2,1)S(1)}, bf16[192,128]{1,0:T(8,128)(2,1)S(1)}, u32[]{:S(2)}, u32[]{:S(2)}) collective-permute-start(bf16[192,128]{1,0:T(8,128)(2,1)S(1)} %get-tuple-element.51), channel_id=1, source_target_pairs={{0,8},{1,9},{2,10},{3,11},{4,12},{5,13},{6,14},{7,15},{8,0},{9,1},... | collective-permute-start | bytes 147464 | tf_op jit(solution)/shard_map/ppermute | solution.py:79
  51.2 1.4 %shard_map.196 = bf16[3,64,512]{2,1,0:T(8,128)(2,1)} custom-call(s32[16]{0:T(128)S(1)} %copy-done.11, f32[2,48,512]{2,1,0:T(8,128)S(1)} %fusion.2.both_ref, s32[2,48]{1,0:T(2,128)S(1)} %copy-done.7, bf16[3,64,512]{2,1,0:T(8,128)(2,1)S(1)} %bitcast.13), custom_call_target="tpu_custom_call" | custom-call | tf_op jit(solution)/shard_map/pallas_call | solution.py:100
  52.6 0.8 %collective-permute-done.15.refs_2_ = bf16[192,128]{1,0:T(8,128)(2,1)S(1)} collective-permute-done((bf16[192,128]{1,0:T(8,128)(2,1)S(1)}, bf16[192,128]{1,0:T(8,128)(2,1)S(1)}, u32[]{:S(2)}, u32[]{:S(2)}) %collective-permute-start.15) | collective-permute-done | bytes 49184 | tf_op jit(solution)/shard_map/ppermute | solution.py:79
  53.4 0.7 %shard_map.195 = bf16[4,8192]{1,0:T(4,128)(2,1)} custom-call(bf16[4,8192]{1,0:T(4,128)(2,1)S(1)} %copy-done.5, f32[192,128]{1,0:T(8,128)S(1)} %get-tuple-element.50.refs_1_, bf16[192,128]{1,0:T(8,128)(2,1)S(1)} %collective-permute-done.15.refs_2_), custom_call_target="tpu_custom_call" | custom-call | tf_op jit(solution)/shard_map/pallas_call | solution.py:100
  (33 shorter events, 0.2 us)
Async XLA Ops:
  1.7 7.0 %collective-permute-start = (bf16[192,128]{1,0:T(8,128)(2,1)S(1)}, bf16[192,128]{1,0:T(8,128)(2,1)S(1)}, u32[]{:S(2)}, u32[]{:S(2)}) collective-permute-start(bf16[192,128]{1,0:T(8,128)(2,1)S(1)} %shard_map.178.refs_0_), channel_id=1, source_target_pairs={{0,8},{1,9},{2,10},{3,11},{4,12},{5,13},{6,14},{7,15},{8,0},{9,1},... | collective-permute-start | bytes 147464 | tf_op jit(solution)/shard_map/ppermute | solution.py:79
  8.7 7.4 %collective-permute-start.1 = (bf16[384,128]{1,0:T(8,128)(2,1)S(1)}, bf16[384,128]{1,0:T(8,128)(2,1)S(1)}, u32[]{:S(2)}, u32[]{:S(2)}) collective-permute-start(bf16[384,128]{1,0:T(8,128)(2,1)S(1)} %shard_map.179.refs_0_), channel_id=1, source_target_pairs={{0,6},{1,7},{2,4},{3,5},{4,2},{5,3},{6,0},{7,1},{8,14},{9,15},{10,... | collective-permute-start | bytes 294920 | tf_op jit(solution)/shard_map/ppermute | solution.py:79
  11.3 5.0 %collective-permute-start.2 = (bf16[384,128]{1,0:T(8,128)(2,1)S(1)}, bf16[384,128]{1,0:T(8,128)(2,1)S(1)}, u32[]{:S(2)}, u32[]{:S(2)}) collective-permute-start(bf16[384,128]{1,0:T(8,128)(2,1)S(1)} %shard_map.179.refs_0_), channel_id=1, source_target_pairs={{0,4},{1,5},{2,6},{3,7},{4,0},{5,1},{6,2},{7,3},{8,12},{9,13},{10,... | collective-permute-start | bytes 294920 | tf_op jit(solution)/shard_map/ppermute | solution.py:79
  11.7 4.7 %collective-permute-start.3 = (bf16[384,128]{1,0:T(8,128)(2,1)S(1)}, bf16[384,128]{1,0:T(8,128)(2,1)S(1)}, u32[]{:S(2)}, u32[]{:S(2)}) collective-permute-start(bf16[384,128]{1,0:T(8,128)(2,1)S(1)} %shard_map.179.refs_0_), channel_id=1, source_target_pairs={{0,2},{1,3},{2,0},{3,1},{4,6},{5,7},{6,4},{7,5},{8,10},{9,11},{10,... | collective-permute-start | bytes 294920 | tf_op jit(solution)/shard_map/ppermute | solution.py:79
  16.5 1.8 %collective-permute-start.4 = (bf16[1536,128]{1,0:T(8,128)(2,1)S(1)}, bf16[1536,128]{1,0:T(8,128)(2,1)S(1)}, u32[]{:S(2)}, u32[]{:S(2)}) collective-permute-start(bf16[1536,128]{1,0:T(8,128)(2,1)S(1)} %shard_map.180.mine_ref), channel_id=1, source_target_pairs={{0,1},{1,0},{2,3},{3,2},{4,5},{5,4},{6,7},{7,6},{8,9},{9,8},{10,11... | collective-permute-start | bytes 1179656 | tf_op jit(solution)/shard_map/ppermute | solution.py:79
  18.4 3.2 %copy-start.2 = (bf16[64,3,512]{2,0,1:T(8,128)(2,1)S(1)}, bf16[64,3,512]{2,0,1:T(8,128)(2,1)}, u32[]{:S(2)}) copy-start(bf16[64,3,512]{2,0,1:T(8,128)(2,1)} %param.28) | copy-start | bytes 589828
  18.4 3.2 %copy-start.3 = (bf16[512,544]{0,1:T(8,128)(2,1)S(1)}, bf16[512,544]{0,1:T(8,128)(2,1)}, u32[]{:S(2)}) copy-start(bf16[512,544]{0,1:T(8,128)(2,1)} %param.21) | copy-start | bytes 1671172
  18.4 3.2 %copy-start.7 = (s32[2,48]{1,0:T(2,128)S(1)}, s32[2,48]{1,0:T(2,128)}, u32[]{:S(2)}) copy-start(s32[2,48]{1,0:T(2,128)} %constant.4.clone.spot_ref) | copy-start | bytes 1156
  18.5 3.2 %copy-start.8 = (f32[4,512]{1,0:T(4,128)S(1)}, f32[4,512]{1,0:T(4,128)}, u32[]{:S(2)}) copy-start(f32[4,512]{1,0:T(4,128)} %taps_ref.1) | copy-start | bytes 24580
  18.5 3.2 %copy-start.12 = (f32[512]{0:T(512)S(1)}, f32[512]{0:T(512)}, u32[]{:S(2)}) copy-start(f32[512]{0:T(512)} %param.20) | copy-start | bytes 6148
  18.5 4.0 %copy-start.11 = (s32[16]{0:T(128)S(1)}, s32[16]{0:T(128)}, u32[]{:S(2)}) copy-start(s32[16]{0:T(128)} %live_ref.5) | copy-start | bytes 196
  22.2 1.3 %collective-permute-start.5 = (f32[24,544]{1,0:T(8,128)S(1)}, f32[24,544]{1,0:T(8,128)S(1)}, u32[]{:S(2)}, u32[]{:S(2)}) collective-permute-start(f32[24,544]{1,0:T(8,128)S(1)} %get-tuple-element.29), channel_id=1, source_target_pairs={{0,1},{1,0},{2,3},{3,2},{4,5},{5,4},{6,7},{7,6},{8,9},{9,8},{10,11... | collective-permute-start | bytes 156680 | tf_op jit(solution)/shard_map/ppermute | solution.py:79
  23.6 11.9 %copy-start = (bf16[64,16,512]{2,1,0:T(8,128)(2,1)S(1)}, bf16[64,16,512]{2,1,0:T(8,128)(2,1)}, u32[]{:S(2)}) copy-start(bf16[64,16,512]{2,1,0:T(8,128)(2,1)} %state_ref.5) | copy-start | bytes 3145732
  23.6 11.9 %copy-start.1 = (bf16[512,512]{1,0:T(8,128)(2,1)S(1)}, bf16[512,512]{1,0:T(8,128)(2,1)}, u32[]{:S(2)}) copy-start(bf16[512,512]{1,0:T(8,128)(2,1)} %step_weight_ref.3) | copy-start | bytes 1572868
  23.6 11.9 %copy-start.4 = (f32[16,512]{1,0:T(8,128)S(1)}, f32[16,512]{1,0:T(8,128)}, u32[]{:S(2)}) copy-start(f32[16,512]{1,0:T(8,128)} %rates_ref.5) | copy-start | bytes 98308
  23.6 11.9 %copy-start.9 = (f32[512]{0:T(512)S(1)}, f32[512]{0:T(512)}, u32[]{:S(2)}) copy-start(f32[512]{0:T(512)} %param.23) | copy-start | bytes 6148
  23.6 11.9 %copy-start.10 = (f32[512]{0:T(512)S(1)}, f32[512]{0:T(512)}, u32[]{:S(2)}) copy-start(f32[512]{0:T(512)} %param.25) | copy-start | bytes 6148
  23.7 13.1 %copy-start.6 = (s32[48,2]{1,0:T(8,128)S(1)}, s32[48,2]{1,0:T(8,128)}, u32[]{:S(2)}) copy-start(s32[48,2]{1,0:T(8,128)} %constant.7.spot_ref) | copy-start | bytes 1156
  23.7 4.3 %collective-permute-start.6 = (bf16[24,576]{1,0:T(8,128)(2,1)S(1)}, bf16[24,576]{1,0:T(8,128)(2,1)S(1)}, u32[]{:S(2)}, u32[]{:S(2)}) collective-permute-start(bf16[24,576]{1,0:T(8,128)(2,1)S(1)} %get-tuple-element.33), channel_id=1, source_target_pairs={{0,9},{1,8},{2,11},{3,10},{4,13},{5,12},{6,15},{7,14},{8,1},{9,0},... | collective-permute-start | bytes 82952 | tf_op jit(solution)/shard_map/ppermute | solution.py:79
  28.1 25.3 %copy-start.5 = (bf16[4,8192]{1,0:T(4,128)(2,1)S(1)}, bf16[4,8192]{1,0:T(4,128)(2,1)}, u32[]{:S(2)}) copy-start(bf16[4,8192]{1,0:T(4,128)(2,1)} %refs_0_.1) | copy-start | bytes 196612
  28.1 5.9 %collective-permute-start.7 = (bf16[24,576]{1,0:T(8,128)(2,1)S(1)}, bf16[24,576]{1,0:T(8,128)(2,1)S(1)}, u32[]{:S(2)}, u32[]{:S(2)}) collective-permute-start(bf16[24,576]{1,0:T(8,128)(2,1)S(1)} %get-tuple-element.35), channel_id=1, source_target_pairs={{0,3},{1,2},{2,1},{3,0},{4,7},{5,6},{6,5},{7,4},{8,11},{9,10},{10,... | collective-permute-start | bytes 82952 | tf_op jit(solution)/shard_map/ppermute | solution.py:79
  29.1 5.0 %collective-permute-start.8 = (bf16[24,576]{1,0:T(8,128)(2,1)S(1)}, bf16[24,576]{1,0:T(8,128)(2,1)S(1)}, u32[]{:S(2)}, u32[]{:S(2)}) collective-permute-start(bf16[24,576]{1,0:T(8,128)(2,1)S(1)} %get-tuple-element.35), channel_id=1, source_target_pairs={{0,5},{1,4},{2,7},{3,6},{4,1},{5,0},{6,3},{7,2},{8,13},{9,12},{10,... | collective-permute-start | bytes 82952 | tf_op jit(solution)/shard_map/ppermute | solution.py:79
  30.6 4.8 %collective-permute-start.9 = (bf16[24,576]{1,0:T(8,128)(2,1)S(1)}, bf16[24,576]{1,0:T(8,128)(2,1)S(1)}, u32[]{:S(2)}, u32[]{:S(2)}) collective-permute-start(bf16[24,576]{1,0:T(8,128)(2,1)S(1)} %get-tuple-element.35), channel_id=1, source_target_pairs={{0,6},{1,7},{2,4},{3,5},{4,2},{5,3},{6,0},{7,1},{8,14},{9,15},{10,... | collective-permute-start | bytes 82952 | tf_op jit(solution)/shard_map/ppermute | solution.py:79
  35.5 1.2 %collective-permute-start.10 = (bf16[24,576]{1,0:T(8,128)(2,1)S(1)}, bf16[24,576]{1,0:T(8,128)(2,1)S(1)}, u32[]{:S(2)}, u32[]{:S(2)}) collective-permute-start(bf16[24,576]{1,0:T(8,128)(2,1)S(1)} %get-tuple-element.36), channel_id=1, source_target_pairs={{0,1},{1,0},{2,3},{3,2},{4,5},{5,4},{6,7},{7,6},{8,9},{9,8},{10,11... | collective-permute-start | bytes 82952 | tf_op jit(solution)/shard_map/ppermute | solution.py:79
  39.1 1.8 %collective-permute-start.11 = (bf16[1536,128]{1,0:T(8,128)(2,1)S(1)}, bf16[1536,128]{1,0:T(8,128)(2,1)S(1)}, u32[]{:S(2)}, u32[]{:S(2)}) collective-permute-start(bf16[1536,128]{1,0:T(8,128)(2,1)S(1)} %get-tuple-element.42), channel_id=1, source_target_pairs={{0,1},{1,0},{2,3},{3,2},{4,5},{5,4},{6,7},{7,6},{8,9},{9,8},{10,11... | collective-permute-start | bytes 1179656 | tf_op jit(solution)/shard_map/ppermute | solution.py:79
  41.0 5.8 %collective-permute-start.12 = (bf16[384,128]{1,0:T(8,128)(2,1)S(1)}, bf16[384,128]{1,0:T(8,128)(2,1)S(1)}, u32[]{:S(2)}, u32[]{:S(2)}) collective-permute-start(bf16[384,128]{1,0:T(8,128)(2,1)S(1)} %get-tuple-element.44), channel_id=1, source_target_pairs={{0,4},{1,5},{2,6},{3,7},{4,0},{5,1},{6,2},{7,3},{8,12},{9,13},{10,... | collective-permute-start | bytes 294920 | tf_op jit(solution)/shard_map/ppermute | solution.py:79
  41.5 5.3 %collective-permute-start.13 = (bf16[384,128]{1,0:T(8,128)(2,1)S(1)}, bf16[384,128]{1,0:T(8,128)(2,1)S(1)}, u32[]{:S(2)}, u32[]{:S(2)}) collective-permute-start(bf16[384,128]{1,0:T(8,128)(2,1)S(1)} %get-tuple-element.45), channel_id=1, source_target_pairs={{0,2},{1,3},{2,0},{3,1},{4,6},{5,7},{6,4},{7,5},{8,10},{9,11},{10,... | collective-permute-start | bytes 294920 | tf_op jit(solution)/shard_map/ppermute | solution.py:79
  42.5 5.8 %collective-permute-start.14 = (bf16[384,128]{1,0:T(8,128)(2,1)S(1)}, bf16[384,128]{1,0:T(8,128)(2,1)S(1)}, u32[]{:S(2)}, u32[]{:S(2)}) collective-permute-start(bf16[384,128]{1,0:T(8,128)(2,1)S(1)} %get-tuple-element.46), channel_id=1, source_target_pairs={{0,6},{1,7},{2,4},{3,5},{4,2},{5,3},{6,0},{7,1},{8,14},{9,15},{10,... | collective-permute-start | bytes 294920 | tf_op jit(solution)/shard_map/ppermute | solution.py:79
  48.4 5.1 %collective-permute-start.15 = (bf16[192,128]{1,0:T(8,128)(2,1)S(1)}, bf16[192,128]{1,0:T(8,128)(2,1)S(1)}, u32[]{:S(2)}, u32[]{:S(2)}) collective-permute-start(bf16[192,128]{1,0:T(8,128)(2,1)S(1)} %get-tuple-element.51), channel_id=1, source_target_pairs={{0,8},{1,9},{2,10},{3,11},{4,12},{5,13},{6,14},{7,15},{8,0},{9,1},... | collective-permute-start | bytes 147464 | tf_op jit(solution)/shard_map/ppermute | solution.py:79

commit v8 on v7

--- a/solution.py
+++ b/solution.py
@@ -143,13 +143,16 @@
         )
 
 
-def spread(folded, fold_ref):
-    rows = fold_ref.shape[0] - folded.shape[0]
+def spread(folded, fold_ref, rows):
     pieces = folded.shape[0] // rows
     for r in range(rows):
         start = r * (pieces + 1)
         fold_ref[start : start + pieces] = folded[r * pieces : (r + 1) * pieces].astype(F32)
-    return rows, pieces
+    return pieces
+
+
+def fold_scratch(rows, pieces):
+    return pltpu.VMEM((-(-rows // 8) * 8 * (pieces + 1) + pieces + 1, LANES), F32)
 
 
 def norm_kernel(far_hidden_ref, far_gain_ref, out_ref, fold_ref, hidden_ref, gain_ref, sems):
@@ -182,13 +185,15 @@
 
 
 def half_kernel(mine_ref, out_ref, fold_ref):
-    rows, pieces = spread(mine_ref, fold_ref)
+    rows = out_ref.shape[0]
+    pieces = spread(mine_ref, fold_ref, rows)
     for c in range(pieces):
         out_ref[:, c * LANES : (c + 1) * LANES] = fold_ref[pl.ds(c, rows, stride=pieces + 1), :]
 
 
 def unfold_kernel(half_ref, other_ref, _, out_ref, fold_ref):
-    rows, pieces = spread(other_ref, fold_ref)
+    rows = half_ref.shape[0]
+    pieces = spread(other_ref, fold_ref, rows)
     for c in range(pieces):
         span = slice(c * LANES, (c + 1) * LANES)
         other = fold_ref[pl.ds(c, rows, stride=pieces + 1), :]
@@ -492,7 +497,8 @@
     total = parts[0][...]
     for part in parts[1:]:
         total = total + part[...].astype(F32)
-    rows, pieces = spread(total, fold_ref)
+    rows = LIVE_MAX
+    pieces = spread(total, fold_ref, rows)
     for c in range(pieces):
         span = slice(c * LANES, (c + 1) * LANES)
         wide = hidden_ref[:, span].astype(F32)
@@ -549,7 +555,7 @@
         (hidden, norm_gain.reshape(1, width)),
         far=2,
         scratch=[
-            pltpu.VMEM((slab + LIVE_MAX, LANES), F32),
+            fold_scratch(LIVE_MAX, pieces),
             pltpu.VMEM(hidden.shape, BF16),
             pltpu.VMEM((1, width), F32),
             pltpu.SemaphoreType.DMA((2,)),
@@ -565,7 +571,7 @@
             [gathered] + [swap(gathered, s, devices) for s in phase], (near_weight,)
         )
     near_weight = load((done, 1.0), near_weight)
-    folded = [pltpu.VMEM((kept // 2 * (pieces + 1), LANES), F32)]
+    folded = [fold_scratch(kept // 2, pieces)]
     half = call(half_kernel, shape((kept // 2, width)), (gathered,), scratch=folded, limit=12)
     normed = call(
         unfold_kernel,
@@ -663,7 +669,7 @@
         scratch=[
             pltpu.VMEM(half_shape, F32),
             pltpu.VMEM((kept, channels), F32),
-            pltpu.VMEM((kept * (pieces + 1), LANES), F32),
+            fold_scratch(kept, pieces),
         ],
         limit=24,
     )
@@ -693,7 +699,7 @@
         last_sum_kernel,
         shape(hidden.shape, BF16),
         (hidden,) + total,
-        scratch=[pltpu.VMEM((slab + LIVE_MAX, LANES), F32)],
+        scratch=[fold_scratch(LIVE_MAX, pieces)],
     )
     return (mixed, new_state, new_conv.transpose(1, 0, 2))
 

time: 54.3 us -> 54.3 us (level)
  no operation moved by 1% of the time
where the time goes in v8:
time: 54.3 us; the launch traced here: 54.1 us
  Pallas kernels  22.6 us (42%)
  starting transfers between devices  19.7 us (36%)
  waiting for transfers between devices  7.6 us (14%)
  matrix products  3.15 us (6%)
  between operations  0.95 us (2%)
    pallas_call x22, Pallas kernels, call(): pl.pallas_call(kernel, out_shape=outs, in_specs=[pl.BlockSpec(memory_spac...  22.6 us
    ppermute x16, starting transfers between devices, swap(): lax.ppermute(value, 'weight', [(i, i ^ shift) for i in range(devices)])  19.7 us
    ppermute x16, waiting for transfers between devices, swap(): lax.ppermute(value, 'weight', [(i, i ^ shift) for i in range(devices)])  7.6 us
    dot_general x1, matrix products, body(): jnp.einsum('rd,dbc->brc', normed, near_weight, preferred_element_type=F32)  3.15 us
  transfers between devices with their start and end apart: 16, of which 10 were waited for; matrix products, arithmetic and copies ran while one was open for 0% of the time, Pallas kernels for 32%

profile of v8, /device:TPU:0, one launch (start us, length us, event | category | flops | bytes accessed | tf_op | source)
XLA Modules:
  0.0 54.1 jit_solution(6972639970771311335)
XLA Ops:
  0.6 1.0 %shard_map.178.refs_0_ = bf16[192,128]{1,0:T(8,128)(2,1)S(1)} custom-call(bf16[4,8192]{1,0:T(4,128)(2,1)} %refs_0_.1, f32[1,8192]{1,0:T(1,128)} %bitcast.21), custom_call_target="tpu_custom_call" | custom-call | tf_op jit(solution)/shard_map/pallas_call | solution.py:100
  1.7 4.1 %collective-permute-start = (bf16[192,128]{1,0:T(8,128)(2,1)S(1)}, bf16[192,128]{1,0:T(8,128)(2,1)S(1)}, u32[]{:S(2)}, u32[]{:S(2)}) collective-permute-start(bf16[192,128]{1,0:T(8,128)(2,1)S(1)} %shard_map.178.refs_0_), channel_id=1, source_target_pairs={{0,8},{1,9},{2,10},{3,11},{4,12},{5,13},{6,14},{7,15},{8,0},{9,1},... | collective-permute-start | bytes 147464 | tf_op jit(solution)/shard_map/ppermute | solution.py:79
  5.8 2.9 %shard_map.175.refs_0_.refs_2_ = bf16[8192,2,512]{2,1,0:T(2,128)(2,1)S(1)} custom-call(bf16[8192,2,512]{2,1,0:T(2,128)(2,1)} %far_ref.7), custom_call_target="tpu_custom_call" | custom-call | tf_op jit(solution)/shard_map/pallas_call | solution.py:100
  8.7 2.6 %collective-permute-start.1 = (bf16[384,128]{1,0:T(8,128)(2,1)S(1)}, bf16[384,128]{1,0:T(8,128)(2,1)S(1)}, u32[]{:S(2)}, u32[]{:S(2)}) collective-permute-start(bf16[384,128]{1,0:T(8,128)(2,1)S(1)} %shard_map.179.refs_0_), channel_id=1, source_target_pairs={{0,6},{1,7},{2,4},{3,5},{4,2},{5,3},{6,0},{7,1},{8,14},{9,15},{10,... | collective-permute-start | bytes 294920 | tf_op jit(solution)/shard_map/ppermute | solution.py:79
  11.3 0.4 collective-permute-start.2
  11.7 0.5 collective-permute-start.3
  12.2 3.8 %shard_map.176.refs_0_.refs_4_ = bf16[8192,2,512]{2,1,0:T(2,128)(2,1)S(1)} custom-call(bf16[8192,2,512]{2,1,0:T(2,128)(2,1)} %far_ref.7, bf16[8192,2,512]{2,1,0:T(2,128)(2,1)S(1)} %shard_map.175.refs_0_.refs_2_), custom_call_target="tpu_custom_call", output_to_operand_aliasing={{}: (1, {})} | custom-call | tf_op jit(solution)/shard_map/pallas_call | solution.py:100
  16.1 0.3 collective-permute-done.2.refs_2_
  16.3 0.1 collective-permute-done.3.refs_3_
  16.5 0.1 collective-permute-start.4
  16.5 1.2 %shard_map.177._ = bf16[8192,2,512]{2,1,0:T(2,128)(2,1)S(1)} custom-call(bf16[8192,2,512]{2,1,0:T(2,128)(2,1)} %far_ref.7, bf16[8192,2,512]{2,1,0:T(2,128)(2,1)S(1)} %shard_map.176.refs_0_.refs_4_), custom_call_target="tpu_custom_call", output_to_operand_aliasing={{}: (1, {})} | custom-call | tf_op jit(solution)/shard_map/pallas_call | solution.py:100
  17.8 0.1 shard_map.181.half_ref
  17.9 0.4 collective-permute-done.4.other_ref
  18.2 0.2 shard_map.182
  18.4 0.0 copy-start.7
  18.5 3.1 %fusion.2.both_ref = f32[2,48,512]{2,1,0:T(8,128)S(1)} fusion(bf16[8192,2,512]{2,1,0:T(2,128)(2,1)S(1)} %shard_map.177._, bf16[48,8192]{1,0:T(8,128)(2,1)S(1)} %shard_map.182), kind=kOutput, calls=%fused_computation.2 | convolution fusion | flops 805306368 | bytes 17760256 | tf_op jit(solution)/shard_map/rd,dbc->brc/dot_general | solution.py:584
  21.6 0.0 copy-done.2
  21.7 0.5 shard_map.183
  22.2 0.2 collective-permute-start.5
  22.4 0.8 %shard_map.184 = (f32[48,512]{1,0:T(8,128)S(1)}, f32[48,128]{1,0:T(8,128)S(1)}, f32[48,512]{1,0:T(8,128)S(1)}) custom-call(s32[16]{0:T(128)S(1)} %copy-done.11, f32[2,48,512]{2,1,0:T(8,128)S(1)} %fusion.2.both_ref, s32[2,48]{1,0:T(2,128)S(1)} %copy-done.7, bf16[48,512]{1,0:T(8,128)(2,1)S(1)} %get-tuple-element.30.mixed_ref), custom_call_target="tpu_custom_call" | custom-call | tf_op jit(solution)/shard_map/pallas_call | solution.py:100
  23.3 0.3 collective-permute-done.5.refs_1_
  23.5 0.1 shard_map.185
  23.7 0.0 copy-start.6
  23.7 1.9 %collective-permute-start.6 = (bf16[24,576]{1,0:T(8,128)(2,1)S(1)}, bf16[24,576]{1,0:T(8,128)(2,1)S(1)}, u32[]{:S(2)}, u32[]{:S(2)}) collective-permute-start(bf16[24,576]{1,0:T(8,128)(2,1)S(1)} %get-tuple-element.33), channel_id=1, source_target_pairs={{0,9},{1,8},{2,11},{3,10},{4,13},{5,12},{6,15},{7,14},{8,1},{9,0},... | collective-permute-start | bytes 82952 | tf_op jit(solution)/shard_map/ppermute | solution.py:79
  25.6 1.7 %shard_map.186.refs_2_.first_ref = bf16[512,2560]{1,0:T(8,128)(2,1)S(1)} custom-call(bf16[512,8192]{1,0:T(8,128)(2,1)} %far_ref.9), custom_call_target="tpu_custom_call" | custom-call | tf_op jit(solution)/shard_map/pallas_call | solution.py:100
  27.3 0.7 %collective-permute-done.6.refs_1_ = bf16[24,576]{1,0:T(8,128)(2,1)S(1)} collective-permute-done((bf16[24,576]{1,0:T(8,128)(2,1)S(1)}, bf16[24,576]{1,0:T(8,128)(2,1)S(1)}, u32[]{:S(2)}, u32[]{:S(2)}) %collective-permute-start.6) | collective-permute-done | bytes 27680 | tf_op jit(solution)/shard_map/ppermute | solution.py:79
  28.0 0.2 shard_map.187
  28.1 0.9 %collective-permute-start.7 = (bf16[24,576]{1,0:T(8,128)(2,1)S(1)}, bf16[24,576]{1,0:T(8,128)(2,1)S(1)}, u32[]{:S(2)}, u32[]{:S(2)}) collective-permute-start(bf16[24,576]{1,0:T(8,128)(2,1)S(1)} %get-tuple-element.35), channel_id=1, source_target_pairs={{0,3},{1,2},{2,1},{3,0},{4,7},{5,6},{6,5},{7,4},{8,11},{9,10},{10,... | collective-permute-start | bytes 82952 | tf_op jit(solution)/shard_map/ppermute | solution.py:79
  29.1 1.5 %collective-permute-start.8 = (bf16[24,576]{1,0:T(8,128)(2,1)S(1)}, bf16[24,576]{1,0:T(8,128)(2,1)S(1)}, u32[]{:S(2)}, u32[]{:S(2)}) collective-permute-start(bf16[24,576]{1,0:T(8,128)(2,1)S(1)} %get-tuple-element.35), channel_id=1, source_target_pairs={{0,5},{1,4},{2,7},{3,6},{4,1},{5,0},{6,3},{7,2},{8,13},{9,12},{10,... | collective-permute-start | bytes 82952 | tf_op jit(solution)/shard_map/ppermute | solution.py:79
  30.6 0.7 %collective-permute-start.9 = (bf16[24,576]{1,0:T(8,128)(2,1)S(1)}, bf16[24,576]{1,0:T(8,128)(2,1)S(1)}, u32[]{:S(2)}, u32[]{:S(2)}) collective-permute-start(bf16[24,576]{1,0:T(8,128)(2,1)S(1)} %get-tuple-element.35), channel_id=1, source_target_pairs={{0,6},{1,7},{2,4},{3,5},{4,2},{5,3},{6,0},{7,1},{8,14},{9,15},{10,... | collective-permute-start | bytes 82952 | tf_op jit(solution)/shard_map/ppermute | solution.py:79
  31.3 2.7 %shard_map.188.refs_4_.last_ref = bf16[512,5632]{1,0:T(8,128)(2,1)S(1)} custom-call(bf16[512,8192]{1,0:T(8,128)(2,1)} %far_ref.9), custom_call_target="tpu_custom_call" | custom-call | tf_op jit(solution)/shard_map/pallas_call | solution.py:100
  34.0 1.3 %collective-permute-done.9.refs_3_ = bf16[24,576]{1,0:T(8,128)(2,1)S(1)} collective-permute-done((bf16[24,576]{1,0:T(8,128)(2,1)S(1)}, bf16[24,576]{1,0:T(8,128)(2,1)S(1)}, u32[]{:S(2)}, u32[]{:S(2)}) %collective-permute-start.9) | collective-permute-done | bytes 27680 | tf_op jit(solution)/shard_map/ppermute | solution.py:79
  35.4 0.2 shard_map.189
  35.6 0.5 shard_map.190
  36.1 0.6 %collective-permute-done.10.other_ref = bf16[24,576]{1,0:T(8,128)(2,1)S(1)} collective-permute-done((bf16[24,576]{1,0:T(8,128)(2,1)S(1)}, bf16[24,576]{1,0:T(8,128)(2,1)S(1)}, u32[]{:S(2)}, u32[]{:S(2)}) %collective-permute-start.10) | collective-permute-done | bytes 27680 | tf_op jit(solution)/shard_map/ppermute | solution.py:79
  36.7 2.3 %shard_map.191 = (f32[1536,128]{1,0:T(8,128)S(1)}, bf16[1536,128]{1,0:T(8,128)(2,1)S(1)}, f32[24,512]{1,0:T(8,128)S(1)}) custom-call(bf16[24,576]{1,0:T(8,128)(2,1)S(1)} %collective-permute-done.10.other_ref, f32[48,512]{1,0:T(8,128)S(1)} %get-tuple-element.37.x_ref, f32[48,512]{1,0:T(8,128)S(1)} %get-tuple-element.31.refs_2_.gate_ref, ...), custom_call_target="tpu_custom_call" | custom-call | tf_op jit(solution)/shard_map/pallas_call | solution.py:100
  39.1 0.2 collective-permute-start.11
  39.3 1.6 %collective-permute-done.11.refs_1_ = bf16[1536,128]{1,0:T(8,128)(2,1)S(1)} collective-permute-done((bf16[1536,128]{1,0:T(8,128)(2,1)S(1)}, bf16[1536,128]{1,0:T(8,128)(2,1)S(1)}, u32[]{:S(2)}, u32[]{:S(2)}) %collective-permute-start.11) | collective-permute-done | bytes 393248 | tf_op jit(solution)/shard_map/ppermute | solution.py:79
  40.9 0.1 shard_map.192
  41.0 0.5 collective-permute-start.12
  41.5 1.0 %collective-permute-start.13 = (bf16[384,128]{1,0:T(8,128)(2,1)S(1)}, bf16[384,128]{1,0:T(8,128)(2,1)S(1)}, u32[]{:S(2)}, u32[]{:S(2)}) collective-permute-start(bf16[384,128]{1,0:T(8,128)(2,1)S(1)} %get-tuple-element.45), channel_id=1, source_target_pairs={{0,2},{1,3},{2,0},{3,1},{4,6},{5,7},{6,4},{7,5},{8,10},{9,11},{10,... | collective-permute-start | bytes 294920 | tf_op jit(solution)/shard_map/ppermute | solution.py:79
  42.5 2.1 %collective-permute-start.14 = (bf16[384,128]{1,0:T(8,128)(2,1)S(1)}, bf16[384,128]{1,0:T(8,128)(2,1)S(1)}, u32[]{:S(2)}, u32[]{:S(2)}) collective-permute-start(bf16[384,128]{1,0:T(8,128)(2,1)S(1)} %get-tuple-element.46), channel_id=1, source_target_pairs={{0,6},{1,7},{2,4},{3,5},{4,2},{5,3},{6,0},{7,1},{8,14},{9,15},{10,... | collective-permute-start | bytes 294920 | tf_op jit(solution)/shard_map/ppermute | solution.py:79
  44.5 2.2 %shard_map.193 = (bf16[64,16,512]{2,1,0:T(8,128)(2,1)}, f32[8,128]{1,0:T(8,128)S(1)}) custom-call(s32[16]{0:T(128)S(1)} %copy-done.11, f32[24,544]{1,0:T(8,128)S(1)} %get-tuple-element.39.low_ref.mine_ref, bf16[24,576]{1,0:T(8,128)(2,1)S(1)} %collective-permute-done.10.other_ref, f32[48,512]{1,0:T(8,128)S(1)} %get-tuple-element.37.x_ref, ...), custom_call_target="tpu_custom_call" | custom-call | tf_op jit(solution)/shard_map/pallas_call | solution.py:100
  46.7 1.6 %collective-permute-done.14.refs_3_ = bf16[384,128]{1,0:T(8,128)(2,1)S(1)} collective-permute-done((bf16[384,128]{1,0:T(8,128)(2,1)S(1)}, bf16[384,128]{1,0:T(8,128)(2,1)S(1)}, u32[]{:S(2)}, u32[]{:S(2)}) %collective-permute-start.14) | collective-permute-done | bytes 98336 | tf_op jit(solution)/shard_map/ppermute | solution.py:79
  48.4 2.9 %collective-permute-start.15 = (bf16[192,128]{1,0:T(8,128)(2,1)S(1)}, bf16[192,128]{1,0:T(8,128)(2,1)S(1)}, u32[]{:S(2)}, u32[]{:S(2)}) collective-permute-start(bf16[192,128]{1,0:T(8,128)(2,1)S(1)} %get-tuple-element.51), channel_id=1, source_target_pairs={{0,8},{1,9},{2,10},{3,11},{4,12},{5,13},{6,14},{7,15},{8,0},{9,1},... | collective-permute-start | bytes 147464 | tf_op jit(solution)/shard_map/ppermute | solution.py:79
  51.2 1.4 %shard_map.196 = bf16[3,64,512]{2,1,0:T(8,128)(2,1)} custom-call(s32[16]{0:T(128)S(1)} %copy-done.11, f32[2,48,512]{2,1,0:T(8,128)S(1)} %fusion.2.both_ref, s32[2,48]{1,0:T(2,128)S(1)} %copy-done.7, bf16[3,64,512]{2,1,0:T(8,128)(2,1)S(1)} %bitcast.13), custom_call_target="tpu_custom_call" | custom-call | tf_op jit(solution)/shard_map/pallas_call | solution.py:100
  52.6 0.8 %collective-permute-done.15.refs_2_ = bf16[192,128]{1,0:T(8,128)(2,1)S(1)} collective-permute-done((bf16[192,128]{1,0:T(8,128)(2,1)S(1)}, bf16[192,128]{1,0:T(8,128)(2,1)S(1)}, u32[]{:S(2)}, u32[]{:S(2)}) %collective-permute-start.15) | collective-permute-done | bytes 49184 | tf_op jit(solution)/shard_map/ppermute | solution.py:79
  53.4 0.7 %shard_map.195 = bf16[4,8192]{1,0:T(4,128)(2,1)} custom-call(bf16[4,8192]{1,0:T(4,128)(2,1)S(1)} %copy-done.5, f32[192,128]{1,0:T(8,128)S(1)} %get-tuple-element.50.refs_1_, bf16[192,128]{1,0:T(8,128)(2,1)S(1)} %collective-permute-done.15.refs_2_), custom_call_target="tpu_custom_call" | custom-call | tf_op jit(solution)/shard_map/pallas_call | solution.py:100
  (33 shorter events, 0.2 us)
Async XLA Ops:
  1.7 7.0 %collective-permute-start = (bf16[192,128]{1,0:T(8,128)(2,1)S(1)}, bf16[192,128]{1,0:T(8,128)(2,1)S(1)}, u32[]{:S(2)}, u32[]{:S(2)}) collective-permute-start(bf16[192,128]{1,0:T(8,128)(2,1)S(1)} %shard_map.178.refs_0_), channel_id=1, source_target_pairs={{0,8},{1,9},{2,10},{3,11},{4,12},{5,13},{6,14},{7,15},{8,0},{9,1},... | collective-permute-start | bytes 147464 | tf_op jit(solution)/shard_map/ppermute | solution.py:79
  8.7 7.4 %collective-permute-start.1 = (bf16[384,128]{1,0:T(8,128)(2,1)S(1)}, bf16[384,128]{1,0:T(8,128)(2,1)S(1)}, u32[]{:S(2)}, u32[]{:S(2)}) collective-permute-start(bf16[384,128]{1,0:T(8,128)(2,1)S(1)} %shard_map.179.refs_0_), channel_id=1, source_target_pairs={{0,6},{1,7},{2,4},{3,5},{4,2},{5,3},{6,0},{7,1},{8,14},{9,15},{10,... | collective-permute-start | bytes 294920 | tf_op jit(solution)/shard_map/ppermute | solution.py:79
  11.3 5.0 %collective-permute-start.2 = (bf16[384,128]{1,0:T(8,128)(2,1)S(1)}, bf16[384,128]{1,0:T(8,128)(2,1)S(1)}, u32[]{:S(2)}, u32[]{:S(2)}) collective-permute-start(bf16[384,128]{1,0:T(8,128)(2,1)S(1)} %shard_map.179.refs_0_), channel_id=1, source_target_pairs={{0,4},{1,5},{2,6},{3,7},{4,0},{5,1},{6,2},{7,3},{8,12},{9,13},{10,... | collective-permute-start | bytes 294920 | tf_op jit(solution)/shard_map/ppermute | solution.py:79
  11.7 4.7 %collective-permute-start.3 = (bf16[384,128]{1,0:T(8,128)(2,1)S(1)}, bf16[384,128]{1,0:T(8,128)(2,1)S(1)}, u32[]{:S(2)}, u32[]{:S(2)}) collective-permute-start(bf16[384,128]{1,0:T(8,128)(2,1)S(1)} %shard_map.179.refs_0_), channel_id=1, source_target_pairs={{0,2},{1,3},{2,0},{3,1},{4,6},{5,7},{6,4},{7,5},{8,10},{9,11},{10,... | collective-permute-start | bytes 294920 | tf_op jit(solution)/shard_map/ppermute | solution.py:79
  16.5 1.8 %collective-permute-start.4 = (bf16[1536,128]{1,0:T(8,128)(2,1)S(1)}, bf16[1536,128]{1,0:T(8,128)(2,1)S(1)}, u32[]{:S(2)}, u32[]{:S(2)}) collective-permute-start(bf16[1536,128]{1,0:T(8,128)(2,1)S(1)} %shard_map.180.mine_ref), channel_id=1, source_target_pairs={{0,1},{1,0},{2,3},{3,2},{4,5},{5,4},{6,7},{7,6},{8,9},{9,8},{10,11... | collective-permute-start | bytes 1179656 | tf_op jit(solution)/shard_map/ppermute | solution.py:79
  18.4 3.2 %copy-start.2 = (bf16[64,3,512]{2,0,1:T(8,128)(2,1)S(1)}, bf16[64,3,512]{2,0,1:T(8,128)(2,1)}, u32[]{:S(2)}) copy-start(bf16[64,3,512]{2,0,1:T(8,128)(2,1)} %param.28) | copy-start | bytes 589828
  18.4 3.2 %copy-start.3 = (bf16[512,544]{0,1:T(8,128)(2,1)S(1)}, bf16[512,544]{0,1:T(8,128)(2,1)}, u32[]{:S(2)}) copy-start(bf16[512,544]{0,1:T(8,128)(2,1)} %param.21) | copy-start | bytes 1671172
  18.4 3.2 %copy-start.7 = (s32[2,48]{1,0:T(2,128)S(1)}, s32[2,48]{1,0:T(2,128)}, u32[]{:S(2)}) copy-start(s32[2,48]{1,0:T(2,128)} %constant.4.clone.spot_ref) | copy-start | bytes 1156
  18.5 3.2 %copy-start.8 = (f32[4,512]{1,0:T(4,128)S(1)}, f32[4,512]{1,0:T(4,128)}, u32[]{:S(2)}) copy-start(f32[4,512]{1,0:T(4,128)} %taps_ref.1) | copy-start | bytes 24580
  18.5 3.2 %copy-start.12 = (f32[512]{0:T(512)S(1)}, f32[512]{0:T(512)}, u32[]{:S(2)}) copy-start(f32[512]{0:T(512)} %param.20) | copy-start | bytes 6148
  18.5 4.0 %copy-start.11 = (s32[16]{0:T(128)S(1)}, s32[16]{0:T(128)}, u32[]{:S(2)}) copy-start(s32[16]{0:T(128)} %live_ref.5) | copy-start | bytes 196
  22.2 1.3 %collective-permute-start.5 = (f32[24,544]{1,0:T(8,128)S(1)}, f32[24,544]{1,0:T(8,128)S(1)}, u32[]{:S(2)}, u32[]{:S(2)}) collective-permute-start(f32[24,544]{1,0:T(8,128)S(1)} %get-tuple-element.29), channel_id=1, source_target_pairs={{0,1},{1,0},{2,3},{3,2},{4,5},{5,4},{6,7},{7,6},{8,9},{9,8},{10,11... | collective-permute-start | bytes 156680 | tf_op jit(solution)/shard_map/ppermute | solution.py:79
  23.6 11.9 %copy-start = (bf16[64,16,512]{2,1,0:T(8,128)(2,1)S(1)}, bf16[64,16,512]{2,1,0:T(8,128)(2,1)}, u32[]{:S(2)}) copy-start(bf16[64,16,512]{2,1,0:T(8,128)(2,1)} %state_ref.5) | copy-start | bytes 3145732
  23.6 11.9 %copy-start.1 = (bf16[512,512]{1,0:T(8,128)(2,1)S(1)}, bf16[512,512]{1,0:T(8,128)(2,1)}, u32[]{:S(2)}) copy-start(bf16[512,512]{1,0:T(8,128)(2,1)} %step_weight_ref.3) | copy-start | bytes 1572868
  23.6 11.9 %copy-start.4 = (f32[16,512]{1,0:T(8,128)S(1)}, f32[16,512]{1,0:T(8,128)}, u32[]{:S(2)}) copy-start(f32[16,512]{1,0:T(8,128)} %rates_ref.5) | copy-start | bytes 98308
  23.6 11.9 %copy-start.9 = (f32[512]{0:T(512)S(1)}, f32[512]{0:T(512)}, u32[]{:S(2)}) copy-start(f32[512]{0:T(512)} %param.23) | copy-start | bytes 6148
  23.6 11.9 %copy-start.10 = (f32[512]{0:T(512)S(1)}, f32[512]{0:T(512)}, u32[]{:S(2)}) copy-start(f32[512]{0:T(512)} %param.25) | copy-start | bytes 6148
  23.7 13.1 %copy-start.6 = (s32[48,2]{1,0:T(8,128)S(1)}, s32[48,2]{1,0:T(8,128)}, u32[]{:S(2)}) copy-start(s32[48,2]{1,0:T(8,128)} %constant.7.spot_ref) | copy-start | bytes 1156
  23.7 4.3 %collective-permute-start.6 = (bf16[24,576]{1,0:T(8,128)(2,1)S(1)}, bf16[24,576]{1,0:T(8,128)(2,1)S(1)}, u32[]{:S(2)}, u32[]{:S(2)}) collective-permute-start(bf16[24,576]{1,0:T(8,128)(2,1)S(1)} %get-tuple-element.33), channel_id=1, source_target_pairs={{0,9},{1,8},{2,11},{3,10},{4,13},{5,12},{6,15},{7,14},{8,1},{9,0},... | collective-permute-start | bytes 82952 | tf_op jit(solution)/shard_map/ppermute | solution.py:79
  28.1 25.3 %copy-start.5 = (bf16[4,8192]{1,0:T(4,128)(2,1)S(1)}, bf16[4,8192]{1,0:T(4,128)(2,1)}, u32[]{:S(2)}) copy-start(bf16[4,8192]{1,0:T(4,128)(2,1)} %refs_0_.1) | copy-start | bytes 196612
  28.1 5.9 %collective-permute-start.7 = (bf16[24,576]{1,0:T(8,128)(2,1)S(1)}, bf16[24,576]{1,0:T(8,128)(2,1)S(1)}, u32[]{:S(2)}, u32[]{:S(2)}) collective-permute-start(bf16[24,576]{1,0:T(8,128)(2,1)S(1)} %get-tuple-element.35), channel_id=1, source_target_pairs={{0,3},{1,2},{2,1},{3,0},{4,7},{5,6},{6,5},{7,4},{8,11},{9,10},{10,... | collective-permute-start | bytes 82952 | tf_op jit(solution)/shard_map/ppermute | solution.py:79
  29.1 5.0 %collective-permute-start.8 = (bf16[24,576]{1,0:T(8,128)(2,1)S(1)}, bf16[24,576]{1,0:T(8,128)(2,1)S(1)}, u32[]{:S(2)}, u32[]{:S(2)}) collective-permute-start(bf16[24,576]{1,0:T(8,128)(2,1)S(1)} %get-tuple-element.35), channel_id=1, source_target_pairs={{0,5},{1,4},{2,7},{3,6},{4,1},{5,0},{6,3},{7,2},{8,13},{9,12},{10,... | collective-permute-start | bytes 82952 | tf_op jit(solution)/shard_map/ppermute | solution.py:79
  30.6 4.8 %collective-permute-start.9 = (bf16[24,576]{1,0:T(8,128)(2,1)S(1)}, bf16[24,576]{1,0:T(8,128)(2,1)S(1)}, u32[]{:S(2)}, u32[]{:S(2)}) collective-permute-start(bf16[24,576]{1,0:T(8,128)(2,1)S(1)} %get-tuple-element.35), channel_id=1, source_target_pairs={{0,6},{1,7},{2,4},{3,5},{4,2},{5,3},{6,0},{7,1},{8,14},{9,15},{10,... | collective-permute-start | bytes 82952 | tf_op jit(solution)/shard_map/ppermute | solution.py:79
  35.5 1.2 %collective-permute-start.10 = (bf16[24,576]{1,0:T(8,128)(2,1)S(1)}, bf16[24,576]{1,0:T(8,128)(2,1)S(1)}, u32[]{:S(2)}, u32[]{:S(2)}) collective-permute-start(bf16[24,576]{1,0:T(8,128)(2,1)S(1)} %get-tuple-element.36), channel_id=1, source_target_pairs={{0,1},{1,0},{2,3},{3,2},{4,5},{5,4},{6,7},{7,6},{8,9},{9,8},{10,11... | collective-permute-start | bytes 82952 | tf_op jit(solution)/shard_map/ppermute | solution.py:79
  39.1 1.8 %collective-permute-start.11 = (bf16[1536,128]{1,0:T(8,128)(2,1)S(1)}, bf16[1536,128]{1,0:T(8,128)(2,1)S(1)}, u32[]{:S(2)}, u32[]{:S(2)}) collective-permute-start(bf16[1536,128]{1,0:T(8,128)(2,1)S(1)} %get-tuple-element.42), channel_id=1, source_target_pairs={{0,1},{1,0},{2,3},{3,2},{4,5},{5,4},{6,7},{7,6},{8,9},{9,8},{10,11... | collective-permute-start | bytes 1179656 | tf_op jit(solution)/shard_map/ppermute | solution.py:79
  41.0 5.8 %collective-permute-start.12 = (bf16[384,128]{1,0:T(8,128)(2,1)S(1)}, bf16[384,128]{1,0:T(8,128)(2,1)S(1)}, u32[]{:S(2)}, u32[]{:S(2)}) collective-permute-start(bf16[384,128]{1,0:T(8,128)(2,1)S(1)} %get-tuple-element.44), channel_id=1, source_target_pairs={{0,4},{1,5},{2,6},{3,7},{4,0},{5,1},{6,2},{7,3},{8,12},{9,13},{10,... | collective-permute-start | bytes 294920 | tf_op jit(solution)/shard_map/ppermute | solution.py:79
  41.5 5.2 %collective-permute-start.13 = (bf16[384,128]{1,0:T(8,128)(2,1)S(1)}, bf16[384,128]{1,0:T(8,128)(2,1)S(1)}, u32[]{:S(2)}, u32[]{:S(2)}) collective-permute-start(bf16[384,128]{1,0:T(8,128)(2,1)S(1)} %get-tuple-element.45), channel_id=1, source_target_pairs={{0,2},{1,3},{2,0},{3,1},{4,6},{5,7},{6,4},{7,5},{8,10},{9,11},{10,... | collective-permute-start | bytes 294920 | tf_op jit(solution)/shard_map/ppermute | solution.py:79
  42.5 5.8 %collective-permute-start.14 = (bf16[384,128]{1,0:T(8,128)(2,1)S(1)}, bf16[384,128]{1,0:T(8,128)(2,1)S(1)}, u32[]{:S(2)}, u32[]{:S(2)}) collective-permute-start(bf16[384,128]{1,0:T(8,128)(2,1)S(1)} %get-tuple-element.46), channel_id=1, source_target_pairs={{0,6},{1,7},{2,4},{3,5},{4,2},{5,3},{6,0},{7,1},{8,14},{9,15},{10,... | collective-permute-start | bytes 294920 | tf_op jit(solution)/shard_map/ppermute | solution.py:79
  48.4 5.1 %collective-permute-start.15 = (bf16[192,128]{1,0:T(8,128)(2,1)S(1)}, bf16[192,128]{1,0:T(8,128)(2,1)S(1)}, u32[]{:S(2)}, u32[]{:S(2)}) collective-permute-start(bf16[192,128]{1,0:T(8,128)(2,1)S(1)} %get-tuple-element.51), channel_id=1, source_target_pairs={{0,8},{1,9},{2,10},{3,11},{4,12},{5,13},{6,14},{7,15},{8,0},{9,1},... | collective-permute-start | bytes 147464 | tf_op jit(solution)/shard_map/ppermute | solution.py:79

commit v9 on v8

--- a/solution.py
+++ b/solution.py
@@ -95,7 +95,7 @@
     return jax.ShapeDtypeStruct(dims, kind)
 
 
-def call(kernel, outs, operands, scalars=0, far=0, scratch=(), limit=8, after=(), aliases=None):
+def call(kernel, outs, operands, scalars=0, far=0, scratch=(), limit=8, after=(), aliases=None, whole=False):
     many = isinstance(outs, tuple)
     return pl.pallas_call(
         kernel,
@@ -103,7 +103,11 @@
         in_specs=[pl.BlockSpec(memory_space=pltpu.SMEM)] * scalars
         + vmem(len(operands) - scalars - far)
         + [pl.BlockSpec(memory_space=pl.ANY)] * (far + len(after)),
-        out_specs=tuple(vmem(len(outs))) if many else vmem(1)[0],
+        out_specs=pl.BlockSpec(memory_space=pl.ANY)
+        if whole
+        else tuple(vmem(len(outs)))
+        if many
+        else vmem(1)[0],
         scratch_shapes=list(scratch),
         input_output_aliases=aliases or {},
         compiler_params=pltpu.CompilerParams(vmem_limit_bytes=limit * MIB),
@@ -546,6 +550,7 @@
             scratch=[pltpu.SemaphoreType.DMA((4,))],
             limit=43,
             after=() if so_far is None else (so_far,),
+            whole=True,
             aliases={} if so_far is None else {1: 0},
         )
 
@@ -637,6 +642,7 @@
             far=1,
             scratch=[pltpu.SemaphoreType.DMA((4,))],
             limit=50,
+            whole=True,
         )
         for start, count in ((0, first_columns), (first_columns, width - first_columns))
     ]

time: 54.3 us -> 54.3 us (level)
  no operation moved by 1% of the time
where the time goes in v9:
time: 54.3 us; the launch traced here: 54.1 us
  Pallas kernels  22.6 us (42%)
  starting transfers between devices  19.7 us (36%)
  waiting for transfers between devices  7.6 us (14%)
  matrix products  3.15 us (6%)
  between operations  0.95 us (2%)
    pallas_call x22, Pallas kernels, call(): pl.pallas_call(kernel, out_shape=outs, in_specs=[pl.BlockSpec(memory_spac...  22.6 us
    ppermute x16, starting transfers between devices, swap(): lax.ppermute(value, 'weight', [(i, i ^ shift) for i in range(devices)])  19.7 us
    ppermute x16, waiting for transfers between devices, swap(): lax.ppermute(value, 'weight', [(i, i ^ shift) for i in range(devices)])  7.6 us
    dot_general x1, matrix products, body(): jnp.einsum('rd,dbc->brc', normed, near_weight, preferred_element_type=F32)  3.15 us
  transfers between devices with their start and end apart: 16, of which 10 were waited for; matrix products, arithmetic and copies ran while one was open for 0% of the time, Pallas kernels for 32%

profile of v9, /device:TPU:0, one launch (start us, length us, event | category | flops | bytes accessed | tf_op | source)
XLA Modules:
  0.0 54.1 jit_solution(6972639970771311335)
XLA Ops:
  0.6 1.0 %shard_map.178.refs_0_ = bf16[192,128]{1,0:T(8,128)(2,1)S(1)} custom-call(bf16[4,8192]{1,0:T(4,128)(2,1)} %refs_0_.1, f32[1,8192]{1,0:T(1,128)} %bitcast.21), custom_call_target="tpu_custom_call" | custom-call | tf_op jit(solution)/shard_map/pallas_call | solution.py:100
  1.7 4.1 %collective-permute-start = (bf16[192,128]{1,0:T(8,128)(2,1)S(1)}, bf16[192,128]{1,0:T(8,128)(2,1)S(1)}, u32[]{:S(2)}, u32[]{:S(2)}) collective-permute-start(bf16[192,128]{1,0:T(8,128)(2,1)S(1)} %shard_map.178.refs_0_), channel_id=1, source_target_pairs={{0,8},{1,9},{2,10},{3,11},{4,12},{5,13},{6,14},{7,15},{8,0},{9,1},... | collective-permute-start | bytes 147464 | tf_op jit(solution)/shard_map/ppermute | solution.py:79
  5.8 2.9 %shard_map.175.refs_0_.refs_2_ = bf16[8192,2,512]{2,1,0:T(2,128)(2,1)S(1)} custom-call(bf16[8192,2,512]{2,1,0:T(2,128)(2,1)} %far_ref.7), custom_call_target="tpu_custom_call" | custom-call | tf_op jit(solution)/shard_map/pallas_call | solution.py:100
  8.7 2.6 %collective-permute-start.1 = (bf16[384,128]{1,0:T(8,128)(2,1)S(1)}, bf16[384,128]{1,0:T(8,128)(2,1)S(1)}, u32[]{:S(2)}, u32[]{:S(2)}) collective-permute-start(bf16[384,128]{1,0:T(8,128)(2,1)S(1)} %shard_map.179.refs_0_), channel_id=1, source_target_pairs={{0,6},{1,7},{2,4},{3,5},{4,2},{5,3},{6,0},{7,1},{8,14},{9,15},{10,... | collective-permute-start | bytes 294920 | tf_op jit(solution)/shard_map/ppermute | solution.py:79
  11.3 0.4 collective-permute-start.2
  11.7 0.5 collective-permute-start.3
  12.2 3.8 %shard_map.176.refs_0_.refs_4_ = bf16[8192,2,512]{2,1,0:T(2,128)(2,1)S(1)} custom-call(bf16[8192,2,512]{2,1,0:T(2,128)(2,1)} %far_ref.7, bf16[8192,2,512]{2,1,0:T(2,128)(2,1)S(1)} %shard_map.175.refs_0_.refs_2_), custom_call_target="tpu_custom_call", output_to_operand_aliasing={{}: (1, {})} | custom-call | tf_op jit(solution)/shard_map/pallas_call | solution.py:100
  16.1 0.3 collective-permute-done.2.refs_2_
  16.3 0.1 collective-permute-done.3.refs_3_
  16.5 0.1 collective-permute-start.4
  16.5 1.2 %shard_map.177._ = bf16[8192,2,512]{2,1,0:T(2,128)(2,1)S(1)} custom-call(bf16[8192,2,512]{2,1,0:T(2,128)(2,1)} %far_ref.7, bf16[8192,2,512]{2,1,0:T(2,128)(2,1)S(1)} %shard_map.176.refs_0_.refs_4_), custom_call_target="tpu_custom_call", output_to_operand_aliasing={{}: (1, {})} | custom-call | tf_op jit(solution)/shard_map/pallas_call | solution.py:100
  17.8 0.1 shard_map.181.half_ref
  17.9 0.4 collective-permute-done.4.other_ref
  18.2 0.2 shard_map.182
  18.4 0.0 copy-start.7
  18.5 3.1 %fusion.2.both_ref = f32[2,48,512]{2,1,0:T(8,128)S(1)} fusion(bf16[8192,2,512]{2,1,0:T(2,128)(2,1)S(1)} %shard_map.177._, bf16[48,8192]{1,0:T(8,128)(2,1)S(1)} %shard_map.182), kind=kOutput, calls=%fused_computation.2 | convolution fusion | flops 805306368 | bytes 17760256 | tf_op jit(solution)/shard_map/rd,dbc->brc/dot_general | solution.py:589
  21.6 0.0 copy-done.2
  21.7 0.5 shard_map.183
  22.2 0.2 collective-permute-start.5
  22.4 0.8 %shard_map.184 = (f32[48,512]{1,0:T(8,128)S(1)}, f32[48,128]{1,0:T(8,128)S(1)}, f32[48,512]{1,0:T(8,128)S(1)}) custom-call(s32[16]{0:T(128)S(1)} %copy-done.11, f32[2,48,512]{2,1,0:T(8,128)S(1)} %fusion.2.both_ref, s32[2,48]{1,0:T(2,128)S(1)} %copy-done.7, bf16[48,512]{1,0:T(8,128)(2,1)S(1)} %get-tuple-element.30.mixed_ref), custom_call_target="tpu_custom_call" | custom-call | tf_op jit(solution)/shard_map/pallas_call | solution.py:100
  23.3 0.3 collective-permute-done.5.refs_1_
  23.5 0.1 shard_map.185
  23.7 0.0 copy-start.6
  23.7 1.9 %collective-permute-start.6 = (bf16[24,576]{1,0:T(8,128)(2,1)S(1)}, bf16[24,576]{1,0:T(8,128)(2,1)S(1)}, u32[]{:S(2)}, u32[]{:S(2)}) collective-permute-start(bf16[24,576]{1,0:T(8,128)(2,1)S(1)} %get-tuple-element.33), channel_id=1, source_target_pairs={{0,9},{1,8},{2,11},{3,10},{4,13},{5,12},{6,15},{7,14},{8,1},{9,0},... | collective-permute-start | bytes 82952 | tf_op jit(solution)/shard_map/ppermute | solution.py:79
  25.6 1.7 %shard_map.186.refs_2_.first_ref = bf16[512,2560]{1,0:T(8,128)(2,1)S(1)} custom-call(bf16[512,8192]{1,0:T(8,128)(2,1)} %far_ref.9), custom_call_target="tpu_custom_call" | custom-call | tf_op jit(solution)/shard_map/pallas_call | solution.py:100
  27.3 0.7 %collective-permute-done.6.refs_1_ = bf16[24,576]{1,0:T(8,128)(2,1)S(1)} collective-permute-done((bf16[24,576]{1,0:T(8,128)(2,1)S(1)}, bf16[24,576]{1,0:T(8,128)(2,1)S(1)}, u32[]{:S(2)}, u32[]{:S(2)}) %collective-permute-start.6) | collective-permute-done | bytes 27680 | tf_op jit(solution)/shard_map/ppermute | solution.py:79
  28.0 0.2 shard_map.187
  28.1 0.9 %collective-permute-start.7 = (bf16[24,576]{1,0:T(8,128)(2,1)S(1)}, bf16[24,576]{1,0:T(8,128)(2,1)S(1)}, u32[]{:S(2)}, u32[]{:S(2)}) collective-permute-start(bf16[24,576]{1,0:T(8,128)(2,1)S(1)} %get-tuple-element.35), channel_id=1, source_target_pairs={{0,3},{1,2},{2,1},{3,0},{4,7},{5,6},{6,5},{7,4},{8,11},{9,10},{10,... | collective-permute-start | bytes 82952 | tf_op jit(solution)/shard_map/ppermute | solution.py:79
  29.1 1.5 %collective-permute-start.8 = (bf16[24,576]{1,0:T(8,128)(2,1)S(1)}, bf16[24,576]{1,0:T(8,128)(2,1)S(1)}, u32[]{:S(2)}, u32[]{:S(2)}) collective-permute-start(bf16[24,576]{1,0:T(8,128)(2,1)S(1)} %get-tuple-element.35), channel_id=1, source_target_pairs={{0,5},{1,4},{2,7},{3,6},{4,1},{5,0},{6,3},{7,2},{8,13},{9,12},{10,... | collective-permute-start | bytes 82952 | tf_op jit(solution)/shard_map/ppermute | solution.py:79
  30.6 0.7 %collective-permute-start.9 = (bf16[24,576]{1,0:T(8,128)(2,1)S(1)}, bf16[24,576]{1,0:T(8,128)(2,1)S(1)}, u32[]{:S(2)}, u32[]{:S(2)}) collective-permute-start(bf16[24,576]{1,0:T(8,128)(2,1)S(1)} %get-tuple-element.35), channel_id=1, source_target_pairs={{0,6},{1,7},{2,4},{3,5},{4,2},{5,3},{6,0},{7,1},{8,14},{9,15},{10,... | collective-permute-start | bytes 82952 | tf_op jit(solution)/shard_map/ppermute | solution.py:79
  31.3 2.7 %shard_map.188.refs_4_.last_ref = bf16[512,5632]{1,0:T(8,128)(2,1)S(1)} custom-call(bf16[512,8192]{1,0:T(8,128)(2,1)} %far_ref.9), custom_call_target="tpu_custom_call" | custom-call | tf_op jit(solution)/shard_map/pallas_call | solution.py:100
  34.0 1.3 %collective-permute-done.9.refs_3_ = bf16[24,576]{1,0:T(8,128)(2,1)S(1)} collective-permute-done((bf16[24,576]{1,0:T(8,128)(2,1)S(1)}, bf16[24,576]{1,0:T(8,128)(2,1)S(1)}, u32[]{:S(2)}, u32[]{:S(2)}) %collective-permute-start.9) | collective-permute-done | bytes 27680 | tf_op jit(solution)/shard_map/ppermute | solution.py:79
  35.4 0.2 shard_map.189
  35.6 0.5 shard_map.190
  36.1 0.6 %collective-permute-done.10.other_ref = bf16[24,576]{1,0:T(8,128)(2,1)S(1)} collective-permute-done((bf16[24,576]{1,0:T(8,128)(2,1)S(1)}, bf16[24,576]{1,0:T(8,128)(2,1)S(1)}, u32[]{:S(2)}, u32[]{:S(2)}) %collective-permute-start.10) | collective-permute-done | bytes 27680 | tf_op jit(solution)/shard_map/ppermute | solution.py:79
  36.7 2.3 %shard_map.191 = (f32[1536,128]{1,0:T(8,128)S(1)}, bf16[1536,128]{1,0:T(8,128)(2,1)S(1)}, f32[24,512]{1,0:T(8,128)S(1)}) custom-call(bf16[24,576]{1,0:T(8,128)(2,1)S(1)} %collective-permute-done.10.other_ref, f32[48,512]{1,0:T(8,128)S(1)} %get-tuple-element.37.x_ref, f32[48,512]{1,0:T(8,128)S(1)} %get-tuple-element.31.refs_2_.gate_ref, ...), custom_call_target="tpu_custom_call" | custom-call | tf_op jit(solution)/shard_map/pallas_call | solution.py:100
  39.1 0.2 collective-permute-start.11
  39.3 1.6 %collective-permute-done.11.refs_1_ = bf16[1536,128]{1,0:T(8,128)(2,1)S(1)} collective-permute-done((bf16[1536,128]{1,0:T(8,128)(2,1)S(1)}, bf16[1536,128]{1,0:T(8,128)(2,1)S(1)}, u32[]{:S(2)}, u32[]{:S(2)}) %collective-permute-start.11) | collective-permute-done | bytes 393248 | tf_op jit(solution)/shard_map/ppermute | solution.py:79
  40.9 0.1 shard_map.192
  41.0 0.5 collective-permute-start.12
  41.5 1.0 %collective-permute-start.13 = (bf16[384,128]{1,0:T(8,128)(2,1)S(1)}, bf16[384,128]{1,0:T(8,128)(2,1)S(1)}, u32[]{:S(2)}, u32[]{:S(2)}) collective-permute-start(bf16[384,128]{1,0:T(8,128)(2,1)S(1)} %get-tuple-element.45), channel_id=1, source_target_pairs={{0,2},{1,3},{2,0},{3,1},{4,6},{5,7},{6,4},{7,5},{8,10},{9,11},{10,... | collective-permute-start | bytes 294920 | tf_op jit(solution)/shard_map/ppermute | solution.py:79
  42.5 2.1 %collective-permute-start.14 = (bf16[384,128]{1,0:T(8,128)(2,1)S(1)}, bf16[384,128]{1,0:T(8,128)(2,1)S(1)}, u32[]{:S(2)}, u32[]{:S(2)}) collective-permute-start(bf16[384,128]{1,0:T(8,128)(2,1)S(1)} %get-tuple-element.46), channel_id=1, source_target_pairs={{0,6},{1,7},{2,4},{3,5},{4,2},{5,3},{6,0},{7,1},{8,14},{9,15},{10,... | collective-permute-start | bytes 294920 | tf_op jit(solution)/shard_map/ppermute | solution.py:79
  44.5 2.2 %shard_map.193 = (bf16[64,16,512]{2,1,0:T(8,128)(2,1)}, f32[8,128]{1,0:T(8,128)S(1)}) custom-call(s32[16]{0:T(128)S(1)} %copy-done.11, f32[24,544]{1,0:T(8,128)S(1)} %get-tuple-element.39.low_ref.mine_ref, bf16[24,576]{1,0:T(8,128)(2,1)S(1)} %collective-permute-done.10.other_ref, f32[48,512]{1,0:T(8,128)S(1)} %get-tuple-element.37.x_ref, ...), custom_call_target="tpu_custom_call" | custom-call | tf_op jit(solution)/shard_map/pallas_call | solution.py:100
  46.7 1.6 %collective-permute-done.14.refs_3_ = bf16[384,128]{1,0:T(8,128)(2,1)S(1)} collective-permute-done((bf16[384,128]{1,0:T(8,128)(2,1)S(1)}, bf16[384,128]{1,0:T(8,128)(2,1)S(1)}, u32[]{:S(2)}, u32[]{:S(2)}) %collective-permute-start.14) | collective-permute-done | bytes 98336 | tf_op jit(solution)/shard_map/ppermute | solution.py:79
  48.4 2.9 %collective-permute-start.15 = (bf16[192,128]{1,0:T(8,128)(2,1)S(1)}, bf16[192,128]{1,0:T(8,128)(2,1)S(1)}, u32[]{:S(2)}, u32[]{:S(2)}) collective-permute-start(bf16[192,128]{1,0:T(8,128)(2,1)S(1)} %get-tuple-element.51), channel_id=1, source_target_pairs={{0,8},{1,9},{2,10},{3,11},{4,12},{5,13},{6,14},{7,15},{8,0},{9,1},... | collective-permute-start | bytes 147464 | tf_op jit(solution)/shard_map/ppermute | solution.py:79
  51.2 1.4 %shard_map.196 = bf16[3,64,512]{2,1,0:T(8,128)(2,1)} custom-call(s32[16]{0:T(128)S(1)} %copy-done.11, f32[2,48,512]{2,1,0:T(8,128)S(1)} %fusion.2.both_ref, s32[2,48]{1,0:T(2,128)S(1)} %copy-done.7, bf16[3,64,512]{2,1,0:T(8,128)(2,1)S(1)} %bitcast.13), custom_call_target="tpu_custom_call" | custom-call | tf_op jit(solution)/shard_map/pallas_call | solution.py:100
  52.6 0.8 %collective-permute-done.15.refs_2_ = bf16[192,128]{1,0:T(8,128)(2,1)S(1)} collective-permute-done((bf16[192,128]{1,0:T(8,128)(2,1)S(1)}, bf16[192,128]{1,0:T(8,128)(2,1)S(1)}, u32[]{:S(2)}, u32[]{:S(2)}) %collective-permute-start.15) | collective-permute-done | bytes 49184 | tf_op jit(solution)/shard_map/ppermute | solution.py:79
  53.4 0.7 %shard_map.195 = bf16[4,8192]{1,0:T(4,128)(2,1)} custom-call(bf16[4,8192]{1,0:T(4,128)(2,1)S(1)} %copy-done.5, f32[192,128]{1,0:T(8,128)S(1)} %get-tuple-element.50.refs_1_, bf16[192,128]{1,0:T(8,128)(2,1)S(1)} %collective-permute-done.15.refs_2_), custom_call_target="tpu_custom_call" | custom-call | tf_op jit(solution)/shard_map/pallas_call | solution.py:100
  (33 shorter events, 0.2 us)
Async XLA Ops:
  1.7 7.0 %collective-permute-start = (bf16[192,128]{1,0:T(8,128)(2,1)S(1)}, bf16[192,128]{1,0:T(8,128)(2,1)S(1)}, u32[]{:S(2)}, u32[]{:S(2)}) collective-permute-start(bf16[192,128]{1,0:T(8,128)(2,1)S(1)} %shard_map.178.refs_0_), channel_id=1, source_target_pairs={{0,8},{1,9},{2,10},{3,11},{4,12},{5,13},{6,14},{7,15},{8,0},{9,1},... | collective-permute-start | bytes 147464 | tf_op jit(solution)/shard_map/ppermute | solution.py:79
  8.7 7.4 %collective-permute-start.1 = (bf16[384,128]{1,0:T(8,128)(2,1)S(1)}, bf16[384,128]{1,0:T(8,128)(2,1)S(1)}, u32[]{:S(2)}, u32[]{:S(2)}) collective-permute-start(bf16[384,128]{1,0:T(8,128)(2,1)S(1)} %shard_map.179.refs_0_), channel_id=1, source_target_pairs={{0,6},{1,7},{2,4},{3,5},{4,2},{5,3},{6,0},{7,1},{8,14},{9,15},{10,... | collective-permute-start | bytes 294920 | tf_op jit(solution)/shard_map/ppermute | solution.py:79
  11.3 5.0 %collective-permute-start.2 = (bf16[384,128]{1,0:T(8,128)(2,1)S(1)}, bf16[384,128]{1,0:T(8,128)(2,1)S(1)}, u32[]{:S(2)}, u32[]{:S(2)}) collective-permute-start(bf16[384,128]{1,0:T(8,128)(2,1)S(1)} %shard_map.179.refs_0_), channel_id=1, source_target_pairs={{0,4},{1,5},{2,6},{3,7},{4,0},{5,1},{6,2},{7,3},{8,12},{9,13},{10,... | collective-permute-start | bytes 294920 | tf_op jit(solution)/shard_map/ppermute | solution.py:79
  11.7 4.7 %collective-permute-start.3 = (bf16[384,128]{1,0:T(8,128)(2,1)S(1)}, bf16[384,128]{1,0:T(8,128)(2,1)S(1)}, u32[]{:S(2)}, u32[]{:S(2)}) collective-permute-start(bf16[384,128]{1,0:T(8,128)(2,1)S(1)} %shard_map.179.refs_0_), channel_id=1, source_target_pairs={{0,2},{1,3},{2,0},{3,1},{4,6},{5,7},{6,4},{7,5},{8,10},{9,11},{10,... | collective-permute-start | bytes 294920 | tf_op jit(solution)/shard_map/ppermute | solution.py:79
  16.5 1.8 %collective-permute-start.4 = (bf16[1536,128]{1,0:T(8,128)(2,1)S(1)}, bf16[1536,128]{1,0:T(8,128)(2,1)S(1)}, u32[]{:S(2)}, u32[]{:S(2)}) collective-permute-start(bf16[1536,128]{1,0:T(8,128)(2,1)S(1)} %shard_map.180.mine_ref), channel_id=1, source_target_pairs={{0,1},{1,0},{2,3},{3,2},{4,5},{5,4},{6,7},{7,6},{8,9},{9,8},{10,11... | collective-permute-start | bytes 1179656 | tf_op jit(solution)/shard_map/ppermute | solution.py:79
  18.4 3.2 %copy-start.2 = (bf16[64,3,512]{2,0,1:T(8,128)(2,1)S(1)}, bf16[64,3,512]{2,0,1:T(8,128)(2,1)}, u32[]{:S(2)}) copy-start(bf16[64,3,512]{2,0,1:T(8,128)(2,1)} %param.28) | copy-start | bytes 589828
  18.4 3.2 %copy-start.3 = (bf16[512,544]{0,1:T(8,128)(2,1)S(1)}, bf16[512,544]{0,1:T(8,128)(2,1)}, u32[]{:S(2)}) copy-start(bf16[512,544]{0,1:T(8,128)(2,1)} %param.21) | copy-start | bytes 1671172
  18.4 3.2 %copy-start.7 = (s32[2,48]{1,0:T(2,128)S(1)}, s32[2,48]{1,0:T(2,128)}, u32[]{:S(2)}) copy-start(s32[2,48]{1,0:T(2,128)} %constant.4.clone.spot_ref) | copy-start | bytes 1156
  18.5 3.2 %copy-start.8 = (f32[4,512]{1,0:T(4,128)S(1)}, f32[4,512]{1,0:T(4,128)}, u32[]{:S(2)}) copy-start(f32[4,512]{1,0:T(4,128)} %taps_ref.1) | copy-start | bytes 24580
  18.5 3.2 %copy-start.12 = (f32[512]{0:T(512)S(1)}, f32[512]{0:T(512)}, u32[]{:S(2)}) copy-start(f32[512]{0:T(512)} %param.20) | copy-start | bytes 6148
  18.5 4.0 %copy-start.11 = (s32[16]{0:T(128)S(1)}, s32[16]{0:T(128)}, u32[]{:S(2)}) copy-start(s32[16]{0:T(128)} %live_ref.5) | copy-start | bytes 196
  22.2 1.3 %collective-permute-start.5 = (f32[24,544]{1,0:T(8,128)S(1)}, f32[24,544]{1,0:T(8,128)S(1)}, u32[]{:S(2)}, u32[]{:S(2)}) collective-permute-start(f32[24,544]{1,0:T(8,128)S(1)} %get-tuple-element.29), channel_id=1, source_target_pairs={{0,1},{1,0},{2,3},{3,2},{4,5},{5,4},{6,7},{7,6},{8,9},{9,8},{10,11... | collective-permute-start | bytes 156680 | tf_op jit(solution)/shard_map/ppermute | solution.py:79
  23.6 11.9 %copy-start = (bf16[64,16,512]{2,1,0:T(8,128)(2,1)S(1)}, bf16[64,16,512]{2,1,0:T(8,128)(2,1)}, u32[]{:S(2)}) copy-start(bf16[64,16,512]{2,1,0:T(8,128)(2,1)} %state_ref.5) | copy-start | bytes 3145732
  23.6 11.9 %copy-start.1 = (bf16[512,512]{1,0:T(8,128)(2,1)S(1)}, bf16[512,512]{1,0:T(8,128)(2,1)}, u32[]{:S(2)}) copy-start(bf16[512,512]{1,0:T(8,128)(2,1)} %step_weight_ref.3) | copy-start | bytes 1572868
  23.6 11.9 %copy-start.4 = (f32[16,512]{1,0:T(8,128)S(1)}, f32[16,512]{1,0:T(8,128)}, u32[]{:S(2)}) copy-start(f32[16,512]{1,0:T(8,128)} %rates_ref.5) | copy-start | bytes 98308
  23.6 11.9 %copy-start.9 = (f32[512]{0:T(512)S(1)}, f32[512]{0:T(512)}, u32[]{:S(2)}) copy-start(f32[512]{0:T(512)} %param.23) | copy-start | bytes 6148
  23.6 11.9 %copy-start.10 = (f32[512]{0:T(512)S(1)}, f32[512]{0:T(512)}, u32[]{:S(2)}) copy-start(f32[512]{0:T(512)} %param.25) | copy-start | bytes 6148
  23.7 13.1 %copy-start.6 = (s32[48,2]{1,0:T(8,128)S(1)}, s32[48,2]{1,0:T(8,128)}, u32[]{:S(2)}) copy-start(s32[48,2]{1,0:T(8,128)} %constant.7.spot_ref) | copy-start | bytes 1156
  23.7 4.3 %collective-permute-start.6 = (bf16[24,576]{1,0:T(8,128)(2,1)S(1)}, bf16[24,576]{1,0:T(8,128)(2,1)S(1)}, u32[]{:S(2)}, u32[]{:S(2)}) collective-permute-start(bf16[24,576]{1,0:T(8,128)(2,1)S(1)} %get-tuple-element.33), channel_id=1, source_target_pairs={{0,9},{1,8},{2,11},{3,10},{4,13},{5,12},{6,15},{7,14},{8,1},{9,0},... | collective-permute-start | bytes 82952 | tf_op jit(solution)/shard_map/ppermute | solution.py:79
  28.1 25.3 %copy-start.5 = (bf16[4,8192]{1,0:T(4,128)(2,1)S(1)}, bf16[4,8192]{1,0:T(4,128)(2,1)}, u32[]{:S(2)}) copy-start(bf16[4,8192]{1,0:T(4,128)(2,1)} %refs_0_.1) | copy-start | bytes 196612
  28.1 5.9 %collective-permute-start.7 = (bf16[24,576]{1,0:T(8,128)(2,1)S(1)}, bf16[24,576]{1,0:T(8,128)(2,1)S(1)}, u32[]{:S(2)}, u32[]{:S(2)}) collective-permute-start(bf16[24,576]{1,0:T(8,128)(2,1)S(1)} %get-tuple-element.35), channel_id=1, source_target_pairs={{0,3},{1,2},{2,1},{3,0},{4,7},{5,6},{6,5},{7,4},{8,11},{9,10},{10,... | collective-permute-start | bytes 82952 | tf_op jit(solution)/shard_map/ppermute | solution.py:79
  29.1 5.0 %collective-permute-start.8 = (bf16[24,576]{1,0:T(8,128)(2,1)S(1)}, bf16[24,576]{1,0:T(8,128)(2,1)S(1)}, u32[]{:S(2)}, u32[]{:S(2)}) collective-permute-start(bf16[24,576]{1,0:T(8,128)(2,1)S(1)} %get-tuple-element.35), channel_id=1, source_target_pairs={{0,5},{1,4},{2,7},{3,6},{4,1},{5,0},{6,3},{7,2},{8,13},{9,12},{10,... | collective-permute-start | bytes 82952 | tf_op jit(solution)/shard_map/ppermute | solution.py:79
  30.6 4.8 %collective-permute-start.9 = (bf16[24,576]{1,0:T(8,128)(2,1)S(1)}, bf16[24,576]{1,0:T(8,128)(2,1)S(1)}, u32[]{:S(2)}, u32[]{:S(2)}) collective-permute-start(bf16[24,576]{1,0:T(8,128)(2,1)S(1)} %get-tuple-element.35), channel_id=1, source_target_pairs={{0,6},{1,7},{2,4},{3,5},{4,2},{5,3},{6,0},{7,1},{8,14},{9,15},{10,... | collective-permute-start | bytes 82952 | tf_op jit(solution)/shard_map/ppermute | solution.py:79
  35.5 1.2 %collective-permute-start.10 = (bf16[24,576]{1,0:T(8,128)(2,1)S(1)}, bf16[24,576]{1,0:T(8,128)(2,1)S(1)}, u32[]{:S(2)}, u32[]{:S(2)}) collective-permute-start(bf16[24,576]{1,0:T(8,128)(2,1)S(1)} %get-tuple-element.36), channel_id=1, source_target_pairs={{0,1},{1,0},{2,3},{3,2},{4,5},{5,4},{6,7},{7,6},{8,9},{9,8},{10,11... | collective-permute-start | bytes 82952 | tf_op jit(solution)/shard_map/ppermute | solution.py:79
  39.1 1.8 %collective-permute-start.11 = (bf16[1536,128]{1,0:T(8,128)(2,1)S(1)}, bf16[1536,128]{1,0:T(8,128)(2,1)S(1)}, u32[]{:S(2)}, u32[]{:S(2)}) collective-permute-start(bf16[1536,128]{1,0:T(8,128)(2,1)S(1)} %get-tuple-element.42), channel_id=1, source_target_pairs={{0,1},{1,0},{2,3},{3,2},{4,5},{5,4},{6,7},{7,6},{8,9},{9,8},{10,11... | collective-permute-start | bytes 1179656 | tf_op jit(solution)/shard_map/ppermute | solution.py:79
  41.0 5.8 %collective-permute-start.12 = (bf16[384,128]{1,0:T(8,128)(2,1)S(1)}, bf16[384,128]{1,0:T(8,128)(2,1)S(1)}, u32[]{:S(2)}, u32[]{:S(2)}) collective-permute-start(bf16[384,128]{1,0:T(8,128)(2,1)S(1)} %get-tuple-element.44), channel_id=1, source_target_pairs={{0,4},{1,5},{2,6},{3,7},{4,0},{5,1},{6,2},{7,3},{8,12},{9,13},{10,... | collective-permute-start | bytes 294920 | tf_op jit(solution)/shard_map/ppermute | solution.py:79
  41.5 5.2 %collective-permute-start.13 = (bf16[384,128]{1,0:T(8,128)(2,1)S(1)}, bf16[384,128]{1,0:T(8,128)(2,1)S(1)}, u32[]{:S(2)}, u32[]{:S(2)}) collective-permute-start(bf16[384,128]{1,0:T(8,128)(2,1)S(1)} %get-tuple-element.45), channel_id=1, source_target_pairs={{0,2},{1,3},{2,0},{3,1},{4,6},{5,7},{6,4},{7,5},{8,10},{9,11},{10,... | collective-permute-start | bytes 294920 | tf_op jit(solution)/shard_map/ppermute | solution.py:79
  42.5 5.8 %collective-permute-start.14 = (bf16[384,128]{1,0:T(8,128)(2,1)S(1)}, bf16[384,128]{1,0:T(8,128)(2,1)S(1)}, u32[]{:S(2)}, u32[]{:S(2)}) collective-permute-start(bf16[384,128]{1,0:T(8,128)(2,1)S(1)} %get-tuple-element.46), channel_id=1, source_target_pairs={{0,6},{1,7},{2,4},{3,5},{4,2},{5,3},{6,0},{7,1},{8,14},{9,15},{10,... | collective-permute-start | bytes 294920 | tf_op jit(solution)/shard_map/ppermute | solution.py:79
  48.4 5.1 %collective-permute-start.15 = (bf16[192,128]{1,0:T(8,128)(2,1)S(1)}, bf16[192,128]{1,0:T(8,128)(2,1)S(1)}, u32[]{:S(2)}, u32[]{:S(2)}) collective-permute-start(bf16[192,128]{1,0:T(8,128)(2,1)S(1)} %get-tuple-element.51), channel_id=1, source_target_pairs={{0,8},{1,9},{2,10},{3,11},{4,12},{5,13},{6,14},{7,15},{8,0},{9,1},... | collective-permute-start | bytes 147464 | tf_op jit(solution)/shard_map/ppermute | solution.py:79

commit v10 on v9

--- a/solution.py
+++ b/solution.py
@@ -289,7 +289,7 @@
     half = keep_ref.shape[0]
     core = side(index)
     keep_ref[...] = low_ref[pl.ds(pl.multiple_of(core * half, 8), half), :]
-    send_ref[...] = low_ref[pl.ds(pl.multiple_of((1 - core) * half, 8), half), :]
+    send_ref[...] = pack(low_ref[pl.ds(pl.multiple_of((1 - core) * half, 8), half), :])
 
 
 def gate_kernel(live_ref, both_ref, spot_ref, mixed_ref, gate_ref, alive_ref, x_ref):
@@ -593,7 +593,7 @@
         functools.partial(conv_kernel, rows_dev),
         (
             shape((kept // 2, low_width)),
-            shape((kept // 2, low_width)),
+            shape((kept // 2, low_width + 2 * NSTATE), BF16),
             shape((kept, channels), BF16),
         ),
         (

time: 54.3 us -> 54.4 us (level)
  no operation moved by 1% of the time
where the time goes in v10:
time: 54.4 us; the launch traced here: 54.1 us
  Pallas kernels  22.8 us (42%)
  starting transfers between devices  19.6 us (36%)
  waiting for transfers between devices  7.54 us (14%)
  matrix products  3.15 us (6%)
  between operations  0.94 us (2%)
    pallas_call x22, Pallas kernels, call(): pl.pallas_call(kernel, out_shape=outs, in_specs=[pl.BlockSpec(memory_spac...  22.8 us
    ppermute x16, starting transfers between devices, swap(): lax.ppermute(value, 'weight', [(i, i ^ shift) for i in range(devices)])  19.6 us
    ppermute x16, waiting for transfers between devices, swap(): lax.ppermute(value, 'weight', [(i, i ^ shift) for i in range(devices)])  7.54 us
    dot_general x1, matrix products, body(): jnp.einsum('rd,dbc->brc', normed, near_weight, preferred_element_type=F32)  3.15 us
  transfers between devices with their start and end apart: 16, of which 10 were waited for; matrix products, arithmetic and copies ran while one was open for 0% of the time, Pallas kernels for 32%

profile of v10, /device:TPU:0, one launch (start us, length us, event | category | flops | bytes accessed | tf_op | source)
XLA Modules:
  0.0 54.1 jit_solution(1484947518048768713)
XLA Ops:
  0.6 1.0 %shard_map.178.refs_0_ = bf16[192,128]{1,0:T(8,128)(2,1)S(1)} custom-call(bf16[4,8192]{1,0:T(4,128)(2,1)} %refs_0_.1, f32[1,8192]{1,0:T(1,128)} %bitcast.21), custom_call_target="tpu_custom_call" | custom-call | tf_op jit(solution)/shard_map/pallas_call | solution.py:100
  1.7 4.1 %collective-permute-start = (bf16[192,128]{1,0:T(8,128)(2,1)S(1)}, bf16[192,128]{1,0:T(8,128)(2,1)S(1)}, u32[]{:S(2)}, u32[]{:S(2)}) collective-permute-start(bf16[192,128]{1,0:T(8,128)(2,1)S(1)} %shard_map.178.refs_0_), channel_id=1, source_target_pairs={{0,8},{1,9},{2,10},{3,11},{4,12},{5,13},{6,14},{7,15},{8,0},{9,1},... | collective-permute-start | bytes 147464 | tf_op jit(solution)/shard_map/ppermute | solution.py:79
  5.8 2.9 %shard_map.175.refs_0_.refs_2_ = bf16[8192,2,512]{2,1,0:T(2,128)(2,1)S(1)} custom-call(bf16[8192,2,512]{2,1,0:T(2,128)(2,1)} %far_ref.7), custom_call_target="tpu_custom_call" | custom-call | tf_op jit(solution)/shard_map/pallas_call | solution.py:100
  8.7 2.6 %collective-permute-start.1 = (bf16[384,128]{1,0:T(8,128)(2,1)S(1)}, bf16[384,128]{1,0:T(8,128)(2,1)S(1)}, u32[]{:S(2)}, u32[]{:S(2)}) collective-permute-start(bf16[384,128]{1,0:T(8,128)(2,1)S(1)} %shard_map.179.refs_0_), channel_id=1, source_target_pairs={{0,6},{1,7},{2,4},{3,5},{4,2},{5,3},{6,0},{7,1},{8,14},{9,15},{10,... | collective-permute-start | bytes 294920 | tf_op jit(solution)/shard_map/ppermute | solution.py:79
  11.3 0.4 collective-permute-start.2
  11.7 0.5 collective-permute-start.3
  12.2 3.8 %shard_map.176.refs_0_.refs_4_ = bf16[8192,2,512]{2,1,0:T(2,128)(2,1)S(1)} custom-call(bf16[8192,2,512]{2,1,0:T(2,128)(2,1)} %far_ref.7, bf16[8192,2,512]{2,1,0:T(2,128)(2,1)S(1)} %shard_map.175.refs_0_.refs_2_), custom_call_target="tpu_custom_call", output_to_operand_aliasing={{}: (1, {})} | custom-call | tf_op jit(solution)/shard_map/pallas_call | solution.py:100
  16.1 0.3 collective-permute-done.2.refs_2_
  16.3 0.1 collective-permute-done.3.refs_3_
  16.5 0.1 collective-permute-start.4
  16.5 1.2 %shard_map.177._ = bf16[8192,2,512]{2,1,0:T(2,128)(2,1)S(1)} custom-call(bf16[8192,2,512]{2,1,0:T(2,128)(2,1)} %far_ref.7, bf16[8192,2,512]{2,1,0:T(2,128)(2,1)S(1)} %shard_map.176.refs_0_.refs_4_), custom_call_target="tpu_custom_call", output_to_operand_aliasing={{}: (1, {})} | custom-call | tf_op jit(solution)/shard_map/pallas_call | solution.py:100
  17.8 0.1 shard_map.181.half_ref
  17.9 0.4 collective-permute-done.4.other_ref
  18.2 0.2 shard_map.182
  18.4 0.0 copy-start.7
  18.5 3.1 %fusion.2.both_ref = f32[2,48,512]{2,1,0:T(8,128)S(1)} fusion(bf16[8192,2,512]{2,1,0:T(2,128)(2,1)S(1)} %shard_map.177._, bf16[48,8192]{1,0:T(8,128)(2,1)S(1)} %shard_map.182), kind=kOutput, calls=%fused_computation.2 | convolution fusion | flops 805306368 | bytes 17760256 | tf_op jit(solution)/shard_map/rd,dbc->brc/dot_general | solution.py:589
  21.6 0.0 copy-done.2
  21.7 0.6 %shard_map.183 = (f32[24,544]{1,0:T(8,128)S(1)}, bf16[24,576]{1,0:T(8,128)(2,1)S(1)}, bf16[48,512]{1,0:T(8,128)(2,1)S(1)}) custom-call(f32[2,48,512]{2,1,0:T(8,128)S(1)} %fusion.2.both_ref, s32[2,48]{1,0:T(2,128)S(1)} %copy-done.7, bf16[3,64,512]{2,1,0:T(8,128)(2,1)S(1)} %bitcast.12, f32[4,512]{1,0:T(4,128)S(1)} %copy-done.8, f32[1,512]{1,0:T(1,128)S(1)} %bitcast.19, ...), custom_call_target="tpu_custom_call" | custom-call | tf_op jit(solution)/shard_map/pallas_call | solution.py:100
  22.3 0.2 collective-permute-start.5
  22.5 0.8 %shard_map.184 = (f32[48,512]{1,0:T(8,128)S(1)}, f32[48,128]{1,0:T(8,128)S(1)}, f32[48,512]{1,0:T(8,128)S(1)}) custom-call(s32[16]{0:T(128)S(1)} %copy-done.11, f32[2,48,512]{2,1,0:T(8,128)S(1)} %fusion.2.both_ref, s32[2,48]{1,0:T(2,128)S(1)} %copy-done.7, bf16[48,512]{1,0:T(8,128)(2,1)S(1)} %get-tuple-element.30.mixed_ref), custom_call_target="tpu_custom_call" | custom-call | tf_op jit(solution)/shard_map/pallas_call | solution.py:100
  23.3 0.2 collective-permute-done.5.refs_1_
  23.5 0.2 shard_map.185
  23.7 0.0 copy-start.6
  23.7 1.9 %collective-permute-start.6 = (bf16[24,576]{1,0:T(8,128)(2,1)S(1)}, bf16[24,576]{1,0:T(8,128)(2,1)S(1)}, u32[]{:S(2)}, u32[]{:S(2)}) collective-permute-start(bf16[24,576]{1,0:T(8,128)(2,1)S(1)} %get-tuple-element.33), channel_id=1, source_target_pairs={{0,9},{1,8},{2,11},{3,10},{4,13},{5,12},{6,15},{7,14},{8,1},{9,0},... | collective-permute-start | bytes 82952 | tf_op jit(solution)/shard_map/ppermute | solution.py:79
  25.6 1.7 %shard_map.186.refs_2_.first_ref = bf16[512,2560]{1,0:T(8,128)(2,1)S(1)} custom-call(bf16[512,8192]{1,0:T(8,128)(2,1)} %far_ref.9), custom_call_target="tpu_custom_call" | custom-call | tf_op jit(solution)/shard_map/pallas_call | solution.py:100
  27.3 0.7 %collective-permute-done.6.refs_1_ = bf16[24,576]{1,0:T(8,128)(2,1)S(1)} collective-permute-done((bf16[24,576]{1,0:T(8,128)(2,1)S(1)}, bf16[24,576]{1,0:T(8,128)(2,1)S(1)}, u32[]{:S(2)}, u32[]{:S(2)}) %collective-permute-start.6) | collective-permute-done | bytes 27680 | tf_op jit(solution)/shard_map/ppermute | solution.py:79
  28.0 0.2 shard_map.187
  28.1 0.9 %collective-permute-start.7 = (bf16[24,576]{1,0:T(8,128)(2,1)S(1)}, bf16[24,576]{1,0:T(8,128)(2,1)S(1)}, u32[]{:S(2)}, u32[]{:S(2)}) collective-permute-start(bf16[24,576]{1,0:T(8,128)(2,1)S(1)} %get-tuple-element.35), channel_id=1, source_target_pairs={{0,3},{1,2},{2,1},{3,0},{4,7},{5,6},{6,5},{7,4},{8,11},{9,10},{10,... | collective-permute-start | bytes 82952 | tf_op jit(solution)/shard_map/ppermute | solution.py:79
  29.1 1.5 %collective-permute-start.8 = (bf16[24,576]{1,0:T(8,128)(2,1)S(1)}, bf16[24,576]{1,0:T(8,128)(2,1)S(1)}, u32[]{:S(2)}, u32[]{:S(2)}) collective-permute-start(bf16[24,576]{1,0:T(8,128)(2,1)S(1)} %get-tuple-element.35), channel_id=1, source_target_pairs={{0,5},{1,4},{2,7},{3,6},{4,1},{5,0},{6,3},{7,2},{8,13},{9,12},{10,... | collective-permute-start | bytes 82952 | tf_op jit(solution)/shard_map/ppermute | solution.py:79
  30.6 0.7 %collective-permute-start.9 = (bf16[24,576]{1,0:T(8,128)(2,1)S(1)}, bf16[24,576]{1,0:T(8,128)(2,1)S(1)}, u32[]{:S(2)}, u32[]{:S(2)}) collective-permute-start(bf16[24,576]{1,0:T(8,128)(2,1)S(1)} %get-tuple-element.35), channel_id=1, source_target_pairs={{0,6},{1,7},{2,4},{3,5},{4,2},{5,3},{6,0},{7,1},{8,14},{9,15},{10,... | collective-permute-start | bytes 82952 | tf_op jit(solution)/shard_map/ppermute | solution.py:79
  31.4 2.7 %shard_map.188.refs_4_.last_ref = bf16[512,5632]{1,0:T(8,128)(2,1)S(1)} custom-call(bf16[512,8192]{1,0:T(8,128)(2,1)} %far_ref.9), custom_call_target="tpu_custom_call" | custom-call | tf_op jit(solution)/shard_map/pallas_call | solution.py:100
  34.1 1.3 %collective-permute-done.9.refs_3_ = bf16[24,576]{1,0:T(8,128)(2,1)S(1)} collective-permute-done((bf16[24,576]{1,0:T(8,128)(2,1)S(1)}, bf16[24,576]{1,0:T(8,128)(2,1)S(1)}, u32[]{:S(2)}, u32[]{:S(2)}) %collective-permute-start.9) | collective-permute-done | bytes 27680 | tf_op jit(solution)/shard_map/ppermute | solution.py:79
  35.4 0.2 shard_map.189
  35.6 0.5 shard_map.190
  36.2 0.6 %collective-permute-done.10.other_ref = bf16[24,576]{1,0:T(8,128)(2,1)S(1)} collective-permute-done((bf16[24,576]{1,0:T(8,128)(2,1)S(1)}, bf16[24,576]{1,0:T(8,128)(2,1)S(1)}, u32[]{:S(2)}, u32[]{:S(2)}) %collective-permute-start.10) | collective-permute-done | bytes 27680 | tf_op jit(solution)/shard_map/ppermute | solution.py:79
  36.8 2.3 %shard_map.191 = (f32[1536,128]{1,0:T(8,128)S(1)}, bf16[1536,128]{1,0:T(8,128)(2,1)S(1)}, f32[24,512]{1,0:T(8,128)S(1)}) custom-call(bf16[24,576]{1,0:T(8,128)(2,1)S(1)} %collective-permute-done.10.other_ref, f32[48,512]{1,0:T(8,128)S(1)} %get-tuple-element.37.x_ref, f32[48,512]{1,0:T(8,128)S(1)} %get-tuple-element.31.refs_2_.gate_ref, ...), custom_call_target="tpu_custom_call" | custom-call | tf_op jit(solution)/shard_map/pallas_call | solution.py:100
  39.1 0.2 collective-permute-start.11
  39.4 1.6 %collective-permute-done.11.refs_1_ = bf16[1536,128]{1,0:T(8,128)(2,1)S(1)} collective-permute-done((bf16[1536,128]{1,0:T(8,128)(2,1)S(1)}, bf16[1536,128]{1,0:T(8,128)(2,1)S(1)}, u32[]{:S(2)}, u32[]{:S(2)}) %collective-permute-start.11) | collective-permute-done | bytes 393248 | tf_op jit(solution)/shard_map/ppermute | solution.py:79
  40.9 0.1 shard_map.192
  41.0 0.5 collective-permute-start.12
  41.5 1.0 %collective-permute-start.13 = (bf16[384,128]{1,0:T(8,128)(2,1)S(1)}, bf16[384,128]{1,0:T(8,128)(2,1)S(1)}, u32[]{:S(2)}, u32[]{:S(2)}) collective-permute-start(bf16[384,128]{1,0:T(8,128)(2,1)S(1)} %get-tuple-element.45), channel_id=1, source_target_pairs={{0,2},{1,3},{2,0},{3,1},{4,6},{5,7},{6,4},{7,5},{8,10},{9,11},{10,... | collective-permute-start | bytes 294920 | tf_op jit(solution)/shard_map/ppermute | solution.py:79
  42.5 2.1 %collective-permute-start.14 = (bf16[384,128]{1,0:T(8,128)(2,1)S(1)}, bf16[384,128]{1,0:T(8,128)(2,1)S(1)}, u32[]{:S(2)}, u32[]{:S(2)}) collective-permute-start(bf16[384,128]{1,0:T(8,128)(2,1)S(1)} %get-tuple-element.46), channel_id=1, source_target_pairs={{0,6},{1,7},{2,4},{3,5},{4,2},{5,3},{6,0},{7,1},{8,14},{9,15},{10,... | collective-permute-start | bytes 294920 | tf_op jit(solution)/shard_map/ppermute | solution.py:79
  44.6 2.2 %shard_map.193 = (bf16[64,16,512]{2,1,0:T(8,128)(2,1)}, f32[8,128]{1,0:T(8,128)S(1)}) custom-call(s32[16]{0:T(128)S(1)} %copy-done.11, f32[24,544]{1,0:T(8,128)S(1)} %get-tuple-element.39.low_ref.mine_ref, bf16[24,576]{1,0:T(8,128)(2,1)S(1)} %collective-permute-done.10.other_ref, f32[48,512]{1,0:T(8,128)S(1)} %get-tuple-element.37.x_ref, ...), custom_call_target="tpu_custom_call" | custom-call | tf_op jit(solution)/shard_map/pallas_call | solution.py:100
  46.8 1.6 %collective-permute-done.14.refs_3_ = bf16[384,128]{1,0:T(8,128)(2,1)S(1)} collective-permute-done((bf16[384,128]{1,0:T(8,128)(2,1)S(1)}, bf16[384,128]{1,0:T(8,128)(2,1)S(1)}, u32[]{:S(2)}, u32[]{:S(2)}) %collective-permute-start.14) | collective-permute-done | bytes 98336 | tf_op jit(solution)/shard_map/ppermute | solution.py:79
  48.4 2.9 %collective-permute-start.15 = (bf16[192,128]{1,0:T(8,128)(2,1)S(1)}, bf16[192,128]{1,0:T(8,128)(2,1)S(1)}, u32[]{:S(2)}, u32[]{:S(2)}) collective-permute-start(bf16[192,128]{1,0:T(8,128)(2,1)S(1)} %get-tuple-element.51), channel_id=1, source_target_pairs={{0,8},{1,9},{2,10},{3,11},{4,12},{5,13},{6,14},{7,15},{8,0},{9,1},... | collective-permute-start | bytes 147464 | tf_op jit(solution)/shard_map/ppermute | solution.py:79
  51.3 1.4 %shard_map.196 = bf16[3,64,512]{2,1,0:T(8,128)(2,1)} custom-call(s32[16]{0:T(128)S(1)} %copy-done.11, f32[2,48,512]{2,1,0:T(8,128)S(1)} %fusion.2.both_ref, s32[2,48]{1,0:T(2,128)S(1)} %copy-done.7, bf16[3,64,512]{2,1,0:T(8,128)(2,1)S(1)} %bitcast.13), custom_call_target="tpu_custom_call" | custom-call | tf_op jit(solution)/shard_map/pallas_call | solution.py:100
  52.6 0.8 %collective-permute-done.15.refs_2_ = bf16[192,128]{1,0:T(8,128)(2,1)S(1)} collective-permute-done((bf16[192,128]{1,0:T(8,128)(2,1)S(1)}, bf16[192,128]{1,0:T(8,128)(2,1)S(1)}, u32[]{:S(2)}, u32[]{:S(2)}) %collective-permute-start.15) | collective-permute-done | bytes 49184 | tf_op jit(solution)/shard_map/ppermute | solution.py:79
  53.5 0.7 %shard_map.195 = bf16[4,8192]{1,0:T(4,128)(2,1)} custom-call(bf16[4,8192]{1,0:T(4,128)(2,1)S(1)} %copy-done.5, f32[192,128]{1,0:T(8,128)S(1)} %get-tuple-element.50.refs_1_, bf16[192,128]{1,0:T(8,128)(2,1)S(1)} %collective-permute-done.15.refs_2_), custom_call_target="tpu_custom_call" | custom-call | tf_op jit(solution)/shard_map/pallas_call | solution.py:100
  (33 shorter events, 0.2 us)
Async XLA Ops:
  1.7 7.0 %collective-permute-start = (bf16[192,128]{1,0:T(8,128)(2,1)S(1)}, bf16[192,128]{1,0:T(8,128)(2,1)S(1)}, u32[]{:S(2)}, u32[]{:S(2)}) collective-permute-start(bf16[192,128]{1,0:T(8,128)(2,1)S(1)} %shard_map.178.refs_0_), channel_id=1, source_target_pairs={{0,8},{1,9},{2,10},{3,11},{4,12},{5,13},{6,14},{7,15},{8,0},{9,1},... | collective-permute-start | bytes 147464 | tf_op jit(solution)/shard_map/ppermute | solution.py:79
  8.7 7.4 %collective-permute-start.1 = (bf16[384,128]{1,0:T(8,128)(2,1)S(1)}, bf16[384,128]{1,0:T(8,128)(2,1)S(1)}, u32[]{:S(2)}, u32[]{:S(2)}) collective-permute-start(bf16[384,128]{1,0:T(8,128)(2,1)S(1)} %shard_map.179.refs_0_), channel_id=1, source_target_pairs={{0,6},{1,7},{2,4},{3,5},{4,2},{5,3},{6,0},{7,1},{8,14},{9,15},{10,... | collective-permute-start | bytes 294920 | tf_op jit(solution)/shard_map/ppermute | solution.py:79
  11.3 5.0 %collective-permute-start.2 = (bf16[384,128]{1,0:T(8,128)(2,1)S(1)}, bf16[384,128]{1,0:T(8,128)(2,1)S(1)}, u32[]{:S(2)}, u32[]{:S(2)}) collective-permute-start(bf16[384,128]{1,0:T(8,128)(2,1)S(1)} %shard_map.179.refs_0_), channel_id=1, source_target_pairs={{0,4},{1,5},{2,6},{3,7},{4,0},{5,1},{6,2},{7,3},{8,12},{9,13},{10,... | collective-permute-start | bytes 294920 | tf_op jit(solution)/shard_map/ppermute | solution.py:79
  11.7 4.7 %collective-permute-start.3 = (bf16[384,128]{1,0:T(8,128)(2,1)S(1)}, bf16[384,128]{1,0:T(8,128)(2,1)S(1)}, u32[]{:S(2)}, u32[]{:S(2)}) collective-permute-start(bf16[384,128]{1,0:T(8,128)(2,1)S(1)} %shard_map.179.refs_0_), channel_id=1, source_target_pairs={{0,2},{1,3},{2,0},{3,1},{4,6},{5,7},{6,4},{7,5},{8,10},{9,11},{10,... | collective-permute-start | bytes 294920 | tf_op jit(solution)/shard_map/ppermute | solution.py:79
  16.5 1.8 %collective-permute-start.4 = (bf16[1536,128]{1,0:T(8,128)(2,1)S(1)}, bf16[1536,128]{1,0:T(8,128)(2,1)S(1)}, u32[]{:S(2)}, u32[]{:S(2)}) collective-permute-start(bf16[1536,128]{1,0:T(8,128)(2,1)S(1)} %shard_map.180.mine_ref), channel_id=1, source_target_pairs={{0,1},{1,0},{2,3},{3,2},{4,5},{5,4},{6,7},{7,6},{8,9},{9,8},{10,11... | collective-permute-start | bytes 1179656 | tf_op jit(solution)/shard_map/ppermute | solution.py:79
  18.4 3.2 %copy-start.2 = (bf16[64,3,512]{2,0,1:T(8,128)(2,1)S(1)}, bf16[64,3,512]{2,0,1:T(8,128)(2,1)}, u32[]{:S(2)}) copy-start(bf16[64,3,512]{2,0,1:T(8,128)(2,1)} %param.28) | copy-start | bytes 589828
  18.4 3.2 %copy-start.3 = (bf16[512,544]{0,1:T(8,128)(2,1)S(1)}, bf16[512,544]{0,1:T(8,128)(2,1)}, u32[]{:S(2)}) copy-start(bf16[512,544]{0,1:T(8,128)(2,1)} %param.21) | copy-start | bytes 1671172
  18.4 3.2 %copy-start.7 = (s32[2,48]{1,0:T(2,128)S(1)}, s32[2,48]{1,0:T(2,128)}, u32[]{:S(2)}) copy-start(s32[2,48]{1,0:T(2,128)} %constant.4.clone.spot_ref) | copy-start | bytes 1156
  18.5 3.2 %copy-start.8 = (f32[4,512]{1,0:T(4,128)S(1)}, f32[4,512]{1,0:T(4,128)}, u32[]{:S(2)}) copy-start(f32[4,512]{1,0:T(4,128)} %taps_ref.1) | copy-start | bytes 24580
  18.5 3.2 %copy-start.12 = (f32[512]{0:T(512)S(1)}, f32[512]{0:T(512)}, u32[]{:S(2)}) copy-start(f32[512]{0:T(512)} %param.20) | copy-start | bytes 6148
  18.5 4.0 %copy-start.11 = (s32[16]{0:T(128)S(1)}, s32[16]{0:T(128)}, u32[]{:S(2)}) copy-start(s32[16]{0:T(128)} %live_ref.5) | copy-start | bytes 196
  22.3 1.2 %collective-permute-start.5 = (bf16[24,576]{1,0:T(8,128)(2,1)S(1)}, bf16[24,576]{1,0:T(8,128)(2,1)S(1)}, u32[]{:S(2)}, u32[]{:S(2)}) collective-permute-start(bf16[24,576]{1,0:T(8,128)(2,1)S(1)} %get-tuple-element.29), channel_id=1, source_target_pairs={{0,1},{1,0},{2,3},{3,2},{4,5},{5,4},{6,7},{7,6},{8,9},{9,8},{10,11... | collective-permute-start | bytes 82952 | tf_op jit(solution)/shard_map/ppermute | solution.py:79
  23.7 11.9 %copy-start = (bf16[64,16,512]{2,1,0:T(8,128)(2,1)S(1)}, bf16[64,16,512]{2,1,0:T(8,128)(2,1)}, u32[]{:S(2)}) copy-start(bf16[64,16,512]{2,1,0:T(8,128)(2,1)} %state_ref.5) | copy-start | bytes 3145732
  23.7 11.9 %copy-start.1 = (bf16[512,512]{1,0:T(8,128)(2,1)S(1)}, bf16[512,512]{1,0:T(8,128)(2,1)}, u32[]{:S(2)}) copy-start(bf16[512,512]{1,0:T(8,128)(2,1)} %step_weight_ref.3) | copy-start | bytes 1572868
  23.7 11.9 %copy-start.4 = (f32[16,512]{1,0:T(8,128)S(1)}, f32[16,512]{1,0:T(8,128)}, u32[]{:S(2)}) copy-start(f32[16,512]{1,0:T(8,128)} %rates_ref.5) | copy-start | bytes 98308
  23.7 11.9 %copy-start.9 = (f32[512]{0:T(512)S(1)}, f32[512]{0:T(512)}, u32[]{:S(2)}) copy-start(f32[512]{0:T(512)} %param.23) | copy-start | bytes 6148
  23.7 11.9 %copy-start.10 = (f32[512]{0:T(512)S(1)}, f32[512]{0:T(512)}, u32[]{:S(2)}) copy-start(f32[512]{0:T(512)} %param.25) | copy-start | bytes 6148
  23.7 13.1 %copy-start.6 = (s32[48,2]{1,0:T(8,128)S(1)}, s32[48,2]{1,0:T(8,128)}, u32[]{:S(2)}) copy-start(s32[48,2]{1,0:T(8,128)} %constant.7.spot_ref) | copy-start | bytes 1156
  23.7 4.3 %collective-permute-start.6 = (bf16[24,576]{1,0:T(8,128)(2,1)S(1)}, bf16[24,576]{1,0:T(8,128)(2,1)S(1)}, u32[]{:S(2)}, u32[]{:S(2)}) collective-permute-start(bf16[24,576]{1,0:T(8,128)(2,1)S(1)} %get-tuple-element.33), channel_id=1, source_target_pairs={{0,9},{1,8},{2,11},{3,10},{4,13},{5,12},{6,15},{7,14},{8,1},{9,0},... | collective-permute-start | bytes 82952 | tf_op jit(solution)/shard_map/ppermute | solution.py:79
  28.1 25.3 %copy-start.5 = (bf16[4,8192]{1,0:T(4,128)(2,1)S(1)}, bf16[4,8192]{1,0:T(4,128)(2,1)}, u32[]{:S(2)}) copy-start(bf16[4,8192]{1,0:T(4,128)(2,1)} %refs_0_.1) | copy-start | bytes 196612
  28.1 5.9 %collective-permute-start.7 = (bf16[24,576]{1,0:T(8,128)(2,1)S(1)}, bf16[24,576]{1,0:T(8,128)(2,1)S(1)}, u32[]{:S(2)}, u32[]{:S(2)}) collective-permute-start(bf16[24,576]{1,0:T(8,128)(2,1)S(1)} %get-tuple-element.35), channel_id=1, source_target_pairs={{0,3},{1,2},{2,1},{3,0},{4,7},{5,6},{6,5},{7,4},{8,11},{9,10},{10,... | collective-permute-start | bytes 82952 | tf_op jit(solution)/shard_map/ppermute | solution.py:79
  29.1 5.0 %collective-permute-start.8 = (bf16[24,576]{1,0:T(8,128)(2,1)S(1)}, bf16[24,576]{1,0:T(8,128)(2,1)S(1)}, u32[]{:S(2)}, u32[]{:S(2)}) collective-permute-start(bf16[24,576]{1,0:T(8,128)(2,1)S(1)} %get-tuple-element.35), channel_id=1, source_target_pairs={{0,5},{1,4},{2,7},{3,6},{4,1},{5,0},{6,3},{7,2},{8,13},{9,12},{10,... | collective-permute-start | bytes 82952 | tf_op jit(solution)/shard_map/ppermute | solution.py:79
  30.6 4.8 %collective-permute-start.9 = (bf16[24,576]{1,0:T(8,128)(2,1)S(1)}, bf16[24,576]{1,0:T(8,128)(2,1)S(1)}, u32[]{:S(2)}, u32[]{:S(2)}) collective-permute-start(bf16[24,576]{1,0:T(8,128)(2,1)S(1)} %get-tuple-element.35), channel_id=1, source_target_pairs={{0,6},{1,7},{2,4},{3,5},{4,2},{5,3},{6,0},{7,1},{8,14},{9,15},{10,... | collective-permute-start | bytes 82952 | tf_op jit(solution)/shard_map/ppermute | solution.py:79
  35.6 1.2 %collective-permute-start.10 = (bf16[24,576]{1,0:T(8,128)(2,1)S(1)}, bf16[24,576]{1,0:T(8,128)(2,1)S(1)}, u32[]{:S(2)}, u32[]{:S(2)}) collective-permute-start(bf16[24,576]{1,0:T(8,128)(2,1)S(1)} %get-tuple-element.36), channel_id=1, source_target_pairs={{0,1},{1,0},{2,3},{3,2},{4,5},{5,4},{6,7},{7,6},{8,9},{9,8},{10,11... | collective-permute-start | bytes 82952 | tf_op jit(solution)/shard_map/ppermute | solution.py:79
  39.1 1.8 %collective-permute-start.11 = (bf16[1536,128]{1,0:T(8,128)(2,1)S(1)}, bf16[1536,128]{1,0:T(8,128)(2,1)S(1)}, u32[]{:S(2)}, u32[]{:S(2)}) collective-permute-start(bf16[1536,128]{1,0:T(8,128)(2,1)S(1)} %get-tuple-element.42), channel_id=1, source_target_pairs={{0,1},{1,0},{2,3},{3,2},{4,5},{5,4},{6,7},{7,6},{8,9},{9,8},{10,11... | collective-permute-start | bytes 1179656 | tf_op jit(solution)/shard_map/ppermute | solution.py:79
  41.0 5.8 %collective-permute-start.12 = (bf16[384,128]{1,0:T(8,128)(2,1)S(1)}, bf16[384,128]{1,0:T(8,128)(2,1)S(1)}, u32[]{:S(2)}, u32[]{:S(2)}) collective-permute-start(bf16[384,128]{1,0:T(8,128)(2,1)S(1)} %get-tuple-element.44), channel_id=1, source_target_pairs={{0,4},{1,5},{2,6},{3,7},{4,0},{5,1},{6,2},{7,3},{8,12},{9,13},{10,... | collective-permute-start | bytes 294920 | tf_op jit(solution)/shard_map/ppermute | solution.py:79
  41.5 5.2 %collective-permute-start.13 = (bf16[384,128]{1,0:T(8,128)(2,1)S(1)}, bf16[384,128]{1,0:T(8,128)(2,1)S(1)}, u32[]{:S(2)}, u32[]{:S(2)}) collective-permute-start(bf16[384,128]{1,0:T(8,128)(2,1)S(1)} %get-tuple-element.45), channel_id=1, source_target_pairs={{0,2},{1,3},{2,0},{3,1},{4,6},{5,7},{6,4},{7,5},{8,10},{9,11},{10,... | collective-permute-start | bytes 294920 | tf_op jit(solution)/shard_map/ppermute | solution.py:79
  42.5 5.8 %collective-permute-start.14 = (bf16[384,128]{1,0:T(8,128)(2,1)S(1)}, bf16[384,128]{1,0:T(8,128)(2,1)S(1)}, u32[]{:S(2)}, u32[]{:S(2)}) collective-permute-start(bf16[384,128]{1,0:T(8,128)(2,1)S(1)} %get-tuple-element.46), channel_id=1, source_target_pairs={{0,6},{1,7},{2,4},{3,5},{4,2},{5,3},{6,0},{7,1},{8,14},{9,15},{10,... | collective-permute-start | bytes 294920 | tf_op jit(solution)/shard_map/ppermute | solution.py:79
  48.4 5.1 %collective-permute-start.15 = (bf16[192,128]{1,0:T(8,128)(2,1)S(1)}, bf16[192,128]{1,0:T(8,128)(2,1)S(1)}, u32[]{:S(2)}, u32[]{:S(2)}) collective-permute-start(bf16[192,128]{1,0:T(8,128)(2,1)S(1)} %get-tuple-element.51), channel_id=1, source_target_pairs={{0,8},{1,9},{2,10},{3,11},{4,12},{5,13},{6,14},{7,15},{8,0},{9,1},... | collective-permute-start | bytes 147464 | tf_op jit(solution)/shard_map/ppermute | solution.py:79
